TPU v7x, 32 devices: a whole 2x2x4 slice. The times are simulated.
32 devices in a mesh: region: 2 (over x), range: 8 (over z, y), radial: 2 (over core).
Axes of the slice: x: 2, y: 2, z: 4, core: 2. Of those that a mesh axis runs over, the one named last changes fastest.
Arguments:
- refractivity: bfloat16 [512, 16, 4096], P(('region', 'radial'), None, 'range'), parts along dimension 0, may hold values from -6 to 6
- source: float32 [2, 8192], P(None, 'region'), parts along dimension 1, may hold values from -6 to 6
- terrain: int32 [512, 16], P(('region', 'radial'), 'range'), parts along dimension 0, may hold values from 0 to 511
- tile_map: int32 [512, 16], P(('region', 'radial'), 'range'), parts along dimension 0, may hold values from 0 to 255, as said below
Outputs:
- coverage: float32 [512, 128], P(('region', 'range', 'radial')), parts along dimension 0
There are 2 independent parts, one for each index of `region`. A program takes and returns all parts, laid end to end along the dimension named above; each array names one. Nothing has to cross between parts.
Inputs may be any that keep to these rules, and one draw needn't show every extreme that they name: `tile_map`: every tile number is named by at least one radial and step.
All inputs are finite; a program needn't handle non-finite values.
Results may differ from a plain program's by a relative error of at most 0.0003.
Values may be sent and summed in bfloat16 or wider, within the bound.
No kernel may reach another device: no remote copies, remote signals or barrier semaphores. Data moves between devices by JAX's collectives and lax.ppermute only.
A program may use at most 64 MiB of HBM per device.

v0:
```python
import math

import jax
import jax.numpy as jnp
from jax import lax
from jax.sharding import PartitionSpec as P

H = 4096
FA = 64
BIN = 32
TILE_DEV = 16


TILT_SLOPE = 2.0
SPREAD_RATE = 0.5
ABSORB_RATE = 0.05
PRECISE = lax.Precision.HIGHEST


def passed_along(value, axis, steps):
    count = lax.axis_size(axis)
    initial, last = (max(0, -steps), min(count, count - steps))
    return lax.ppermute(value, axis, [(source, source + steps) for source in range(initial, last)])


def dft_table(extent):
    indices = jnp.arange(extent, dtype=jnp.int32)
    product = indices[:, None] * indices[None, :] % extent
    angles = -2.0 * math.pi / extent * product.astype(jnp.float32)
    return (jnp.cos(angles), jnp.sin(angles))


def make_tables(height, factor):
    factor_b = height // factor
    inner_table = dft_table(factor_b)
    outer_table = dft_table(factor)
    q_second = jnp.arange(factor_b, dtype=jnp.int32)[:, None]
    n_first = jnp.arange(factor, dtype=jnp.int32)[None, :]
    twiddle_angle = -2.0 * math.pi / height * (q_second * n_first).astype(jnp.float32)
    twiddle = (jnp.cos(twiddle_angle), jnp.sin(twiddle_angle))
    frequency = n_first * factor_b + q_second
    signed = jnp.where(frequency >= height // 2, frequency - height, frequency).astype(jnp.float32)
    wavenumber = 2.0 * math.pi / height * signed
    turning = -SPREAD_RATE * wavenumber * wavenumber
    spreading = (jnp.cos(turning), jnp.sin(turning))
    return (inner_table, outer_table, twiddle, spreading)


def complex_mix(pattern, real_part, imag_part, matrix_real, matrix_imag):

    def single(operand, matrix):
        return jnp.einsum(pattern, operand, matrix, precision=PRECISE)

    return (
        single(real_part, matrix_real) - single(imag_part, matrix_imag),
        single(real_part, matrix_imag) + single(imag_part, matrix_real),
    )


def propagate(wave_field, tables):
    inner_table, outer_table, twiddle, spreading = tables
    batch_rows = wave_field.shape[1]
    height = wave_field.shape[2]
    factor = outer_table[0].shape[0]
    factor_b = inner_table[0].shape[0]
    real_part = wave_field[0].reshape(batch_rows, factor_b, factor)
    imag_part = wave_field[1].reshape(batch_rows, factor_b, factor)
    real_part, imag_part = complex_mix(
        "bkn,kq->bqn", real_part, imag_part, inner_table[0], inner_table[1]
    )
    real_part, imag_part = (
        real_part * twiddle[0] - imag_part * twiddle[1],
        real_part * twiddle[1] + imag_part * twiddle[0],
    )
    real_part, imag_part = complex_mix(
        "bqn,nm->bqm", real_part, imag_part, outer_table[0], outer_table[1]
    )
    real_part, imag_part = (
        real_part * spreading[0] - imag_part * spreading[1],
        real_part * spreading[1] + imag_part * spreading[0],
    )
    real_part, imag_part = complex_mix(
        "bqm,mn->bqn", real_part, imag_part, outer_table[0], -outer_table[1]
    )
    real_part, imag_part = (
        real_part * twiddle[0] + imag_part * twiddle[1],
        imag_part * twiddle[0] - real_part * twiddle[1],
    )
    real_part, imag_part = complex_mix(
        "bqn,qk->bkn", real_part, imag_part, inner_table[0], -inner_table[1]
    )
    normalize = 1.0 / height
    return (
        real_part.reshape(batch_rows, height) * normalize,
        imag_part.reshape(batch_rows, height) * normalize,
    )


def advance(wave_field, refract_rows, terrain_rows, tables):
    height = wave_field.shape[2]
    real_part, imag_part = propagate(wave_field, tables)
    height_index = jnp.arange(height, dtype=jnp.int32)
    relative = height_index.astype(jnp.float32) / height
    top_depth = jnp.maximum(relative - 0.75, 0.0) * 4.0
    phase_angle = refract_rows.astype(jnp.float32) + TILT_SLOPE * relative
    retained = jnp.where(
        height_index[None, :] >= terrain_rows[:, None],
        jnp.exp(-ABSORB_RATE * top_depth * top_depth),
        0.0,
    )
    cosine = jnp.cos(phase_angle)
    sine_part = jnp.sin(phase_angle)
    new_real = (real_part * cosine - imag_part * sine_part) * retained
    new_imag = (real_part * sine_part + imag_part * cosine) * retained
    return jnp.stack([new_real, new_imag])


def bin_power(wave_field, bin_width):
    energy = wave_field[0] * wave_field[0] + wave_field[1] * wave_field[1]
    return jnp.mean(energy.reshape(energy.shape[0], -1, bin_width), axis=2)


def tile_onehot(tile_ids, cell_tiles):
    return (tile_ids[:, None] == cell_tiles[None, :]).astype(jnp.float32)


def local(refractivity, source, terrain, tile_map):
    tables = make_tables(H, FA)
    tiles = TILE_DEV * lax.axis_size("range") * lax.axis_size("radial")
    tile_ids = jnp.arange(tiles, dtype=jnp.int32)
    totals = jnp.zeros((tiles, H // BIN), jnp.float32)
    levels = lax.all_to_all(refractivity, "range", split_axis=1, concat_axis=2, tiled=True)
    groups = 8
    batch_width = levels.shape[0] // groups
    local_steps = levels.shape[1]
    tile_counts = jnp.sum(tile_onehot(tile_ids, tile_map.reshape(-1)), axis=1)
    sections = lax.axis_size("range")
    section = lax.axis_index("range")
    launch = jnp.broadcast_to(source[:, None, :], (2, batch_width, H))

    def march_batch(inbound, running, batch_index):
        wave_field = jnp.where(section == 0, launch, inbound)
        refract_rows = lax.dynamic_slice_in_dim(levels, batch_index * batch_width, batch_width, 0)
        terrain_rows = lax.dynamic_slice_in_dim(terrain, batch_index * batch_width, batch_width, 0)
        cell_rows = lax.dynamic_slice_in_dim(tile_map, batch_index * batch_width, batch_width, 0)
        for step_index in range(local_steps):
            wave_field = advance(
                wave_field, refract_rows[:, step_index], terrain_rows[:, step_index], tables
            )
            power = bin_power(wave_field, BIN)
            onehot = tile_onehot(tile_ids, cell_rows[:, step_index])
            running = running + jnp.dot(onehot, power, precision=PRECISE)
        return (wave_field, running)

    def clock_tick(state_pair, tick_index):
        inbound, running = state_pair
        batch_index = tick_index - section
        active = jnp.logical_and(batch_index >= 0, batch_index < groups)
        clipped = jnp.clip(batch_index, 0, groups - 1)

        def busy_branch():
            return march_batch(inbound, running, clipped)

        def waiting_branch():
            return (jnp.zeros_like(inbound), running)

        outgoing, running = lax.cond(active, busy_branch, waiting_branch)
        inbound = passed_along(outgoing, "range", 1)
        return ((inbound, running), None)

    empty_field = jnp.zeros((2, batch_width, H), jnp.float32)
    ticks = jnp.arange(groups + sections - 1, dtype=jnp.int32)
    (_, totals), _ = lax.scan(clock_tick, (empty_field, totals), ticks)
    owned_totals, owned_counts = (
        lax.psum_scatter(totals, ("range", "radial"), scatter_dimension=0, tiled=True),
        lax.psum_scatter(tile_counts, ("range", "radial"), scatter_dimension=0, tiled=True),
    )
    return owned_totals / owned_counts[:, None]


def solution(mesh):
    in_specs = (
        P(("region", "radial"), None, "range"),
        P(None, "region"),
        P(("region", "radial"), "range"),
        P(("region", "radial"), "range"),
    )
    out_specs = P(("region", "range", "radial"), None)
    return jax.shard_map(local, mesh=mesh, in_specs=in_specs, out_specs=out_specs, check_vma=False)
```

profile of v0, /device:TPU:0, one launch (start us, length us, event | category | flops | bytes accessed | tf_op | source)
XLA Modules:
  0.0 1320.0 jit_solution(11332104106141007220)
XLA Ops:
  6.5 4.1 copy.182
  10.6 7.3 all-to-all-start
  18.5 47.6 %all-to-all-done = bf16[128,16,512]{2,0,1:T(8,128)(2,1)S(1)} async-done(((bf16[128,16,512]{2,0,1:T(8,128)(2,1)}), bf16[128,16,512]{2,0,1:T(8,128)(2,1)S(1)}, u32[]{:S(2)}, u32[]{:S(2)}) %all-to-all-start) | async-done | bytes 2097184 | tf_op jit(solution)/shard_map/all_to_all | solution.py:132
  68.3 995.0 %while.19 = (s32[]{:T(128)}, f32[2,16,4096]{2,1,0:T(8,128)S(1)}, f32[256,128]{1,0:T(8,128)S(1)}, s32[15]{0:T(128)}, s32[]{:T(128)}, /*index=5*/bf16[128,2,4096]{...) while((s32[]{:T(128)}, f32[2,16,4096]{2,1,0:T(8,128)S(1)}, ...), condition=%wide.region_5.6_spmd.clone.clone.clone, body=%wide.region_0.5_spmd.clone.clone.clone.sunk | while | flops 1633443840 | bytes 51172832 | solution.py:173
  71.2 64.3 %conditional.5 = (f32[2,16,4096]{2,1,0:T(8,128)}, f32[256,128]{1,0:T(8,128)S(1)}) conditional(s32[]{:T(128)} %convert_element_type.275, f32[256,128]{1,0:T(8,128)S(1)} %get-tuple-element.1145, (s32[]{:T(128)}, f32[2,4096]{1,0:T(2,128)}, f32[2,16,4096]{2,1,0:T(8,128)S(1)}, f32[64,64]{1,0:T(8,128)S(1)}, f32[64,64]{1,0:T(8,128)S(1)}, ...), branch_computations={%region_1.1_spmd, %region_2.4_spmd.clone} | conditional | flops 1633341440 | bytes 49024908 | solution.py:167
  91.4 3.7 select_multiply_fusion.4
  120.5 2.3 mul.1488
  124.5 10.2 fusion.34
  136.8 10.6 collective-permute-done
  150.3 64.1 %conditional.5 = (f32[2,16,4096]{2,1,0:T(8,128)}, f32[256,128]{1,0:T(8,128)S(1)}) conditional(s32[]{:T(128)} %convert_element_type.275, f32[256,128]{1,0:T(8,128)S(1)} %get-tuple-element.1145, (s32[]{:T(128)}, f32[2,4096]{1,0:T(2,128)}, f32[2,16,4096]{2,1,0:T(8,128)S(1)}, f32[64,64]{1,0:T(8,128)S(1)}, f32[64,64]{1,0:T(8,128)S(1)}, ...), branch_computations={%region_1.1_spmd, %region_2.4_spmd.clone} | conditional | flops 1633341440 | bytes 49024908 | solution.py:167
  170.7 3.7 select_multiply_fusion.4
  199.4 2.3 mul.1488
  203.4 10.2 fusion.34
  214.4 4.3 collective-permute-start
  218.7 9.6 collective-permute-done
  231.5 64.1 %conditional.5 = (f32[2,16,4096]{2,1,0:T(8,128)}, f32[256,128]{1,0:T(8,128)S(1)}) conditional(s32[]{:T(128)} %convert_element_type.275, f32[256,128]{1,0:T(8,128)S(1)} %get-tuple-element.1145, (s32[]{:T(128)}, f32[2,4096]{1,0:T(2,128)}, f32[2,16,4096]{2,1,0:T(8,128)S(1)}, f32[64,64]{1,0:T(8,128)S(1)}, f32[64,64]{1,0:T(8,128)S(1)}, ...), branch_computations={%region_1.1_spmd, %region_2.4_spmd.clone} | conditional | flops 1633341440 | bytes 49024908 | solution.py:167
  251.5 3.7 select_multiply_fusion.4
  280.3 2.3 mul.1488
  284.3 10.2 fusion.34
  295.6 4.1 collective-permute-start
  299.7 8.7 collective-permute-done
  311.3 64.0 %conditional.5 = (f32[2,16,4096]{2,1,0:T(8,128)}, f32[256,128]{1,0:T(8,128)S(1)}) conditional(s32[]{:T(128)} %convert_element_type.275, f32[256,128]{1,0:T(8,128)S(1)} %get-tuple-element.1145, (s32[]{:T(128)}, f32[2,4096]{1,0:T(2,128)}, f32[2,16,4096]{2,1,0:T(8,128)S(1)}, f32[64,64]{1,0:T(8,128)S(1)}, f32[64,64]{1,0:T(8,128)S(1)}, ...), branch_computations={%region_1.1_spmd, %region_2.4_spmd.clone} | conditional | flops 1633341440 | bytes 49024908 | solution.py:167
  331.4 3.7 select_multiply_fusion.4
  364.3 10.2 fusion.34
  375.3 4.7 collective-permute-start
  380.0 7.8 collective-permute-done
  390.7 64.1 %conditional.5 = (f32[2,16,4096]{2,1,0:T(8,128)}, f32[256,128]{1,0:T(8,128)S(1)}) conditional(s32[]{:T(128)} %convert_element_type.275, f32[256,128]{1,0:T(8,128)S(1)} %get-tuple-element.1145, (s32[]{:T(128)}, f32[2,4096]{1,0:T(2,128)}, f32[2,16,4096]{2,1,0:T(8,128)S(1)}, f32[64,64]{1,0:T(8,128)S(1)}, f32[64,64]{1,0:T(8,128)S(1)}, ...), branch_computations={%region_1.1_spmd, %region_2.4_spmd.clone} | conditional | flops 1633341440 | bytes 49024908 | solution.py:167
  411.0 3.7 select_multiply_fusion.4
  443.8 10.2 fusion.34
  454.8 4.2 collective-permute-start
  458.9 7.1 collective-permute-done
  469.2 64.1 %conditional.5 = (f32[2,16,4096]{2,1,0:T(8,128)}, f32[256,128]{1,0:T(8,128)S(1)}) conditional(s32[]{:T(128)} %convert_element_type.275, f32[256,128]{1,0:T(8,128)S(1)} %get-tuple-element.1145, (s32[]{:T(128)}, f32[2,4096]{1,0:T(2,128)}, f32[2,16,4096]{2,1,0:T(8,128)S(1)}, f32[64,64]{1,0:T(8,128)S(1)}, f32[64,64]{1,0:T(8,128)S(1)}, ...), branch_computations={%region_1.1_spmd, %region_2.4_spmd.clone} | conditional | flops 1633341440 | bytes 49024908 | solution.py:167
  489.3 3.7 select_multiply_fusion.4
  518.1 2.3 mul.1488
  522.1 10.2 fusion.34
  533.3 5.4 collective-permute-start
  538.7 7.0 collective-permute-done
  548.6 64.0 %conditional.5 = (f32[2,16,4096]{2,1,0:T(8,128)}, f32[256,128]{1,0:T(8,128)S(1)}) conditional(s32[]{:T(128)} %convert_element_type.275, f32[256,128]{1,0:T(8,128)S(1)} %get-tuple-element.1145, (s32[]{:T(128)}, f32[2,4096]{1,0:T(2,128)}, f32[2,16,4096]{2,1,0:T(8,128)S(1)}, f32[64,64]{1,0:T(8,128)S(1)}, f32[64,64]{1,0:T(8,128)S(1)}, ...), branch_computations={%region_1.1_spmd, %region_2.4_spmd.clone} | conditional | flops 1633341440 | bytes 49024908 | solution.py:167
  568.7 3.7 select_multiply_fusion.4
  601.6 10.2 fusion.34
  612.5 5.4 collective-permute-start
  618.0 7.0 collective-permute-done
  627.9 64.1 %conditional.5 = (f32[2,16,4096]{2,1,0:T(8,128)}, f32[256,128]{1,0:T(8,128)S(1)}) conditional(s32[]{:T(128)} %convert_element_type.275, f32[256,128]{1,0:T(8,128)S(1)} %get-tuple-element.1145, (s32[]{:T(128)}, f32[2,4096]{1,0:T(2,128)}, f32[2,16,4096]{2,1,0:T(8,128)S(1)}, f32[64,64]{1,0:T(8,128)S(1)}, f32[64,64]{1,0:T(8,128)S(1)}, ...), branch_computations={%region_1.1_spmd, %region_2.4_spmd.clone} | conditional | flops 1633341440 | bytes 49024908 | solution.py:167
  648.2 3.7 select_multiply_fusion.4
  680.9 10.2 fusion.34
  692.0 4.8 collective-permute-start
  696.8 7.0 collective-permute-done
  706.9 6.7 conditional.5
  713.6 62.8 %collective-permute-start = (f32[2,16,4096]{2,1,0:T(8,128)}, f32[2,16,4096]{2,1,0:T(8,128)S(1)}, u32[]{:S(2)}, u32[]{:S(2)}) collective-permute-start(f32[2,16,4096]{2,1,0:T(8,128)} %get-tuple-element.1124), channel_id=1, source_target_pairs={{0,2},{2,4},{4,6},{6,8},{8,10},{10,12},{12,14},{1,3},{3,5},{5,7},{... | collective-permute-start | bytes 1572872 | tf_op jit(solution)/shard_map/while/body/eval_jaxpr/ppermute | solution.py:23
  776.4 7.0 collective-permute-done
  787.1 11.2 collective-permute-start
  798.3 7.0 collective-permute-done
  808.8 62.5 %collective-permute-start = (f32[2,16,4096]{2,1,0:T(8,128)}, f32[2,16,4096]{2,1,0:T(8,128)S(1)}, u32[]{:S(2)}, u32[]{:S(2)}) collective-permute-start(f32[2,16,4096]{2,1,0:T(8,128)} %get-tuple-element.1124), channel_id=1, source_target_pairs={{0,2},{2,4},{4,6},{6,8},{8,10},{10,12},{12,14},{1,3},{3,5},{5,7},{... | collective-permute-start | bytes 1572872 | tf_op jit(solution)/shard_map/while/body/eval_jaxpr/ppermute | solution.py:23
  871.4 7.0 collective-permute-done
  881.9 11.3 collective-permute-start
  893.3 7.0 collective-permute-done
  903.8 58.4 %collective-permute-start = (f32[2,16,4096]{2,1,0:T(8,128)}, f32[2,16,4096]{2,1,0:T(8,128)S(1)}, u32[]{:S(2)}, u32[]{:S(2)}) collective-permute-start(f32[2,16,4096]{2,1,0:T(8,128)} %get-tuple-element.1124), channel_id=1, source_target_pairs={{0,2},{2,4},{4,6},{6,8},{8,10},{10,12},{12,14},{1,3},{3,5},{5,7},{... | collective-permute-start | bytes 1572872 | tf_op jit(solution)/shard_map/while/body/eval_jaxpr/ppermute | solution.py:23
  962.2 7.0 collective-permute-done
  972.7 10.4 collective-permute-start
  983.2 7.0 collective-permute-done
  993.7 61.4 %collective-permute-start = (f32[2,16,4096]{2,1,0:T(8,128)}, f32[2,16,4096]{2,1,0:T(8,128)S(1)}, u32[]{:S(2)}, u32[]{:S(2)}) collective-permute-start(f32[2,16,4096]{2,1,0:T(8,128)} %get-tuple-element.1124), channel_id=1, source_target_pairs={{0,2},{2,4},{4,6},{6,8},{8,10},{10,12},{12,14},{1,3},{3,5},{5,7},{... | collective-permute-start | bytes 1572872 | tf_op jit(solution)/shard_map/while/body/eval_jaxpr/ppermute | solution.py:23
  1055.1 7.0 collective-permute-done
  1067.0 220.0 %all-reduce = f32[256]{0:T(256)S(1)} all-reduce(f32[256]{0:T(256)S(1)} %convert_reduce_fusion), channel_id=3, replica_groups=mesh['region'=2,'range'=8,'radial'=2] {'range','radial'}, use_global_device_ids=true, to_apply=%region_8.9.clone | all-reduce | flops 256 | bytes 2048
  1287.1 24.4 %reduce-scatter.2.cloned.1.call-done = f32[16,128]{1,0:T(8,128)} async-done(((f32[256,128]{1,0:T(8,128)}), f32[16,128]{1,0:T(8,128)}) %reduce-scatter.2.cloned.1.call-update) | async-done | bytes 8208 | tf_op jit(solution)/shard_map/reduce_scatter | solution.py:175
  (749 shorter events, 435.7 us)
Async XLA Ops:
  10.6 55.5 %all-to-all-start = ((bf16[128,16,512]{2,0,1:T(8,128)(2,1)}), bf16[128,16,512]{2,0,1:T(8,128)(2,1)S(1)}, u32[]{:S(2)}, u32[]{:S(2)}) async-start(bf16[128,16,512]{2,0,1:T(8,128)(2,1)} %copy.182), calls=%async_computation | async-start | bytes 4194304 | tf_op jit(solution)/shard_map/all_to_all | solution.py:132
  17.9 1293.6 %reduce-scatter.2.cloned.1.call-start = ((), (), s32[]{:S(2)}) async-start(), calls=%async_computation.2 | async-start | bytes 139264 | tf_op jit(solution)/shard_map/reduce_scatter | solution.py:175
  71.2 0.9 copy-start.2
  89.5 1.9 copy-start.1
  115.4 4.1 copy-start
  124.5 10.2 copy-start.3
  124.5 10.2 copy-start.5
  135.5 11.9 collective-permute-start
  150.4 0.9 copy-start.2
  168.8 1.9 copy-start.1
  194.3 4.1 copy-start
  203.4 10.2 copy-start.3
  203.4 10.2 copy-start.5
  214.4 13.9 %collective-permute-start = (f32[2,16,4096]{2,1,0:T(8,128)}, f32[2,16,4096]{2,1,0:T(8,128)S(1)}, u32[]{:S(2)}, u32[]{:S(2)}) collective-permute-start(f32[2,16,4096]{2,1,0:T(8,128)} %get-tuple-element.1124), channel_id=1, source_target_pairs={{0,2},{2,4},{4,6},{6,8},{8,10},{10,12},{12,14},{1,3},{3,5},{5,7},{... | collective-permute-start | bytes 1572872 | tf_op jit(solution)/shard_map/while/body/eval_jaxpr/ppermute | solution.py:23
  231.5 0.9 copy-start.2
  249.7 1.9 copy-start.1
  275.2 4.1 copy-start
  284.3 10.2 copy-start.3
  284.3 10.2 copy-start.5
  295.6 12.8 collective-permute-start
  311.3 0.9 copy-start.2
  329.5 1.9 copy-start.1
  355.2 4.1 copy-start
  364.3 10.2 copy-start.3
  364.3 10.2 copy-start.5
  375.3 12.5 collective-permute-start
  390.7 0.9 copy-start.2
  409.1 1.9 copy-start.1
  434.7 4.1 copy-start
  443.7 10.2 copy-start.3
  443.7 10.2 copy-start.5
  454.8 11.3 collective-permute-start
  469.2 0.9 copy-start.2
  487.4 1.9 copy-start.1
  513.0 4.1 copy-start
  522.1 10.2 copy-start.3
  522.1 10.2 copy-start.5
  533.3 12.4 collective-permute-start
  548.6 0.9 copy-start.2
  566.8 1.9 copy-start.1
  592.5 4.1 copy-start
  601.5 10.2 copy-start.3
  601.6 10.2 copy-start.5
  612.5 12.4 collective-permute-start
  627.9 0.9 copy-start.2
  646.3 1.9 copy-start.1
  671.9 4.1 copy-start
  680.9 10.2 copy-start.3
  680.9 10.2 copy-start.5
  692.0 11.8 collective-permute-start
  713.6 69.7 %collective-permute-start = (f32[2,16,4096]{2,1,0:T(8,128)}, f32[2,16,4096]{2,1,0:T(8,128)S(1)}, u32[]{:S(2)}, u32[]{:S(2)}) collective-permute-start(f32[2,16,4096]{2,1,0:T(8,128)} %get-tuple-element.1124), channel_id=1, source_target_pairs={{0,2},{2,4},{4,6},{6,8},{8,10},{10,12},{12,14},{1,3},{3,5},{5,7},{... | collective-permute-start | bytes 1572872 | tf_op jit(solution)/shard_map/while/body/eval_jaxpr/ppermute | solution.py:23
  787.1 18.1 %collective-permute-start = (f32[2,16,4096]{2,1,0:T(8,128)}, f32[2,16,4096]{2,1,0:T(8,128)S(1)}, u32[]{:S(2)}, u32[]{:S(2)}) collective-permute-start(f32[2,16,4096]{2,1,0:T(8,128)} %get-tuple-element.1124), channel_id=1, source_target_pairs={{0,2},{2,4},{4,6},{6,8},{8,10},{10,12},{12,14},{1,3},{3,5},{5,7},{... | collective-permute-start | bytes 1572872 | tf_op jit(solution)/shard_map/while/body/eval_jaxpr/ppermute | solution.py:23
  808.8 69.5 %collective-permute-start = (f32[2,16,4096]{2,1,0:T(8,128)}, f32[2,16,4096]{2,1,0:T(8,128)S(1)}, u32[]{:S(2)}, u32[]{:S(2)}) collective-permute-start(f32[2,16,4096]{2,1,0:T(8,128)} %get-tuple-element.1124), channel_id=1, source_target_pairs={{0,2},{2,4},{4,6},{6,8},{8,10},{10,12},{12,14},{1,3},{3,5},{5,7},{... | collective-permute-start | bytes 1572872 | tf_op jit(solution)/shard_map/while/body/eval_jaxpr/ppermute | solution.py:23
  881.9 18.3 %collective-permute-start = (f32[2,16,4096]{2,1,0:T(8,128)}, f32[2,16,4096]{2,1,0:T(8,128)S(1)}, u32[]{:S(2)}, u32[]{:S(2)}) collective-permute-start(f32[2,16,4096]{2,1,0:T(8,128)} %get-tuple-element.1124), channel_id=1, source_target_pairs={{0,2},{2,4},{4,6},{6,8},{8,10},{10,12},{12,14},{1,3},{3,5},{5,7},{... | collective-permute-start | bytes 1572872 | tf_op jit(solution)/shard_map/while/body/eval_jaxpr/ppermute | solution.py:23
  903.8 65.3 %collective-permute-start = (f32[2,16,4096]{2,1,0:T(8,128)}, f32[2,16,4096]{2,1,0:T(8,128)S(1)}, u32[]{:S(2)}, u32[]{:S(2)}) collective-permute-start(f32[2,16,4096]{2,1,0:T(8,128)} %get-tuple-element.1124), channel_id=1, source_target_pairs={{0,2},{2,4},{4,6},{6,8},{8,10},{10,12},{12,14},{1,3},{3,5},{5,7},{... | collective-permute-start | bytes 1572872 | tf_op jit(solution)/shard_map/while/body/eval_jaxpr/ppermute | solution.py:23
  972.7 17.4 %collective-permute-start = (f32[2,16,4096]{2,1,0:T(8,128)}, f32[2,16,4096]{2,1,0:T(8,128)S(1)}, u32[]{:S(2)}, u32[]{:S(2)}) collective-permute-start(f32[2,16,4096]{2,1,0:T(8,128)} %get-tuple-element.1124), channel_id=1, source_target_pairs={{0,2},{2,4},{4,6},{6,8},{8,10},{10,12},{12,14},{1,3},{3,5},{5,7},{... | collective-permute-start | bytes 1572872 | tf_op jit(solution)/shard_map/while/body/eval_jaxpr/ppermute | solution.py:23
  993.7 68.4 %collective-permute-start = (f32[2,16,4096]{2,1,0:T(8,128)}, f32[2,16,4096]{2,1,0:T(8,128)S(1)}, u32[]{:S(2)}, u32[]{:S(2)}) collective-permute-start(f32[2,16,4096]{2,1,0:T(8,128)} %get-tuple-element.1124), channel_id=1, source_target_pairs={{0,2},{2,4},{4,6},{6,8},{8,10},{10,12},{12,14},{1,3},{3,5},{5,7},{... | collective-permute-start | bytes 1572872 | tf_op jit(solution)/shard_map/while/body/eval_jaxpr/ppermute | solution.py:23
  1063.4 0.6 copy-start.4
Sparse Core Ops, SparseCore 0:
  1064.1 247.2 reduce-scatter.1
where the time goes:
time: 1330 us; the launch traced here: 1320 us
  starting transfers between devices  320 us (24%)
  matrix products  261 us (20%)
  blocking collectives  220 us (17%)
  waiting for transfers between devices  185 us (14%)
  local copies, waits for them, and re-layouts  153 us (12%)
  other arithmetic  140 us (11%)
  loops' own time  27.1 us (2%)
  between operations  14.4 us (1%)
    ppermute x15, starting transfers between devices, passed_along(): lax.ppermute(value, axis, [(source, source + steps) for source in range(i...  312 us
    dot_general x256, matrix products, single(): return jnp.einsum(pattern, operand, matrix, precision=PRECISE)  257 us
    unnamed x1, blocking collectives  220 us
    ppermute x15, waiting for transfers between devices, passed_along(): lax.ppermute(value, axis, [(source, source + steps) for source in range(i...  113 us
    reduce_sum x8, other arithmetic, bin_power(): return jnp.mean(energy.reshape(energy.shape[0], -1, bin_width), axis=2)  81.7 us
    all_to_all x1, waiting for transfers between devices, local(): lax.all_to_all(refractivity, 'range', split_axis=1, concat_axis=2, tiled=...  47.6 us
    mul x40, local copies, waits for them, and re-layouts, propagate(): real_part.reshape(batch_rows, height) * normalize  32 us
    mul x40, local copies, waits for them, and re-layouts, propagate(): imag_part.reshape(batch_rows, height) * normalize  30.7 us
  transfers between devices with their start and end apart: 17, of which 17 were waited for; matrix products, arithmetic and copies ran while one was open for 0% of the time, Pallas kernels for 0%

commit v1 on v0

v1 whole, which is shorter than its diff:
```python
import functools
import math

import jax
import jax.numpy as jnp
import ml_dtypes
import numpy as np
from jax import lax
from jax.experimental import pallas as pl
from jax.experimental.pallas import tpu as pltpu
from jax.sharding import PartitionSpec as P

H = 4096
BIN = 32
LANES = 128
ROWS = H // LANES
FOUR = 4
EIGHT = 8
BINS = H // BIN
TILE_DEV = 16
TILT_SLOPE = 2.0
SPREAD_RATE = 0.5
ABSORB_RATE = 0.05
TERRAIN_ROWS = 4
CHUNKS = (1.0,)
GROUP = 2

F32 = jnp.float32
BF16 = jnp.bfloat16


def split_np(table):
    high = table.astype(np.float32).astype(ml_dtypes.bfloat16)
    low = (table - high.astype(np.float64)).astype(ml_dtypes.bfloat16)
    return high, low


def tables():
    n = np.arange(LANES)
    angle = -2.0 * np.pi / LANES * (n[:, None] * n[None, :] % LANES)
    c, s = np.cos(angle), np.sin(angle)
    forward = np.block([[c, s], [-s, c]])
    inverse = np.block([[c, -s], [s, c]])
    weights = []
    for matrix in (forward, inverse):
        high, low = split_np(matrix)
        weights.append(np.concatenate([high, high, low], axis=0))
    q = np.arange(ROWS)
    angle = -2.0 * np.pi / H * (q[:, None] * n[None, :])
    twiddle = np.stack([np.cos(angle), np.sin(angle)]).astype(np.float32)
    frequency = q[:, None] + ROWS * n[None, :]
    signed = np.where(frequency >= H // 2, frequency - H, frequency)
    turning = -SPREAD_RATE * (2.0 * np.pi / H * signed) ** 2
    spread = (np.stack([np.cos(turning), np.sin(turning)]) / H).astype(np.float32)
    rel = np.arange(H).reshape(ROWS, LANES) / H
    tilt = (TILT_SLOPE * rel - 1.0).astype(np.float32)
    depth = np.maximum(rel - 0.75, 0.0) * 4.0
    absorb = np.exp(-ABSORB_RATE * depth * depth).astype(np.float32)
    bins = np.zeros((2 * LANES, BINS), np.float64)
    for lane in range(2 * LANES):
        bins[lane, (lane % LANES) // BIN :: LANES // BIN] = 1.0 / BIN
    return weights[0], weights[1], twiddle, spread, tilt, absorb, bins.astype(ml_dtypes.bfloat16)


def phase_polynomials():
    root = 2.0 ** 0.25
    sin_scale = root * math.sqrt(2.0)
    cos_scale = 2.0 * math.sqrt(2.0) / sin_scale
    limit = 7.001
    nodes = 0.5 * limit * limit * (1.0 + np.cos(np.pi * (np.arange(64) + 0.5) / 64))
    phi = np.sqrt(nodes)
    sine = np.polynomial.chebyshev.Chebyshev.fit(
        nodes, sin_scale * np.sin(phi / 4) / phi, 4, domain=[0, limit * limit]
    ).convert(kind=np.polynomial.Polynomial)
    cosine = np.polynomial.chebyshev.Chebyshev.fit(
        nodes, cos_scale * np.cos(phi / 4), 4, domain=[0, limit * limit]
    ).convert(kind=np.polynomial.Polynomial)
    return [float(v) for v in sine.coef], [float(v) for v in cosine.coef]


def unit(number, extent):
    angle = -2.0 * math.pi * (number % extent) / extent
    return math.cos(angle), math.sin(angle)


def cmul_const(value, factor):
    re, im = value
    c, s = factor
    if abs(s) < 1e-12 and c > 0:
        return value
    if abs(c) < 1e-12:
        return (im, -re) if s < 0 else (-im, re)
    return re * c - im * s, re * s + im * c


def add(a, b):
    return a[0] + b[0], a[1] + b[1]


def sub(a, b):
    return a[0] - b[0], a[1] - b[1]


def turn(a, sign):
    return (a[1], -a[0]) if sign < 0 else (-a[1], a[0])


def dft4(x, sign):
    a, b = add(x[0], x[2]), sub(x[0], x[2])
    c, d = add(x[1], x[3]), turn(sub(x[1], x[3]), sign)
    return [add(a, c), add(b, d), sub(a, c), sub(b, d)]


def eighth(a, sign):
    h = math.sqrt(0.5)
    re, im = a
    if sign < 0:
        return (re + im) * h, (im - re) * h
    return (re - im) * h, (re + im) * h


def dft8(x, sign):
    even = dft4(x[0::2], sign)
    odd = dft4(x[1::2], sign)
    odd = [odd[0], eighth(odd[1], sign), turn(odd[2], sign), turn(eighth(odd[3], sign), sign)]
    return [add(even[i], odd[i]) for i in range(4)] + [sub(even[i], odd[i]) for i in range(4)]


def split(value):
    high = value.astype(BF16)
    low = (value - high.astype(F32)).astype(BF16)
    return high, low


def march_kernel(
    steps, batch, heights, first,
    levels, terrain, cells, start_re, start_im, totals_in,
    w_forward, w_inverse, twiddle, spread, tilt, absorb, bins,
    end_re, end_im, totals,
    back_re, back_im, energy, power,
):
    sine, cosine = phase_polynomials()

    def enter(columns, jl, put_re, put_im):
        parts = dft4(columns, -1)
        for ql in range(FOUR):
            re, im = cmul_const(parts[ql], unit(ql * jl, ROWS))
            put_re[ql * EIGHT + jl] = re
            put_im[ql * EIGHT + jl] = im

    if first:
        for jl in range(EIGHT):
            columns = []
            for jh in range(FOUR):
                j = EIGHT * jh + jl
                shape = (batch, LANES)
                columns.append((
                    jnp.broadcast_to(start_re[j : j + 1, :], shape),
                    jnp.broadcast_to(start_im[j : j + 1, :], shape),
                ))
            enter(columns, jl, end_re, end_im)
    else:
        end_re[...] = start_re[...]
        end_im[...] = start_im[...]

    lane = lax.broadcasted_iota(jnp.int32, (batch, LANES), 1)

    def joined(pieces):
        re_high, re_low = split(jnp.concatenate([p[0] for p in pieces], axis=0))
        im_high, im_low = split(jnp.concatenate([p[1] for p in pieces], axis=0))
        return jnp.concatenate([re_high, im_high, re_low, im_low, re_high, im_high], axis=1)

    def parted(product, count):
        return [
            (product[i * batch : (i + 1) * batch, :LANES], product[i * batch : (i + 1) * batch, LANES:])
            for i in range(count)
        ]

    def step(t, carry):
        for base in range(0, FOUR, GROUP):
            qs = [ql + FOUR * qh for ql in range(base, base + GROUP) for qh in range(EIGHT)]
            pieces = []
            for ql in range(base, base + GROUP):
                column = [(end_re[ql * EIGHT + jl], end_im[ql * EIGHT + jl]) for jl in range(EIGHT)]
                for qh, (re, im) in enumerate(dft8(column, -1)):
                    q = ql + FOUR * qh
                    c, s = twiddle[0, q : q + 1, :], twiddle[1, q : q + 1, :]
                    pieces.append((re * c - im * s, re * s + im * c))
            product = jnp.dot(joined(pieces), w_forward[...], preferred_element_type=F32)
            pieces = []
            for q, (re, im) in zip(qs, parted(product, len(qs))):
                c, s = spread[0, q : q + 1, :], spread[1, q : q + 1, :]
                pieces.append((re * c - im * s, re * s + im * c))
            product = jnp.dot(joined(pieces), w_inverse[...], preferred_element_type=F32)
            pieces = []
            for q, (re, im) in zip(qs, parted(product, len(qs))):
                c, s = twiddle[0, q : q + 1, :], twiddle[1, q : q + 1, :]
                pieces.append((re * c + im * s, im * c - re * s))
            for i in range(GROUP):
                column = dft8(pieces[i * EIGHT : (i + 1) * EIGHT], 1)
                for jl in range(EIGHT):
                    back_re[(base + i) * EIGHT + jl] = column[jl][0]
                    back_im[(base + i) * EIGHT + jl] = column[jl][1]

        for jl in range(EIGHT):
            column = []
            for ql in range(FOUR):
                c, s = unit(ql * jl, ROWS)
                column.append(cmul_const((back_re[ql * EIGHT + jl], back_im[ql * EIGHT + jl]), (c, -s)))
            column = dft4(column, 1)
            moved = []
            for jh in range(FOUR):
                j = EIGHT * jh + jl
                place = j * LANES
                raw = levels[place // heights, t, :, place % heights : place % heights + LANES]
                phi = raw.astype(F32) + tilt[j : j + 1, :]
                u = phi * phi
                sin_poly, cos_poly = sine[-1], cosine[-1]
                for a, b in zip(sine[-2::-1], cosine[-2::-1]):
                    sin_poly = sin_poly * u + a
                    cos_poly = cos_poly * u + b
                small = sin_poly * phi
                double = small * cos_poly
                turned_c = 1.0 - double * double
                turned_s = double * (math.sqrt(2.0) - small * small)
                re, im = column[jh]
                if (j + 1) * LANES > 3 * H // 4:
                    loss = absorb[j : j + 1, :]
                    re, im = re * loss, im * loss
                re, im = re * turned_c - im * turned_s, re * turned_s + im * turned_c
                if j < TERRAIN_ROWS:
                    open_air = lane + j * LANES >= terrain[t]
                    re, im = jnp.where(open_air, re, 0.0), jnp.where(open_air, im, 0.0)
                high, low = split(re * re + im * im)
                energy[j * batch : (j + 1) * batch, :] = jnp.concatenate([high, low], axis=1)
                moved.append((re, im))
            enter(moved, jl, end_re, end_im)

        summed = jnp.dot(energy[...], bins[...], preferred_element_type=F32)
        row = summed[:batch]
        for j in range(1, ROWS):
            row = jnp.where(lane // (LANES // BIN) == j, summed[j * batch : (j + 1) * batch], row)
        power[pl.ds(pl.multiple_of(t * batch, batch), batch), :] = row
        return carry

    lax.fori_loop(0, steps, step, 0)

    count = steps * batch
    tiles = totals.shape[0]
    hot = (lax.broadcasted_iota(jnp.int32, (tiles, count), 0) == cells[...]).astype(F32).astype(BF16)
    value = power[...]
    high, rest = value.astype(BF16), None
    rest = value - high.astype(F32)
    middle = rest.astype(BF16)
    low = (rest - middle.astype(F32)).astype(BF16)
    gain = jnp.dot(hot, high, preferred_element_type=F32)
    gain += jnp.dot(hot, middle, preferred_element_type=F32)
    gain += jnp.dot(hot, low, preferred_element_type=F32)
    if first:
        totals[...] = gain
    else:
        totals[...] = totals_in[...] + gain


def march(levels, terrain, cells, start, totals, consts, tiles, first):
    sources, steps, batch, heights = levels.shape
    state = jax.ShapeDtypeStruct((ROWS, batch, LANES), F32)
    vmem = pl.BlockSpec(memory_space=pltpu.VMEM)
    call = pl.pallas_call(
        functools.partial(march_kernel, steps, batch, heights, first),
        out_shape=(state, state, jax.ShapeDtypeStruct((tiles, BINS), F32)),
        in_specs=[vmem] * 13,
        out_specs=(vmem, vmem, vmem),
        scratch_shapes=[
            pltpu.VMEM((ROWS, batch, LANES), F32),
            pltpu.VMEM((ROWS, batch, LANES), F32),
            pltpu.VMEM((ROWS * batch, 2 * LANES), BF16),
            pltpu.VMEM((steps * batch, BINS), F32),
        ],
        compiler_params=pltpu.CompilerParams(vmem_limit_bytes=48 * 1024 * 1024),
        cost_estimate=pl.CostEstimate(
            flops=steps * batch * H * 3 * 8 * LANES, bytes_accessed=4 * 1024 * 1024, transcendentals=0
        ),
    )
    return call(levels, terrain, cells, *start, totals, *consts)


def local(refractivity, source, terrain, tile_map):
    sections = lax.axis_size("range")
    owners = sections * lax.axis_size("radial")
    tiles = TILE_DEV * owners
    radials, steps, heights = refractivity.shape
    own = radials // sections
    batch = -(-own // 16) * 16

    small = jnp.stack([terrain, tile_map])
    everyone = lax.all_gather(small, ("range", "radial"))
    everyone = everyone.reshape(sections, lax.axis_size("radial"), *small.shape)
    my_ids = (lax.axis_index("range") * lax.axis_size("radial") + lax.axis_index("radial")) * TILE_DEV
    my_ids = my_ids + jnp.arange(TILE_DEV, dtype=jnp.int32)
    counts = jnp.sum(
        (my_ids[:, None] == everyone[:, :, 1].reshape(1, -1)).astype(F32), axis=1
    )
    mine = lax.dynamic_index_in_dim(everyone, lax.axis_index("radial"), 1, keepdims=False)
    mine = lax.dynamic_slice_in_dim(mine, lax.axis_index("range") * own, own, 2)
    mine = jnp.transpose(mine, (1, 0, 3, 2)).reshape(2, steps, own)
    pad = ((0, 0), (0, batch - own))
    terrain_all = jnp.pad(mine[0], pad)
    cells_all = jnp.pad(mine[1], pad, constant_values=-1)
    terrain_all = jnp.broadcast_to(terrain_all[:, :, None], (steps, batch, LANES))

    consts = [jnp.asarray(v) for v in tables()]
    edges = [0]
    for share in CHUNKS:
        edges.append(edges[-1] + max(1, round(share * steps)))
    start = (source[0].reshape(ROWS, LANES), source[1].reshape(ROWS, LANES))
    totals = jnp.zeros((tiles, BINS), F32)
    pieces = []
    for begin, end in zip(edges[:-1], edges[1:]):
        piece = refractivity[:, begin:end].reshape(sections, own, end - begin, heights)
        piece = jnp.transpose(piece, (0, 2, 1, 3))
        pieces.append(lax.all_to_all(piece, "range", 0, 0, tiled=True))
    for piece, begin, end in zip(pieces, edges[:-1], edges[1:]):
        piece = jnp.pad(piece, ((0, 0), (0, 0), (0, batch - own), (0, 0)))
        *start, totals = march(
            piece, terrain_all[begin:end], cells_all[begin:end].reshape(1, -1),
            start, totals, consts, tiles, begin == 0,
        )
    sent = lax.all_to_all(
        totals.reshape(owners, TILE_DEV, BINS), ("range", "radial"), 0, 0, tiled=True
    )
    return jnp.sum(sent, axis=0) / counts[:, None]


def solution(mesh):
    in_specs = (
        P(("region", "radial"), None, "range"),
        P(None, "region"),
        P(("region", "radial"), "range"),
        P(("region", "radial"), "range"),
    )
    out_specs = P(("region", "range", "radial"), None)
    return jax.shard_map(local, mesh=mesh, in_specs=in_specs, out_specs=out_specs, check_vma=False)
```

time: 1330 us -> 105 us (0.08)
  starting transfers between devices: 320 us -> 17.8 us
  matrix products: 261 us -> 0 us
  waiting for transfers between devices: 185 us -> 6.84 us
  blocking collectives: 220 us -> 50.7 us
  local copies, waits for them, and re-layouts: 153 us -> 5.36 us
  other arithmetic: 140 us -> 0.92 us
  loops' own time: 27.1 us -> 0 us
  Pallas kernels: 0 us -> 22.6 us
  between operations: 14.4 us -> 0.21 us
    ppermute x15 -> x0, starting transfers between devices: 312 us -> none  [passed_along(): lax.ppermute(value, axis, [(source, source + steps) for source in range(i...]
    dot_general x272 -> x0, matrix products: 261 us -> none  [the longest x256 257 us: single(): return jnp.einsum(pattern, operand, matrix, precision=PRECISE)]
    unnamed x1 -> x0, blocking collectives: 220 us -> none
    ppermute x15 -> x0, waiting for transfers between devices: 113 us -> none  [passed_along(): lax.ppermute(value, axis, [(source, source + steps) for source in range(i...]
    reduce_sum x9 -> x2, other arithmetic: 81.8 us -> 0.24 us  [the longest x1 0.22 us: local(): jnp.sum((my_ids[:, None] == everyone[:, :, 1].reshape(1, -1)).astype(F32)...]
    mul x88 -> x0, local copies, waits for them, and re-layouts: 68.5 us -> none  [the longest x40 32 us: propagate(): real_part.reshape(batch_rows, height) * normalize]
    all_gather x0 -> x1, blocking collectives: none -> 50.7 us  [local(): everyone = lax.all_gather(small, ('range', 'radial'))]
    all_to_all x1 -> x2, waiting for transfers between devices: 47.6 us -> 6.84 us  [the longest x1 6.84 us: local(): lax.all_to_all(totals.reshape(owners, TILE_DEV, BINS), ('range', 'radial'...]
  transfers between devices with their start and end apart: 17 -> 2, of which waited for: 17 -> 1; matrix products, arithmetic and copies ran while one was open for 0% -> 1% of each run, Pallas kernels for 0% -> 0%
where the time goes in v1:
time: 105 us; the launch traced here: 104 us
  blocking collectives  50.7 us (48%)
  Pallas kernels  22.6 us (22%)
  starting transfers between devices  17.8 us (17%)
  waiting for transfers between devices  6.84 us (7%)
  local copies, waits for them, and re-layouts  5.36 us (5%)
    all_gather x1, blocking collectives, local(): everyone = lax.all_gather(small, ('range', 'radial'))  50.7 us
    pallas_call x1, Pallas kernels, march(): return call(levels, terrain, cells, *start, totals, *consts)  22.6 us
    all_to_all x1, starting transfers between devices, local(): lax.all_to_all(totals.reshape(owners, TILE_DEV, BINS), ('range', 'radial'...  10.3 us
    all_to_all x1, starting transfers between devices, local(): pieces.append(lax.all_to_all(piece, 'range', 0, 0, tiled=True))  7.42 us
    all_to_all x1, waiting for transfers between devices, local(): lax.all_to_all(totals.reshape(owners, TILE_DEV, BINS), ('range', 'radial'...  6.84 us
    reshape x1, local copies, waits for them, and re-layouts, local(): refractivity[:, begin:end].reshape(sections, own, end - begin, heights)  4.16 us
  transfers between devices with their start and end apart: 2, of which 1 were waited for; matrix products, arithmetic and copies ran while one was open for 1% of the time, Pallas kernels for 0%

profile of v1, /device:TPU:0, one launch (start us, length us, event | category | flops | bytes accessed | tf_op | source)
XLA Modules:
  0.0 104.3 jit_solution(4428471308190040623)
XLA Ops:
  0.0 4.2 %copy.25 = bf16[8,16,16,512]{3,1,2,0:T(8,128)(2,1)} copy(bf16[8,16,16,512]{3,2,1,0:T(8,128)(2,1)} %bitcast.22) | data formatting | bytes 4194304 | tf_op jit(solution)/shard_map/reshape | solution.py:320
  4.2 0.0 copy-start.8
  4.2 0.0 copy-start.9
  4.2 0.0 copy-start.7
  4.2 0.0 copy-start
  4.2 0.0 copy-start.1
  4.2 0.0 copy-start.2
  4.2 0.0 copy-start.3
  4.2 0.0 copy-start.4
  4.2 0.0 copy-start.5
  4.2 0.0 copy-start.6
  4.2 7.4 %all-to-all-start = ((bf16[8,16,16,512]{3,2,1,0:T(8,128)(2,1)}), bf16[8,16,16,512]{3,2,1,0:T(8,128)(2,1)S(1)}, u32[]{:S(2)}, u32[]{:S(2)}) async-start(bf16[8,16,16,512]{3,2,1,0:T(8,128)(2,1)} %bitcast.21), calls=%async_computation | async-start | bytes 4194304 | tf_op jit(solution)/shard_map/all_to_all | solution.py:322
  11.7 0.0 copy-done.8
  11.7 0.0 copy-done.9
  11.7 50.7 %all-gather = s32[32,128,2]{1,2,0:T(2,128)S(1)} all-gather(s32[2,128,2]{1,2,0:T(2,128)S(1)} %pad_add_fusion), channel_id=2, replica_groups=mesh['region'=2,'range'=8,'radial'=2] {'range','radial'}, dimensions={0}, use_global_device_ids=true | all-gather | bytes 34816 | tf_op jit(solution)/shard_map/all_gather | solution.py:297
  62.4 0.1 copy_bitcast_fusion.1
  62.4 0.1 reshape.29.cells
  62.5 0.0 copy-done.7
  62.6 0.0 all-to-all-done.levels
  62.6 0.1 broadcast_in_dim.14.terrain
  62.7 0.0 copy-done
  62.7 0.0 copy-done.1
  62.7 0.0 copy-done.2
  62.7 0.0 copy-done.3
  62.7 0.0 copy-done.4
  62.7 0.0 copy-done.5
  62.8 0.0 copy-done.6
  62.8 22.6 %shard_map.109 = (f32[32,16,128]{2,1,0:T(8,128)}, f32[32,16,128]{2,1,0:T(8,128)}, f32[256,128]{1,0:T(8,128)}) custom-call(bf16[8,16,16,512]{3,2,1,0:T(8,128)(2,1)S(1)} %all-to-all-done.levels, s32[16,16,128]{2,1,0:T(8,128)S(1)} %broadcast_in_dim.14.terrain, s32[1,256]{1,0:T(1,128)S(1)} %reshape.29.cells, f32[32,128]{1,0:T(8,128)S(1)} %bitcast.20, ...), custom_call_target="tpu_custom_call" | custom-call | flops 3221225472 | bytes 4194304 | tf_op jit(solution)/shard_map/pallas_call | solution.py:285
  85.3 10.3 %all-to-all-start.1 = ((f32[16,16,128]{2,1,0:T(8,128)}), f32[16,16,128]{2,1,0:T(8,128)S(1)}, u32[]{:S(2)}, u32[]{:S(2)}) async-start(f32[16,16,128]{2,1,0:T(8,128)} %bitcast.11), calls=%async_computation.1 | async-start | bytes 262144 | tf_op jit(solution)/shard_map/all_to_all | solution.py:329
  95.7 0.4 copy.22
  96.1 0.5 eq.16
  96.6 0.2 convert_reduce_fusion
  96.8 6.8 %all-to-all-done.1 = f32[16,16,128]{2,1,0:T(8,128)S(1)} async-done(((f32[16,16,128]{2,1,0:T(8,128)}), f32[16,16,128]{2,1,0:T(8,128)S(1)}, u32[]{:S(2)}, u32[]{:S(2)}) %all-to-all-start.1) | async-done | bytes 131104 | tf_op jit(solution)/shard_map/all_to_all | solution.py:329
  103.6 0.7 broadcast_divide_fusion
  (7 shorter events, 0.1 us)
Async XLA Ops:
  4.2 7.5 %copy-start.8 = (s32[128,2]{0,1:T(2,128)S(1)}, s32[128,2]{0,1:T(2,128)}, u32[]{:S(2)}) copy-start(s32[128,2]{0,1:T(2,128)} %param.14) | copy-start | bytes 3076
  4.2 7.5 %copy-start.9 = (s32[128,2]{0,1:T(2,128)S(1)}, s32[128,2]{0,1:T(2,128)}, u32[]{:S(2)}) copy-start(s32[128,2]{0,1:T(2,128)} %param.13) | copy-start | bytes 3076
  4.2 58.4 %copy-start.7 = (f32[2,4096]{1,0:T(2,128)S(1)}, f32[2,4096]{1,0:T(2,128)}, u32[]{:S(2)}) copy-start(f32[2,4096]{1,0:T(2,128)} %param.12) | copy-start | bytes 98308
  4.2 58.5 %copy-start = (bf16[768,256]{1,0:T(8,128)(2,1)S(1)}, bf16[768,256]{1,0:T(8,128)(2,1)}, u32[]{:S(2)}) copy-start(bf16[768,256]{1,0:T(8,128)(2,1)} %constant.64.clone.w_forward) | copy-start | bytes 1179652
  4.2 58.5 %copy-start.1 = (bf16[768,256]{1,0:T(8,128)(2,1)S(1)}, bf16[768,256]{1,0:T(8,128)(2,1)}, u32[]{:S(2)}) copy-start(bf16[768,256]{1,0:T(8,128)(2,1)} %constant.65.clone.w_inverse) | copy-start | bytes 1179652
  4.2 58.5 %copy-start.2 = (bf16[256,128]{1,0:T(8,128)(2,1)S(1)}, bf16[256,128]{1,0:T(8,128)(2,1)}, u32[]{:S(2)}) copy-start(bf16[256,128]{1,0:T(8,128)(2,1)} %constant.70.clone.bins) | copy-start | bytes 196612
  4.2 58.5 %copy-start.3 = (f32[2,32,128]{2,1,0:T(8,128)S(1)}, f32[2,32,128]{2,1,0:T(8,128)}, u32[]{:S(2)}) copy-start(f32[2,32,128]{2,1,0:T(8,128)} %constant.66.clone.twiddle) | copy-start | bytes 98308
  4.2 58.5 %copy-start.4 = (f32[2,32,128]{2,1,0:T(8,128)S(1)}, f32[2,32,128]{2,1,0:T(8,128)}, u32[]{:S(2)}) copy-start(f32[2,32,128]{2,1,0:T(8,128)} %constant.67.clone.spread) | copy-start | bytes 98308
  4.2 58.5 %copy-start.5 = (f32[32,128]{1,0:T(8,128)S(1)}, f32[32,128]{1,0:T(8,128)}, u32[]{:S(2)}) copy-start(f32[32,128]{1,0:T(8,128)} %constant.68.clone.tilt) | copy-start | bytes 49156
  4.2 58.5 %copy-start.6 = (f32[32,128]{1,0:T(8,128)S(1)}, f32[32,128]{1,0:T(8,128)}, u32[]{:S(2)}) copy-start(f32[32,128]{1,0:T(8,128)} %constant.69.clone.absorb) | copy-start | bytes 49156
  4.2 58.3 %all-to-all-start = ((bf16[8,16,16,512]{3,2,1,0:T(8,128)(2,1)}), bf16[8,16,16,512]{3,2,1,0:T(8,128)(2,1)S(1)}, u32[]{:S(2)}, u32[]{:S(2)}) async-start(bf16[8,16,16,512]{3,2,1,0:T(8,128)(2,1)} %bitcast.21), calls=%async_computation | async-start | bytes 4194304 | tf_op jit(solution)/shard_map/all_to_all | solution.py:322
  85.3 18.3 %all-to-all-start.1 = ((f32[16,16,128]{2,1,0:T(8,128)}), f32[16,16,128]{2,1,0:T(8,128)S(1)}, u32[]{:S(2)}, u32[]{:S(2)}) async-start(f32[16,16,128]{2,1,0:T(8,128)} %bitcast.11), calls=%async_computation.1 | async-start | bytes 262144 | tf_op jit(solution)/shard_map/all_to_all | solution.py:329

commit v2 on v1

--- a/solution.py
+++ b/solution.py
@@ -22,7 +22,7 @@
 SPREAD_RATE = 0.5
 ABSORB_RATE = 0.05
 TERRAIN_ROWS = 4
-CHUNKS = (1.0,)
+CHUNKS = (0.3125, 0.4375, 0.25)
 GROUP = 2
 
 F32 = jnp.float32
@@ -132,14 +132,17 @@
     return high, low
 
 
-def march_kernel(
-    steps, batch, heights, first,
-    levels, terrain, cells, start_re, start_im, totals_in,
-    w_forward, w_inverse, twiddle, spread, tilt, absorb, bins,
-    end_re, end_im, totals,
-    back_re, back_im, energy, power,
-):
+def march_kernel(steps, batch, heights, first, sections, section, *refs):
+    slabs, refs = refs[:sections], refs[sections:]
+    (
+        terrain, cells, start_re, start_im, totals_in,
+        w_forward, w_inverse, twiddle, spread, tilt, absorb, bins,
+        end_re, end_im, totals,
+        levels, back_re, back_im, energy, power,
+    ) = refs
     sine, cosine = phase_polynomials()
+    for d in range(sections):
+        levels[section[0] ^ d] = slabs[d][...]
 
     def enter(columns, jl, put_re, put_im):
         parts = dft4(columns, -1)
@@ -262,16 +265,19 @@
         totals[...] = totals_in[...] + gain
 
 
-def march(levels, terrain, cells, start, totals, consts, tiles, first):
-    sources, steps, batch, heights = levels.shape
+def march(section, slabs, terrain, cells, start, totals, consts, tiles, first):
+    sections = len(slabs)
+    steps, batch, heights = slabs[0].shape
     state = jax.ShapeDtypeStruct((ROWS, batch, LANES), F32)
     vmem = pl.BlockSpec(memory_space=pltpu.VMEM)
+    smem = pl.BlockSpec(memory_space=pltpu.SMEM)
     call = pl.pallas_call(
-        functools.partial(march_kernel, steps, batch, heights, first),
+        functools.partial(march_kernel, steps, batch, heights, first, sections),
         out_shape=(state, state, jax.ShapeDtypeStruct((tiles, BINS), F32)),
-        in_specs=[vmem] * 13,
+        in_specs=[smem] + [vmem] * (sections + 12),
         out_specs=(vmem, vmem, vmem),
         scratch_shapes=[
+            pltpu.VMEM((sections, steps, batch, heights), BF16),
             pltpu.VMEM((ROWS, batch, LANES), F32),
             pltpu.VMEM((ROWS, batch, LANES), F32),
             pltpu.VMEM((ROWS * batch, 2 * LANES), BF16),
@@ -279,10 +285,46 @@
         ],
         compiler_params=pltpu.CompilerParams(vmem_limit_bytes=48 * 1024 * 1024),
         cost_estimate=pl.CostEstimate(
-            flops=steps * batch * H * 3 * 8 * LANES, bytes_accessed=4 * 1024 * 1024, transcendentals=0
+            flops=steps * 1_600_000_000, bytes_accessed=4 * 1024 * 1024, transcendentals=0
         ),
-    )
-    return call(levels, terrain, cells, *start, totals, *consts)
+        name="march",
+    )
+    return call(section, *slabs, terrain, cells, *start, totals, *consts)
+
+
+def cut_kernel(begin, end, own, section, levels, *refs):
+    slabs, rows = refs[:-1], refs[-1]
+    steps, heights = levels.shape[1:]
+    columns = [slice(c * LANES, (c + 1) * LANES) for c in range(heights // LANES)]
+    for d, slab in enumerate(slabs):
+        base = (section[0] ^ d) * own
+        for b in range(own):
+            for c, column in enumerate(columns):
+                rows[c, b * steps : (b + 1) * steps, :] = levels[base + b, :, column].astype(F32)
+        for t in range(begin, end):
+            for c, column in enumerate(columns):
+                taken = rows[c, pl.ds(t, own, stride=steps), :].astype(BF16)
+                if own < slab.shape[1]:
+                    taken = jnp.pad(taken, ((0, slab.shape[1] - own), (0, 0)))
+                slab[t - begin, :, column] = taken
+
+
+def cut(section, levels, begin, end, sections, own, batch):
+    steps, heights = levels.shape[1:]
+    slab = jax.ShapeDtypeStruct((end - begin, batch, heights), BF16)
+    vmem = pl.BlockSpec(memory_space=pltpu.VMEM)
+    smem = pl.BlockSpec(memory_space=pltpu.SMEM)
+    call = pl.pallas_call(
+        functools.partial(cut_kernel, begin, end, own),
+        out_shape=(slab,) * sections,
+        in_specs=[smem, vmem],
+        out_specs=(vmem,) * sections,
+        scratch_shapes=[pltpu.VMEM((heights // LANES, own * steps, LANES), F32)],
+        compiler_params=pltpu.CompilerParams(vmem_limit_bytes=32 * 1024 * 1024),
+        cost_estimate=pl.CostEstimate(flops=1_000_000_000, bytes_accessed=4 * 1024 * 1024, transcendentals=0),
+        name="cut",
+    )
+    return call(section, levels)
 
 
 def local(refractivity, source, terrain, tile_map):
@@ -293,37 +335,40 @@
     own = radials // sections
     batch = -(-own // 16) * 16
 
-    small = jnp.stack([terrain, tile_map])
-    everyone = lax.all_gather(small, ("range", "radial"))
-    everyone = everyone.reshape(sections, lax.axis_size("radial"), *small.shape)
+    small = jnp.concatenate([terrain.T, tile_map.T])
+    edges = [0]
+    for share in CHUNKS:
+        edges.append(edges[-1] + max(1, round(share * steps)))
+    section = lax.axis_index("range").astype(jnp.int32).reshape(1)
+    pieces = []
+    for begin, end in zip(edges[:-1], edges[1:]):
+        slabs = list(cut(section, refractivity, begin, end, sections, own, batch))
+        for d in reversed(range(1, sections)):
+            slabs[d] = lax.ppermute(slabs[d], "range", [(i, i ^ d) for i in range(sections)])
+        pieces.append(slabs)
+    everyone = lax.all_to_all(
+        jnp.broadcast_to(small, (owners, *small.shape)), ("range", "radial"), 0, 0, tiled=True
+    )
+    everyone = everyone.reshape(sections, lax.axis_size("radial"), 2, -1, radials)
     my_ids = (lax.axis_index("range") * lax.axis_size("radial") + lax.axis_index("radial")) * TILE_DEV
     my_ids = my_ids + jnp.arange(TILE_DEV, dtype=jnp.int32)
     counts = jnp.sum(
         (my_ids[:, None] == everyone[:, :, 1].reshape(1, -1)).astype(F32), axis=1
     )
     mine = lax.dynamic_index_in_dim(everyone, lax.axis_index("radial"), 1, keepdims=False)
-    mine = lax.dynamic_slice_in_dim(mine, lax.axis_index("range") * own, own, 2)
-    mine = jnp.transpose(mine, (1, 0, 3, 2)).reshape(2, steps, own)
+    mine = lax.dynamic_slice_in_dim(mine, lax.axis_index("range") * own, own, 3)
+    mine = jnp.transpose(mine, (1, 0, 2, 3)).reshape(2, steps, own)
     pad = ((0, 0), (0, batch - own))
     terrain_all = jnp.pad(mine[0], pad)
     cells_all = jnp.pad(mine[1], pad, constant_values=-1)
     terrain_all = jnp.broadcast_to(terrain_all[:, :, None], (steps, batch, LANES))
 
     consts = [jnp.asarray(v) for v in tables()]
-    edges = [0]
-    for share in CHUNKS:
-        edges.append(edges[-1] + max(1, round(share * steps)))
     start = (source[0].reshape(ROWS, LANES), source[1].reshape(ROWS, LANES))
     totals = jnp.zeros((tiles, BINS), F32)
-    pieces = []
-    for begin, end in zip(edges[:-1], edges[1:]):
-        piece = refractivity[:, begin:end].reshape(sections, own, end - begin, heights)
-        piece = jnp.transpose(piece, (0, 2, 1, 3))
-        pieces.append(lax.all_to_all(piece, "range", 0, 0, tiled=True))
     for piece, begin, end in zip(pieces, edges[:-1], edges[1:]):
-        piece = jnp.pad(piece, ((0, 0), (0, 0), (0, batch - own), (0, 0)))
         *start, totals = march(
-            piece, terrain_all[begin:end], cells_all[begin:end].reshape(1, -1),
+            section, piece, terrain_all[begin:end], cells_all[begin:end].reshape(1, -1),
             start, totals, consts, tiles, begin == 0,
         )
     sent = lax.all_to_all(

time: 105 us -> 114 us (1.086)
  blocking collectives: 50.7 us -> 0 us
  starting transfers between devices: 17.8 us -> 45.2 us
  waiting for transfers between devices: 6.84 us -> 25.6 us
  local copies, waits for them, and re-layouts: 5.36 us -> 13.2 us
  Pallas kernels: 22.6 us -> 27.6 us
    all_gather x1 -> x0, blocking collectives: 50.7 us -> none  [local(): everyone = lax.all_gather(small, ('range', 'radial'))]
    ppermute x0 -> x21, starting transfers between devices: none -> 34.2 us  [local(): lax.ppermute(slabs[d], 'range', [(i, i ^ d) for i in range(sections)])]
    ppermute x0 -> x21, waiting for transfers between devices: none -> 17.9 us  [local(): lax.ppermute(slabs[d], 'range', [(i, i ^ d) for i in range(sections)])]
    unnamed x21 -> x62, local copies, waits for them, and re-layouts: 0.42 us -> 11.2 us
    all_to_all x1, starting transfers between devices: 10.3 us -> 3.53 us  [local(): lax.all_to_all(totals.reshape(owners, TILE_DEV, BINS), ('range', 'radial'...]
    pallas_call x1 -> x6, Pallas kernels: 22.6 us -> 27.6 us  [the longest x3 24.4 us: march(): return call(section, *slabs, terrain, cells, *start, totals, *consts)]
    reshape x1 -> x0, local copies, waits for them, and re-layouts: 4.16 us -> none  [local(): refractivity[:, begin:end].reshape(sections, own, end - begin, heights)]
  transfers between devices with their start and end apart: 2 -> 23, of which waited for: 1 -> 6; matrix products, arithmetic and copies ran while one was open for 1% -> 1% of each run, Pallas kernels for 0% -> 18%
where the time goes in v2:
time: 114 us
  starting transfers between devices  45.2 us (40%)
  Pallas kernels  27.6 us (24%)
  waiting for transfers between devices  25.6 us (22%)
  local copies, waits for them, and re-layouts  13.2 us (12%)
  other arithmetic  1.62 us (1%)
    ppermute x21, starting transfers between devices, local(): lax.ppermute(slabs[d], 'range', [(i, i ^ d) for i in range(sections)])  34.2 us
    pallas_call x3, Pallas kernels, march(): return call(section, *slabs, terrain, cells, *start, totals, *consts)  24.4 us
    ppermute x21, waiting for transfers between devices, local(): lax.ppermute(slabs[d], 'range', [(i, i ^ d) for i in range(sections)])  17.9 us
    unnamed x62, local copies, waits for them, and re-layouts  11.2 us
    all_to_all x1, waiting for transfers between devices, local(): lax.all_to_all(totals.reshape(owners, TILE_DEV, BINS), ('range', 'radial'...  7.67 us
    all_to_all x1, starting transfers between devices, local(): lax.all_to_all(jnp.broadcast_to(small, (owners, *small.shape)), ('range',...  7.44 us
    all_to_all x1, starting transfers between devices, local(): lax.all_to_all(totals.reshape(owners, TILE_DEV, BINS), ('range', 'radial'...  3.53 us
    pallas_call x3, Pallas kernels, cut(): return call(section, levels)  3.23 us
  transfers between devices with their start and end apart: 23, of which 6 were waited for; matrix products, arithmetic and copies ran while one was open for 1% of the time, Pallas kernels for 18%

profile of v2, /device:TPU:0, one launch (start us, length us, event | category | flops | bytes accessed | tf_op | source)
XLA Modules:
  0.0 113.6 jit_solution(5629628368094667974)
XLA Ops:
  0.0 0.7 pad_add_fusion
  0.7 0.6 broadcast_in_dim.20
  1.3 7.4 %all-to-all-start = ((s32[16,4,128]{2,1,0:T(4,128)}), s32[16,4,128]{2,1,0:T(4,128)}, u32[]{:S(2)}, u32[]{:S(2)}) async-start(s32[16,4,128]{2,1,0:T(4,128)} %broadcast_in_dim.20), calls=%async_computation | async-start | bytes 65536 | tf_op jit(solution)/shard_map/all_to_all | solution.py:349
  8.8 0.0 copy-start
  8.8 1.6 %copy-done = bf16[128,16,512]{2,1,0:T(8,128)(2,1)S(1)} copy-done((bf16[128,16,512]{2,1,0:T(8,128)(2,1)S(1)}, bf16[128,16,512]{2,1,0:T(8,128)(2,1)}, u32[]{:S(2)}) %copy-start) | copy-done | bytes 2097176
  10.4 1.2 %cut.5 = (bf16[5,16,512]{2,1,0:T(8,128)(2,1)S(1)}, bf16[5,16,512]{2,1,0:T(8,128)(2,1)}, bf16[5,16,512]{2,1,0:T(8,128)(2,1)}, bf16[5,16,512]{2,1,0:T(8,128)(2,1)}...) custom-call(s32[1]{0:T(128)} %bitcast.section, ...), custom_call_target="tpu_custom_call" | custom-call | flops 1000000000 | bytes 4194304 | tf_op jit(solution)/shard_map/cut/pallas_call | solution.py:327
  11.6 0.6 copy-done.26
  12.2 1.9 %collective-permute-start.14 = (bf16[5,16,512]{2,1,0:T(8,128)(2,1)}, bf16[5,16,512]{2,1,0:T(8,128)(2,1)S(1)}, u32[]{:S(2)}, u32[]{:S(2)}) collective-permute-start(bf16[5,16,512]{2,1,0:T(8,128)(2,1)} %get-tuple-element.53), channel_id=1, source_target_pairs={{0,2},{2,0},{4,6},{6,4},{8,10},{10,8},{12,14},{14,12},{1,3},{3,1},... | collective-permute-start | bytes 245768 | tf_op jit(solution)/shard_map/ppermute | solution.py:347
  14.1 1.5 %collective-permute-start.15 = (bf16[5,16,512]{2,1,0:T(8,128)(2,1)}, bf16[5,16,512]{2,1,0:T(8,128)(2,1)S(1)}, u32[]{:S(2)}, u32[]{:S(2)}) collective-permute-start(bf16[5,16,512]{2,1,0:T(8,128)(2,1)} %get-tuple-element.54), channel_id=1, source_target_pairs={{0,4},{2,6},{4,0},{6,2},{8,12},{10,14},{12,8},{14,10},{1,5},{3,7},... | collective-permute-start | bytes 245768 | tf_op jit(solution)/shard_map/ppermute | solution.py:347
  15.6 0.2 collective-permute-start.16
  15.7 2.8 %collective-permute-start.17 = (bf16[5,16,512]{2,1,0:T(8,128)(2,1)}, bf16[5,16,512]{2,1,0:T(8,128)(2,1)S(1)}, u32[]{:S(2)}, u32[]{:S(2)}) collective-permute-start(bf16[5,16,512]{2,1,0:T(8,128)(2,1)} %get-tuple-element.56), channel_id=1, source_target_pairs={{0,8},{2,10},{4,12},{6,14},{8,0},{10,2},{12,4},{14,6},{1,9},{3,11}... | collective-permute-start | bytes 245768 | tf_op jit(solution)/shard_map/ppermute | solution.py:347
  18.5 1.1 cut.3
  19.6 0.6 copy-done.4
  20.2 0.6 copy-done.6
  20.9 0.6 copy-done.8
  21.5 0.6 copy-done.10
  22.1 0.6 copy-done.28
  22.7 1.5 %collective-permute-start = (bf16[4,16,512]{2,1,0:T(8,128)(2,1)}, bf16[4,16,512]{2,1,0:T(8,128)(2,1)}, u32[]{:S(2)}, u32[]{:S(2)}) collective-permute-start(bf16[4,16,512]{2,1,0:T(8,128)(2,1)} %get-tuple-element.37), channel_id=1, source_target_pairs={{0,2},{2,0},{4,6},{6,4},{8,10},{10,8},{12,14},{14,12},{1,3},{3,1},... | collective-permute-start | bytes 196616 | tf_op jit(solution)/shard_map/ppermute | solution.py:347
  24.3 0.9 cut.4
  25.1 0.6 copy-done.24
  25.8 0.8 copy.27
  26.5 0.1 constant_dynamic-slice_fusion
  26.6 0.7 collective-permute-done.refs_1_
  27.3 1.5 %collective-permute-start.1 = (bf16[4,16,512]{2,1,0:T(8,128)(2,1)}, bf16[4,16,512]{2,1,0:T(8,128)(2,1)S(1)}, u32[]{:S(2)}, u32[]{:S(2)}) collective-permute-start(bf16[4,16,512]{2,1,0:T(8,128)(2,1)} %copy-done.12), channel_id=1, source_target_pairs={{0,4},{2,6},{4,0},{6,2},{8,12},{10,14},{12,8},{14,10},{1,5},{3,7},... | collective-permute-start | bytes 196616 | tf_op jit(solution)/shard_map/ppermute | solution.py:347
  28.8 3.0 %collective-permute-done.1.refs_2_ = bf16[4,16,512]{2,1,0:T(8,128)(2,1)S(1)} collective-permute-done((bf16[4,16,512]{2,1,0:T(8,128)(2,1)}, bf16[4,16,512]{2,1,0:T(8,128)(2,1)S(1)}, u32[]{:S(2)}, u32[]{:S(2)}) %collective-permute-start.1) | collective-permute-done | bytes 65568 | tf_op jit(solution)/shard_map/ppermute | solution.py:347
  31.8 1.5 %collective-permute-start.18 = (bf16[5,16,512]{2,1,0:T(8,128)(2,1)S(1)}, bf16[5,16,512]{2,1,0:T(8,128)(2,1)S(1)}, u32[]{:S(2)}, u32[]{:S(2)}) collective-permute-start(bf16[5,16,512]{2,1,0:T(8,128)(2,1)S(1)} %get-tuple-element.57), channel_id=1, source_target_pairs={{0,10},{2,8},{4,14},{6,12},{8,2},{10,0},{12,6},{14,4},{1,11},{3,9}... | collective-permute-start | bytes 245768 | tf_op jit(solution)/shard_map/ppermute | solution.py:347
  33.2 3.6 %collective-permute-start.19 = (bf16[5,16,512]{2,1,0:T(8,128)(2,1)S(1)}, bf16[5,16,512]{2,1,0:T(8,128)(2,1)S(1)}, u32[]{:S(2)}, u32[]{:S(2)}) collective-permute-start(bf16[5,16,512]{2,1,0:T(8,128)(2,1)S(1)} %get-tuple-element.58), channel_id=1, source_target_pairs={{0,12},{2,14},{4,8},{6,10},{8,4},{10,6},{12,0},{14,2},{1,13},{3,15... | collective-permute-start | bytes 245768 | tf_op jit(solution)/shard_map/ppermute | solution.py:347
  36.8 0.5 collective-permute-start.20
  37.3 0.4 collective-permute-start.10
  37.6 3.3 %collective-permute-start.11 = (bf16[7,16,512]{2,1,0:T(8,128)(2,1)S(1)}, bf16[7,16,512]{2,1,0:T(8,128)(2,1)S(1)}, u32[]{:S(2)}, u32[]{:S(2)}) collective-permute-start(bf16[7,16,512]{2,1,0:T(8,128)(2,1)S(1)} %get-tuple-element.49), channel_id=1, source_target_pairs={{0,10},{2,8},{4,14},{6,12},{8,2},{10,0},{12,6},{14,4},{1,11},{3,9}... | collective-permute-start | bytes 344072 | tf_op jit(solution)/shard_map/ppermute | solution.py:347
  41.0 0.1 reshape.39.refs_9_
  41.0 0.1 reshape.38.refs_9_
  41.1 0.1 reshape.37.refs_9_
  41.2 8.6 %collective-permute-done.18.refs_5_ = bf16[5,16,512]{2,1,0:T(8,128)(2,1)S(1)} collective-permute-done((bf16[5,16,512]{2,1,0:T(8,128)(2,1)S(1)}, bf16[5,16,512]{2,1,0:T(8,128)(2,1)S(1)}, u32[]{:S(2)}, u32[]{:S(2)}) %collective-permute-start.18) | collective-permute-done | bytes 81952 | tf_op jit(solution)/shard_map/ppermute | solution.py:347
  49.8 1.5 %collective-permute-start.12 = (bf16[7,16,512]{2,1,0:T(8,128)(2,1)S(1)}, bf16[7,16,512]{2,1,0:T(8,128)(2,1)S(1)}, u32[]{:S(2)}, u32[]{:S(2)}) collective-permute-start(bf16[7,16,512]{2,1,0:T(8,128)(2,1)S(1)} %get-tuple-element.50), channel_id=1, source_target_pairs={{0,12},{2,14},{4,8},{6,10},{8,4},{10,6},{12,0},{14,2},{1,13},{3,15... | collective-permute-start | bytes 344072 | tf_op jit(solution)/shard_map/ppermute | solution.py:347
  51.3 3.2 %collective-permute-start.13 = (bf16[7,16,512]{2,1,0:T(8,128)(2,1)S(1)}, bf16[7,16,512]{2,1,0:T(8,128)(2,1)S(1)}, u32[]{:S(2)}, u32[]{:S(2)}) collective-permute-start(bf16[7,16,512]{2,1,0:T(8,128)(2,1)S(1)} %get-tuple-element.51), channel_id=1, source_target_pairs={{0,14},{2,12},{4,10},{6,8},{8,6},{10,4},{12,2},{14,0},{1,15},{3,13... | collective-permute-start | bytes 344072 | tf_op jit(solution)/shard_map/ppermute | solution.py:347
  54.6 0.6 collective-permute-start.7
  55.1 1.9 %collective-permute-done.10.refs_4_ = bf16[7,16,512]{2,1,0:T(8,128)(2,1)S(1)} collective-permute-done((bf16[7,16,512]{2,1,0:T(8,128)(2,1)S(1)}, bf16[7,16,512]{2,1,0:T(8,128)(2,1)S(1)}, u32[]{:S(2)}, u32[]{:S(2)}) %collective-permute-start.10) | collective-permute-done | bytes 114720 | tf_op jit(solution)/shard_map/ppermute | solution.py:347
  57.0 3.7 %collective-permute-done.11.refs_5_ = bf16[7,16,512]{2,1,0:T(8,128)(2,1)S(1)} collective-permute-done((bf16[7,16,512]{2,1,0:T(8,128)(2,1)S(1)}, bf16[7,16,512]{2,1,0:T(8,128)(2,1)S(1)}, u32[]{:S(2)}, u32[]{:S(2)}) %collective-permute-start.11) | collective-permute-done | bytes 114720 | tf_op jit(solution)/shard_map/ppermute | solution.py:347
  60.7 0.1 broadcast_in_dim.24.refs_8_
  60.8 0.0 copy-start.13
  60.9 1.0 copy-done.13
  61.8 1.0 copy-done.15
  62.8 0.8 copy-done.17
  63.7 0.8 copy-done.20
  64.4 0.7 copy-done.23
  65.2 0.9 copy-done.27
  66.1 0.0 copy-start.14
  66.1 0.0 copy-start.16
  66.1 0.0 copy-start.18
  66.1 0.0 copy-start.21
  66.1 7.1 %march.3 = (f32[32,16,128]{2,1,0:T(8,128)S(1)}, f32[32,16,128]{2,1,0:T(8,128)S(1)}, f32[256,128]{1,0:T(8,128)S(1)}) custom-call(s32[1]{0:T(128)} %bitcast.section, bf16[5,16,512]{2,1,0:T(8,128)(2,1)S(1)} %copy-done.27, bf16[5,16,512]{2,1,0:T(8,128)(2,1)S(1)} %collective-permute-done.14.refs_1_, bf16[5,16,512]{2,1,0:T(8,128)(2,1)S(1)} %collective-permute-done.15.refs_2_, ...), custom_call_target="tpu_custom_call" | custom-call | flops 8000000000 | bytes 4194304 | tf_op jit(solution)/shard_map/march/pallas_call | solution.py:292
  73.3 3.0 %collective-permute-start.2 = (bf16[4,16,512]{2,1,0:T(8,128)(2,1)S(1)}, bf16[4,16,512]{2,1,0:T(8,128)(2,1)S(1)}, u32[]{:S(2)}, u32[]{:S(2)}) collective-permute-start(bf16[4,16,512]{2,1,0:T(8,128)(2,1)S(1)} %copy-done.11), channel_id=1, source_target_pairs={{0,6},{2,4},{4,2},{6,0},{8,14},{10,12},{12,10},{14,8},{1,7},{3,5},... | collective-permute-start | bytes 196616 | tf_op jit(solution)/shard_map/ppermute | solution.py:347
  76.3 3.8 %collective-permute-start.4 = (bf16[4,16,512]{2,1,0:T(8,128)(2,1)S(1)}, bf16[4,16,512]{2,1,0:T(8,128)(2,1)S(1)}, u32[]{:S(2)}, u32[]{:S(2)}) collective-permute-start(bf16[4,16,512]{2,1,0:T(8,128)(2,1)S(1)} %copy-done.7), channel_id=1, source_target_pairs={{0,10},{2,8},{4,14},{6,12},{8,2},{10,0},{12,6},{14,4},{1,11},{3,9}... | collective-permute-start | bytes 196616 | tf_op jit(solution)/shard_map/ppermute | solution.py:347
  80.1 1.3 %collective-permute-start.5 = (bf16[4,16,512]{2,1,0:T(8,128)(2,1)S(1)}, bf16[4,16,512]{2,1,0:T(8,128)(2,1)S(1)}, u32[]{:S(2)}, u32[]{:S(2)}) collective-permute-start(bf16[4,16,512]{2,1,0:T(8,128)(2,1)S(1)} %copy-done.5), channel_id=1, source_target_pairs={{0,12},{2,14},{4,8},{6,10},{8,4},{10,6},{12,0},{14,2},{1,13},{3,15... | collective-permute-start | bytes 196616 | tf_op jit(solution)/shard_map/ppermute | solution.py:347
  81.4 2.6 %collective-permute-start.6 = (bf16[4,16,512]{2,1,0:T(8,128)(2,1)S(1)}, bf16[4,16,512]{2,1,0:T(8,128)(2,1)S(1)}, u32[]{:S(2)}, u32[]{:S(2)}) collective-permute-start(bf16[4,16,512]{2,1,0:T(8,128)(2,1)S(1)} %copy-done.3), channel_id=1, source_target_pairs={{0,14},{2,12},{4,10},{6,8},{8,6},{10,4},{12,2},{14,0},{1,15},{3,13... | collective-permute-start | bytes 196616 | tf_op jit(solution)/shard_map/ppermute | solution.py:347
  83.9 0.1 broadcast_in_dim.23.refs_8_
  84.1 10.0 %march.4 = (f32[32,16,128]{2,1,0:T(8,128)S(1)}, f32[32,16,128]{2,1,0:T(8,128)S(1)}, f32[256,128]{1,0:T(8,128)S(1)}) custom-call(s32[1]{0:T(128)} %bitcast.section, bf16[7,16,512]{2,1,0:T(8,128)(2,1)S(1)} %copy-done.25, bf16[7,16,512]{2,1,0:T(8,128)(2,1)S(1)} %collective-permute-done.7.refs_1_, bf16[7,16,512]{2,1,0:T(8,128)(2,1)S(1)} %collective-permute-done.8.refs_2_, ...), custom_call_target="tpu_custom_call" | custom-call | flops 11200000000 | bytes 4194304 | tf_op jit(solution)/shard_map/march/pallas_call | solution.py:292
  94.1 0.1 broadcast_in_dim.21.refs_8_
  94.2 7.3 %march.5 = (f32[32,16,128]{2,1,0:T(8,128)}, f32[32,16,128]{2,1,0:T(8,128)}, f32[256,128]{1,0:T(8,128)}) custom-call(s32[1]{0:T(128)} %bitcast.section, bf16[4,16,512]{2,1,0:T(8,128)(2,1)S(1)} %copy-done.29, bf16[4,16,512]{2,1,0:T(8,128)(2,1)} %collective-permute-done.refs_1_, bf16[4,16,512]{2,1,0:T(8,128)(2,1)S(1)} %collective-permute-done.1.refs_2_, ...), custom_call_target="tpu_custom_call" | custom-call | flops 6400000000 | bytes 4194304 | tf_op jit(solution)/shard_map/march/pallas_call | solution.py:292
  101.5 3.5 %all-to-all-start.1 = ((f32[16,16,128]{2,1,0:T(8,128)}), f32[16,16,128]{2,1,0:T(8,128)S(1)}, u32[]{:S(2)}, u32[]{:S(2)}) async-start(f32[16,16,128]{2,1,0:T(8,128)} %bitcast.12), calls=%async_computation.1 | async-start | bytes 262144 | tf_op jit(solution)/shard_map/all_to_all | solution.py:374
  105.1 0.2 convert_reduce_fusion
  105.3 7.7 %all-to-all-done.1 = f32[16,16,128]{2,1,0:T(8,128)S(1)} async-done(((f32[16,16,128]{2,1,0:T(8,128)}), f32[16,16,128]{2,1,0:T(8,128)S(1)}, u32[]{:S(2)}, u32[]{:S(2)}) %all-to-all-start.1) | async-done | bytes 131104 | tf_op jit(solution)/shard_map/all_to_all | solution.py:374
  113.0 0.7 broadcast_divide_fusion
  (78 shorter events, 0.2 us)
Async XLA Ops:
  1.3 24.5 %all-to-all-start = ((s32[16,4,128]{2,1,0:T(4,128)}), s32[16,4,128]{2,1,0:T(4,128)}, u32[]{:S(2)}, u32[]{:S(2)}) async-start(s32[16,4,128]{2,1,0:T(4,128)} %broadcast_in_dim.20), calls=%async_computation | async-start | bytes 65536 | tf_op jit(solution)/shard_map/all_to_all | solution.py:349
  8.8 1.6 %copy-start = (bf16[128,16,512]{2,1,0:T(8,128)(2,1)S(1)}, bf16[128,16,512]{2,1,0:T(8,128)(2,1)}, u32[]{:S(2)}) copy-start(bf16[128,16,512]{2,1,0:T(8,128)(2,1)} %levels.5) | copy-start | bytes 6291460
  11.6 0.6 copy-start.26
  12.2 11.9 %copy-start.30 = (f32[2,4096]{1,0:T(2,128)S(1)}, f32[2,4096]{1,0:T(2,128)}, u32[]{:S(2)}) copy-start(f32[2,4096]{1,0:T(2,128)} %param.12) | copy-start | bytes 98308
  12.2 12.0 %copy-start.1 = (bf16[128,16,512]{2,1,0:T(8,128)(2,1)S(1)}, bf16[128,16,512]{2,1,0:T(8,128)(2,1)}, u32[]{:S(2)}) copy-start(bf16[128,16,512]{2,1,0:T(8,128)(2,1)} %levels.5) | copy-start | bytes 6291460
  12.2 21.0 %collective-permute-start.14 = (bf16[5,16,512]{2,1,0:T(8,128)(2,1)}, bf16[5,16,512]{2,1,0:T(8,128)(2,1)S(1)}, u32[]{:S(2)}, u32[]{:S(2)}) collective-permute-start(bf16[5,16,512]{2,1,0:T(8,128)(2,1)} %get-tuple-element.53), channel_id=1, source_target_pairs={{0,2},{2,0},{4,6},{6,4},{8,10},{10,8},{12,14},{14,12},{1,3},{3,1},... | collective-permute-start | bytes 245768 | tf_op jit(solution)/shard_map/ppermute | solution.py:347
  14.1 22.7 %collective-permute-start.15 = (bf16[5,16,512]{2,1,0:T(8,128)(2,1)}, bf16[5,16,512]{2,1,0:T(8,128)(2,1)S(1)}, u32[]{:S(2)}, u32[]{:S(2)}) collective-permute-start(bf16[5,16,512]{2,1,0:T(8,128)(2,1)} %get-tuple-element.54), channel_id=1, source_target_pairs={{0,4},{2,6},{4,0},{6,2},{8,12},{10,14},{12,8},{14,10},{1,5},{3,7},... | collective-permute-start | bytes 245768 | tf_op jit(solution)/shard_map/ppermute | solution.py:347
  15.6 21.7 %collective-permute-start.16 = (bf16[5,16,512]{2,1,0:T(8,128)(2,1)}, bf16[5,16,512]{2,1,0:T(8,128)(2,1)S(1)}, u32[]{:S(2)}, u32[]{:S(2)}) collective-permute-start(bf16[5,16,512]{2,1,0:T(8,128)(2,1)} %get-tuple-element.55), channel_id=1, source_target_pairs={{0,6},{2,4},{4,2},{6,0},{8,14},{10,12},{12,10},{14,8},{1,7},{3,5},... | collective-permute-start | bytes 245768 | tf_op jit(solution)/shard_map/ppermute | solution.py:347
  15.7 21.9 %collective-permute-start.17 = (bf16[5,16,512]{2,1,0:T(8,128)(2,1)}, bf16[5,16,512]{2,1,0:T(8,128)(2,1)S(1)}, u32[]{:S(2)}, u32[]{:S(2)}) collective-permute-start(bf16[5,16,512]{2,1,0:T(8,128)(2,1)} %get-tuple-element.56), channel_id=1, source_target_pairs={{0,8},{2,10},{4,12},{6,14},{8,0},{10,2},{12,4},{14,6},{1,9},{3,11}... | collective-permute-start | bytes 245768 | tf_op jit(solution)/shard_map/ppermute | solution.py:347
  19.6 0.6 copy-start.4
  20.2 0.6 copy-start.6
  20.9 0.6 copy-start.8
  21.5 0.6 copy-start.10
  22.1 0.6 copy-start.28
  22.7 1.5 %copy-start.2 = (bf16[4,16,512]{2,1,0:T(8,128)(2,1)}, bf16[4,16,512]{2,1,0:T(8,128)(2,1)S(1)}, u32[]{:S(2)}) copy-start(bf16[4,16,512]{2,1,0:T(8,128)(2,1)S(1)} %get-tuple-element.43) | copy-start | bytes 196612
  22.7 1.5 %copy-start.12 = (bf16[4,16,512]{2,1,0:T(8,128)(2,1)}, bf16[4,16,512]{2,1,0:T(8,128)(2,1)S(1)}, u32[]{:S(2)}) copy-start(bf16[4,16,512]{2,1,0:T(8,128)(2,1)S(1)} %get-tuple-element.38) | copy-start | bytes 196612
  22.7 4.6 %collective-permute-start = (bf16[4,16,512]{2,1,0:T(8,128)(2,1)}, bf16[4,16,512]{2,1,0:T(8,128)(2,1)}, u32[]{:S(2)}, u32[]{:S(2)}) collective-permute-start(bf16[4,16,512]{2,1,0:T(8,128)(2,1)} %get-tuple-element.37), channel_id=1, source_target_pairs={{0,2},{2,0},{4,6},{6,4},{8,10},{10,8},{12,14},{14,12},{1,3},{3,1},... | collective-permute-start | bytes 196616 | tf_op jit(solution)/shard_map/ppermute | solution.py:347
  24.2 36.6 %copy-start.19 = (f32[2,32,128]{2,1,0:T(8,128)S(1)}, f32[2,32,128]{2,1,0:T(8,128)}, u32[]{:S(2)}) copy-start(f32[2,32,128]{2,1,0:T(8,128)} %constant.66.clone.refs_15_) | copy-start | bytes 98308
  24.2 36.7 %copy-start.22 = (f32[32,128]{1,0:T(8,128)S(1)}, f32[32,128]{1,0:T(8,128)}, u32[]{:S(2)}) copy-start(f32[32,128]{1,0:T(8,128)} %constant.68.clone.refs_17_) | copy-start | bytes 49156
  25.1 0.7 copy-start.24
  27.3 4.5 %collective-permute-start.1 = (bf16[4,16,512]{2,1,0:T(8,128)(2,1)}, bf16[4,16,512]{2,1,0:T(8,128)(2,1)S(1)}, u32[]{:S(2)}, u32[]{:S(2)}) collective-permute-start(bf16[4,16,512]{2,1,0:T(8,128)(2,1)} %copy-done.12), channel_id=1, source_target_pairs={{0,4},{2,6},{4,0},{6,2},{8,12},{10,14},{12,8},{14,10},{1,5},{3,7},... | collective-permute-start | bytes 196616 | tf_op jit(solution)/shard_map/ppermute | solution.py:347
  31.8 18.1 %collective-permute-start.18 = (bf16[5,16,512]{2,1,0:T(8,128)(2,1)S(1)}, bf16[5,16,512]{2,1,0:T(8,128)(2,1)S(1)}, u32[]{:S(2)}, u32[]{:S(2)}) collective-permute-start(bf16[5,16,512]{2,1,0:T(8,128)(2,1)S(1)} %get-tuple-element.57), channel_id=1, source_target_pairs={{0,10},{2,8},{4,14},{6,12},{8,2},{10,0},{12,6},{14,4},{1,11},{3,9}... | collective-permute-start | bytes 245768 | tf_op jit(solution)/shard_map/ppermute | solution.py:347
  33.2 18.1 %collective-permute-start.19 = (bf16[5,16,512]{2,1,0:T(8,128)(2,1)S(1)}, bf16[5,16,512]{2,1,0:T(8,128)(2,1)S(1)}, u32[]{:S(2)}, u32[]{:S(2)}) collective-permute-start(bf16[5,16,512]{2,1,0:T(8,128)(2,1)S(1)} %get-tuple-element.58), channel_id=1, source_target_pairs={{0,12},{2,14},{4,8},{6,10},{8,4},{10,6},{12,0},{14,2},{1,13},{3,15... | collective-permute-start | bytes 245768 | tf_op jit(solution)/shard_map/ppermute | solution.py:347
  36.8 17.8 %collective-permute-start.20 = (bf16[5,16,512]{2,1,0:T(8,128)(2,1)S(1)}, bf16[5,16,512]{2,1,0:T(8,128)(2,1)S(1)}, u32[]{:S(2)}, u32[]{:S(2)}) collective-permute-start(bf16[5,16,512]{2,1,0:T(8,128)(2,1)S(1)} %get-tuple-element.59), channel_id=1, source_target_pairs={{0,14},{2,12},{4,10},{6,8},{8,6},{10,4},{12,2},{14,0},{1,15},{3,13... | collective-permute-start | bytes 245768 | tf_op jit(solution)/shard_map/ppermute | solution.py:347
  37.3 19.8 %collective-permute-start.10 = (bf16[7,16,512]{2,1,0:T(8,128)(2,1)S(1)}, bf16[7,16,512]{2,1,0:T(8,128)(2,1)S(1)}, u32[]{:S(2)}, u32[]{:S(2)}) collective-permute-start(bf16[7,16,512]{2,1,0:T(8,128)(2,1)S(1)} %get-tuple-element.48), channel_id=1, source_target_pairs={{0,8},{2,10},{4,12},{6,14},{8,0},{10,2},{12,4},{14,6},{1,9},{3,11}... | collective-permute-start | bytes 344072 | tf_op jit(solution)/shard_map/ppermute | solution.py:347
  37.6 23.1 %collective-permute-start.11 = (bf16[7,16,512]{2,1,0:T(8,128)(2,1)S(1)}, bf16[7,16,512]{2,1,0:T(8,128)(2,1)S(1)}, u32[]{:S(2)}, u32[]{:S(2)}) collective-permute-start(bf16[7,16,512]{2,1,0:T(8,128)(2,1)S(1)} %get-tuple-element.49), channel_id=1, source_target_pairs={{0,10},{2,8},{4,14},{6,12},{8,2},{10,0},{12,6},{14,4},{1,11},{3,9}... | collective-permute-start | bytes 344072 | tf_op jit(solution)/shard_map/ppermute | solution.py:347
  49.8 23.4 %collective-permute-start.12 = (bf16[7,16,512]{2,1,0:T(8,128)(2,1)S(1)}, bf16[7,16,512]{2,1,0:T(8,128)(2,1)S(1)}, u32[]{:S(2)}, u32[]{:S(2)}) collective-permute-start(bf16[7,16,512]{2,1,0:T(8,128)(2,1)S(1)} %get-tuple-element.50), channel_id=1, source_target_pairs={{0,12},{2,14},{4,8},{6,10},{8,4},{10,6},{12,0},{14,2},{1,13},{3,15... | collective-permute-start | bytes 344072 | tf_op jit(solution)/shard_map/ppermute | solution.py:347
  51.3 24.9 %collective-permute-start.13 = (bf16[7,16,512]{2,1,0:T(8,128)(2,1)S(1)}, bf16[7,16,512]{2,1,0:T(8,128)(2,1)S(1)}, u32[]{:S(2)}, u32[]{:S(2)}) collective-permute-start(bf16[7,16,512]{2,1,0:T(8,128)(2,1)S(1)} %get-tuple-element.51), channel_id=1, source_target_pairs={{0,14},{2,12},{4,10},{6,8},{8,6},{10,4},{12,2},{14,0},{1,15},{3,13... | collective-permute-start | bytes 344072 | tf_op jit(solution)/shard_map/ppermute | solution.py:347
  54.6 21.7 %collective-permute-start.7 = (bf16[7,16,512]{2,1,0:T(8,128)(2,1)S(1)}, bf16[7,16,512]{2,1,0:T(8,128)(2,1)S(1)}, u32[]{:S(2)}, u32[]{:S(2)}) collective-permute-start(bf16[7,16,512]{2,1,0:T(8,128)(2,1)S(1)} %get-tuple-element.45), channel_id=1, source_target_pairs={{0,2},{2,0},{4,6},{6,4},{8,10},{10,8},{12,14},{14,12},{1,3},{3,1},... | collective-permute-start | bytes 344072 | tf_op jit(solution)/shard_map/ppermute | solution.py:347
  57.0 23.1 %collective-permute-start.8 = (bf16[7,16,512]{2,1,0:T(8,128)(2,1)S(1)}, bf16[7,16,512]{2,1,0:T(8,128)(2,1)S(1)}, u32[]{:S(2)}, u32[]{:S(2)}) collective-permute-start(bf16[7,16,512]{2,1,0:T(8,128)(2,1)S(1)} %get-tuple-element.46), channel_id=1, source_target_pairs={{0,4},{2,6},{4,0},{6,2},{8,12},{10,14},{12,8},{14,10},{1,5},{3,7},... | collective-permute-start | bytes 344072 | tf_op jit(solution)/shard_map/ppermute | solution.py:347
  60.7 20.6 %collective-permute-start.9 = (bf16[7,16,512]{2,1,0:T(8,128)(2,1)S(1)}, bf16[7,16,512]{2,1,0:T(8,128)(2,1)S(1)}, u32[]{:S(2)}, u32[]{:S(2)}) collective-permute-start(bf16[7,16,512]{2,1,0:T(8,128)(2,1)S(1)} %get-tuple-element.47), channel_id=1, source_target_pairs={{0,6},{2,4},{4,2},{6,0},{8,14},{10,12},{12,10},{14,8},{1,7},{3,5},... | collective-permute-start | bytes 344072 | tf_op jit(solution)/shard_map/ppermute | solution.py:347
  60.8 1.0 copy-start.13
  61.8 1.0 copy-start.15
  62.8 0.8 copy-start.17
  63.7 0.8 copy-start.20
  64.4 0.7 copy-start.23
  65.2 0.9 copy-start.27
  66.0 7.2 %copy-start.11 = (bf16[4,16,512]{2,1,0:T(8,128)(2,1)S(1)}, bf16[4,16,512]{2,1,0:T(8,128)(2,1)}, u32[]{:S(2)}) copy-start(bf16[4,16,512]{2,1,0:T(8,128)(2,1)} %copy-done.10) | copy-start | bytes 196612
  66.0 10.2 %copy-start.9 = (bf16[4,16,512]{2,1,0:T(8,128)(2,1)S(1)}, bf16[4,16,512]{2,1,0:T(8,128)(2,1)}, u32[]{:S(2)}) copy-start(bf16[4,16,512]{2,1,0:T(8,128)(2,1)} %copy-done.8) | copy-start | bytes 196612
  66.0 10.2 %copy-start.7 = (bf16[4,16,512]{2,1,0:T(8,128)(2,1)S(1)}, bf16[4,16,512]{2,1,0:T(8,128)(2,1)}, u32[]{:S(2)}) copy-start(bf16[4,16,512]{2,1,0:T(8,128)(2,1)} %copy-done.6) | copy-start | bytes 196612
  66.0 14.0 %copy-start.5 = (bf16[4,16,512]{2,1,0:T(8,128)(2,1)S(1)}, bf16[4,16,512]{2,1,0:T(8,128)(2,1)}, u32[]{:S(2)}) copy-start(bf16[4,16,512]{2,1,0:T(8,128)(2,1)} %copy-done.4) | copy-start | bytes 196612
  66.0 15.3 %copy-start.3 = (bf16[4,16,512]{2,1,0:T(8,128)(2,1)S(1)}, bf16[4,16,512]{2,1,0:T(8,128)(2,1)}, u32[]{:S(2)}) copy-start(bf16[4,16,512]{2,1,0:T(8,128)(2,1)} %copy-done.2) | copy-start | bytes 196612
  66.1 18.0 %copy-start.14 = (bf16[768,256]{1,0:T(8,128)(2,1)S(1)}, bf16[768,256]{1,0:T(8,128)(2,1)}, u32[]{:S(2)}) copy-start(bf16[768,256]{1,0:T(8,128)(2,1)} %constant.64.clone.refs_13_) | copy-start | bytes 1179652
  66.1 18.0 %copy-start.16 = (bf16[768,256]{1,0:T(8,128)(2,1)S(1)}, bf16[768,256]{1,0:T(8,128)(2,1)}, u32[]{:S(2)}) copy-start(bf16[768,256]{1,0:T(8,128)(2,1)} %constant.65.clone.refs_14_) | copy-start | bytes 1179652
  66.1 18.0 %copy-start.18 = (bf16[256,128]{1,0:T(8,128)(2,1)S(1)}, bf16[256,128]{1,0:T(8,128)(2,1)}, u32[]{:S(2)}) copy-start(bf16[256,128]{1,0:T(8,128)(2,1)} %constant.70.clone.refs_19_) | copy-start | bytes 196612
  66.1 17.9 %copy-start.21 = (f32[2,32,128]{2,1,0:T(8,128)S(1)}, f32[2,32,128]{2,1,0:T(8,128)}, u32[]{:S(2)}) copy-start(f32[2,32,128]{2,1,0:T(8,128)} %constant.67.clone.refs_16_) | copy-start | bytes 98308
  66.1 17.9 %copy-start.25 = (bf16[7,16,512]{2,1,0:T(8,128)(2,1)S(1)}, bf16[7,16,512]{2,1,0:T(8,128)(2,1)}, u32[]{:S(2)}) copy-start(bf16[7,16,512]{2,1,0:T(8,128)(2,1)} %copy-done.24) | copy-start | bytes 344068
  73.3 20.8 %collective-permute-start.2 = (bf16[4,16,512]{2,1,0:T(8,128)(2,1)S(1)}, bf16[4,16,512]{2,1,0:T(8,128)(2,1)S(1)}, u32[]{:S(2)}, u32[]{:S(2)}) collective-permute-start(bf16[4,16,512]{2,1,0:T(8,128)(2,1)S(1)} %copy-done.11), channel_id=1, source_target_pairs={{0,6},{2,4},{4,2},{6,0},{8,14},{10,12},{12,10},{14,8},{1,7},{3,5},... | collective-permute-start | bytes 196616 | tf_op jit(solution)/shard_map/ppermute | solution.py:347
  76.3 17.8 %collective-permute-start.3 = (bf16[4,16,512]{2,1,0:T(8,128)(2,1)S(1)}, bf16[4,16,512]{2,1,0:T(8,128)(2,1)S(1)}, u32[]{:S(2)}, u32[]{:S(2)}) collective-permute-start(bf16[4,16,512]{2,1,0:T(8,128)(2,1)S(1)} %copy-done.9), channel_id=1, source_target_pairs={{0,8},{2,10},{4,12},{6,14},{8,0},{10,2},{12,4},{14,6},{1,9},{3,11}... | collective-permute-start | bytes 196616 | tf_op jit(solution)/shard_map/ppermute | solution.py:347
  76.3 17.8 %collective-permute-start.4 = (bf16[4,16,512]{2,1,0:T(8,128)(2,1)S(1)}, bf16[4,16,512]{2,1,0:T(8,128)(2,1)S(1)}, u32[]{:S(2)}, u32[]{:S(2)}) collective-permute-start(bf16[4,16,512]{2,1,0:T(8,128)(2,1)S(1)} %copy-done.7), channel_id=1, source_target_pairs={{0,10},{2,8},{4,14},{6,12},{8,2},{10,0},{12,6},{14,4},{1,11},{3,9}... | collective-permute-start | bytes 196616 | tf_op jit(solution)/shard_map/ppermute | solution.py:347
  80.1 14.0 %collective-permute-start.5 = (bf16[4,16,512]{2,1,0:T(8,128)(2,1)S(1)}, bf16[4,16,512]{2,1,0:T(8,128)(2,1)S(1)}, u32[]{:S(2)}, u32[]{:S(2)}) collective-permute-start(bf16[4,16,512]{2,1,0:T(8,128)(2,1)S(1)} %copy-done.5), channel_id=1, source_target_pairs={{0,12},{2,14},{4,8},{6,10},{8,4},{10,6},{12,0},{14,2},{1,13},{3,15... | collective-permute-start | bytes 196616 | tf_op jit(solution)/shard_map/ppermute | solution.py:347
  81.4 12.8 %collective-permute-start.6 = (bf16[4,16,512]{2,1,0:T(8,128)(2,1)S(1)}, bf16[4,16,512]{2,1,0:T(8,128)(2,1)S(1)}, u32[]{:S(2)}, u32[]{:S(2)}) collective-permute-start(bf16[4,16,512]{2,1,0:T(8,128)(2,1)S(1)} %copy-done.3), channel_id=1, source_target_pairs={{0,14},{2,12},{4,10},{6,8},{8,6},{10,4},{12,2},{14,0},{1,15},{3,13... | collective-permute-start | bytes 196616 | tf_op jit(solution)/shard_map/ppermute | solution.py:347
  84.1 10.2 %copy-start.29 = (bf16[4,16,512]{2,1,0:T(8,128)(2,1)S(1)}, bf16[4,16,512]{2,1,0:T(8,128)(2,1)}, u32[]{:S(2)}) copy-start(bf16[4,16,512]{2,1,0:T(8,128)(2,1)} %copy-done.28) | copy-start | bytes 196612
  101.5 11.5 %all-to-all-start.1 = ((f32[16,16,128]{2,1,0:T(8,128)}), f32[16,16,128]{2,1,0:T(8,128)S(1)}, u32[]{:S(2)}, u32[]{:S(2)}) async-start(f32[16,16,128]{2,1,0:T(8,128)} %bitcast.12), calls=%async_computation.1 | async-start | bytes 262144 | tf_op jit(solution)/shard_map/all_to_all | solution.py:374

commit v3 on v2

--- a/solution.py
+++ b/solution.py
@@ -22,7 +22,7 @@
 SPREAD_RATE = 0.5
 ABSORB_RATE = 0.05
 TERRAIN_ROWS = 4
-CHUNKS = (0.3125, 0.4375, 0.25)
+WHOLE_SHARE = 0.6875
 GROUP = 2
 
 F32 = jnp.float32
@@ -132,17 +132,20 @@
     return high, low
 
 
-def march_kernel(steps, batch, heights, first, sections, section, *refs):
-    slabs, refs = refs[:sections], refs[sections:]
+def march_kernel(steps, batch, heights, first, count, section, *refs):
+    slabs, refs = refs[:count], refs[count:]
     (
         terrain, cells, start_re, start_im, totals_in,
         w_forward, w_inverse, twiddle, spread, tilt, absorb, bins,
         end_re, end_im, totals,
-        levels, back_re, back_im, energy, power,
+        levels, arrived, back_re, back_im, energy, power,
     ) = refs
     sine, cosine = phase_polynomials()
-    for d in range(sections):
-        levels[section[0] ^ d] = slabs[d][...]
+    copies = []
+    for d, slab in enumerate(slabs):
+        place = levels if count == 1 else levels.at[section[0] ^ d]
+        copies.append(pltpu.make_async_copy(slab, place, arrived.at[d]))
+        copies[-1].start()
 
     def enter(columns, jl, put_re, put_im):
         parts = dft4(columns, -1)
@@ -179,31 +182,43 @@
             for i in range(count)
         ]
 
+    def binned(t):
+        summed = jnp.dot(energy[...], bins[...], preferred_element_type=F32)
+        row = summed[:batch]
+        for j in range(1, ROWS):
+            row = jnp.where(lane // (LANES // BIN) == j, summed[j * batch : (j + 1) * batch], row)
+        power[pl.ds(pl.multiple_of(t * batch, batch), batch), :] = row
+
     def step(t, carry):
-        for base in range(0, FOUR, GROUP):
-            qs = [ql + FOUR * qh for ql in range(base, base + GROUP) for qh in range(EIGHT)]
+        groups = [list(range(base, base + GROUP)) for base in range(0, FOUR, GROUP)]
+        rows = [[ql + FOUR * qh for ql in group for qh in range(EIGHT)] for group in groups]
+        products = []
+        for group in groups:
             pieces = []
-            for ql in range(base, base + GROUP):
+            for ql in group:
                 column = [(end_re[ql * EIGHT + jl], end_im[ql * EIGHT + jl]) for jl in range(EIGHT)]
                 for qh, (re, im) in enumerate(dft8(column, -1)):
                     q = ql + FOUR * qh
                     c, s = twiddle[0, q : q + 1, :], twiddle[1, q : q + 1, :]
                     pieces.append((re * c - im * s, re * s + im * c))
-            product = jnp.dot(joined(pieces), w_forward[...], preferred_element_type=F32)
+            products.append(jnp.dot(joined(pieces), w_forward[...], preferred_element_type=F32))
+        binned(jnp.maximum(t - 1, 0))
+        for i, qs in enumerate(rows):
             pieces = []
-            for q, (re, im) in zip(qs, parted(product, len(qs))):
+            for q, (re, im) in zip(qs, parted(products[i], len(qs))):
                 c, s = spread[0, q : q + 1, :], spread[1, q : q + 1, :]
                 pieces.append((re * c - im * s, re * s + im * c))
-            product = jnp.dot(joined(pieces), w_inverse[...], preferred_element_type=F32)
+            products[i] = jnp.dot(joined(pieces), w_inverse[...], preferred_element_type=F32)
+        for i, qs in enumerate(rows):
             pieces = []
-            for q, (re, im) in zip(qs, parted(product, len(qs))):
+            for q, (re, im) in zip(qs, parted(products[i], len(qs))):
                 c, s = twiddle[0, q : q + 1, :], twiddle[1, q : q + 1, :]
                 pieces.append((re * c + im * s, im * c - re * s))
-            for i in range(GROUP):
-                column = dft8(pieces[i * EIGHT : (i + 1) * EIGHT], 1)
+            for k, ql in enumerate(groups[i]):
+                column = dft8(pieces[k * EIGHT : (k + 1) * EIGHT], 1)
                 for jl in range(EIGHT):
-                    back_re[(base + i) * EIGHT + jl] = column[jl][0]
-                    back_im[(base + i) * EIGHT + jl] = column[jl][1]
+                    back_re[ql * EIGHT + jl] = column[jl][0]
+                    back_im[ql * EIGHT + jl] = column[jl][1]
 
         for jl in range(EIGHT):
             column = []
@@ -238,21 +253,18 @@
                 energy[j * batch : (j + 1) * batch, :] = jnp.concatenate([high, low], axis=1)
                 moved.append((re, im))
             enter(moved, jl, end_re, end_im)
-
-        summed = jnp.dot(energy[...], bins[...], preferred_element_type=F32)
-        row = summed[:batch]
-        for j in range(1, ROWS):
-            row = jnp.where(lane // (LANES // BIN) == j, summed[j * batch : (j + 1) * batch], row)
-        power[pl.ds(pl.multiple_of(t * batch, batch), batch), :] = row
         return carry
 
+    energy[...] = jnp.zeros_like(energy)
+    for copy in copies:
+        copy.wait()
     lax.fori_loop(0, steps, step, 0)
-
-    count = steps * batch
+    binned(steps - 1)
+
     tiles = totals.shape[0]
-    hot = (lax.broadcasted_iota(jnp.int32, (tiles, count), 0) == cells[...]).astype(F32).astype(BF16)
+    hot = (lax.broadcasted_iota(jnp.int32, (tiles, steps * batch), 0) == cells[...]).astype(F32).astype(BF16)
     value = power[...]
-    high, rest = value.astype(BF16), None
+    high = value.astype(BF16)
     rest = value - high.astype(F32)
     middle = rest.astype(BF16)
     low = (rest - middle.astype(F32)).astype(BF16)
@@ -266,18 +278,20 @@
 
 
 def march(section, slabs, terrain, cells, start, totals, consts, tiles, first):
-    sections = len(slabs)
-    steps, batch, heights = slabs[0].shape
+    steps, batch, heights = slabs[0].shape[-3:]
+    sections = H // heights
     state = jax.ShapeDtypeStruct((ROWS, batch, LANES), F32)
     vmem = pl.BlockSpec(memory_space=pltpu.VMEM)
     smem = pl.BlockSpec(memory_space=pltpu.SMEM)
+    anywhere = pl.BlockSpec(memory_space=pl.ANY)
     call = pl.pallas_call(
-        functools.partial(march_kernel, steps, batch, heights, first, sections),
+        functools.partial(march_kernel, steps, batch, heights, first, len(slabs)),
         out_shape=(state, state, jax.ShapeDtypeStruct((tiles, BINS), F32)),
-        in_specs=[smem] + [vmem] * (sections + 12),
+        in_specs=[smem] + [anywhere] * len(slabs) + [vmem] * 12,
         out_specs=(vmem, vmem, vmem),
         scratch_shapes=[
             pltpu.VMEM((sections, steps, batch, heights), BF16),
+            pltpu.SemaphoreType.DMA((len(slabs),)),
             pltpu.VMEM((ROWS, batch, LANES), F32),
             pltpu.VMEM((ROWS, batch, LANES), F32),
             pltpu.VMEM((ROWS * batch, 2 * LANES), BF16),
@@ -292,21 +306,52 @@
     return call(section, *slabs, terrain, cells, *start, totals, *consts)
 
 
+def turned(levels, base, rows, begin, end, own, put):
+    steps, heights = levels.shape[1:]
+    columns = [slice(c * LANES, (c + 1) * LANES) for c in range(heights // LANES)]
+    for b in range(own):
+        for c, column in enumerate(columns):
+            rows[c, b * steps : (b + 1) * steps, :] = levels[base + b, :, column].astype(F32)
+    for t in range(begin, end):
+        for c, column in enumerate(columns):
+            put(t - begin, column, rows[c, pl.ds(t, own, stride=steps), :].astype(BF16))
+
+
+def filled(taken, batch):
+    if taken.shape[0] < batch:
+        return jnp.pad(taken, ((0, batch - taken.shape[0]), (0, 0)))
+    return taken
+
+
+def deal_kernel(begin, end, levels, out, rows):
+    def put(t, column, taken):
+        out[0, t, :, column] = filled(taken, out.shape[2])
+
+    turned(levels, 0, rows, begin, end, levels.shape[0], put)
+
+
+def deal(levels, begin, end, sections, own, batch):
+    steps, heights = levels.shape[1:]
+    return pl.pallas_call(
+        functools.partial(deal_kernel, begin, end),
+        grid=(sections,),
+        out_shape=jax.ShapeDtypeStruct((sections, end - begin, batch, heights), BF16),
+        in_specs=[pl.BlockSpec((own, steps, heights), lambda d: (d, 0, 0))],
+        out_specs=pl.BlockSpec((1, end - begin, batch, heights), lambda d: (d, 0, 0, 0)),
+        scratch_shapes=[pltpu.VMEM((heights // LANES, own * steps, LANES), F32)],
+        compiler_params=pltpu.CompilerParams(vmem_limit_bytes=32 * 1024 * 1024),
+        cost_estimate=pl.CostEstimate(flops=1_000_000_000, bytes_accessed=4 * 1024 * 1024, transcendentals=0),
+        name="deal",
+    )(levels)
+
+
 def cut_kernel(begin, end, own, section, levels, *refs):
     slabs, rows = refs[:-1], refs[-1]
-    steps, heights = levels.shape[1:]
-    columns = [slice(c * LANES, (c + 1) * LANES) for c in range(heights // LANES)]
     for d, slab in enumerate(slabs):
-        base = (section[0] ^ d) * own
-        for b in range(own):
-            for c, column in enumerate(columns):
-                rows[c, b * steps : (b + 1) * steps, :] = levels[base + b, :, column].astype(F32)
-        for t in range(begin, end):
-            for c, column in enumerate(columns):
-                taken = rows[c, pl.ds(t, own, stride=steps), :].astype(BF16)
-                if own < slab.shape[1]:
-                    taken = jnp.pad(taken, ((0, slab.shape[1] - own), (0, 0)))
-                slab[t - begin, :, column] = taken
+        def put(t, column, taken, slab=slab):
+            slab[t, :, column] = filled(taken, slab.shape[1])
+
+        turned(levels, (section[0] ^ d) * own, rows, begin, end, own, put)
 
 
 def cut(section, levels, begin, end, sections, own, batch):
@@ -327,6 +372,23 @@
     return call(section, levels)
 
 
+def gather_small(value):
+    radial, sections = lax.axis_index("radial"), lax.axis_size("range")
+    other = lax.ppermute(value, "radial", [(0, 1), (1, 0)])
+    pair = jnp.stack([jnp.where(radial == 0, value, other), jnp.where(radial == 0, other, value)])
+    section = lax.axis_index("range")
+    held = jnp.zeros((sections, *pair.shape), pair.dtype)
+    held = lax.dynamic_update_index_in_dim(held, pair, section, 0)
+    width = 1
+    while width < sections:
+        base = section // width * width
+        part = lax.dynamic_slice_in_dim(held, base, width, 0)
+        part = lax.ppermute(part, "range", [(i, i ^ width) for i in range(sections)])
+        held = lax.dynamic_update_slice_in_dim(held, part, base ^ width, 0)
+        width *= 2
+    return held
+
+
 def local(refractivity, source, terrain, tile_map):
     sections = lax.axis_size("range")
     owners = sections * lax.axis_size("radial")
@@ -336,20 +398,17 @@
     batch = -(-own // 16) * 16
 
     small = jnp.concatenate([terrain.T, tile_map.T])
-    edges = [0]
-    for share in CHUNKS:
-        edges.append(edges[-1] + max(1, round(share * steps)))
+    middle = round(WHOLE_SHARE * steps)
     section = lax.axis_index("range").astype(jnp.int32).reshape(1)
-    pieces = []
-    for begin, end in zip(edges[:-1], edges[1:]):
-        slabs = list(cut(section, refractivity, begin, end, sections, own, batch))
-        for d in reversed(range(1, sections)):
-            slabs[d] = lax.ppermute(slabs[d], "range", [(i, i ^ d) for i in range(sections)])
-        pieces.append(slabs)
-    everyone = lax.all_to_all(
-        jnp.broadcast_to(small, (owners, *small.shape)), ("range", "radial"), 0, 0, tiled=True
-    )
-    everyone = everyone.reshape(sections, lax.axis_size("radial"), 2, -1, radials)
+    dealt = deal(refractivity, 0, middle, sections, own, batch)
+    refractivity, dealt = lax.optimization_barrier((refractivity, dealt))
+    whole = lax.all_to_all(dealt, "range", 0, 0, tiled=True)
+    slabs = list(cut(section, refractivity, middle, steps, sections, own, batch))
+    small, slabs[0] = lax.optimization_barrier((small, slabs[0]))
+    everyone = gather_small(small)
+    for d in reversed(range(1, sections)):
+        slabs[d] = lax.ppermute(slabs[d], "range", [(i, i ^ d) for i in range(sections)])
+    everyone = everyone.reshape(*everyone.shape[:2], 2, -1, radials)
     my_ids = (lax.axis_index("range") * lax.axis_size("radial") + lax.axis_index("radial")) * TILE_DEV
     my_ids = my_ids + jnp.arange(TILE_DEV, dtype=jnp.int32)
     counts = jnp.sum(
@@ -366,7 +425,7 @@
     consts = [jnp.asarray(v) for v in tables()]
     start = (source[0].reshape(ROWS, LANES), source[1].reshape(ROWS, LANES))
     totals = jnp.zeros((tiles, BINS), F32)
-    for piece, begin, end in zip(pieces, edges[:-1], edges[1:]):
+    for piece, begin, end in (([whole], 0, middle), (slabs, middle, steps)):
         *start, totals = march(
             section, piece, terrain_all[begin:end], cells_all[begin:end].reshape(1, -1),
             start, totals, consts, tiles, begin == 0,

time: 114 us -> 96.9 us (0.85)
  starting transfers between devices: 45.2 us -> 30.5 us
    ppermute x21 -> x7, starting transfers between devices: 34.2 us -> 10.7 us  [local(): lax.ppermute(slabs[d], 'range', [(i, i ^ d) for i in range(sections)])]
    ppermute x21 -> x7, waiting for transfers between devices: 17.9 us -> 0.02 us  [local(): lax.ppermute(slabs[d], 'range', [(i, i ^ d) for i in range(sections)])]
    ppermute x0 -> x4, waiting for transfers between devices: none -> 16.8 us  [the longest x3 15.7 us: gather_small(): lax.ppermute(part, 'range', [(i, i ^ width) for i in range(sections)])]
    ppermute x0 -> x4, starting transfers between devices: none -> 8.94 us  [the longest x3 8.87 us: gather_small(): lax.ppermute(part, 'range', [(i, i ^ width) for i in range(sections)])]
    pallas_call x0 -> x1, Pallas kernels: none -> 3.5 us  [deal(): pl.pallas_call(functools.partial(deal_kernel, begin, end), grid=(sections...]
    pallas_call x3 -> x1, Pallas kernels: 3.23 us -> 0.57 us  [cut(): return call(section, levels)]
    pallas_call x3 -> x2, Pallas kernels: 24.4 us -> 22.9 us  [march(): return call(section, *slabs, terrain, cells, *start, totals, *consts)]
    unnamed x62 -> x46, local copies, waits for them, and re-layouts: 11.2 us -> 11.7 us
  transfers between devices with their start and end apart: 23 -> 13, of which waited for: 6 -> 5; matrix products, arithmetic and copies ran while one was open for 1% -> 2% of each run, Pallas kernels for 18% -> 16%
where the time goes in v3:
time: 96.9 us; the launch traced here: 96.2 us
  starting transfers between devices  30.5 us (31%)
  Pallas kernels  26.9 us (28%)
  waiting for transfers between devices  24.5 us (25%)
  local copies, waits for them, and re-layouts  13 us (13%)
    pallas_call x2, Pallas kernels, march(): return call(section, *slabs, terrain, cells, *start, totals, *consts)  22.9 us
    ppermute x3, waiting for transfers between devices, gather_small(): lax.ppermute(part, 'range', [(i, i ^ width) for i in range(sections)])  15.7 us
    unnamed x46, local copies, waits for them, and re-layouts  11.7 us
    ppermute x7, starting transfers between devices, local(): lax.ppermute(slabs[d], 'range', [(i, i ^ d) for i in range(sections)])  10.7 us
    ppermute x3, starting transfers between devices, gather_small(): lax.ppermute(part, 'range', [(i, i ^ width) for i in range(sections)])  8.87 us
    all_to_all x1, waiting for transfers between devices, local(): lax.all_to_all(totals.reshape(owners, TILE_DEV, BINS), ('range', 'radial'...  7.65 us
    all_to_all x1, starting transfers between devices, local(): whole = lax.all_to_all(dealt, 'range', 0, 0, tiled=True)  7.41 us
    all_to_all x1, starting transfers between devices, local(): lax.all_to_all(totals.reshape(owners, TILE_DEV, BINS), ('range', 'radial'...  3.52 us
  transfers between devices with their start and end apart: 13, of which 5 were waited for; matrix products, arithmetic and copies ran while one was open for 2% of the time, Pallas kernels for 16%

profile of v3, /device:TPU:0, one launch (start us, length us, event | category | flops | bytes accessed | tf_op | source)
XLA Modules:
  0.0 96.2 jit_solution(17013030492217732294)
XLA Ops:
  0.0 1.6 %copy-done = bf16[128,16,512]{2,1,0:T(8,128)(2,1)S(1)} copy-done((bf16[128,16,512]{2,1,0:T(8,128)(2,1)S(1)}, bf16[128,16,512]{2,1,0:T(8,128)(2,1)}, u32[]{:S(2)}) %copy-start) | copy-done | bytes 2097176
  1.6 3.5 %deal.1 = bf16[8,11,16,512]{3,2,1,0:T(8,128)(2,1)} custom-call(bf16[128,16,512]{2,1,0:T(8,128)(2,1)S(1)} %copy-done), custom_call_target="tpu_custom_call" | custom-call | flops 1000000000 | bytes 4194304 | tf_op jit(solution)/shard_map/deal/pallas_call | solution.py:335
  5.1 7.4 %all-to-all-start = ((bf16[8,11,16,512]{3,2,1,0:T(8,128)(2,1)}), bf16[8,11,16,512]{3,2,1,0:T(8,128)(2,1)S(1)}, u32[]{:S(2)}, u32[]{:S(2)}) async-start(bf16[8,11,16,512]{3,2,1,0:T(8,128)(2,1)} %deal.1), calls=%async_computation | async-start | bytes 2883584 | tf_op jit(solution)/shard_map/all_to_all | solution.py:405
  12.5 0.0 copy-done.1
  12.5 0.0 copy-start.21
  12.5 0.0 copy-start.22
  12.5 0.0 copy-start.17
  12.5 0.6 cut.1
  13.1 0.0 copy-start.2
  13.1 0.6 copy-done.2
  13.8 0.6 copy-done.3
  14.4 0.6 copy-done.4
  15.0 0.6 copy-done.5
  15.6 0.6 copy-done.6
  16.3 0.6 copy-done.7
  16.9 0.6 copy-done.8
  17.5 0.6 copy-done.19
  18.2 0.0 copy-done.21
  18.2 0.0 copy-done.22
  18.2 0.1 collective-permute-start.7
  18.3 1.1 %collective-permute-done.7 = s32[4,128]{1,0:T(4,128)S(1)} collective-permute-done((s32[4,128]{1,0:T(4,128)S(1)}, s32[4,128]{1,0:T(4,128)S(1)}, u32[]{:S(2)}, u32[]{:S(2)}) %collective-permute-start.7) | collective-permute-done | bytes 2080 | tf_op jit(solution)/shard_map/ppermute | solution.py:377
  19.5 2.1 %collective-permute-start.8 = (s32[1,2,4,128]{3,2,1,0:T(4,128)S(1)}, s32[1,2,4,128]{3,2,1,0:T(4,128)S(1)}, u32[]{:S(2)}, u32[]{:S(2)}) collective-permute-start(s32[1,2,4,128]{3,2,1,0:T(4,128)S(1)} %constant_dynamic-slice_fusion.3), channel_id=1, source_target_pairs={{0,2},{2,0},{4,6},{6,4},{8,10},{10,8},{12,14},{14,12},{1,3},{3,1},... | collective-permute-start | bytes 12296 | tf_op jit(solution)/shard_map/ppermute | solution.py:386
  21.5 2.1 %collective-permute-done.8 = s32[1,2,4,128]{3,2,1,0:T(4,128)S(1)} collective-permute-done((s32[1,2,4,128]{3,2,1,0:T(4,128)S(1)}, s32[1,2,4,128]{3,2,1,0:T(4,128)S(1)}, u32[]{:S(2)}, u32[]{:S(2)}) %collective-permute-start.8) | collective-permute-done | bytes 4128 | tf_op jit(solution)/shard_map/ppermute | solution.py:386
  23.7 2.5 %collective-permute-start.9 = (s32[2,2,4,128]{3,2,1,0:T(4,128)S(1)}, s32[2,2,4,128]{3,2,1,0:T(4,128)S(1)}, u32[]{:S(2)}, u32[]{:S(2)}) collective-permute-start(s32[2,2,4,128]{3,2,1,0:T(4,128)S(1)} %constant_dynamic-slice_fusion.2), channel_id=1, source_target_pairs={{0,4},{2,6},{4,0},{6,2},{8,12},{10,14},{12,8},{14,10},{1,5},{3,7},... | collective-permute-start | bytes 24584 | tf_op jit(solution)/shard_map/ppermute | solution.py:386
  26.2 2.4 %collective-permute-start = (bf16[5,16,512]{2,1,0:T(8,128)(2,1)}, bf16[5,16,512]{2,1,0:T(8,128)(2,1)S(1)}, u32[]{:S(2)}, u32[]{:S(2)}) collective-permute-start(bf16[5,16,512]{2,1,0:T(8,128)(2,1)} %copy-done.8), channel_id=1, source_target_pairs={{0,2},{2,0},{4,6},{6,4},{8,10},{10,8},{12,14},{14,12},{1,3},{3,1},... | collective-permute-start | bytes 245768 | tf_op jit(solution)/shard_map/ppermute | solution.py:410
  28.6 0.1 collective-permute-start.1
  28.6 1.4 %collective-permute-start.2 = (bf16[5,16,512]{2,1,0:T(8,128)(2,1)}, bf16[5,16,512]{2,1,0:T(8,128)(2,1)S(1)}, u32[]{:S(2)}, u32[]{:S(2)}) collective-permute-start(bf16[5,16,512]{2,1,0:T(8,128)(2,1)} %copy-done.6), channel_id=1, source_target_pairs={{0,6},{2,4},{4,2},{6,0},{8,14},{10,12},{12,10},{14,8},{1,7},{3,5},... | collective-permute-start | bytes 245768 | tf_op jit(solution)/shard_map/ppermute | solution.py:410
  30.0 2.1 %collective-permute-start.3 = (bf16[5,16,512]{2,1,0:T(8,128)(2,1)}, bf16[5,16,512]{2,1,0:T(8,128)(2,1)S(1)}, u32[]{:S(2)}, u32[]{:S(2)}) collective-permute-start(bf16[5,16,512]{2,1,0:T(8,128)(2,1)} %copy-done.5), channel_id=1, source_target_pairs={{0,8},{2,10},{4,12},{6,14},{8,0},{10,2},{12,4},{14,6},{1,9},{3,11}... | collective-permute-start | bytes 245768 | tf_op jit(solution)/shard_map/ppermute | solution.py:410
  32.1 5.7 %collective-permute-done.9 = s32[2,2,4,128]{3,2,1,0:T(4,128)S(1)} collective-permute-done((s32[2,2,4,128]{3,2,1,0:T(4,128)S(1)}, s32[2,2,4,128]{3,2,1,0:T(4,128)S(1)}, u32[]{:S(2)}, u32[]{:S(2)}) %collective-permute-start.9) | collective-permute-done | bytes 8224 | tf_op jit(solution)/shard_map/ppermute | solution.py:386
  37.8 4.3 %collective-permute-start.10 = (s32[4,2,4,128]{3,2,1,0:T(4,128)S(1)}, s32[4,2,4,128]{3,2,1,0:T(4,128)S(1)}, u32[]{:S(2)}, u32[]{:S(2)}) collective-permute-start(s32[4,2,4,128]{3,2,1,0:T(4,128)S(1)} %constant_dynamic-slice_fusion.1), channel_id=1, source_target_pairs={{0,8},{2,10},{4,12},{6,14},{8,0},{10,2},{12,4},{14,6},{1,9},{3,11}... | collective-permute-start | bytes 49160 | tf_op jit(solution)/shard_map/ppermute | solution.py:386
  42.1 0.9 fusion.1
  43.0 7.9 %collective-permute-done.10 = s32[4,2,4,128]{3,2,1,0:T(4,128)S(1)} collective-permute-done((s32[4,2,4,128]{3,2,1,0:T(4,128)S(1)}, s32[4,2,4,128]{3,2,1,0:T(4,128)S(1)}, u32[]{:S(2)}, u32[]{:S(2)}) %collective-permute-start.10) | collective-permute-done | bytes 16416 | tf_op jit(solution)/shard_map/ppermute | solution.py:386
  50.9 0.4 collective-permute-start.4
  51.3 0.1 copy_bitcast_fusion
  51.4 0.1 reshape.32.refs_2_
  51.5 0.1 reshape.31.refs_9_
  51.6 0.0 collective-permute-done.refs_1_
  51.6 1.5 %collective-permute-start.5 = (bf16[5,16,512]{2,1,0:T(8,128)(2,1)}, bf16[5,16,512]{2,1,0:T(8,128)(2,1)S(1)}, u32[]{:S(2)}, u32[]{:S(2)}) collective-permute-start(bf16[5,16,512]{2,1,0:T(8,128)(2,1)} %copy-done.3), channel_id=1, source_target_pairs={{0,12},{2,14},{4,8},{6,10},{8,4},{10,6},{12,0},{14,2},{1,13},{3,15... | collective-permute-start | bytes 245768 | tf_op jit(solution)/shard_map/ppermute | solution.py:410
  53.1 0.0 collective-permute-done.1.refs_2_
  53.1 2.8 %collective-permute-start.6 = (bf16[5,16,512]{2,1,0:T(8,128)(2,1)}, bf16[5,16,512]{2,1,0:T(8,128)(2,1)S(1)}, u32[]{:S(2)}, u32[]{:S(2)}) collective-permute-start(bf16[5,16,512]{2,1,0:T(8,128)(2,1)} %copy-done.2), channel_id=1, source_target_pairs={{0,14},{2,12},{4,10},{6,8},{8,6},{10,4},{12,2},{14,0},{1,15},{3,13... | collective-permute-start | bytes 245768 | tf_op jit(solution)/shard_map/ppermute | solution.py:410
  55.9 0.0 all-to-all-done.refs_0_
  55.9 0.1 broadcast_in_dim.26.refs_1_
  56.0 0.0 copy-done.17
  56.0 0.0 copy-start.9
  56.0 1.0 %copy-done.9 = bf16[768,256]{1,0:T(8,128)(2,1)S(1)} copy-done((bf16[768,256]{1,0:T(8,128)(2,1)S(1)}, bf16[768,256]{1,0:T(8,128)(2,1)}, u32[]{:S(2)}) %copy-start.9) | copy-done | bytes 393240
  57.0 1.0 %copy-done.11 = bf16[768,256]{1,0:T(8,128)(2,1)S(1)} copy-done((bf16[768,256]{1,0:T(8,128)(2,1)S(1)}, bf16[768,256]{1,0:T(8,128)(2,1)}, u32[]{:S(2)}) %copy-start.11) | copy-done | bytes 393240
  58.0 0.8 copy-done.12
  58.8 0.8 copy-done.14
  59.6 0.8 copy-done.16
  60.4 0.7 copy-done.18
  61.1 14.4 %march.2 = (f32[32,16,128]{2,1,0:T(8,128)S(1)}, f32[32,16,128]{2,1,0:T(8,128)S(1)}, f32[256,128]{1,0:T(8,128)S(1)}) custom-call(s32[1]{0:T(128)} %bitcast.section, bf16[8,11,16,512]{3,2,1,0:T(8,128)(2,1)S(1)} %all-to-all-done.refs_0_, s32[11,16,128]{2,1,0:T(8,128)S(1)} %broadcast_in_dim.26.refs_1_, s32[1,176]{1,0:T(1,128)S(1)} %reshape.32.refs_2_, ...), custom_call_target="tpu_custom_call" | custom-call | flops 17600000000 | bytes 4194304 | tf_op jit(solution)/shard_map/march/pallas_call | solution.py:306
  75.5 0.0 collective-permute-done.2.refs_3_
  75.5 0.0 collective-permute-done.3.refs_4_
  75.5 0.0 collective-permute-done.4.refs_5_
  75.5 0.0 collective-permute-done.5.refs_6_
  75.5 0.0 collective-permute-done.6.refs_7_
  75.5 0.1 broadcast_in_dim.25.refs_8_
  75.6 0.0 copy-done.10
  75.6 0.0 copy-done.13
  75.6 8.5 %march.3 = (f32[32,16,128]{2,1,0:T(8,128)}, f32[32,16,128]{2,1,0:T(8,128)}, f32[256,128]{1,0:T(8,128)}) custom-call(s32[1]{0:T(128)} %bitcast.section, bf16[5,16,512]{2,1,0:T(8,128)(2,1)S(1)} %copy-done.20, bf16[5,16,512]{2,1,0:T(8,128)(2,1)S(1)} %collective-permute-done.refs_1_, bf16[5,16,512]{2,1,0:T(8,128)(2,1)S(1)} %collective-permute-done.1.refs_2_, ...), custom_call_target="tpu_custom_call" | custom-call | flops 8000000000 | bytes 4194304 | tf_op jit(solution)/shard_map/march/pallas_call | solution.py:306
  84.1 3.5 %all-to-all-start.1 = ((f32[16,16,128]{2,1,0:T(8,128)}), f32[16,16,128]{2,1,0:T(8,128)S(1)}, u32[]{:S(2)}, u32[]{:S(2)}) async-start(f32[16,16,128]{2,1,0:T(8,128)} %bitcast.14), calls=%async_computation.1 | async-start | bytes 262144 | tf_op jit(solution)/shard_map/all_to_all | solution.py:433
  87.7 0.2 convert_reduce_fusion
  87.9 7.6 %all-to-all-done.1 = f32[16,16,128]{2,1,0:T(8,128)S(1)} async-done(((f32[16,16,128]{2,1,0:T(8,128)}), f32[16,16,128]{2,1,0:T(8,128)S(1)}, u32[]{:S(2)}, u32[]{:S(2)}) %all-to-all-start.1) | async-done | bytes 131104 | tf_op jit(solution)/shard_map/all_to_all | solution.py:433
  95.6 0.7 broadcast_divide_fusion
  (37 shorter events, 0.2 us)
Async XLA Ops:
  0.0 1.6 %copy-start = (bf16[128,16,512]{2,1,0:T(8,128)(2,1)S(1)}, bf16[128,16,512]{2,1,0:T(8,128)(2,1)}, u32[]{:S(2)}) copy-start(bf16[128,16,512]{2,1,0:T(8,128)(2,1)} %levels.2) | copy-start | bytes 6291460
  5.1 7.4 %copy-start.1 = (bf16[128,16,512]{2,1,0:T(8,128)(2,1)S(1)}, bf16[128,16,512]{2,1,0:T(8,128)(2,1)}, u32[]{:S(2)}) copy-start(bf16[128,16,512]{2,1,0:T(8,128)(2,1)} %levels.2) | copy-start | bytes 6291460
  5.1 50.8 %all-to-all-start = ((bf16[8,11,16,512]{3,2,1,0:T(8,128)(2,1)}), bf16[8,11,16,512]{3,2,1,0:T(8,128)(2,1)S(1)}, u32[]{:S(2)}, u32[]{:S(2)}) async-start(bf16[8,11,16,512]{3,2,1,0:T(8,128)(2,1)} %deal.1), calls=%async_computation | async-start | bytes 2883584 | tf_op jit(solution)/shard_map/all_to_all | solution.py:405
  12.5 5.7 %copy-start.21 = (s32[128,2]{0,1:T(2,128)S(1)}, s32[128,2]{0,1:T(2,128)}, u32[]{:S(2)}) copy-start(s32[128,2]{0,1:T(2,128)} %param.14) | copy-start | bytes 3076
  12.5 5.6 %copy-start.22 = (s32[128,2]{0,1:T(2,128)S(1)}, s32[128,2]{0,1:T(2,128)}, u32[]{:S(2)}) copy-start(s32[128,2]{0,1:T(2,128)} %param.13) | copy-start | bytes 3076
  12.5 43.5 %copy-start.17 = (f32[32,128]{1,0:T(8,128)S(1)}, f32[32,128]{1,0:T(8,128)}, u32[]{:S(2)}) copy-start(f32[32,128]{1,0:T(8,128)} %constant.107.clone.refs_11_.refs_18_) | copy-start | bytes 49156
  13.1 0.6 copy-start.2
  13.8 0.6 copy-start.3
  14.4 0.6 copy-start.4
  15.0 0.6 copy-start.5
  15.6 0.6 copy-start.6
  16.3 0.6 copy-start.7
  16.9 0.6 copy-start.8
  17.5 0.6 copy-start.19
  18.2 1.2 %collective-permute-start.7 = (s32[4,128]{1,0:T(4,128)S(1)}, s32[4,128]{1,0:T(4,128)S(1)}, u32[]{:S(2)}, u32[]{:S(2)}) collective-permute-start(s32[4,128]{1,0:T(4,128)S(1)} %pad_add_fusion), channel_id=1, source_target_pairs={{0,1},{1,0},{2,3},{3,2},{4,5},{5,4},{6,7},{7,6},{8,9},{9,8},{10,11... | collective-permute-start | bytes 6152 | tf_op jit(solution)/shard_map/ppermute | solution.py:377
  19.5 4.2 %collective-permute-start.8 = (s32[1,2,4,128]{3,2,1,0:T(4,128)S(1)}, s32[1,2,4,128]{3,2,1,0:T(4,128)S(1)}, u32[]{:S(2)}, u32[]{:S(2)}) collective-permute-start(s32[1,2,4,128]{3,2,1,0:T(4,128)S(1)} %constant_dynamic-slice_fusion.3), channel_id=1, source_target_pairs={{0,2},{2,0},{4,6},{6,4},{8,10},{10,8},{12,14},{14,12},{1,3},{3,1},... | collective-permute-start | bytes 12296 | tf_op jit(solution)/shard_map/ppermute | solution.py:386
  23.7 14.1 %collective-permute-start.9 = (s32[2,2,4,128]{3,2,1,0:T(4,128)S(1)}, s32[2,2,4,128]{3,2,1,0:T(4,128)S(1)}, u32[]{:S(2)}, u32[]{:S(2)}) collective-permute-start(s32[2,2,4,128]{3,2,1,0:T(4,128)S(1)} %constant_dynamic-slice_fusion.2), channel_id=1, source_target_pairs={{0,4},{2,6},{4,0},{6,2},{8,12},{10,14},{12,8},{14,10},{1,5},{3,7},... | collective-permute-start | bytes 24584 | tf_op jit(solution)/shard_map/ppermute | solution.py:386
  26.2 25.4 %collective-permute-start = (bf16[5,16,512]{2,1,0:T(8,128)(2,1)}, bf16[5,16,512]{2,1,0:T(8,128)(2,1)S(1)}, u32[]{:S(2)}, u32[]{:S(2)}) collective-permute-start(bf16[5,16,512]{2,1,0:T(8,128)(2,1)} %copy-done.8), channel_id=1, source_target_pairs={{0,2},{2,0},{4,6},{6,4},{8,10},{10,8},{12,14},{14,12},{1,3},{3,1},... | collective-permute-start | bytes 245768 | tf_op jit(solution)/shard_map/ppermute | solution.py:410
  28.6 24.5 %collective-permute-start.1 = (bf16[5,16,512]{2,1,0:T(8,128)(2,1)}, bf16[5,16,512]{2,1,0:T(8,128)(2,1)S(1)}, u32[]{:S(2)}, u32[]{:S(2)}) collective-permute-start(bf16[5,16,512]{2,1,0:T(8,128)(2,1)} %copy-done.7), channel_id=1, source_target_pairs={{0,4},{2,6},{4,0},{6,2},{8,12},{10,14},{12,8},{14,10},{1,5},{3,7},... | collective-permute-start | bytes 245768 | tf_op jit(solution)/shard_map/ppermute | solution.py:410
  28.6 46.8 %collective-permute-start.2 = (bf16[5,16,512]{2,1,0:T(8,128)(2,1)}, bf16[5,16,512]{2,1,0:T(8,128)(2,1)S(1)}, u32[]{:S(2)}, u32[]{:S(2)}) collective-permute-start(bf16[5,16,512]{2,1,0:T(8,128)(2,1)} %copy-done.6), channel_id=1, source_target_pairs={{0,6},{2,4},{4,2},{6,0},{8,14},{10,12},{12,10},{14,8},{1,7},{3,5},... | collective-permute-start | bytes 245768 | tf_op jit(solution)/shard_map/ppermute | solution.py:410
  30.0 45.5 %collective-permute-start.3 = (bf16[5,16,512]{2,1,0:T(8,128)(2,1)}, bf16[5,16,512]{2,1,0:T(8,128)(2,1)S(1)}, u32[]{:S(2)}, u32[]{:S(2)}) collective-permute-start(bf16[5,16,512]{2,1,0:T(8,128)(2,1)} %copy-done.5), channel_id=1, source_target_pairs={{0,8},{2,10},{4,12},{6,14},{8,0},{10,2},{12,4},{14,6},{1,9},{3,11}... | collective-permute-start | bytes 245768 | tf_op jit(solution)/shard_map/ppermute | solution.py:410
  37.8 13.1 %collective-permute-start.10 = (s32[4,2,4,128]{3,2,1,0:T(4,128)S(1)}, s32[4,2,4,128]{3,2,1,0:T(4,128)S(1)}, u32[]{:S(2)}, u32[]{:S(2)}) collective-permute-start(s32[4,2,4,128]{3,2,1,0:T(4,128)S(1)} %constant_dynamic-slice_fusion.1), channel_id=1, source_target_pairs={{0,8},{2,10},{4,12},{6,14},{8,0},{10,2},{12,4},{14,6},{1,9},{3,11}... | collective-permute-start | bytes 49160 | tf_op jit(solution)/shard_map/ppermute | solution.py:386
  50.9 24.6 %collective-permute-start.4 = (bf16[5,16,512]{2,1,0:T(8,128)(2,1)}, bf16[5,16,512]{2,1,0:T(8,128)(2,1)S(1)}, u32[]{:S(2)}, u32[]{:S(2)}) collective-permute-start(bf16[5,16,512]{2,1,0:T(8,128)(2,1)} %copy-done.4), channel_id=1, source_target_pairs={{0,10},{2,8},{4,14},{6,12},{8,2},{10,0},{12,6},{14,4},{1,11},{3,9}... | collective-permute-start | bytes 245768 | tf_op jit(solution)/shard_map/ppermute | solution.py:410
  51.6 23.9 %collective-permute-start.5 = (bf16[5,16,512]{2,1,0:T(8,128)(2,1)}, bf16[5,16,512]{2,1,0:T(8,128)(2,1)S(1)}, u32[]{:S(2)}, u32[]{:S(2)}) collective-permute-start(bf16[5,16,512]{2,1,0:T(8,128)(2,1)} %copy-done.3), channel_id=1, source_target_pairs={{0,12},{2,14},{4,8},{6,10},{8,4},{10,6},{12,0},{14,2},{1,13},{3,15... | collective-permute-start | bytes 245768 | tf_op jit(solution)/shard_map/ppermute | solution.py:410
  53.1 22.4 %collective-permute-start.6 = (bf16[5,16,512]{2,1,0:T(8,128)(2,1)}, bf16[5,16,512]{2,1,0:T(8,128)(2,1)S(1)}, u32[]{:S(2)}, u32[]{:S(2)}) collective-permute-start(bf16[5,16,512]{2,1,0:T(8,128)(2,1)} %copy-done.2), channel_id=1, source_target_pairs={{0,14},{2,12},{4,10},{6,8},{8,6},{10,4},{12,2},{14,0},{1,15},{3,13... | collective-permute-start | bytes 245768 | tf_op jit(solution)/shard_map/ppermute | solution.py:410
  56.0 1.0 %copy-start.9 = (bf16[768,256]{1,0:T(8,128)(2,1)S(1)}, bf16[768,256]{1,0:T(8,128)(2,1)}, u32[]{:S(2)}) copy-start(bf16[768,256]{1,0:T(8,128)(2,1)} %constant.103.clone.refs_7_.refs_14_) | copy-start | bytes 1179652
  57.0 1.0 %copy-start.11 = (bf16[768,256]{1,0:T(8,128)(2,1)S(1)}, bf16[768,256]{1,0:T(8,128)(2,1)}, u32[]{:S(2)}) copy-start(bf16[768,256]{1,0:T(8,128)(2,1)} %constant.102.clone.refs_6_.refs_13_) | copy-start | bytes 1179652
  58.0 0.8 copy-start.12
  58.8 0.8 copy-start.14
  59.6 0.8 copy-start.16
  60.4 0.7 copy-start.18
  61.1 14.5 %copy-start.10 = (bf16[768,256]{1,0:T(8,128)(2,1)S(1)}, bf16[768,256]{1,0:T(8,128)(2,1)}, u32[]{:S(2)}) copy-start(bf16[768,256]{1,0:T(8,128)(2,1)} %constant.103.clone.refs_7_.refs_14_) | copy-start | bytes 1179652
  61.1 14.5 %copy-start.13 = (bf16[256,128]{1,0:T(8,128)(2,1)S(1)}, bf16[256,128]{1,0:T(8,128)(2,1)}, u32[]{:S(2)}) copy-start(bf16[256,128]{1,0:T(8,128)(2,1)} %constant.108.clone.refs_12_.refs_19_) | copy-start | bytes 196612
  61.1 14.5 %copy-start.15 = (f32[2,32,128]{2,1,0:T(8,128)S(1)}, f32[2,32,128]{2,1,0:T(8,128)}, u32[]{:S(2)}) copy-start(f32[2,32,128]{2,1,0:T(8,128)} %constant.105.clone.refs_9_.refs_16_) | copy-start | bytes 98308
  61.1 14.5 %copy-start.20 = (bf16[5,16,512]{2,1,0:T(8,128)(2,1)S(1)}, bf16[5,16,512]{2,1,0:T(8,128)(2,1)}, u32[]{:S(2)}) copy-start(bf16[5,16,512]{2,1,0:T(8,128)(2,1)} %copy-done.19) | copy-start | bytes 245764
  84.1 11.4 %all-to-all-start.1 = ((f32[16,16,128]{2,1,0:T(8,128)}), f32[16,16,128]{2,1,0:T(8,128)S(1)}, u32[]{:S(2)}, u32[]{:S(2)}) async-start(f32[16,16,128]{2,1,0:T(8,128)} %bitcast.14), calls=%async_computation.1 | async-start | bytes 262144 | tf_op jit(solution)/shard_map/all_to_all | solution.py:433

commit v4 on v3

--- a/solution.py
+++ b/solution.py
@@ -24,6 +24,8 @@
 TERRAIN_ROWS = 4
 WHOLE_SHARE = 0.6875
 GROUP = 2
+DIGIT = 32
+DIGIT_ROWS = 8
 
 F32 = jnp.float32
 BF16 = jnp.bfloat16
@@ -132,20 +134,25 @@
     return high, low
 
 
-def march_kernel(steps, batch, heights, first, count, section, *refs):
+def march_kernel(begin, steps, batch, own, first, last, count, section, *refs):
     slabs, refs = refs[:count], refs[count:]
-    (
-        terrain, cells, start_re, start_im, totals_in,
-        w_forward, w_inverse, twiddle, spread, tilt, absorb, bins,
-        end_re, end_im, totals,
-        levels, arrived, back_re, back_im, energy, power,
-    ) = refs
+    (start_re, start_im, named, totals_in, w_forward, w_inverse, twiddle, spread, tilt, absorb, bins), refs = (
+        refs[:11], refs[11:]
+    )
+    (totals, end_re, end_im, cells), refs = (refs[:4], refs[4:]) if first else ((*refs[:3], named), refs[3:])
+    levels, arrived, back_re, back_im, energy, power = refs
     sine, cosine = phase_polynomials()
-    copies = []
-    for d, slab in enumerate(slabs):
-        place = levels if count == 1 else levels.at[section[0] ^ d]
-        copies.append(pltpu.make_async_copy(slab, place, arrived.at[d]))
-        copies[-1].start()
+    heights = levels.shape[2]
+    copies = [(slab, levels if first else levels.at[section[0] ^ d]) for d, slab in enumerate(slabs)]
+    if not first:
+        copies += [(start_re, end_re), (start_im, end_im)]
+    copies = [pltpu.make_async_copy(*pair, arrived.at[i]) for i, pair in enumerate(copies)]
+    for copy in copies:
+        copy.start()
+    lane = lax.broadcasted_iota(jnp.int32, (batch, LANES), 1)
+    radial = lax.broadcasted_iota(jnp.int32, (batch, LANES), 0)
+    my_lane = lane == section[0] * own + radial
+    at_once = cells.shape[1] // 2
 
     def enter(columns, jl, put_re, put_im):
         parts = dft4(columns, -1)
@@ -165,11 +172,6 @@
                     jnp.broadcast_to(start_im[j : j + 1, :], shape),
                 ))
             enter(columns, jl, end_re, end_im)
-    else:
-        end_re[...] = start_re[...]
-        end_im[...] = start_im[...]
-
-    lane = lax.broadcasted_iota(jnp.int32, (batch, LANES), 1)
 
     def joined(pieces):
         re_high, re_low = split(jnp.concatenate([p[0] for p in pieces], axis=0))
@@ -220,6 +222,8 @@
                     back_re[ql * EIGHT + jl] = column[jl][0]
                     back_im[ql * EIGHT + jl] = column[jl][1]
 
+        row = cells[(begin + t) // at_once, pl.ds((begin + t) % at_once, 1), :]
+        ground = jnp.sum(jnp.where(my_lane, row, 0), axis=1, keepdims=True)
         for jl in range(EIGHT):
             column = []
             for ql in range(FOUR):
@@ -230,7 +234,10 @@
             for jh in range(FOUR):
                 j = EIGHT * jh + jl
                 place = j * LANES
-                raw = levels[place // heights, t, :, place % heights : place % heights + LANES]
+                raw = levels[
+                    place // heights, pl.ds(pl.multiple_of(t * batch, batch), batch),
+                    place % heights : place % heights + LANES,
+                ]
                 phi = raw.astype(F32) + tilt[j : j + 1, :]
                 u = phi * phi
                 sin_poly, cos_poly = sine[-1], cosine[-1]
@@ -247,7 +254,7 @@
                     re, im = re * loss, im * loss
                 re, im = re * turned_c - im * turned_s, re * turned_s + im * turned_c
                 if j < TERRAIN_ROWS:
-                    open_air = lane + j * LANES >= terrain[t]
+                    open_air = lane + j * LANES >= ground
                     re, im = jnp.where(open_air, re, 0.0), jnp.where(open_air, im, 0.0)
                 high, low = split(re * re + im * im)
                 energy[j * batch : (j + 1) * batch, :] = jnp.concatenate([high, low], axis=1)
@@ -256,13 +263,31 @@
         return carry
 
     energy[...] = jnp.zeros_like(energy)
+    power[...] = jnp.zeros_like(power)
     for copy in copies:
         copy.wait()
+    if first:
+        for source in range(cells.shape[0]):
+            rows = levels[source, steps * batch :, :LANES].astype(F32).astype(jnp.int32)
+            half = DIGIT_ROWS // 2
+            cells[source] = rows[:half] * DIGIT + rows[half:]
     lax.fori_loop(0, steps, step, 0)
     binned(steps - 1)
 
-    tiles = totals.shape[0]
-    hot = (lax.broadcasted_iota(jnp.int32, (tiles, steps * batch), 0) == cells[...]).astype(F32).astype(BF16)
+    lane = lax.broadcasted_iota(jnp.int32, (1, LANES), 1)
+    fit = LANES // batch
+    tile_rows = []
+    for t in range(steps):
+        row = cells[(begin + t) // at_once, at_once + (begin + t) % at_once, :].reshape(1, LANES)
+        row = pltpu.roll(row, lax.rem(batch * (t % fit) - section[0] * own + LANES, LANES), 1)
+        row = jnp.where(lane % batch < own, row, -1)
+        if t % fit == 0:
+            tile_rows.append(jnp.where(lane < batch, row, -1))
+        else:
+            tile_rows[-1] = jnp.where(lane // batch == t % fit, row, tile_rows[-1])
+    tile_row = jnp.concatenate(tile_rows, axis=1)
+    tiles, cell_count = totals.shape[0], tile_row.shape[1]
+    hot = (lax.broadcasted_iota(jnp.int32, (tiles, cell_count), 0) == tile_row).astype(F32).astype(BF16)
     value = power[...]
     high = value.astype(BF16)
     rest = value - high.astype(F32)
@@ -277,33 +302,39 @@
         totals[...] = totals_in[...] + gain
 
 
-def march(section, slabs, terrain, cells, start, totals, consts, tiles, first):
-    steps, batch, heights = slabs[0].shape[-3:]
+def march(section, slabs, begin, steps, batch, own, start, named, totals, consts, first, last):
+    heights = slabs[0].shape[-1]
     sections = H // heights
-    state = jax.ShapeDtypeStruct((ROWS, batch, LANES), F32)
+    field = jax.ShapeDtypeStruct((ROWS, batch, LANES), F32)
+    held = pltpu.VMEM(field.shape, F32)
     vmem = pl.BlockSpec(memory_space=pltpu.VMEM)
     smem = pl.BlockSpec(memory_space=pltpu.SMEM)
     anywhere = pl.BlockSpec(memory_space=pl.ANY)
+    outputs = [jax.ShapeDtypeStruct(totals.shape, F32)]
+    if not last:
+        outputs += [field, field]
+    if first:
+        outputs += [jax.ShapeDtypeStruct(named.shape, jnp.int32)]
     call = pl.pallas_call(
-        functools.partial(march_kernel, steps, batch, heights, first, len(slabs)),
-        out_shape=(state, state, jax.ShapeDtypeStruct((tiles, BINS), F32)),
-        in_specs=[smem] + [anywhere] * len(slabs) + [vmem] * 12,
-        out_specs=(vmem, vmem, vmem),
-        scratch_shapes=[
-            pltpu.VMEM((sections, steps, batch, heights), BF16),
-            pltpu.SemaphoreType.DMA((len(slabs),)),
-            pltpu.VMEM((ROWS, batch, LANES), F32),
-            pltpu.VMEM((ROWS, batch, LANES), F32),
+        functools.partial(march_kernel, begin, steps, batch, own, first, last, len(slabs)),
+        out_shape=outputs,
+        in_specs=[smem] + [anywhere] * len(slabs) + [vmem if first else anywhere] * 2 + [vmem] * 9,
+        out_specs=[vmem] * len(outputs),
+        scratch_shapes=([held, held] if last else []) + [
+            pltpu.VMEM((sections, *slabs[0].shape[-2:]), BF16),
+            pltpu.SemaphoreType.DMA((len(slabs) + 2,)),
+            held,
+            held,
             pltpu.VMEM((ROWS * batch, 2 * LANES), BF16),
-            pltpu.VMEM((steps * batch, BINS), F32),
+            pltpu.VMEM((-(-steps * batch // LANES) * LANES, BINS), F32),
         ],
-        compiler_params=pltpu.CompilerParams(vmem_limit_bytes=48 * 1024 * 1024),
+        compiler_params=pltpu.CompilerParams(vmem_limit_bytes=20 * 1024 * 1024),
         cost_estimate=pl.CostEstimate(
             flops=steps * 1_600_000_000, bytes_accessed=4 * 1024 * 1024, transcendentals=0
         ),
         name="march",
     )
-    return call(section, *slabs, terrain, cells, *start, totals, *consts)
+    return call(section, *slabs, *start, named, totals, *consts)
 
 
 def turned(levels, base, rows, begin, end, own, put):
@@ -323,70 +354,65 @@
     return taken
 
 
-def deal_kernel(begin, end, levels, out, rows):
-    def put(t, column, taken):
-        out[0, t, :, column] = filled(taken, out.shape[2])
-
-    turned(levels, 0, rows, begin, end, levels.shape[0], put)
-
-
-def deal(levels, begin, end, sections, own, batch):
+def deal_kernel(begin, end, own, steps, batch, levels, digits, out):
+    count = (end - begin) * batch
+    row = lax.broadcasted_iota(jnp.int32, (count, own * steps), 0)
+    column = lax.broadcasted_iota(jnp.int32, (count, own * steps), 1)
+    wanted = (row % batch) * steps + row // batch + begin
+    chosen = jnp.logical_and(column == wanted, row % batch < own)
+    moved = jnp.dot(
+        chosen.astype(F32).astype(BF16),
+        levels[...].reshape(own * steps, levels.shape[2]),
+        preferred_element_type=F32,
+    )
+    out[0, :count, :] = moved.astype(BF16)
+    out[0, count:, :] = jnp.zeros((DIGIT_ROWS, levels.shape[2]), BF16)
+    out[0, count:, : digits.shape[1]] = digits[...]
+
+
+def deal(levels, digits, begin, end, sections, own, batch):
     steps, heights = levels.shape[1:]
+    count = (end - begin) * batch + DIGIT_ROWS
     return pl.pallas_call(
-        functools.partial(deal_kernel, begin, end),
+        functools.partial(deal_kernel, begin, end, own, steps, batch),
         grid=(sections,),
-        out_shape=jax.ShapeDtypeStruct((sections, end - begin, batch, heights), BF16),
-        in_specs=[pl.BlockSpec((own, steps, heights), lambda d: (d, 0, 0))],
-        out_specs=pl.BlockSpec((1, end - begin, batch, heights), lambda d: (d, 0, 0, 0)),
-        scratch_shapes=[pltpu.VMEM((heights // LANES, own * steps, LANES), F32)],
-        compiler_params=pltpu.CompilerParams(vmem_limit_bytes=32 * 1024 * 1024),
+        out_shape=jax.ShapeDtypeStruct((sections, count, heights), BF16),
+        in_specs=[
+            pl.BlockSpec((own, steps, heights), lambda d: (d, 0, 0)),
+            pl.BlockSpec(digits.shape, lambda d: (0, 0)),
+        ],
+        out_specs=pl.BlockSpec((1, count, heights), lambda d: (d, 0, 0)),
+        compiler_params=pltpu.CompilerParams(vmem_limit_bytes=60 * 1024 * 1024),
         cost_estimate=pl.CostEstimate(flops=1_000_000_000, bytes_accessed=4 * 1024 * 1024, transcendentals=0),
         name="deal",
-    )(levels)
-
-
-def cut_kernel(begin, end, own, section, levels, *refs):
+    )(levels, digits)
+
+
+def cut_kernel(begin, end, own, batch, section, levels, *refs):
     slabs, rows = refs[:-1], refs[-1]
     for d, slab in enumerate(slabs):
         def put(t, column, taken, slab=slab):
-            slab[t, :, column] = filled(taken, slab.shape[1])
+            slab[t * batch : (t + 1) * batch, column] = filled(taken, batch)
 
         turned(levels, (section[0] ^ d) * own, rows, begin, end, own, put)
 
 
 def cut(section, levels, begin, end, sections, own, batch):
     steps, heights = levels.shape[1:]
-    slab = jax.ShapeDtypeStruct((end - begin, batch, heights), BF16)
+    slab = jax.ShapeDtypeStruct(((end - begin) * batch, heights), BF16)
     vmem = pl.BlockSpec(memory_space=pltpu.VMEM)
     smem = pl.BlockSpec(memory_space=pltpu.SMEM)
     call = pl.pallas_call(
-        functools.partial(cut_kernel, begin, end, own),
+        functools.partial(cut_kernel, begin, end, own, batch),
         out_shape=(slab,) * sections,
         in_specs=[smem, vmem],
         out_specs=(vmem,) * sections,
         scratch_shapes=[pltpu.VMEM((heights // LANES, own * steps, LANES), F32)],
-        compiler_params=pltpu.CompilerParams(vmem_limit_bytes=32 * 1024 * 1024),
+        compiler_params=pltpu.CompilerParams(vmem_limit_bytes=60 * 1024 * 1024),
         cost_estimate=pl.CostEstimate(flops=1_000_000_000, bytes_accessed=4 * 1024 * 1024, transcendentals=0),
         name="cut",
     )
     return call(section, levels)
-
-
-def gather_small(value):
-    radial, sections = lax.axis_index("radial"), lax.axis_size("range")
-    other = lax.ppermute(value, "radial", [(0, 1), (1, 0)])
-    pair = jnp.stack([jnp.where(radial == 0, value, other), jnp.where(radial == 0, other, value)])
-    section = lax.axis_index("range")
-    held = jnp.zeros((sections, *pair.shape), pair.dtype)
-    held = lax.dynamic_update_index_in_dim(held, pair, section, 0)
-    width = 1
-    while width < sections:
-        base = section // width * width
-        part = lax.dynamic_slice_in_dim(held, base, width, 0)
-        part = lax.ppermute(part, "range", [(i, i ^ width) for i in range(sections)])
-        held = lax.dynamic_update_slice_in_dim(held, part, base ^ width, 0)
-        width *= 2
-    return held
 
 
 def local(refractivity, source, terrain, tile_map):
@@ -398,41 +424,40 @@
     batch = -(-own // 16) * 16
 
     small = jnp.concatenate([terrain.T, tile_map.T])
+    digits = jnp.concatenate([small // DIGIT, small % DIGIT]).astype(BF16)
     middle = round(WHOLE_SHARE * steps)
     section = lax.axis_index("range").astype(jnp.int32).reshape(1)
-    dealt = deal(refractivity, 0, middle, sections, own, batch)
+    dealt = deal(refractivity, digits, 0, middle, sections, own, batch)
     refractivity, dealt = lax.optimization_barrier((refractivity, dealt))
     whole = lax.all_to_all(dealt, "range", 0, 0, tiled=True)
     slabs = list(cut(section, refractivity, middle, steps, sections, own, batch))
-    small, slabs[0] = lax.optimization_barrier((small, slabs[0]))
-    everyone = gather_small(small)
-    for d in reversed(range(1, sections)):
+    for d in range(1, sections):
         slabs[d] = lax.ppermute(slabs[d], "range", [(i, i ^ d) for i in range(sections)])
-    everyone = everyone.reshape(*everyone.shape[:2], 2, -1, radials)
-    my_ids = (lax.axis_index("range") * lax.axis_size("radial") + lax.axis_index("radial")) * TILE_DEV
-    my_ids = my_ids + jnp.arange(TILE_DEV, dtype=jnp.int32)
-    counts = jnp.sum(
-        (my_ids[:, None] == everyone[:, :, 1].reshape(1, -1)).astype(F32), axis=1
-    )
-    mine = lax.dynamic_index_in_dim(everyone, lax.axis_index("radial"), 1, keepdims=False)
-    mine = lax.dynamic_slice_in_dim(mine, lax.axis_index("range") * own, own, 3)
-    mine = jnp.transpose(mine, (1, 0, 2, 3)).reshape(2, steps, own)
-    pad = ((0, 0), (0, batch - own))
-    terrain_all = jnp.pad(mine[0], pad)
-    cells_all = jnp.pad(mine[1], pad, constant_values=-1)
-    terrain_all = jnp.broadcast_to(terrain_all[:, :, None], (steps, batch, LANES))
 
     consts = [jnp.asarray(v) for v in tables()]
     start = (source[0].reshape(ROWS, LANES), source[1].reshape(ROWS, LANES))
     totals = jnp.zeros((tiles, BINS), F32)
-    for piece, begin, end in (([whole], 0, middle), (slabs, middle, steps)):
-        *start, totals = march(
-            section, piece, terrain_all[begin:end], cells_all[begin:end].reshape(1, -1),
-            start, totals, consts, tiles, begin == 0,
-        )
+    named = jnp.zeros((sections, DIGIT_ROWS // 2, radials), jnp.int32)
+    totals, *start, named = march(
+        section, [whole], 0, middle, batch, own, start, named, totals, consts, True, False
+    )
+    (totals,) = march(
+        section, slabs, middle, steps - middle, batch, own, start, named, totals, consts, False, True
+    )
+
+    named, totals = lax.optimization_barrier((named, totals))
     sent = lax.all_to_all(
         totals.reshape(owners, TILE_DEV, BINS), ("range", "radial"), 0, 0, tiled=True
     )
+    pair = lax.axis_index("range") * lax.axis_size("radial")
+    radial = lax.axis_index("radial")
+    tile_ids = named[:, DIGIT_ROWS // 4 :].reshape(1, -1)
+
+    def count_of(core):
+        ids = (pair + core) * TILE_DEV + jnp.arange(TILE_DEV, dtype=jnp.int32)
+        return jnp.sum((ids[:, None] == tile_ids).astype(F32), axis=1)
+
+    counts = count_of(radial) + lax.ppermute(count_of(1 - radial), "radial", [(0, 1), (1, 0)])
     return jnp.sum(sent, axis=0) / counts[:, None]
 
 

time: 96.9 us -> 94.4 us (0.974)
  local copies, waits for them, and re-layouts: 13 us -> 0.1 us
  waiting for transfers between devices: 24.5 us -> 33.6 us
  Pallas kernels: 26.9 us -> 32.1 us
  starting transfers between devices: 30.5 us -> 25.7 us
  other arithmetic: 0.94 us -> 2.22 us
    ppermute x4 -> x1, waiting for transfers between devices: 16.8 us -> 0.85 us  [local(): lax.ppermute(count_of(1 - radial), 'radial', [(0, 1), (1, 0)])]
    ppermute x7, waiting for transfers between devices: 0.02 us -> 14.5 us  [local(): lax.ppermute(slabs[d], 'range', [(i, i ^ d) for i in range(sections)])]
    all_to_all x1, waiting for transfers between devices: 0.01 us -> 11.8 us  [local(): whole = lax.all_to_all(dealt, 'range', 0, 0, tiled=True)]
    unnamed x46 -> x18, local copies, waits for them, and re-layouts: 11.7 us -> 0.06 us
    ppermute x4 -> x1, starting transfers between devices: 8.94 us -> 0.34 us  [local(): lax.ppermute(count_of(1 - radial), 'radial', [(0, 1), (1, 0)])]
    ppermute x7, starting transfers between devices: 10.7 us -> 14.6 us  [local(): lax.ppermute(slabs[d], 'range', [(i, i ^ d) for i in range(sections)])]
    pallas_call x3, Pallas kernels: 26.4 us -> 29.1 us  [the longest x2 22.9 us: march(): return call(section, *slabs, *start, named, totals, *consts)]
    pallas_call x1, Pallas kernels: 0.57 us -> 3.04 us  [cut(): return call(section, levels)]
  transfers between devices with their start and end apart: 13 -> 10, of which waited for: 5 -> 5; matrix products, arithmetic and copies ran while one was open for 2% -> 0% of each run, Pallas kernels for 16% -> 19%
where the time goes in v4:
time: 94.4 us; the launch traced here: 94 us
  waiting for transfers between devices  33.6 us (36%)
  Pallas kernels  32.1 us (34%)
  starting transfers between devices  25.7 us (27%)
  other arithmetic  2.22 us (2%)
    pallas_call x2, Pallas kernels, march(): return call(section, *slabs, *start, named, totals, *consts)  22.9 us
    ppermute x7, starting transfers between devices, local(): lax.ppermute(slabs[d], 'range', [(i, i ^ d) for i in range(sections)])  14.6 us
    ppermute x7, waiting for transfers between devices, local(): lax.ppermute(slabs[d], 'range', [(i, i ^ d) for i in range(sections)])  14.5 us
    all_to_all x1, waiting for transfers between devices, local(): whole = lax.all_to_all(dealt, 'range', 0, 0, tiled=True)  11.8 us
    all_to_all x1, starting transfers between devices, local(): whole = lax.all_to_all(dealt, 'range', 0, 0, tiled=True)  7.28 us
    all_to_all x1, waiting for transfers between devices, local(): lax.all_to_all(totals.reshape(owners, TILE_DEV, BINS), ('range', 'radial'...  6.46 us
    pallas_call x1, Pallas kernels, deal(): pl.pallas_call(functools.partial(deal_kernel, begin, end, own, steps, bat...  6.23 us
    all_to_all x1, starting transfers between devices, local(): lax.all_to_all(totals.reshape(owners, TILE_DEV, BINS), ('range', 'radial'...  3.52 us
  transfers between devices with their start and end apart: 10, of which 5 were waited for; matrix products, arithmetic and copies ran while one was open for 0% of the time, Pallas kernels for 19%

profile of v4, /device:TPU:0, one launch (start us, length us, event | category | flops | bytes accessed | tf_op | source)
XLA Modules:
  0.0 94.0 jit_solution(11134676392342830363)
XLA Ops:
  0.0 0.7 fusion
  0.7 0.6 pad_maximum_fusion.digits
  1.3 6.2 %deal.1 = bf16[8,184,512]{2,1,0:T(8,128)(2,1)} custom-call(bf16[128,16,512]{2,1,0:T(8,128)(2,1)} %levels.2, bf16[8,128]{1,0:T(8,128)(2,1)} %pad_maximum_fusion.digits), custom_call_target="tpu_custom_call" | custom-call | flops 1000000000 | bytes 4194304 | tf_op jit(solution)/shard_map/deal/pallas_call | solution.py:376
  7.5 7.3 %all-to-all-start = ((bf16[8,184,512]{2,1,0:T(8,128)(2,1)}), bf16[8,184,512]{2,1,0:T(8,128)(2,1)S(1)}, u32[]{:S(2)}, u32[]{:S(2)}) async-start(bf16[8,184,512]{2,1,0:T(8,128)(2,1)} %deal.1), calls=%async_computation | async-start | bytes 3014656 | tf_op jit(solution)/shard_map/all_to_all | solution.py:432
  14.8 0.0 copy-start.8
  14.8 0.0 copy-start
  14.8 0.0 copy-start.1
  14.8 0.0 copy-start.2
  14.9 0.0 copy-start.3
  14.9 0.0 copy-start.4
  14.9 0.0 copy-start.5
  14.9 0.0 copy-start.6
  14.9 3.0 %cut.1 = (bf16[80,512]{1,0:T(8,128)(2,1)}, bf16[80,512]{1,0:T(8,128)(2,1)}, bf16[80,512]{1,0:T(8,128)(2,1)}, bf16[80,512]{1,0:T(8,128)(2,1)}, bf16[80,512]{1,0:T...) custom-call(s32[1]{0:T(128)} %bitcast.section, bf16[128,16,512]{2,1,0:T(8,128)(2,1)} %levels.2), custom_call_target="tpu_custom_call" | custom-call | flops 1000000000 | bytes 4194304 | tf_op jit(solution)/shard_map/cut/pallas_call | solution.py:415
  17.9 2.0 %collective-permute-start = (bf16[80,512]{1,0:T(8,128)(2,1)}, bf16[80,512]{1,0:T(8,128)(2,1)S(1)}, u32[]{:S(2)}, u32[]{:S(2)}) collective-permute-start(bf16[80,512]{1,0:T(8,128)(2,1)} %get-tuple-element.25), channel_id=1, source_target_pairs={{0,2},{2,0},{4,6},{6,4},{8,10},{10,8},{12,14},{14,12},{1,3},{3,1},... | collective-permute-start | bytes 245768 | tf_op jit(solution)/shard_map/ppermute | solution.py:435
  20.0 1.5 %collective-permute-start.1 = (bf16[80,512]{1,0:T(8,128)(2,1)}, bf16[80,512]{1,0:T(8,128)(2,1)S(1)}, u32[]{:S(2)}, u32[]{:S(2)}) collective-permute-start(bf16[80,512]{1,0:T(8,128)(2,1)} %get-tuple-element.26), channel_id=1, source_target_pairs={{0,4},{2,6},{4,0},{6,2},{8,12},{10,14},{12,8},{14,10},{1,5},{3,7},... | collective-permute-start | bytes 245768 | tf_op jit(solution)/shard_map/ppermute | solution.py:435
  21.4 0.0 collective-permute-start.2
  21.4 2.9 %collective-permute-start.3 = (bf16[80,512]{1,0:T(8,128)(2,1)}, bf16[80,512]{1,0:T(8,128)(2,1)S(1)}, u32[]{:S(2)}, u32[]{:S(2)}) collective-permute-start(bf16[80,512]{1,0:T(8,128)(2,1)} %get-tuple-element.28), channel_id=1, source_target_pairs={{0,8},{2,10},{4,12},{6,14},{8,0},{10,2},{12,4},{14,6},{1,9},{3,11}... | collective-permute-start | bytes 245768 | tf_op jit(solution)/shard_map/ppermute | solution.py:435
  24.3 1.5 %collective-permute-start.4 = (bf16[80,512]{1,0:T(8,128)(2,1)}, bf16[80,512]{1,0:T(8,128)(2,1)S(1)}, u32[]{:S(2)}, u32[]{:S(2)}) collective-permute-start(bf16[80,512]{1,0:T(8,128)(2,1)} %get-tuple-element.29), channel_id=1, source_target_pairs={{0,10},{2,8},{4,14},{6,12},{8,2},{10,0},{12,6},{14,4},{1,11},{3,9}... | collective-permute-start | bytes 245768 | tf_op jit(solution)/shard_map/ppermute | solution.py:435
  25.8 0.0 copy-done.8
  25.8 3.8 %collective-permute-done.refs_1_ = bf16[80,512]{1,0:T(8,128)(2,1)S(1)} collective-permute-done((bf16[80,512]{1,0:T(8,128)(2,1)}, bf16[80,512]{1,0:T(8,128)(2,1)S(1)}, u32[]{:S(2)}, u32[]{:S(2)}) %collective-permute-start) | collective-permute-done | bytes 81952 | tf_op jit(solution)/shard_map/ppermute | solution.py:435
  29.6 2.6 %collective-permute-start.5 = (bf16[80,512]{1,0:T(8,128)(2,1)}, bf16[80,512]{1,0:T(8,128)(2,1)S(1)}, u32[]{:S(2)}, u32[]{:S(2)}) collective-permute-start(bf16[80,512]{1,0:T(8,128)(2,1)} %get-tuple-element.30), channel_id=1, source_target_pairs={{0,12},{2,14},{4,8},{6,10},{8,4},{10,6},{12,0},{14,2},{1,13},{3,15... | collective-permute-start | bytes 245768 | tf_op jit(solution)/shard_map/ppermute | solution.py:435
  32.2 10.7 %collective-permute-done.1.refs_2_ = bf16[80,512]{1,0:T(8,128)(2,1)S(1)} collective-permute-done((bf16[80,512]{1,0:T(8,128)(2,1)}, bf16[80,512]{1,0:T(8,128)(2,1)S(1)}, u32[]{:S(2)}, u32[]{:S(2)}) %collective-permute-start.1) | collective-permute-done | bytes 81952 | tf_op jit(solution)/shard_map/ppermute | solution.py:435
  42.9 4.1 %collective-permute-start.6 = (bf16[80,512]{1,0:T(8,128)(2,1)}, bf16[80,512]{1,0:T(8,128)(2,1)S(1)}, u32[]{:S(2)}, u32[]{:S(2)}) collective-permute-start(bf16[80,512]{1,0:T(8,128)(2,1)} %get-tuple-element.31), channel_id=1, source_target_pairs={{0,14},{2,12},{4,10},{6,8},{8,6},{10,4},{12,2},{14,0},{1,15},{3,13... | collective-permute-start | bytes 245768 | tf_op jit(solution)/shard_map/ppermute | solution.py:435
  47.1 11.8 %all-to-all-done.refs_0_ = bf16[8,184,512]{2,1,0:T(8,128)(2,1)S(1)} async-done(((bf16[8,184,512]{2,1,0:T(8,128)(2,1)}), bf16[8,184,512]{2,1,0:T(8,128)(2,1)S(1)}, u32[]{:S(2)}, u32[]{:S(2)}) %all-to-all-start) | async-done | bytes 1507360 | tf_op jit(solution)/shard_map/all_to_all | solution.py:432
  58.9 0.0 copy-done
  58.9 0.0 copy-done.1
  58.9 0.0 copy-done.2
  58.9 0.0 copy-done.3
  58.9 0.0 copy-done.4
  58.9 0.0 copy-done.5
  58.9 0.0 copy-done.6
  58.9 0.0 copy-start.7
  59.0 14.5 %march.2 = (f32[256,128]{1,0:T(8,128)S(1)}, f32[32,16,128]{2,1,0:T(8,128)S(1)}, f32[32,16,128]{2,1,0:T(8,128)S(1)}, s32[8,4,128]{2,1,0:T(4,128)S(1)}) custom-call(s32[1]{0:T(128)} %bitcast.section, bf16[8,184,512]{2,1,0:T(8,128)(2,1)S(1)} %all-to-all-done.refs_0_, f32[32,128]{1,0:T(8,128)S(1)} %bitcast.8, f32[32,128]{1,0:T(8,128)S(1)} %bitcast.7, ...), custom_call_target="tpu_custom_call" | custom-call | flops 17600000000 | bytes 4194304 | tf_op jit(solution)/shard_map/march/pallas_call | solution.py:337
  73.4 0.0 collective-permute-done.2.refs_3_
  73.4 0.0 collective-permute-done.3.refs_4_
  73.4 0.0 collective-permute-done.4.refs_5_
  73.5 0.0 collective-permute-done.5.refs_6_
  73.5 0.0 collective-permute-done.6.refs_7_
  73.5 0.0 copy-done.7
  73.5 8.4 %march.3 = f32[256,128]{1,0:T(8,128)} custom-call(s32[1]{0:T(128)} %bitcast.section, bf16[80,512]{1,0:T(8,128)(2,1)S(1)} %copy-done.7, bf16[80,512]{1,0:T(8,128)(2,1)S(1)} %collective-permute-done.refs_1_, bf16[80,512]{1,0:T(8,128)(2,1)S(1)} %collective-permute-done.1.refs_2_, bf16[80,512]{1,0:T(8,128)(2,1)S(1)} %collective-permute-done.2.refs_3_, ...), custom_call_target="tpu_custom_call" | custom-call | flops 8000000000 | bytes 4194304 | tf_op jit(solution)/shard_map/march/pallas_call | solution.py:337
  81.9 3.5 %all-to-all-start.1 = ((f32[16,16,128]{2,1,0:T(8,128)}), f32[16,16,128]{2,1,0:T(8,128)S(1)}, u32[]{:S(2)}, u32[]{:S(2)}) async-start(f32[16,16,128]{2,1,0:T(8,128)} %bitcast.5), calls=%async_computation.1 | async-start | bytes 262144 | tf_op jit(solution)/shard_map/all_to_all | solution.py:449
  85.5 0.2 convert_reduce_fusion
  85.7 0.3 collective-permute-start.7
  86.0 0.8 collective-permute-done.7
  86.9 6.5 %all-to-all-done.1 = f32[16,16,128]{2,1,0:T(8,128)S(1)} async-done(((f32[16,16,128]{2,1,0:T(8,128)}), f32[16,16,128]{2,1,0:T(8,128)S(1)}, u32[]{:S(2)}, u32[]{:S(2)}) %all-to-all-start.1) | async-done | bytes 131104 | tf_op jit(solution)/shard_map/all_to_all | solution.py:449
  93.3 0.7 broadcast_divide_fusion
  (7 shorter events, 0.1 us)
Async XLA Ops:
  7.5 51.3 %all-to-all-start = ((bf16[8,184,512]{2,1,0:T(8,128)(2,1)}), bf16[8,184,512]{2,1,0:T(8,128)(2,1)S(1)}, u32[]{:S(2)}, u32[]{:S(2)}) async-start(bf16[8,184,512]{2,1,0:T(8,128)(2,1)} %deal.1), calls=%async_computation | async-start | bytes 3014656 | tf_op jit(solution)/shard_map/all_to_all | solution.py:432
  14.8 11.0 %copy-start.8 = (f32[2,4096]{1,0:T(2,128)S(1)}, f32[2,4096]{1,0:T(2,128)}, u32[]{:S(2)}) copy-start(f32[2,4096]{1,0:T(2,128)} %param.12) | copy-start | bytes 98308
  14.8 44.1 %copy-start = (bf16[768,256]{1,0:T(8,128)(2,1)S(1)}, bf16[768,256]{1,0:T(8,128)(2,1)}, u32[]{:S(2)}) copy-start(bf16[768,256]{1,0:T(8,128)(2,1)} %constant.59.clone.refs_5_.refs_12_) | copy-start | bytes 1179652
  14.8 44.1 %copy-start.1 = (bf16[768,256]{1,0:T(8,128)(2,1)S(1)}, bf16[768,256]{1,0:T(8,128)(2,1)}, u32[]{:S(2)}) copy-start(bf16[768,256]{1,0:T(8,128)(2,1)} %constant.60.clone.refs_6_.refs_13_) | copy-start | bytes 1179652
  14.8 44.1 %copy-start.2 = (bf16[256,128]{1,0:T(8,128)(2,1)S(1)}, bf16[256,128]{1,0:T(8,128)(2,1)}, u32[]{:S(2)}) copy-start(bf16[256,128]{1,0:T(8,128)(2,1)} %constant.65.clone.refs_11_.refs_18_) | copy-start | bytes 196612
  14.9 44.0 %copy-start.3 = (f32[2,32,128]{2,1,0:T(8,128)S(1)}, f32[2,32,128]{2,1,0:T(8,128)}, u32[]{:S(2)}) copy-start(f32[2,32,128]{2,1,0:T(8,128)} %constant.61.clone.refs_7_.refs_14_) | copy-start | bytes 98308
  14.9 44.0 %copy-start.4 = (f32[2,32,128]{2,1,0:T(8,128)S(1)}, f32[2,32,128]{2,1,0:T(8,128)}, u32[]{:S(2)}) copy-start(f32[2,32,128]{2,1,0:T(8,128)} %constant.62.clone.refs_8_.refs_15_) | copy-start | bytes 98308
  14.9 44.0 %copy-start.5 = (f32[32,128]{1,0:T(8,128)S(1)}, f32[32,128]{1,0:T(8,128)}, u32[]{:S(2)}) copy-start(f32[32,128]{1,0:T(8,128)} %constant.63.clone.refs_9_.refs_16_) | copy-start | bytes 49156
  14.9 44.0 %copy-start.6 = (f32[32,128]{1,0:T(8,128)S(1)}, f32[32,128]{1,0:T(8,128)}, u32[]{:S(2)}) copy-start(f32[32,128]{1,0:T(8,128)} %constant.64.clone.refs_10_.refs_17_) | copy-start | bytes 49156
  17.9 11.6 %collective-permute-start = (bf16[80,512]{1,0:T(8,128)(2,1)}, bf16[80,512]{1,0:T(8,128)(2,1)S(1)}, u32[]{:S(2)}, u32[]{:S(2)}) collective-permute-start(bf16[80,512]{1,0:T(8,128)(2,1)} %get-tuple-element.25), channel_id=1, source_target_pairs={{0,2},{2,0},{4,6},{6,4},{8,10},{10,8},{12,14},{14,12},{1,3},{3,1},... | collective-permute-start | bytes 245768 | tf_op jit(solution)/shard_map/ppermute | solution.py:435
  20.0 23.0 %collective-permute-start.1 = (bf16[80,512]{1,0:T(8,128)(2,1)}, bf16[80,512]{1,0:T(8,128)(2,1)S(1)}, u32[]{:S(2)}, u32[]{:S(2)}) collective-permute-start(bf16[80,512]{1,0:T(8,128)(2,1)} %get-tuple-element.26), channel_id=1, source_target_pairs={{0,4},{2,6},{4,0},{6,2},{8,12},{10,14},{12,8},{14,10},{1,5},{3,7},... | collective-permute-start | bytes 245768 | tf_op jit(solution)/shard_map/ppermute | solution.py:435
  21.4 52.0 %collective-permute-start.2 = (bf16[80,512]{1,0:T(8,128)(2,1)}, bf16[80,512]{1,0:T(8,128)(2,1)S(1)}, u32[]{:S(2)}, u32[]{:S(2)}) collective-permute-start(bf16[80,512]{1,0:T(8,128)(2,1)} %get-tuple-element.27), channel_id=1, source_target_pairs={{0,6},{2,4},{4,2},{6,0},{8,14},{10,12},{12,10},{14,8},{1,7},{3,5},... | collective-permute-start | bytes 245768 | tf_op jit(solution)/shard_map/ppermute | solution.py:435
  21.4 52.0 %collective-permute-start.3 = (bf16[80,512]{1,0:T(8,128)(2,1)}, bf16[80,512]{1,0:T(8,128)(2,1)S(1)}, u32[]{:S(2)}, u32[]{:S(2)}) collective-permute-start(bf16[80,512]{1,0:T(8,128)(2,1)} %get-tuple-element.28), channel_id=1, source_target_pairs={{0,8},{2,10},{4,12},{6,14},{8,0},{10,2},{12,4},{14,6},{1,9},{3,11}... | collective-permute-start | bytes 245768 | tf_op jit(solution)/shard_map/ppermute | solution.py:435
  24.3 49.1 %collective-permute-start.4 = (bf16[80,512]{1,0:T(8,128)(2,1)}, bf16[80,512]{1,0:T(8,128)(2,1)S(1)}, u32[]{:S(2)}, u32[]{:S(2)}) collective-permute-start(bf16[80,512]{1,0:T(8,128)(2,1)} %get-tuple-element.29), channel_id=1, source_target_pairs={{0,10},{2,8},{4,14},{6,12},{8,2},{10,0},{12,6},{14,4},{1,11},{3,9}... | collective-permute-start | bytes 245768 | tf_op jit(solution)/shard_map/ppermute | solution.py:435
  29.6 43.9 %collective-permute-start.5 = (bf16[80,512]{1,0:T(8,128)(2,1)}, bf16[80,512]{1,0:T(8,128)(2,1)S(1)}, u32[]{:S(2)}, u32[]{:S(2)}) collective-permute-start(bf16[80,512]{1,0:T(8,128)(2,1)} %get-tuple-element.30), channel_id=1, source_target_pairs={{0,12},{2,14},{4,8},{6,10},{8,4},{10,6},{12,0},{14,2},{1,13},{3,15... | collective-permute-start | bytes 245768 | tf_op jit(solution)/shard_map/ppermute | solution.py:435
  42.9 30.5 %collective-permute-start.6 = (bf16[80,512]{1,0:T(8,128)(2,1)}, bf16[80,512]{1,0:T(8,128)(2,1)S(1)}, u32[]{:S(2)}, u32[]{:S(2)}) collective-permute-start(bf16[80,512]{1,0:T(8,128)(2,1)} %get-tuple-element.31), channel_id=1, source_target_pairs={{0,14},{2,12},{4,10},{6,8},{8,6},{10,4},{12,2},{14,0},{1,15},{3,13... | collective-permute-start | bytes 245768 | tf_op jit(solution)/shard_map/ppermute | solution.py:435
  58.9 14.5 %copy-start.7 = (bf16[80,512]{1,0:T(8,128)(2,1)S(1)}, bf16[80,512]{1,0:T(8,128)(2,1)}, u32[]{:S(2)}) copy-start(bf16[80,512]{1,0:T(8,128)(2,1)} %get-tuple-element.24.refs_0_) | copy-start | bytes 245764
  81.9 11.4 %all-to-all-start.1 = ((f32[16,16,128]{2,1,0:T(8,128)}), f32[16,16,128]{2,1,0:T(8,128)S(1)}, u32[]{:S(2)}, u32[]{:S(2)}) async-start(f32[16,16,128]{2,1,0:T(8,128)} %bitcast.5), calls=%async_computation.1 | async-start | bytes 262144 | tf_op jit(solution)/shard_map/all_to_all | solution.py:449
  85.7 1.2 %collective-permute-start.7 = (f32[16]{0:T(128)S(1)}, f32[16]{0:T(128)S(1)}, u32[]{:S(2)}, u32[]{:S(2)}) collective-permute-start(f32[16]{0:T(128)S(1)} %get-tuple-element.37), channel_id=1, source_target_pairs={{0,1},{1,0},{2,3},{3,2},{4,5},{5,4},{6,7},{7,6},{8,9},{9,8},{10,11... | collective-permute-start | bytes 200 | tf_op jit(solution)/shard_map/ppermute | solution.py:460

commit v5 on v4

--- a/solution.py
+++ b/solution.py
@@ -22,7 +22,7 @@
 SPREAD_RATE = 0.5
 ABSORB_RATE = 0.05
 TERRAIN_ROWS = 4
-WHOLE_SHARE = 0.6875
+EARLY_SHARE = 0.6875
 GROUP = 2
 DIGIT = 32
 DIGIT_ROWS = 8
@@ -143,9 +143,13 @@
     levels, arrived, back_re, back_im, energy, power = refs
     sine, cosine = phase_polynomials()
     heights = levels.shape[2]
-    copies = [(slab, levels if first else levels.at[section[0] ^ d]) for d, slab in enumerate(slabs)]
-    if not first:
-        copies += [(start_re, end_re), (start_im, end_im)]
+    half = levels.shape[0] // 2
+    if first:
+        places = [levels.at[pl.ds(section[0] // half * half, half)]]
+        places += [levels.at[section[0] ^ d] for d in range(half, 2 * half)]
+    else:
+        places = [levels]
+    copies = list(zip(slabs, places))
     copies = [pltpu.make_async_copy(*pair, arrived.at[i]) for i, pair in enumerate(copies)]
     for copy in copies:
         copy.start()
@@ -172,6 +176,9 @@
                     jnp.broadcast_to(start_im[j : j + 1, :], shape),
                 ))
             enter(columns, jl, end_re, end_im)
+    else:
+        end_re[...] = start_re[...]
+        end_im[...] = start_im[...]
 
     def joined(pieces):
         re_high, re_low = split(jnp.concatenate([p[0] for p in pieces], axis=0))
@@ -318,11 +325,11 @@
     call = pl.pallas_call(
         functools.partial(march_kernel, begin, steps, batch, own, first, last, len(slabs)),
         out_shape=outputs,
-        in_specs=[smem] + [anywhere] * len(slabs) + [vmem if first else anywhere] * 2 + [vmem] * 9,
+        in_specs=[smem] + [anywhere] * len(slabs) + [vmem] * 11,
         out_specs=[vmem] * len(outputs),
         scratch_shapes=([held, held] if last else []) + [
             pltpu.VMEM((sections, *slabs[0].shape[-2:]), BF16),
-            pltpu.SemaphoreType.DMA((len(slabs) + 2,)),
+            pltpu.SemaphoreType.DMA((len(slabs),)),
             held,
             held,
             pltpu.VMEM((ROWS * batch, 2 * LANES), BF16),
@@ -337,82 +344,96 @@
     return call(section, *slabs, *start, named, totals, *consts)
 
 
-def turned(levels, base, rows, begin, end, own, put):
+def turn_steps(block, rows, begin, end, out):
+    own, steps, heights = block.shape
+    batch = out.shape[0] // (end - begin)
+    for c in range(heights // LANES):
+        column = slice(c * LANES, (c + 1) * LANES)
+        for b in range(own):
+            rows[c, b * steps : (b + 1) * steps, :] = block[b, :, column].astype(F32)
+        for t in range(begin, end):
+            taken = rows[c, pl.ds(t, own, stride=steps), :].astype(BF16)
+            if own < batch:
+                taken = jnp.pad(taken, ((0, batch - own), (0, 0)))
+            out[(t - begin) * batch : (t - begin + 1) * batch, column] = taken
+
+
+def fill_slabs(begin, end, own, batch, owners, levels, digits, slabs, blocks, turned, rows, sems):
+    count = (end - begin) * batch
+    arrive = [
+        pltpu.make_async_copy(levels.at[pl.ds(owner * own, own)], blocks.at[i], sems.at[0, i])
+        for i, owner in enumerate(owners)
+    ]
+    leave = [pltpu.make_async_copy(turned.at[i], slab, sems.at[1, i]) for i, slab in enumerate(slabs)]
+    for copy in arrive:
+        copy.start()
+    for i in range(len(slabs)):
+        arrive[i].wait()
+        turn_steps(blocks.at[i], rows, begin, end, turned.at[i, :count, :])
+        if turned.shape[1] > count:
+            turned[i, count:, :] = jnp.zeros((DIGIT_ROWS, turned.shape[2]), BF16)
+            turned[i, count:, : digits.shape[1]] = digits[...]
+        leave[i].start()
+    for copy in leave:
+        copy.wait()
+
+
+def slab_scratch(number, own, steps, heights, count):
+    return [
+        pltpu.VMEM((number, own, steps, heights), BF16),
+        pltpu.VMEM((number, count, heights), BF16),
+        pltpu.VMEM((heights // LANES, own * steps, LANES), F32),
+        pltpu.SemaphoreType.DMA((2, number)),
+    ]
+
+
+def cut(section, levels, digits, begin, end, own, batch, partners, extra):
     steps, heights = levels.shape[1:]
-    columns = [slice(c * LANES, (c + 1) * LANES) for c in range(heights // LANES)]
-    for b in range(own):
-        for c, column in enumerate(columns):
-            rows[c, b * steps : (b + 1) * steps, :] = levels[base + b, :, column].astype(F32)
-    for t in range(begin, end):
-        for c, column in enumerate(columns):
-            put(t - begin, column, rows[c, pl.ds(t, own, stride=steps), :].astype(BF16))
-
-
-def filled(taken, batch):
-    if taken.shape[0] < batch:
-        return jnp.pad(taken, ((0, batch - taken.shape[0]), (0, 0)))
-    return taken
-
-
-def deal_kernel(begin, end, own, steps, batch, levels, digits, out):
-    count = (end - begin) * batch
-    row = lax.broadcasted_iota(jnp.int32, (count, own * steps), 0)
-    column = lax.broadcasted_iota(jnp.int32, (count, own * steps), 1)
-    wanted = (row % batch) * steps + row // batch + begin
-    chosen = jnp.logical_and(column == wanted, row % batch < own)
-    moved = jnp.dot(
-        chosen.astype(F32).astype(BF16),
-        levels[...].reshape(own * steps, levels.shape[2]),
-        preferred_element_type=F32,
-    )
-    out[0, :count, :] = moved.astype(BF16)
-    out[0, count:, :] = jnp.zeros((DIGIT_ROWS, levels.shape[2]), BF16)
-    out[0, count:, : digits.shape[1]] = digits[...]
-
-
-def deal(levels, digits, begin, end, sections, own, batch):
+    count = (end - begin) * batch + extra
+    vmem = pl.BlockSpec(memory_space=pltpu.VMEM)
+    smem = pl.BlockSpec(memory_space=pltpu.SMEM)
+    anywhere = pl.BlockSpec(memory_space=pl.ANY)
+
+    def kernel(section, levels, digits, *refs):
+        slabs, scratch = refs[: len(partners)], refs[len(partners) :]
+        fill_slabs(begin, end, own, batch, [section[0] ^ d for d in partners], levels, digits, slabs, *scratch)
+
+    call = pl.pallas_call(
+        kernel,
+        out_shape=[jax.ShapeDtypeStruct((count, heights), BF16)] * len(partners),
+        in_specs=[smem, anywhere, vmem],
+        out_specs=[anywhere] * len(partners),
+        scratch_shapes=slab_scratch(len(partners), own, steps, heights, count),
+        compiler_params=pltpu.CompilerParams(vmem_limit_bytes=58 * 1024 * 1024),
+        cost_estimate=pl.CostEstimate(flops=1_000_000_000, bytes_accessed=4 * 1024 * 1024, transcendentals=0),
+        name="cut",
+    )
+    return call(section, levels, digits)
+
+
+def deal(section, levels, digits, begin, end, own, batch, group, extra):
     steps, heights = levels.shape[1:]
-    count = (end - begin) * batch + DIGIT_ROWS
-    return pl.pallas_call(
-        functools.partial(deal_kernel, begin, end, own, steps, batch),
-        grid=(sections,),
-        out_shape=jax.ShapeDtypeStruct((sections, count, heights), BF16),
-        in_specs=[
-            pl.BlockSpec((own, steps, heights), lambda d: (d, 0, 0)),
-            pl.BlockSpec(digits.shape, lambda d: (0, 0)),
-        ],
-        out_specs=pl.BlockSpec((1, count, heights), lambda d: (d, 0, 0)),
-        compiler_params=pltpu.CompilerParams(vmem_limit_bytes=60 * 1024 * 1024),
+    count = (end - begin) * batch + extra
+    vmem = pl.BlockSpec(memory_space=pltpu.VMEM)
+    smem = pl.BlockSpec(memory_space=pltpu.SMEM)
+    anywhere = pl.BlockSpec(memory_space=pl.ANY)
+
+    def kernel(section, levels, digits, out, *scratch):
+        base = section[0] // group * group
+        fill_slabs(begin, end, own, batch, [base + i for i in range(group)], levels, digits,
+                   [out.at[i] for i in range(group)], *scratch)
+
+    call = pl.pallas_call(
+        kernel,
+        out_shape=jax.ShapeDtypeStruct((group, count, heights), BF16),
+        in_specs=[smem, anywhere, vmem],
+        out_specs=anywhere,
+        scratch_shapes=slab_scratch(group, own, steps, heights, count),
+        compiler_params=pltpu.CompilerParams(vmem_limit_bytes=58 * 1024 * 1024),
         cost_estimate=pl.CostEstimate(flops=1_000_000_000, bytes_accessed=4 * 1024 * 1024, transcendentals=0),
         name="deal",
-    )(levels, digits)
-
-
-def cut_kernel(begin, end, own, batch, section, levels, *refs):
-    slabs, rows = refs[:-1], refs[-1]
-    for d, slab in enumerate(slabs):
-        def put(t, column, taken, slab=slab):
-            slab[t * batch : (t + 1) * batch, column] = filled(taken, batch)
-
-        turned(levels, (section[0] ^ d) * own, rows, begin, end, own, put)
-
-
-def cut(section, levels, begin, end, sections, own, batch):
-    steps, heights = levels.shape[1:]
-    slab = jax.ShapeDtypeStruct(((end - begin) * batch, heights), BF16)
-    vmem = pl.BlockSpec(memory_space=pltpu.VMEM)
-    smem = pl.BlockSpec(memory_space=pltpu.SMEM)
-    call = pl.pallas_call(
-        functools.partial(cut_kernel, begin, end, own, batch),
-        out_shape=(slab,) * sections,
-        in_specs=[smem, vmem],
-        out_specs=(vmem,) * sections,
-        scratch_shapes=[pltpu.VMEM((heights // LANES, own * steps, LANES), F32)],
-        compiler_params=pltpu.CompilerParams(vmem_limit_bytes=60 * 1024 * 1024),
-        cost_estimate=pl.CostEstimate(flops=1_000_000_000, bytes_accessed=4 * 1024 * 1024, transcendentals=0),
-        name="cut",
-    )
-    return call(section, levels)
+    )
+    return call(section, levels, digits)
 
 
 def local(refractivity, source, terrain, tile_map):
@@ -425,24 +446,30 @@
 
     small = jnp.concatenate([terrain.T, tile_map.T])
     digits = jnp.concatenate([small // DIGIT, small % DIGIT]).astype(BF16)
-    middle = round(WHOLE_SHARE * steps)
+    middle = round(EARLY_SHARE * steps)
     section = lax.axis_index("range").astype(jnp.int32).reshape(1)
-    dealt = deal(refractivity, digits, 0, middle, sections, own, batch)
-    refractivity, dealt = lax.optimization_barrier((refractivity, dealt))
-    whole = lax.all_to_all(dealt, "range", 0, 0, tiled=True)
-    slabs = list(cut(section, refractivity, middle, steps, sections, own, batch))
-    for d in range(1, sections):
-        slabs[d] = lax.ppermute(slabs[d], "range", [(i, i ^ d) for i in range(sections)])
+    half = sections // 2
+    slabs = []
+    cuts = cut(section, refractivity, digits, 0, middle, own, batch, range(half, sections), DIGIT_ROWS)
+    for d, slab in zip(range(half, sections), cuts):
+        slabs.append(lax.ppermute(slab, "range", [(i, i ^ d) for i in range(sections)]))
+    refractivity, digits, cuts = lax.optimization_barrier((refractivity, digits, cuts))
+    near = deal(section, refractivity, digits, 0, middle, own, batch, half, DIGIT_ROWS)
+    groups = [list(range(half)), list(range(half, sections))]
+    near = lax.all_to_all(near, "range", 0, 0, axis_index_groups=groups, tiled=True)
+    late = deal(section, refractivity, digits, middle, steps, own, batch, sections, 0)
+    late, near, slabs[-1] = lax.optimization_barrier((late, near, slabs[-1]))
+    late = lax.all_to_all(late, "range", 0, 0, tiled=True)
 
     consts = [jnp.asarray(v) for v in tables()]
     start = (source[0].reshape(ROWS, LANES), source[1].reshape(ROWS, LANES))
     totals = jnp.zeros((tiles, BINS), F32)
     named = jnp.zeros((sections, DIGIT_ROWS // 2, radials), jnp.int32)
     totals, *start, named = march(
-        section, [whole], 0, middle, batch, own, start, named, totals, consts, True, False
+        section, [near] + slabs, 0, middle, batch, own, start, named, totals, consts, True, False
     )
     (totals,) = march(
-        section, slabs, middle, steps - middle, batch, own, start, named, totals, consts, False, True
+        section, [late], middle, steps - middle, batch, own, start, named, totals, consts, False, True
     )
 
     named, totals = lax.optimization_barrier((named, totals))

time: 94.4 us -> 96.4 us (1.021)
  starting transfers between devices: 25.7 us -> 36.7 us
  waiting for transfers between devices: 33.6 us -> 22.7 us
  local copies, waits for them, and re-layouts: 0.1 us -> 1.75 us
    all_to_all x1 -> x2, waiting for transfers between devices: 11.8 us -> 0.01 us  [the longest x1 0.01 us: local(): lax.all_to_all(near, 'range', 0, 0, axis_index_groups=groups, tiled=True)]
    all_to_all x1 -> x2, starting transfers between devices: 7.28 us -> 17.8 us  [the longest x1 12.5 us: local(): late = lax.all_to_all(late, 'range', 0, 0, tiled=True)]
    all_to_all x1, starting transfers between devices: 3.52 us -> 10.6 us  [local(): lax.all_to_all(totals.reshape(owners, TILE_DEV, BINS), ('range', 'radial'...]
    ppermute x7 -> x4, starting transfers between devices: 14.6 us -> 7.88 us  [local(): lax.ppermute(slab, 'range', [(i, i ^ d) for i in range(sections)])]
    unnamed x18 -> x26, local copies, waits for them, and re-layouts: 0.06 us -> 1.71 us
    ppermute x7 -> x4, waiting for transfers between devices: 14.5 us -> 15.5 us  [local(): lax.ppermute(slab, 'range', [(i, i ^ d) for i in range(sections)])]
    pallas_call x2 -> x3, Pallas kernels: 9.27 us -> 9.09 us  [the longest x2 6.13 us: deal(): return call(section, levels, digits)]
  transfers between devices with their start and end apart: 10 -> 8, of which waited for: 5 -> 5; matrix products, arithmetic and copies ran while one was open for 0% -> 0% of each run, Pallas kernels for 19% -> 20%
where the time goes in v5:
time: 96.4 us; the launch traced here: 95.9 us
  starting transfers between devices  36.7 us (38%)
  Pallas kernels  32.3 us (34%)
  waiting for transfers between devices  22.7 us (24%)
  other arithmetic  2.22 us (2%)
  local copies, waits for them, and re-layouts  1.75 us (2%)
    pallas_call x2, Pallas kernels, march(): return call(section, *slabs, *start, named, totals, *consts)  23.2 us
    ppermute x4, waiting for transfers between devices, local(): lax.ppermute(slab, 'range', [(i, i ^ d) for i in range(sections)])  15.5 us
    all_to_all x1, starting transfers between devices, local(): late = lax.all_to_all(late, 'range', 0, 0, tiled=True)  12.5 us
    all_to_all x1, starting transfers between devices, local(): lax.all_to_all(totals.reshape(owners, TILE_DEV, BINS), ('range', 'radial'...  10.6 us
    ppermute x4, starting transfers between devices, local(): lax.ppermute(slab, 'range', [(i, i ^ d) for i in range(sections)])  7.88 us
    all_to_all x1, waiting for transfers between devices, local(): lax.all_to_all(totals.reshape(owners, TILE_DEV, BINS), ('range', 'radial'...  6.41 us
    pallas_call x2, Pallas kernels, deal(): return call(section, levels, digits)  6.13 us
    all_to_all x1, starting transfers between devices, local(): lax.all_to_all(near, 'range', 0, 0, axis_index_groups=groups, tiled=True)  5.26 us
  transfers between devices with their start and end apart: 8, of which 5 were waited for; matrix products, arithmetic and copies ran while one was open for 0% of the time, Pallas kernels for 20%

profile of v5, /device:TPU:0, one launch (start us, length us, event | category | flops | bytes accessed | tf_op | source)
XLA Modules:
  0.0 95.9 jit_solution(10323266069194160769)
XLA Ops:
  0.0 0.7 fusion
  0.7 0.6 pad_maximum_fusion.digits
  1.3 3.0 %cut.1 = (bf16[184,512]{1,0:T(8,128)(2,1)}, bf16[184,512]{1,0:T(8,128)(2,1)}, bf16[184,512]{1,0:T(8,128)(2,1)}, bf16[184,512]{1,0:T(8,128)(2,1)}) custom-call(s32[1]{0:T(128)} %bitcast.section, bf16[128,16,512]{2,1,0:T(8,128)(2,1)} %levels.3, bf16[8,128]{1,0:T(8,128)(2,1)} %pad_maximum_fusion.digits), custom_call_target="tpu_custom_call" | custom-call | flops 1000000000 | bytes 4194304 | tf_op jit(solution)/shard_map/cut/pallas_call | solution.py:411
  4.3 0.0 copy-start.12
  4.3 0.0 copy-start.11
  4.3 0.0 copy-start.10
  4.3 0.0 copy-start.9
  4.3 3.0 %deal.3 = bf16[4,184,512]{2,1,0:T(8,128)(2,1)} custom-call(s32[1]{0:T(128)} %bitcast.section, bf16[128,16,512]{2,1,0:T(8,128)(2,1)} %levels.3, bf16[8,128]{1,0:T(8,128)(2,1)} %pad_maximum_fusion.digits), custom_call_target="tpu_custom_call" | custom-call | flops 1000000000 | bytes 4194304 | tf_op jit(solution)/shard_map/deal/pallas_call | solution.py:436
  7.3 5.3 %all-to-all-start = ((bf16[4,184,512]{2,1,0:T(8,128)(2,1)}), bf16[4,184,512]{2,1,0:T(8,128)(2,1)S(1)}, u32[]{:S(2)}, u32[]{:S(2)}) async-start(bf16[4,184,512]{2,1,0:T(8,128)(2,1)} %deal.3), calls=%async_computation | async-start | bytes 1507328 | tf_op jit(solution)/shard_map/all_to_all | solution.py:459
  12.6 0.0 copy-done.12
  12.6 4.9 %collective-permute-start = (bf16[184,512]{1,0:T(8,128)(2,1)S(1)}, bf16[184,512]{1,0:T(8,128)(2,1)S(1)}, u32[]{:S(2)}, u32[]{:S(2)}) collective-permute-start(bf16[184,512]{1,0:T(8,128)(2,1)S(1)} %copy-done.12), channel_id=1, source_target_pairs={{0,14},{2,12},{4,10},{6,8},{8,6},{10,4},{12,2},{14,0},{1,15},{3,13... | collective-permute-start | bytes 565256 | tf_op jit(solution)/shard_map/ppermute | solution.py:455
  17.6 0.0 collective-permute-start.1
  17.6 0.0 copy-done.11
  17.6 2.9 %collective-permute-start.2 = (bf16[184,512]{1,0:T(8,128)(2,1)S(1)}, bf16[184,512]{1,0:T(8,128)(2,1)S(1)}, u32[]{:S(2)}, u32[]{:S(2)}) collective-permute-start(bf16[184,512]{1,0:T(8,128)(2,1)S(1)} %copy-done.11), channel_id=1, source_target_pairs={{0,10},{2,8},{4,14},{6,12},{8,2},{10,0},{12,6},{14,4},{1,11},{3,9}... | collective-permute-start | bytes 565256 | tf_op jit(solution)/shard_map/ppermute | solution.py:455
  20.5 0.0 copy-done.10
  20.5 0.0 collective-permute-start.3
  20.5 0.0 copy-done.9
  20.5 0.0 copy-start
  20.5 0.0 copy-start.1
  20.6 0.0 copy-start.2
  20.6 0.0 copy-start.3
  20.6 0.0 copy-start.4
  20.6 0.0 copy-start.5
  20.6 0.0 copy-start.6
  20.6 3.1 %deal.2 = bf16[8,80,512]{2,1,0:T(8,128)(2,1)} custom-call(s32[1]{0:T(128)} %bitcast.section, bf16[128,16,512]{2,1,0:T(8,128)(2,1)} %levels.3, bf16[8,128]{1,0:T(8,128)(2,1)} %pad_maximum_fusion.digits), custom_call_target="tpu_custom_call" | custom-call | flops 1000000000 | bytes 4194304 | tf_op jit(solution)/shard_map/deal/pallas_call | solution.py:436
  23.7 9.5 %collective-permute-done.refs_4_ = bf16[184,512]{1,0:T(8,128)(2,1)S(1)} collective-permute-done((bf16[184,512]{1,0:T(8,128)(2,1)S(1)}, bf16[184,512]{1,0:T(8,128)(2,1)S(1)}, u32[]{:S(2)}, u32[]{:S(2)}) %collective-permute-start) | collective-permute-done | bytes 188448 | tf_op jit(solution)/shard_map/ppermute | solution.py:455
  33.2 0.0 all-to-all-done.refs_0_
  33.2 12.5 %all-to-all-start.1 = ((bf16[8,80,512]{2,1,0:T(8,128)(2,1)}), bf16[8,80,512]{2,1,0:T(8,128)(2,1)S(1)}, u32[]{:S(2)}, u32[]{:S(2)}) async-start(bf16[8,80,512]{2,1,0:T(8,128)(2,1)} %deal.2), calls=%async_computation.1 | async-start | bytes 1310720 | tf_op jit(solution)/shard_map/all_to_all | solution.py:462
  45.8 1.9 %collective-permute-done.1.refs_1_ = bf16[184,512]{1,0:T(8,128)(2,1)S(1)} collective-permute-done((bf16[184,512]{1,0:T(8,128)(2,1)}, bf16[184,512]{1,0:T(8,128)(2,1)S(1)}, u32[]{:S(2)}, u32[]{:S(2)}) %collective-permute-start.1) | collective-permute-done | bytes 188448 | tf_op jit(solution)/shard_map/ppermute | solution.py:455
  47.7 4.1 %collective-permute-done.2.refs_2_ = bf16[184,512]{1,0:T(8,128)(2,1)S(1)} collective-permute-done((bf16[184,512]{1,0:T(8,128)(2,1)S(1)}, bf16[184,512]{1,0:T(8,128)(2,1)S(1)}, u32[]{:S(2)}, u32[]{:S(2)}) %collective-permute-start.2) | collective-permute-done | bytes 188448 | tf_op jit(solution)/shard_map/ppermute | solution.py:455
  51.8 0.0 collective-permute-done.3.refs_3_
  51.8 0.0 copy-done
  51.8 0.0 copy-done.1
  51.8 0.0 copy-done.2
  51.8 0.0 copy-done.3
  51.8 0.0 copy-done.4
  51.8 0.0 copy-done.5
  51.8 0.0 copy-done.6
  51.9 15.7 %march.2 = (f32[256,128]{1,0:T(8,128)S(1)}, f32[32,16,128]{2,1,0:T(8,128)S(1)}, f32[32,16,128]{2,1,0:T(8,128)S(1)}, s32[8,4,128]{2,1,0:T(4,128)S(1)}) custom-call(s32[1]{0:T(128)} %bitcast.section, bf16[4,184,512]{2,1,0:T(8,128)(2,1)S(1)} %all-to-all-done.refs_0_, bf16[184,512]{1,0:T(8,128)(2,1)S(1)} %collective-permute-done.1.refs_1_, ...), custom_call_target="tpu_custom_call" | custom-call | flops 17600000000 | bytes 4194304 | tf_op jit(solution)/shard_map/march/pallas_call | solution.py:344
  67.5 0.0 copy-start.7
  67.5 0.7 copy-done.7
  68.2 0.0 all-to-all-done.1.refs_0_
  68.2 0.0 copy-start.8
  68.2 0.9 copy-done.8
  69.2 7.5 %march.3 = f32[256,128]{1,0:T(8,128)} custom-call(s32[1]{0:T(128)} %bitcast.section, bf16[8,80,512]{2,1,0:T(8,128)(2,1)S(1)} %all-to-all-done.1.refs_0_, f32[32,16,128]{2,1,0:T(8,128)S(1)} %get-tuple-element.30.refs_1_, f32[32,16,128]{2,1,0:T(8,128)S(1)} %copy-done.8, s32[8,4,128]{2,1,0:T(4,128)S(1)} %get-tuple-element.34.refs_3_, ...), custom_call_target="tpu_custom_call" | custom-call | flops 8000000000 | bytes 4194304 | tf_op jit(solution)/shard_map/march/pallas_call | solution.py:344
  76.7 10.6 %all-to-all-start.2 = ((f32[16,16,128]{2,1,0:T(8,128)}), f32[16,16,128]{2,1,0:T(8,128)S(1)}, u32[]{:S(2)}, u32[]{:S(2)}) async-start(f32[16,16,128]{2,1,0:T(8,128)} %bitcast.5), calls=%async_computation.2 | async-start | bytes 262144 | tf_op jit(solution)/shard_map/all_to_all | solution.py:476
  87.3 0.2 convert_reduce_fusion
  87.6 0.5 collective-permute-start.4
  88.0 0.8 collective-permute-done.4
  88.8 6.4 %all-to-all-done.2 = f32[16,16,128]{2,1,0:T(8,128)S(1)} async-done(((f32[16,16,128]{2,1,0:T(8,128)}), f32[16,16,128]{2,1,0:T(8,128)S(1)}, u32[]{:S(2)}, u32[]{:S(2)}) %all-to-all-start.2) | async-done | bytes 131104 | tf_op jit(solution)/shard_map/all_to_all | solution.py:476
  95.3 0.7 broadcast_divide_fusion
  (7 shorter events, 0.1 us)
Async XLA Ops:
  4.3 8.3 %copy-start.12 = (bf16[184,512]{1,0:T(8,128)(2,1)S(1)}, bf16[184,512]{1,0:T(8,128)(2,1)}, u32[]{:S(2)}) copy-start(bf16[184,512]{1,0:T(8,128)(2,1)} %get-tuple-element.23) | copy-start | bytes 565252
  4.3 13.3 %copy-start.11 = (bf16[184,512]{1,0:T(8,128)(2,1)S(1)}, bf16[184,512]{1,0:T(8,128)(2,1)}, u32[]{:S(2)}) copy-start(bf16[184,512]{1,0:T(8,128)(2,1)} %get-tuple-element.21) | copy-start | bytes 565252
  4.3 16.2 %copy-start.10 = (bf16[184,512]{1,0:T(8,128)(2,1)S(1)}, bf16[184,512]{1,0:T(8,128)(2,1)}, u32[]{:S(2)}) copy-start(bf16[184,512]{1,0:T(8,128)(2,1)} %get-tuple-element.22) | copy-start | bytes 565252
  4.3 16.2 %copy-start.9 = (f32[2,4096]{1,0:T(2,128)S(1)}, f32[2,4096]{1,0:T(2,128)}, u32[]{:S(2)}) copy-start(f32[2,4096]{1,0:T(2,128)} %param.12) | copy-start | bytes 98308
  7.3 25.9 %all-to-all-start = ((bf16[4,184,512]{2,1,0:T(8,128)(2,1)}), bf16[4,184,512]{2,1,0:T(8,128)(2,1)S(1)}, u32[]{:S(2)}, u32[]{:S(2)}) async-start(bf16[4,184,512]{2,1,0:T(8,128)(2,1)} %deal.3), calls=%async_computation | async-start | bytes 1507328 | tf_op jit(solution)/shard_map/all_to_all | solution.py:459
  12.6 20.6 %collective-permute-start = (bf16[184,512]{1,0:T(8,128)(2,1)S(1)}, bf16[184,512]{1,0:T(8,128)(2,1)S(1)}, u32[]{:S(2)}, u32[]{:S(2)}) collective-permute-start(bf16[184,512]{1,0:T(8,128)(2,1)S(1)} %copy-done.12), channel_id=1, source_target_pairs={{0,14},{2,12},{4,10},{6,8},{8,6},{10,4},{12,2},{14,0},{1,15},{3,13... | collective-permute-start | bytes 565256 | tf_op jit(solution)/shard_map/ppermute | solution.py:455
  17.6 30.1 %collective-permute-start.1 = (bf16[184,512]{1,0:T(8,128)(2,1)}, bf16[184,512]{1,0:T(8,128)(2,1)S(1)}, u32[]{:S(2)}, u32[]{:S(2)}) collective-permute-start(bf16[184,512]{1,0:T(8,128)(2,1)} %get-tuple-element.20), channel_id=1, source_target_pairs={{0,8},{2,10},{4,12},{6,14},{8,0},{10,2},{12,4},{14,6},{1,9},{3,11}... | collective-permute-start | bytes 565256 | tf_op jit(solution)/shard_map/ppermute | solution.py:455
  17.6 34.2 %collective-permute-start.2 = (bf16[184,512]{1,0:T(8,128)(2,1)S(1)}, bf16[184,512]{1,0:T(8,128)(2,1)S(1)}, u32[]{:S(2)}, u32[]{:S(2)}) collective-permute-start(bf16[184,512]{1,0:T(8,128)(2,1)S(1)} %copy-done.11), channel_id=1, source_target_pairs={{0,10},{2,8},{4,14},{6,12},{8,2},{10,0},{12,6},{14,4},{1,11},{3,9}... | collective-permute-start | bytes 565256 | tf_op jit(solution)/shard_map/ppermute | solution.py:455
  20.5 31.3 %collective-permute-start.3 = (bf16[184,512]{1,0:T(8,128)(2,1)S(1)}, bf16[184,512]{1,0:T(8,128)(2,1)S(1)}, u32[]{:S(2)}, u32[]{:S(2)}) collective-permute-start(bf16[184,512]{1,0:T(8,128)(2,1)S(1)} %copy-done.10), channel_id=1, source_target_pairs={{0,12},{2,14},{4,8},{6,10},{8,4},{10,6},{12,0},{14,2},{1,13},{3,15... | collective-permute-start | bytes 565256 | tf_op jit(solution)/shard_map/ppermute | solution.py:455
  20.5 31.3 %copy-start = (bf16[768,256]{1,0:T(8,128)(2,1)S(1)}, bf16[768,256]{1,0:T(8,128)(2,1)}, u32[]{:S(2)}) copy-start(bf16[768,256]{1,0:T(8,128)(2,1)} %constant.59.clone.refs_9_.refs_5_) | copy-start | bytes 1179652
  20.5 31.3 %copy-start.1 = (bf16[768,256]{1,0:T(8,128)(2,1)S(1)}, bf16[768,256]{1,0:T(8,128)(2,1)}, u32[]{:S(2)}) copy-start(bf16[768,256]{1,0:T(8,128)(2,1)} %constant.60.clone.refs_10_.refs_6_) | copy-start | bytes 1179652
  20.6 31.3 %copy-start.2 = (bf16[256,128]{1,0:T(8,128)(2,1)S(1)}, bf16[256,128]{1,0:T(8,128)(2,1)}, u32[]{:S(2)}) copy-start(bf16[256,128]{1,0:T(8,128)(2,1)} %constant.65.clone.refs_15_.refs_11_) | copy-start | bytes 196612
  20.6 31.3 %copy-start.3 = (f32[2,32,128]{2,1,0:T(8,128)S(1)}, f32[2,32,128]{2,1,0:T(8,128)}, u32[]{:S(2)}) copy-start(f32[2,32,128]{2,1,0:T(8,128)} %constant.61.clone.refs_11_.refs_7_) | copy-start | bytes 98308
  20.6 31.2 %copy-start.4 = (f32[2,32,128]{2,1,0:T(8,128)S(1)}, f32[2,32,128]{2,1,0:T(8,128)}, u32[]{:S(2)}) copy-start(f32[2,32,128]{2,1,0:T(8,128)} %constant.62.clone.refs_12_.refs_8_) | copy-start | bytes 98308
  20.6 31.2 %copy-start.5 = (f32[32,128]{1,0:T(8,128)S(1)}, f32[32,128]{1,0:T(8,128)}, u32[]{:S(2)}) copy-start(f32[32,128]{1,0:T(8,128)} %constant.63.clone.refs_13_.refs_9_) | copy-start | bytes 49156
  20.6 31.2 %copy-start.6 = (f32[32,128]{1,0:T(8,128)S(1)}, f32[32,128]{1,0:T(8,128)}, u32[]{:S(2)}) copy-start(f32[32,128]{1,0:T(8,128)} %constant.64.clone.refs_14_.refs_10_) | copy-start | bytes 49156
  33.2 35.0 %all-to-all-start.1 = ((bf16[8,80,512]{2,1,0:T(8,128)(2,1)}), bf16[8,80,512]{2,1,0:T(8,128)(2,1)S(1)}, u32[]{:S(2)}, u32[]{:S(2)}) async-start(bf16[8,80,512]{2,1,0:T(8,128)(2,1)} %deal.2), calls=%async_computation.1 | async-start | bytes 1310720 | tf_op jit(solution)/shard_map/all_to_all | solution.py:462
  67.5 0.7 copy-start.7
  68.2 1.0 copy-start.8
  76.7 18.5 %all-to-all-start.2 = ((f32[16,16,128]{2,1,0:T(8,128)}), f32[16,16,128]{2,1,0:T(8,128)S(1)}, u32[]{:S(2)}, u32[]{:S(2)}) async-start(f32[16,16,128]{2,1,0:T(8,128)} %bitcast.5), calls=%async_computation.2 | async-start | bytes 262144 | tf_op jit(solution)/shard_map/all_to_all | solution.py:476
  87.6 1.3 %collective-permute-start.4 = (f32[16]{0:T(128)S(1)}, f32[16]{0:T(128)S(1)}, u32[]{:S(2)}, u32[]{:S(2)}) collective-permute-start(f32[16]{0:T(128)S(1)} %get-tuple-element.35), channel_id=1, source_target_pairs={{0,1},{1,0},{2,3},{3,2},{4,5},{5,4},{6,7},{7,6},{8,9},{9,8},{10,11... | collective-permute-start | bytes 200 | tf_op jit(solution)/shard_map/ppermute | solution.py:487

commit v6 on v1

v6 whole, which is shorter than its diff:
```python
import functools
import math

import jax
import jax.numpy as jnp
import ml_dtypes
import numpy as np
from jax import lax
from jax.experimental import pallas as pl
from jax.experimental.pallas import tpu as pltpu
from jax.sharding import PartitionSpec as P

H = 4096
BIN = 32
LANES = 128
ROWS = H // LANES
FOUR = 4
EIGHT = 8
BINS = H // BIN
TILE_DEV = 16
TILT_SLOPE = 2.0
SPREAD_RATE = 0.5
ABSORB_RATE = 0.05
TERRAIN_ROWS = 4
SUB = 8

F32 = jnp.float32
BF16 = jnp.bfloat16


def split_np(table):
    high = table.astype(np.float32).astype(ml_dtypes.bfloat16)
    low = (table - high.astype(np.float64)).astype(ml_dtypes.bfloat16)
    return high, low


def tables():
    n = np.arange(LANES)
    angle = -2.0 * np.pi / LANES * (n[:, None] * n[None, :] % LANES)
    c, s = np.cos(angle), np.sin(angle)
    forward = np.block([[c, s], [-s, c]])
    inverse = np.block([[c, -s], [s, c]])
    weights = []
    for matrix in (forward, inverse):
        high, low = split_np(matrix)
        weights.append(np.concatenate([high, high, low], axis=0))
    q = np.arange(ROWS)
    angle = -2.0 * np.pi / H * (q[:, None] * n[None, :])
    twiddle = np.stack([np.cos(angle), np.sin(angle)]).astype(np.float32)
    frequency = q[:, None] + ROWS * n[None, :]
    signed = np.where(frequency >= H // 2, frequency - H, frequency)
    turning = -SPREAD_RATE * (2.0 * np.pi / H * signed) ** 2
    spread = (np.stack([np.cos(turning), np.sin(turning)]) / H).astype(np.float32)
    rel = np.arange(H).reshape(ROWS, LANES) / H
    tilt = (TILT_SLOPE * rel - 1.0).astype(np.float32)
    depth = np.maximum(rel - 0.75, 0.0) * 4.0
    absorb = np.exp(-ABSORB_RATE * depth * depth).astype(np.float32)
    bins = np.zeros((2 * LANES, BINS), np.float64)
    for lane in range(2 * LANES):
        bins[lane, (lane % LANES) // BIN :: LANES // BIN] = 1.0 / BIN
    return weights[0], weights[1], twiddle, spread, tilt, absorb, bins.astype(ml_dtypes.bfloat16)


def phase_polynomials():
    root = 2.0 ** 0.25
    sin_scale = root * math.sqrt(2.0)
    cos_scale = 2.0 * math.sqrt(2.0) / sin_scale
    limit = 7.001
    nodes = 0.5 * limit * limit * (1.0 + np.cos(np.pi * (np.arange(64) + 0.5) / 64))
    phi = np.sqrt(nodes)
    sine = np.polynomial.chebyshev.Chebyshev.fit(
        nodes, sin_scale * np.sin(phi / 4) / phi, 4, domain=[0, limit * limit]
    ).convert(kind=np.polynomial.Polynomial)
    cosine = np.polynomial.chebyshev.Chebyshev.fit(
        nodes, cos_scale * np.cos(phi / 4), 4, domain=[0, limit * limit]
    ).convert(kind=np.polynomial.Polynomial)
    return [float(v) for v in sine.coef], [float(v) for v in cosine.coef]


def unit(number, extent):
    angle = -2.0 * math.pi * (number % extent) / extent
    return math.cos(angle), math.sin(angle)


def cmul_const(value, factor):
    re, im = value
    c, s = factor
    if abs(s) < 1e-12 and c > 0:
        return value
    if abs(c) < 1e-12:
        return (im, -re) if s < 0 else (-im, re)
    return re * c - im * s, re * s + im * c


def add(a, b):
    return a[0] + b[0], a[1] + b[1]


def sub(a, b):
    return a[0] - b[0], a[1] - b[1]


def add_turned(a, b, sign):
    if sign < 0:
        return a[0] + b[1], a[1] - b[0]
    return a[0] - b[1], a[1] + b[0]


def dft4(x, sign):
    a, b = add(x[0], x[2]), sub(x[0], x[2])
    c, d = add(x[1], x[3]), sub(x[1], x[3])
    return [add(a, c), add_turned(b, d, sign), sub(a, c), add_turned(b, d, -sign)]


def eighth(a, sign):
    h = math.sqrt(0.5)
    re, im = a
    if sign < 0:
        return (re + im) * h, (im - re) * h
    return (re - im) * h, (re + im) * h


def dft8(x, sign):
    even = dft4(x[0::2], sign)
    odd = dft4(x[1::2], sign)
    odd[1], odd[3] = eighth(odd[1], sign), eighth(odd[3], sign)
    low = [add(even[0], odd[0]), add(even[1], odd[1]), add_turned(even[2], odd[2], sign), add_turned(even[3], odd[3], sign)]
    high = [sub(even[0], odd[0]), sub(even[1], odd[1]), add_turned(even[2], odd[2], -sign), add_turned(even[3], odd[3], -sign)]
    return low + high


def split(value):
    high = value.astype(BF16)
    low = (value - high.astype(F32)).astype(BF16)
    return high, low


def march_kernel(own, received, cells, start, w_forward, w_inverse, twiddle, spread, tilt, absorb, bins, section,
                 totals, levels, arrived, wide, field, back, energy, power):
    sine, cosine = phase_polynomials()
    sections, batch, steps, heights = levels.shape
    halves = batch // SUB
    copy = pltpu.make_async_copy(received, levels, arrived)
    copy.start()
    lane = lax.broadcasted_iota(jnp.int32, (SUB, LANES), 1)
    radial = lax.broadcasted_iota(jnp.int32, (SUB, LANES), 0)
    at_once = cells.shape[1] // 2

    def enter(half, columns, jl):
        parts = dft4(columns, -1)
        for ql in range(FOUR):
            re, im = cmul_const(parts[ql], unit(ql * jl, ROWS))
            field[half, 0, ql * EIGHT + jl] = re
            field[half, 1, ql * EIGHT + jl] = im

    def joined(pieces):
        re_high, re_low = split(jnp.concatenate([p[0] for p in pieces], axis=0))
        im_high, im_low = split(jnp.concatenate([p[1] for p in pieces], axis=0))
        return jnp.concatenate([re_high, im_high, re_low, im_low, re_high, im_high], axis=1)

    def parted(product):
        return [
            (product[i * SUB : (i + 1) * SUB, :LANES], product[i * SUB : (i + 1) * SUB, LANES:]) for i in range(ROWS)
        ]

    rows = [ql + FOUR * qh for ql in range(FOUR) for qh in range(EIGHT)]

    def forward(half):
        pieces = []
        for ql in range(FOUR):
            column = [(field[half, 0, ql * EIGHT + jl], field[half, 1, ql * EIGHT + jl]) for jl in range(EIGHT)]
            for qh, (re, im) in enumerate(dft8(column, -1)):
                q = ql + FOUR * qh
                c, s = twiddle[0, q : q + 1, :], twiddle[1, q : q + 1, :]
                pieces.append((re * c - im * s, re * s + im * c))
        return jnp.dot(joined(pieces), w_forward[...], preferred_element_type=F32)

    def inverse(product):
        pieces = []
        for q, (re, im) in zip(rows, parted(product)):
            c, s = spread[0, q : q + 1, :], spread[1, q : q + 1, :]
            pieces.append((re * c - im * s, re * s + im * c))
        return jnp.dot(joined(pieces), w_inverse[...], preferred_element_type=F32)

    def leave(half, product):
        pieces = []
        for q, (re, im) in zip(rows, parted(product)):
            c, s = twiddle[0, q : q + 1, :], twiddle[1, q : q + 1, :]
            pieces.append((re * c + im * s, im * c - re * s))
        for ql in range(FOUR):
            column = dft8(pieces[ql * EIGHT : (ql + 1) * EIGHT], 1)
            for jl in range(EIGHT):
                back[half, 0, ql * EIGHT + jl] = column[jl][0]
                back[half, 1, ql * EIGHT + jl] = column[jl][1]

    def rotate(half, t, ground, jls):
        for jl in jls:
            column = []
            for ql in range(FOUR):
                c, s = unit(ql * jl, ROWS)
                column.append(
                    cmul_const((back[half, 0, ql * EIGHT + jl], back[half, 1, ql * EIGHT + jl]), (c, -s))
                )
            column = dft4(column, 1)
            moved = []
            for jh in range(FOUR):
                j = EIGHT * jh + jl
                phi = wide[j, pl.ds(half * SUB * steps + t, SUB, stride=steps), :] + tilt[j : j + 1, :]
                u = phi * phi
                sin_poly, cos_poly = sine[-1], cosine[-1]
                for a, b in zip(sine[-2::-1], cosine[-2::-1]):
                    sin_poly = sin_poly * u + a
                    cos_poly = cos_poly * u + b
                small = sin_poly * phi
                double = small * cos_poly
                turned_c = 1.0 - double * double
                turned_s = double * (math.sqrt(2.0) - small * small)
                re, im = column[jh]
                if (j + 1) * LANES > 3 * H // 4:
                    loss = absorb[j : j + 1, :]
                    re, im = re * loss, im * loss
                re, im = re * turned_c - im * turned_s, re * turned_s + im * turned_c
                if j < TERRAIN_ROWS:
                    open_air = lane + j * LANES >= ground
                    re, im = jnp.where(open_air, re, 0.0), jnp.where(open_air, im, 0.0)
                value = re * re + im * im
                high = value.astype(BF16).astype(F32)
                energy[half, j * SUB : (j + 1) * SUB, :LANES] = high
                energy[half, j * SUB : (j + 1) * SUB, LANES:] = value - high
                moved.append((re, im))
            enter(half, moved, jl)

    def binned(half, t):
        summed = jnp.dot(energy[half].astype(BF16), bins[...], preferred_element_type=F32)
        row = summed[:SUB]
        for j in range(1, ROWS):
            row = jnp.where(lane // (LANES // BIN) == j, summed[j * SUB : (j + 1) * SUB], row)
        power[pl.ds(pl.multiple_of(t * batch + half * SUB, SUB), SUB), :] = row

    def ground_of(half, t):
        row = cells[t // at_once, pl.ds(t % at_once, 1), :]
        my_lane = lane == section[0] * own + half * SUB + radial
        return jnp.sum(jnp.where(my_lane, row, 0), axis=1, keepdims=True)

    def turn_of(t, resting, moving):
        ground = ground_of(resting, t)
        product = forward(moving)
        rotate(resting, t, ground, range(EIGHT // 2))
        product = inverse(product)
        rotate(resting, t, ground, range(EIGHT // 2, EIGHT))
        leave(moving, product)
        binned(resting, t)

    def step(t, carry):
        for half in range(halves):
            turn_of(t, half, (half + 1) % halves)
        return carry

    for half in range(halves):
        for jl in range(EIGHT):
            columns = []
            for jh in range(FOUR):
                j = EIGHT * jh + jl
                columns.append(tuple(jnp.broadcast_to(start[k, j : j + 1, :], (SUB, LANES)) for k in range(2)))
            enter(half, columns, jl)
    power[...] = jnp.zeros_like(power)
    leave(0, inverse(forward(0)))
    copy.wait()
    per_source = heights // LANES

    def widen(source, carry):
        for b in range(batch):
            for c in range(per_source):
                raw = levels[source, b, :, c * LANES : (c + 1) * LANES]
                wide[source * per_source + c, b * steps : (b + 1) * steps, :] = raw.astype(F32)
        return carry

    lax.fori_loop(0, sections, widen, 0)
    lax.fori_loop(0, steps, step, 0)

    lane = lax.broadcasted_iota(jnp.int32, (1, LANES), 1)
    fit = LANES // batch
    tile_rows = []
    for t in range(steps):
        row = cells[t // at_once, at_once + t % at_once, :].reshape(1, LANES)
        row = pltpu.roll(row, lax.rem(batch * (t % fit) - section[0] * own + LANES, LANES), 1)
        row = jnp.where(lane % batch < own, row, -1)
        if t % fit == 0:
            tile_rows.append(jnp.where(lane < batch, row, -1))
        else:
            tile_rows[-1] = jnp.where(lane // batch == t % fit, row, tile_rows[-1])
    tile_row = jnp.concatenate(tile_rows, axis=1)
    tiles, cell_count = totals.shape[0], tile_row.shape[1]
    hot = (lax.broadcasted_iota(jnp.int32, (tiles, cell_count), 0) == tile_row).astype(F32).astype(BF16)
    value = power[...]
    high = value.astype(BF16)
    rest = value - high.astype(F32)
    middle = rest.astype(BF16)
    low = (rest - middle.astype(F32)).astype(BF16)
    gain = jnp.dot(hot, high, preferred_element_type=F32)
    gain += jnp.dot(hot, middle, preferred_element_type=F32)
    gain += jnp.dot(hot, low, preferred_element_type=F32)
    totals[...] = gain


def march(section, received, cells, start, consts, tiles, own):
    sections, batch, steps, heights = received.shape
    halves = batch // SUB
    vmem = pl.BlockSpec(memory_space=pltpu.VMEM)
    smem = pl.BlockSpec(memory_space=pltpu.SMEM)
    call = pl.pallas_call(
        functools.partial(march_kernel, own),
        out_shape=jax.ShapeDtypeStruct((tiles, BINS), F32),
        in_specs=[pl.BlockSpec(memory_space=pl.ANY)] + [vmem] * 9 + [smem],
        out_specs=vmem,
        scratch_shapes=[
            pltpu.VMEM(received.shape, BF16),
            pltpu.SemaphoreType.DMA,
            pltpu.VMEM((ROWS, batch * steps, LANES), F32),
            pltpu.VMEM((halves, 2, ROWS, SUB, LANES), F32),
            pltpu.VMEM((halves, 2, ROWS, SUB, LANES), F32),
            pltpu.VMEM((halves, ROWS * SUB, 2 * LANES), F32),
            pltpu.VMEM((-(-steps * batch // LANES) * LANES, BINS), F32),
        ],
        compiler_params=pltpu.CompilerParams(vmem_limit_bytes=44 * 1024 * 1024),
        cost_estimate=pl.CostEstimate(
            flops=steps * 1_600_000_000, bytes_accessed=4 * 1024 * 1024, transcendentals=0
        ),
        name="march",
    )
    return call(received, cells, start, *consts, section)


def gather_small(value):
    radial, sections = lax.axis_index("radial"), lax.axis_size("range")
    other = lax.ppermute(value, "radial", [(0, 1), (1, 0)])
    pair = jnp.stack([jnp.where(radial == 0, value, other), jnp.where(radial == 0, other, value)])
    section = lax.axis_index("range")
    held = jnp.zeros((sections, *pair.shape), pair.dtype)
    held = lax.dynamic_update_index_in_dim(held, pair, section, 0)
    width = 1
    while width < sections:
        base = section // width * width
        part = lax.dynamic_slice_in_dim(held, base, width, 0)
        part = lax.ppermute(part, "range", [(i, i ^ width) for i in range(sections)])
        held = lax.dynamic_update_slice_in_dim(held, part, base ^ width, 0)
        width *= 2
    return held


def local(refractivity, source, terrain, tile_map):
    sections = lax.axis_size("range")
    owners = sections * lax.axis_size("radial")
    radials, steps, heights = refractivity.shape
    own = radials // sections
    batch = -(-own // 16) * 16
    section = lax.axis_index("range").astype(jnp.int32).reshape(1)

    received = refractivity.reshape(sections, own, steps, heights)
    received = lax.all_to_all(received, "range", 0, 0, tiled=True)
    received = jnp.pad(received, ((0, 0), (0, batch - own), (0, 0), (0, 0)))
    everyone = gather_small(jnp.concatenate([terrain.T, tile_map.T]))
    cells = lax.dynamic_index_in_dim(everyone, lax.axis_index("radial"), 1, keepdims=False)
    start = source.reshape(2, ROWS, LANES)
    totals = march(
        section, received, cells, start, [jnp.asarray(v) for v in tables()], TILE_DEV * owners, own
    )

    everyone, totals = lax.optimization_barrier((everyone, totals))
    sent = lax.all_to_all(
        totals.reshape(owners, TILE_DEV, BINS), ("range", "radial"), 0, 0, tiled=True
    )
    ids = (lax.axis_index("range") * lax.axis_size("radial") + lax.axis_index("radial")) * TILE_DEV
    ids = ids + jnp.arange(TILE_DEV, dtype=jnp.int32)
    counts = jnp.sum((ids[:, None] == everyone[:, :, terrain.shape[1] :].reshape(1, -1)).astype(F32), axis=1)
    return jnp.sum(sent, axis=0) / counts[:, None]


def solution(mesh):
    in_specs = (
        P(("region", "radial"), None, "range"),
        P(None, "region"),
        P(("region", "radial"), "range"),
        P(("region", "radial"), "range"),
    )
    out_specs = P(("region", "range", "radial"), None)
    return jax.shard_map(local, mesh=mesh, in_specs=in_specs, out_specs=out_specs, check_vma=False)
```

time: 105 us -> 93.7 us (0.89)
  blocking collectives: 50.7 us -> 0 us
  waiting for transfers between devices: 6.84 us -> 49 us
  local copies, waits for them, and re-layouts: 5.36 us -> 0.12 us
  Pallas kernels: 22.6 us -> 24.5 us
    all_gather x1 -> x0, blocking collectives: 50.7 us -> none  [local(): everyone = lax.all_gather(small, ('range', 'radial'))]
    ppermute x0 -> x4, waiting for transfers between devices: none -> 41.3 us  [the longest x3 40.2 us: gather_small(): lax.ppermute(part, 'range', [(i, i ^ width) for i in range(sections)])]
    ppermute x0 -> x4, starting transfers between devices: none -> 7.47 us  [the longest x3 7.4 us: gather_small(): lax.ppermute(part, 'range', [(i, i ^ width) for i in range(sections)])]
    all_to_all x1, starting transfers between devices: 10.3 us -> 3.75 us  [local(): lax.all_to_all(totals.reshape(owners, TILE_DEV, BINS), ('range', 'radial'...]
    reshape x2 -> x0, local copies, waits for them, and re-layouts: 4.25 us -> none  [the longest x1 4.16 us: local(): refractivity[:, begin:end].reshape(sections, own, end - begin, heights)]
    pallas_call x1, Pallas kernels: 22.6 us -> 24.5 us  [march(): return call(received, cells, start, *consts, section)]
  transfers between devices with their start and end apart: 2 -> 6, of which waited for: 1 -> 5; matrix products, arithmetic and copies ran while one was open for 1% -> 0% of each run, Pallas kernels for 0% -> 0%
where the time goes in v6:
time: 93.7 us; the launch traced here: 93.5 us
  waiting for transfers between devices  49 us (52%)
  Pallas kernels  24.5 us (26%)
  starting transfers between devices  18.7 us (20%)
  other arithmetic  0.95 us (1%)
    ppermute x3, waiting for transfers between devices, gather_small(): lax.ppermute(part, 'range', [(i, i ^ width) for i in range(sections)])  40.2 us
    pallas_call x1, Pallas kernels, march(): return call(received, cells, start, *consts, section)  24.5 us
    all_to_all x1, waiting for transfers between devices, local(): lax.all_to_all(totals.reshape(owners, TILE_DEV, BINS), ('range', 'radial'...  7.68 us
    all_to_all x1, starting transfers between devices, local(): received = lax.all_to_all(received, 'range', 0, 0, tiled=True)  7.44 us
    ppermute x3, starting transfers between devices, gather_small(): lax.ppermute(part, 'range', [(i, i ^ width) for i in range(sections)])  7.4 us
    all_to_all x1, starting transfers between devices, local(): lax.all_to_all(totals.reshape(owners, TILE_DEV, BINS), ('range', 'radial'...  3.75 us
  transfers between devices with their start and end apart: 6, of which 5 were waited for; matrix products, arithmetic and copies ran while one was open for 0% of the time, Pallas kernels for 0%

profile of v6, /device:TPU:0, one launch (start us, length us, event | category | flops | bytes accessed | tf_op | source)
XLA Modules:
  0.0 93.5 jit_solution(13685962138995450199)
XLA Ops:
  0.0 0.0 copy-start.8
  0.0 0.0 copy-start.9
  0.0 0.0 copy-start.7
  0.0 0.0 copy-start
  0.0 0.0 copy-start.1
  0.0 0.0 copy-start.2
  0.0 0.0 copy-start.3
  0.0 0.0 copy-start.4
  0.1 0.0 copy-start.5
  0.1 0.0 copy-start.6
  0.1 7.4 %all-to-all-start = ((bf16[8,16,16,512]{3,2,1,0:T(8,128)(2,1)}), bf16[8,16,16,512]{3,2,1,0:T(8,128)(2,1)S(1)}, u32[]{:S(2)}, u32[]{:S(2)}) async-start(bf16[8,16,16,512]{3,2,1,0:T(8,128)(2,1)} %bitcast.21), calls=%async_computation | async-start | bytes 4194304 | tf_op jit(solution)/shard_map/all_to_all | solution.py:360
  7.5 0.0 copy-done.8
  7.5 0.0 copy-done.9
  7.6 0.1 collective-permute-start
  7.6 1.1 %collective-permute-done = s32[4,128]{1,0:T(4,128)S(1)} collective-permute-done((s32[4,128]{1,0:T(4,128)S(1)}, s32[4,128]{1,0:T(4,128)S(1)}, u32[]{:S(2)}, u32[]{:S(2)}) %collective-permute-start) | collective-permute-done | bytes 2080 | tf_op jit(solution)/shard_map/ppermute | solution.py:336
  8.8 2.1 %collective-permute-start.1 = (s32[1,2,4,128]{3,2,1,0:T(4,128)S(1)}, s32[1,2,4,128]{3,2,1,0:T(4,128)S(1)}, u32[]{:S(2)}, u32[]{:S(2)}) collective-permute-start(s32[1,2,4,128]{3,2,1,0:T(4,128)S(1)} %constant_dynamic-slice_fusion.2), channel_id=1, source_target_pairs={{0,2},{2,0},{4,6},{6,4},{8,10},{10,8},{12,14},{14,12},{1,3},{3,1},... | collective-permute-start | bytes 12296 | tf_op jit(solution)/shard_map/ppermute | solution.py:345
  10.9 13.8 %collective-permute-done.1 = s32[1,2,4,128]{3,2,1,0:T(4,128)S(1)} collective-permute-done((s32[1,2,4,128]{3,2,1,0:T(4,128)S(1)}, s32[1,2,4,128]{3,2,1,0:T(4,128)S(1)}, u32[]{:S(2)}, u32[]{:S(2)}) %collective-permute-start.1) | collective-permute-done | bytes 4128 | tf_op jit(solution)/shard_map/ppermute | solution.py:345
  24.7 1.7 %collective-permute-start.2 = (s32[2,2,4,128]{3,2,1,0:T(4,128)S(1)}, s32[2,2,4,128]{3,2,1,0:T(4,128)S(1)}, u32[]{:S(2)}, u32[]{:S(2)}) collective-permute-start(s32[2,2,4,128]{3,2,1,0:T(4,128)S(1)} %constant_dynamic-slice_fusion.1), channel_id=1, source_target_pairs={{0,4},{2,6},{4,0},{6,2},{8,12},{10,14},{12,8},{14,10},{1,5},{3,7},... | collective-permute-start | bytes 24584 | tf_op jit(solution)/shard_map/ppermute | solution.py:345
  26.4 16.2 %collective-permute-done.2 = s32[2,2,4,128]{3,2,1,0:T(4,128)S(1)} collective-permute-done((s32[2,2,4,128]{3,2,1,0:T(4,128)S(1)}, s32[2,2,4,128]{3,2,1,0:T(4,128)S(1)}, u32[]{:S(2)}, u32[]{:S(2)}) %collective-permute-start.2) | collective-permute-done | bytes 8224 | tf_op jit(solution)/shard_map/ppermute | solution.py:345
  42.7 3.6 %collective-permute-start.3 = (s32[4,2,4,128]{3,2,1,0:T(4,128)S(1)}, s32[4,2,4,128]{3,2,1,0:T(4,128)S(1)}, u32[]{:S(2)}, u32[]{:S(2)}) collective-permute-start(s32[4,2,4,128]{3,2,1,0:T(4,128)S(1)} %constant_dynamic-slice_fusion), channel_id=1, source_target_pairs={{0,8},{2,10},{4,12},{6,14},{8,0},{10,2},{12,4},{14,6},{1,9},{3,11}... | collective-permute-start | bytes 49160 | tf_op jit(solution)/shard_map/ppermute | solution.py:345
  46.3 0.0 copy-done.7
  46.3 10.2 %collective-permute-done.3 = s32[4,2,4,128]{3,2,1,0:T(4,128)S(1)} collective-permute-done((s32[4,2,4,128]{3,2,1,0:T(4,128)S(1)}, s32[4,2,4,128]{3,2,1,0:T(4,128)S(1)}, u32[]{:S(2)}, u32[]{:S(2)}) %collective-permute-start.3) | collective-permute-done | bytes 16416 | tf_op jit(solution)/shard_map/ppermute | solution.py:345
  56.5 0.0 all-to-all-done.received
  56.5 0.0 copy-done
  56.5 0.0 copy-done.1
  56.5 0.0 copy-done.2
  56.5 0.0 copy-done.3
  56.5 0.0 copy-done.4
  56.5 0.0 copy-done.5
  56.5 0.0 copy-done.6
  56.6 24.5 %march.1 = f32[256,128]{1,0:T(8,128)} custom-call(bf16[8,16,16,512]{3,2,1,0:T(8,128)(2,1)S(1)} %all-to-all-done.received, s32[8,4,128]{2,1,0:T(4,128)S(1)} %dynamic-slice_bitcast_fusion.cells, f32[2,32,128]{2,1,0:T(8,128)S(1)} %bitcast.20, bf16[768,256]{1,0:T(8,128)(2,1)S(1)} %copy-done.1, bf16[768,256]{1,0:T(8,128)(2,1)S(1)} %copy-done, ...), custom_call_target="tpu_custom_call" | custom-call | flops 25600000000 | bytes 4194304 | tf_op jit(solution)/shard_map/march/pallas_call | solution.py:331
  81.1 3.8 %all-to-all-start.1 = ((f32[16,16,128]{2,1,0:T(8,128)}), f32[16,16,128]{2,1,0:T(8,128)S(1)}, u32[]{:S(2)}, u32[]{:S(2)}) async-start(f32[16,16,128]{2,1,0:T(8,128)} %bitcast.8), calls=%async_computation.1 | async-start | bytes 262144 | tf_op jit(solution)/shard_map/all_to_all | solution.py:370
  84.9 0.2 convert_reduce_fusion
  85.1 7.7 %all-to-all-done.1 = f32[16,16,128]{2,1,0:T(8,128)S(1)} async-done(((f32[16,16,128]{2,1,0:T(8,128)}), f32[16,16,128]{2,1,0:T(8,128)S(1)}, u32[]{:S(2)}, u32[]{:S(2)}) %all-to-all-start.1) | async-done | bytes 131104 | tf_op jit(solution)/shard_map/all_to_all | solution.py:370
  92.8 0.7 broadcast_divide_fusion
  (15 shorter events, 0.1 us)
Async XLA Ops:
  0.0 7.5 %copy-start.8 = (s32[128,2]{0,1:T(2,128)S(1)}, s32[128,2]{0,1:T(2,128)}, u32[]{:S(2)}) copy-start(s32[128,2]{0,1:T(2,128)} %param.14) | copy-start | bytes 3076
  0.0 7.5 %copy-start.9 = (s32[128,2]{0,1:T(2,128)S(1)}, s32[128,2]{0,1:T(2,128)}, u32[]{:S(2)}) copy-start(s32[128,2]{0,1:T(2,128)} %param.13) | copy-start | bytes 3076
  0.0 46.3 %copy-start.7 = (f32[2,4096]{1,0:T(2,128)S(1)}, f32[2,4096]{1,0:T(2,128)}, u32[]{:S(2)}) copy-start(f32[2,4096]{1,0:T(2,128)} %param.12) | copy-start | bytes 98308
  0.0 56.5 %copy-start = (bf16[768,256]{1,0:T(8,128)(2,1)S(1)}, bf16[768,256]{1,0:T(8,128)(2,1)}, u32[]{:S(2)}) copy-start(bf16[768,256]{1,0:T(8,128)(2,1)} %constant.74.clone.w_inverse) | copy-start | bytes 1179652
  0.0 56.5 %copy-start.1 = (bf16[768,256]{1,0:T(8,128)(2,1)S(1)}, bf16[768,256]{1,0:T(8,128)(2,1)}, u32[]{:S(2)}) copy-start(bf16[768,256]{1,0:T(8,128)(2,1)} %constant.73.clone.w_forward) | copy-start | bytes 1179652
  0.0 56.5 %copy-start.2 = (bf16[256,128]{1,0:T(8,128)(2,1)S(1)}, bf16[256,128]{1,0:T(8,128)(2,1)}, u32[]{:S(2)}) copy-start(bf16[256,128]{1,0:T(8,128)(2,1)} %constant.79.clone.bins) | copy-start | bytes 196612
  0.0 56.5 %copy-start.3 = (f32[2,32,128]{2,1,0:T(8,128)S(1)}, f32[2,32,128]{2,1,0:T(8,128)}, u32[]{:S(2)}) copy-start(f32[2,32,128]{2,1,0:T(8,128)} %constant.76.clone.spread) | copy-start | bytes 98308
  0.0 56.5 %copy-start.4 = (f32[2,32,128]{2,1,0:T(8,128)S(1)}, f32[2,32,128]{2,1,0:T(8,128)}, u32[]{:S(2)}) copy-start(f32[2,32,128]{2,1,0:T(8,128)} %constant.75.clone.twiddle) | copy-start | bytes 98308
  0.1 56.5 %copy-start.5 = (f32[32,128]{1,0:T(8,128)S(1)}, f32[32,128]{1,0:T(8,128)}, u32[]{:S(2)}) copy-start(f32[32,128]{1,0:T(8,128)} %constant.78.clone.absorb) | copy-start | bytes 49156
  0.1 56.5 %copy-start.6 = (f32[32,128]{1,0:T(8,128)S(1)}, f32[32,128]{1,0:T(8,128)}, u32[]{:S(2)}) copy-start(f32[32,128]{1,0:T(8,128)} %constant.77.clone.tilt) | copy-start | bytes 49156
  0.1 56.4 %all-to-all-start = ((bf16[8,16,16,512]{3,2,1,0:T(8,128)(2,1)}), bf16[8,16,16,512]{3,2,1,0:T(8,128)(2,1)S(1)}, u32[]{:S(2)}, u32[]{:S(2)}) async-start(bf16[8,16,16,512]{3,2,1,0:T(8,128)(2,1)} %bitcast.21), calls=%async_computation | async-start | bytes 4194304 | tf_op jit(solution)/shard_map/all_to_all | solution.py:360
  7.6 1.2 %collective-permute-start = (s32[4,128]{1,0:T(4,128)S(1)}, s32[4,128]{1,0:T(4,128)S(1)}, u32[]{:S(2)}, u32[]{:S(2)}) collective-permute-start(s32[4,128]{1,0:T(4,128)S(1)} %pad_add_fusion), channel_id=1, source_target_pairs={{0,1},{1,0},{2,3},{3,2},{4,5},{5,4},{6,7},{7,6},{8,9},{9,8},{10,11... | collective-permute-start | bytes 6152 | tf_op jit(solution)/shard_map/ppermute | solution.py:336
  8.8 15.9 %collective-permute-start.1 = (s32[1,2,4,128]{3,2,1,0:T(4,128)S(1)}, s32[1,2,4,128]{3,2,1,0:T(4,128)S(1)}, u32[]{:S(2)}, u32[]{:S(2)}) collective-permute-start(s32[1,2,4,128]{3,2,1,0:T(4,128)S(1)} %constant_dynamic-slice_fusion.2), channel_id=1, source_target_pairs={{0,2},{2,0},{4,6},{6,4},{8,10},{10,8},{12,14},{14,12},{1,3},{3,1},... | collective-permute-start | bytes 12296 | tf_op jit(solution)/shard_map/ppermute | solution.py:345
  24.7 18.0 %collective-permute-start.2 = (s32[2,2,4,128]{3,2,1,0:T(4,128)S(1)}, s32[2,2,4,128]{3,2,1,0:T(4,128)S(1)}, u32[]{:S(2)}, u32[]{:S(2)}) collective-permute-start(s32[2,2,4,128]{3,2,1,0:T(4,128)S(1)} %constant_dynamic-slice_fusion.1), channel_id=1, source_target_pairs={{0,4},{2,6},{4,0},{6,2},{8,12},{10,14},{12,8},{14,10},{1,5},{3,7},... | collective-permute-start | bytes 24584 | tf_op jit(solution)/shard_map/ppermute | solution.py:345
  42.7 13.8 %collective-permute-start.3 = (s32[4,2,4,128]{3,2,1,0:T(4,128)S(1)}, s32[4,2,4,128]{3,2,1,0:T(4,128)S(1)}, u32[]{:S(2)}, u32[]{:S(2)}) collective-permute-start(s32[4,2,4,128]{3,2,1,0:T(4,128)S(1)} %constant_dynamic-slice_fusion), channel_id=1, source_target_pairs={{0,8},{2,10},{4,12},{6,14},{8,0},{10,2},{12,4},{14,6},{1,9},{3,11}... | collective-permute-start | bytes 49160 | tf_op jit(solution)/shard_map/ppermute | solution.py:345
  81.1 11.7 %all-to-all-start.1 = ((f32[16,16,128]{2,1,0:T(8,128)}), f32[16,16,128]{2,1,0:T(8,128)S(1)}, u32[]{:S(2)}, u32[]{:S(2)}) async-start(f32[16,16,128]{2,1,0:T(8,128)} %bitcast.8), calls=%async_computation.1 | async-start | bytes 262144 | tf_op jit(solution)/shard_map/all_to_all | solution.py:370

commit v7 on v6

--- a/solution.py
+++ b/solution.py
@@ -43,7 +43,7 @@
     weights = []
     for matrix in (forward, inverse):
         high, low = split_np(matrix)
-        weights.append(np.concatenate([high, high, low], axis=0))
+        weights.append(np.stack([high, low]))
     q = np.arange(ROWS)
     angle = -2.0 * np.pi / H * (q[:, None] * n[None, :])
     twiddle = np.stack([np.cos(angle), np.sin(angle)]).astype(np.float32)
@@ -135,63 +135,107 @@
     return high, low
 
 
-def march_kernel(own, received, cells, start, w_forward, w_inverse, twiddle, spread, tilt, absorb, bins, section,
-                 totals, levels, arrived, wide, field, back, energy, power):
+def enter(field, columns, jl):
+    parts = dft4(columns, -1)
+    for ql in range(FOUR):
+        re, im = cmul_const(parts[ql], unit(ql * jl, ROWS))
+        field[0, ql * EIGHT + jl] = re
+        field[1, ql * EIGHT + jl] = im
+
+
+def joined(pieces):
+    re_high, re_low = split(jnp.concatenate([p[0] for p in pieces], axis=0))
+    im_high, im_low = split(jnp.concatenate([p[1] for p in pieces], axis=0))
+    return jnp.concatenate([re_high, im_high, re_low, im_low, re_high, im_high], axis=1)
+
+
+def weighted(left, weights):
+    return jnp.dot(left, jnp.concatenate([weights[0], weights[0], weights[1]]), preferred_element_type=F32)
+
+
+def spread_rows(table, wide):
+    for index in np.ndindex(table.shape[:-2]):
+        for row in range(table.shape[-2]):
+            place = (*index, row)
+            wide[place] = jnp.broadcast_to(table[(*index, pl.ds(row, 1))], (SUB, LANES))
+
+
+def parted(product):
+    return [(product[i * SUB : (i + 1) * SUB, :LANES], product[i * SUB : (i + 1) * SUB, LANES:]) for i in range(ROWS)]
+
+
+Q_ROWS = [ql + FOUR * qh for ql in range(FOUR) for qh in range(EIGHT)]
+
+
+def forward(field, w_forward, twiddle):
+    pieces = []
+    for ql in range(FOUR):
+        column = [(field[0, ql * EIGHT + jl], field[1, ql * EIGHT + jl]) for jl in range(EIGHT)]
+        for qh, (re, im) in enumerate(dft8(column, -1)):
+            q = ql + FOUR * qh
+            c, s = twiddle[0, q], twiddle[1, q]
+            pieces.append((re * c - im * s, re * s + im * c))
+    return weighted(joined(pieces), w_forward)
+
+
+def inverse(product, w_inverse, spread):
+    pieces = []
+    for q, (re, im) in zip(Q_ROWS, parted(product)):
+        c, s = spread[0, q], spread[1, q]
+        pieces.append((re * c - im * s, re * s + im * c))
+    return weighted(joined(pieces), w_inverse)
+
+
+def leave(back, product, twiddle):
+    pieces = []
+    for q, (re, im) in zip(Q_ROWS, parted(product)):
+        c, s = twiddle[0, q], twiddle[1, q]
+        pieces.append((re * c + im * s, im * c - re * s))
+    for ql in range(FOUR):
+        column = dft8(pieces[ql * EIGHT : (ql + 1) * EIGHT], 1)
+        for jl in range(EIGHT):
+            back[0, ql * EIGHT + jl] = column[jl][0]
+            back[1, ql * EIGHT + jl] = column[jl][1]
+
+
+def launch_kernel(start, w_forward, w_inverse, twiddle_table, spread_table, back, field, twiddle, spread):
+    spread_rows(twiddle_table, twiddle)
+    spread_rows(spread_table, spread)
+    for jl in range(EIGHT):
+        columns = []
+        for jh in range(FOUR):
+            j = EIGHT * jh + jl
+            columns.append(tuple(jnp.broadcast_to(start[k, j : j + 1, :], (SUB, LANES)) for k in range(2)))
+        enter(field, columns, jl)
+    product = inverse(forward(field, w_forward, twiddle), w_inverse, spread)
+    leave(back, product, twiddle)
+
+
+def launch(start, consts):
+    vmem = pl.BlockSpec(memory_space=pltpu.VMEM)
+    return pl.pallas_call(
+        launch_kernel,
+        out_shape=[jax.ShapeDtypeStruct((2, ROWS, SUB, LANES), F32)] * 2,
+        in_specs=[vmem] * 5,
+        out_specs=[vmem] * 2,
+        scratch_shapes=[pltpu.VMEM((2, ROWS, SUB, LANES), F32)] * 2,
+        compiler_params=pltpu.CompilerParams(vmem_limit_bytes=8 * 1024 * 1024),
+        cost_estimate=pl.CostEstimate(flops=1_000_000_000, bytes_accessed=1024 * 1024, transcendentals=0),
+        name="launch",
+    )(start, *consts[:4])
+
+
+def march_kernel(own, levels, cells, launched, entered, w_forward, w_inverse, *refs):
+    tables, (bins, section, totals, wide, field, back, energy, power), wide_tables = refs[:4], refs[4:12], refs[12:]
+    for table, place in zip(tables, wide_tables):
+        spread_rows(table, place)
+    twiddle, spread, tilt, absorb = wide_tables
     sine, cosine = phase_polynomials()
     sections, batch, steps, heights = levels.shape
     halves = batch // SUB
-    copy = pltpu.make_async_copy(received, levels, arrived)
-    copy.start()
     lane = lax.broadcasted_iota(jnp.int32, (SUB, LANES), 1)
     radial = lax.broadcasted_iota(jnp.int32, (SUB, LANES), 0)
     at_once = cells.shape[1] // 2
-
-    def enter(half, columns, jl):
-        parts = dft4(columns, -1)
-        for ql in range(FOUR):
-            re, im = cmul_const(parts[ql], unit(ql * jl, ROWS))
-            field[half, 0, ql * EIGHT + jl] = re
-            field[half, 1, ql * EIGHT + jl] = im
-
-    def joined(pieces):
-        re_high, re_low = split(jnp.concatenate([p[0] for p in pieces], axis=0))
-        im_high, im_low = split(jnp.concatenate([p[1] for p in pieces], axis=0))
-        return jnp.concatenate([re_high, im_high, re_low, im_low, re_high, im_high], axis=1)
-
-    def parted(product):
-        return [
-            (product[i * SUB : (i + 1) * SUB, :LANES], product[i * SUB : (i + 1) * SUB, LANES:]) for i in range(ROWS)
-        ]
-
-    rows = [ql + FOUR * qh for ql in range(FOUR) for qh in range(EIGHT)]
-
-    def forward(half):
-        pieces = []
-        for ql in range(FOUR):
-            column = [(field[half, 0, ql * EIGHT + jl], field[half, 1, ql * EIGHT + jl]) for jl in range(EIGHT)]
-            for qh, (re, im) in enumerate(dft8(column, -1)):
-                q = ql + FOUR * qh
-                c, s = twiddle[0, q : q + 1, :], twiddle[1, q : q + 1, :]
-                pieces.append((re * c - im * s, re * s + im * c))
-        return jnp.dot(joined(pieces), w_forward[...], preferred_element_type=F32)
-
-    def inverse(product):
-        pieces = []
-        for q, (re, im) in zip(rows, parted(product)):
-            c, s = spread[0, q : q + 1, :], spread[1, q : q + 1, :]
-            pieces.append((re * c - im * s, re * s + im * c))
-        return jnp.dot(joined(pieces), w_inverse[...], preferred_element_type=F32)
-
-    def leave(half, product):
-        pieces = []
-        for q, (re, im) in zip(rows, parted(product)):
-            c, s = twiddle[0, q : q + 1, :], twiddle[1, q : q + 1, :]
-            pieces.append((re * c + im * s, im * c - re * s))
-        for ql in range(FOUR):
-            column = dft8(pieces[ql * EIGHT : (ql + 1) * EIGHT], 1)
-            for jl in range(EIGHT):
-                back[half, 0, ql * EIGHT + jl] = column[jl][0]
-                back[half, 1, ql * EIGHT + jl] = column[jl][1]
 
     def rotate(half, t, ground, jls):
         for jl in jls:
@@ -205,7 +249,7 @@
             moved = []
             for jh in range(FOUR):
                 j = EIGHT * jh + jl
-                phi = wide[j, pl.ds(half * SUB * steps + t, SUB, stride=steps), :] + tilt[j : j + 1, :]
+                phi = wide[j, pl.ds(half * SUB * steps + t, SUB, stride=steps), :] + tilt[j]
                 u = phi * phi
                 sin_poly, cos_poly = sine[-1], cosine[-1]
                 for a, b in zip(sine[-2::-1], cosine[-2::-1]):
@@ -217,7 +261,7 @@
                 turned_s = double * (math.sqrt(2.0) - small * small)
                 re, im = column[jh]
                 if (j + 1) * LANES > 3 * H // 4:
-                    loss = absorb[j : j + 1, :]
+                    loss = absorb[j]
                     re, im = re * loss, im * loss
                 re, im = re * turned_c - im * turned_s, re * turned_s + im * turned_c
                 if j < TERRAIN_ROWS:
@@ -228,7 +272,7 @@
                 energy[half, j * SUB : (j + 1) * SUB, :LANES] = high
                 energy[half, j * SUB : (j + 1) * SUB, LANES:] = value - high
                 moved.append((re, im))
-            enter(half, moved, jl)
+            enter(field.at[half], moved, jl)
 
     def binned(half, t):
         summed = jnp.dot(energy[half].astype(BF16), bins[...], preferred_element_type=F32)
@@ -244,11 +288,11 @@
 
     def turn_of(t, resting, moving):
         ground = ground_of(resting, t)
-        product = forward(moving)
+        product = forward(field.at[moving], w_forward, twiddle)
         rotate(resting, t, ground, range(EIGHT // 2))
-        product = inverse(product)
+        product = inverse(product, w_inverse, spread)
         rotate(resting, t, ground, range(EIGHT // 2, EIGHT))
-        leave(moving, product)
+        leave(back.at[moving], product, twiddle)
         binned(resting, t)
 
     def step(t, carry):
@@ -256,16 +300,10 @@
             turn_of(t, half, (half + 1) % halves)
         return carry
 
+    power[...] = jnp.zeros_like(power)
     for half in range(halves):
-        for jl in range(EIGHT):
-            columns = []
-            for jh in range(FOUR):
-                j = EIGHT * jh + jl
-                columns.append(tuple(jnp.broadcast_to(start[k, j : j + 1, :], (SUB, LANES)) for k in range(2)))
-            enter(half, columns, jl)
-    power[...] = jnp.zeros_like(power)
-    leave(0, inverse(forward(0)))
-    copy.wait()
+        back[half] = launched[...]
+        field[half] = entered[...]
     per_source = heights // LANES
 
     def widen(source, carry):
@@ -303,7 +341,7 @@
     totals[...] = gain
 
 
-def march(section, received, cells, start, consts, tiles, own):
+def march(section, received, cells, launched, consts, tiles, own):
     sections, batch, steps, heights = received.shape
     halves = batch // SUB
     vmem = pl.BlockSpec(memory_space=pltpu.VMEM)
@@ -311,24 +349,22 @@
     call = pl.pallas_call(
         functools.partial(march_kernel, own),
         out_shape=jax.ShapeDtypeStruct((tiles, BINS), F32),
-        in_specs=[pl.BlockSpec(memory_space=pl.ANY)] + [vmem] * 9 + [smem],
+        in_specs=[vmem] * 11 + [smem],
         out_specs=vmem,
         scratch_shapes=[
-            pltpu.VMEM(received.shape, BF16),
-            pltpu.SemaphoreType.DMA,
             pltpu.VMEM((ROWS, batch * steps, LANES), F32),
             pltpu.VMEM((halves, 2, ROWS, SUB, LANES), F32),
             pltpu.VMEM((halves, 2, ROWS, SUB, LANES), F32),
             pltpu.VMEM((halves, ROWS * SUB, 2 * LANES), F32),
             pltpu.VMEM((-(-steps * batch // LANES) * LANES, BINS), F32),
-        ],
-        compiler_params=pltpu.CompilerParams(vmem_limit_bytes=44 * 1024 * 1024),
+        ] + [pltpu.VMEM((*table.shape[:-1], SUB, LANES), F32) for table in consts[2:6]],
+        compiler_params=pltpu.CompilerParams(vmem_limit_bytes=10 * 1024 * 1024 + 4 * H * batch * steps),
         cost_estimate=pl.CostEstimate(
             flops=steps * 1_600_000_000, bytes_accessed=4 * 1024 * 1024, transcendentals=0
         ),
         name="march",
     )
-    return call(received, cells, start, *consts, section)
+    return call(received, cells, *launched, *consts, section)
 
 
 def gather_small(value):
@@ -337,14 +373,9 @@
     pair = jnp.stack([jnp.where(radial == 0, value, other), jnp.where(radial == 0, other, value)])
     section = lax.axis_index("range")
     held = jnp.zeros((sections, *pair.shape), pair.dtype)
-    held = lax.dynamic_update_index_in_dim(held, pair, section, 0)
-    width = 1
-    while width < sections:
-        base = section // width * width
-        part = lax.dynamic_slice_in_dim(held, base, width, 0)
-        part = lax.ppermute(part, "range", [(i, i ^ width) for i in range(sections)])
-        held = lax.dynamic_update_slice_in_dim(held, part, base ^ width, 0)
-        width *= 2
+    for d in range(sections):
+        part = lax.ppermute(pair, "range", [(i, i ^ d) for i in range(sections)]) if d else pair
+        held = lax.dynamic_update_index_in_dim(held, part, section ^ d, 0)
     return held
 
 
@@ -361,10 +392,9 @@
     received = jnp.pad(received, ((0, 0), (0, batch - own), (0, 0), (0, 0)))
     everyone = gather_small(jnp.concatenate([terrain.T, tile_map.T]))
     cells = lax.dynamic_index_in_dim(everyone, lax.axis_index("radial"), 1, keepdims=False)
-    start = source.reshape(2, ROWS, LANES)
-    totals = march(
-        section, received, cells, start, [jnp.asarray(v) for v in tables()], TILE_DEV * owners, own
-    )
+    consts = [jnp.asarray(v) for v in tables()]
+    launched = launch(source.reshape(2, ROWS, LANES), consts)
+    totals = march(section, received, cells, launched, consts, TILE_DEV * owners, own)
 
     everyone, totals = lax.optimization_barrier((everyone, totals))
     sent = lax.all_to_all(

time: 93.7 us -> 93.5 us (level)
  waiting for transfers between devices: 49 us -> 42.5 us
  starting transfers between devices: 18.7 us -> 25.1 us
    ppermute x3 -> x7, starting transfers between devices: 7.4 us -> 14 us  [gather_small(): lax.ppermute(pair, 'range', [(i, i ^ d) for i in range(sections)])]
    ppermute x3 -> x7, waiting for transfers between devices: 40.2 us -> 34.4 us  [gather_small(): lax.ppermute(pair, 'range', [(i, i ^ d) for i in range(sections)])]
    pallas_call x1 -> x2, Pallas kernels: 24.5 us -> 24.3 us  [the longest x1 23.6 us: march(): return call(received, cells, *launched, *consts, section)]
  transfers between devices with their start and end apart: 6 -> 10, of which waited for: 5 -> 6; matrix products, arithmetic and copies ran while one was open for 0% -> 0% of each run, Pallas kernels for 0% -> 1%
where the time goes in v7:
time: 93.5 us; the launch traced here: 93.3 us
  waiting for transfers between devices  42.5 us (45%)
  starting transfers between devices  25.1 us (27%)
  Pallas kernels  24.3 us (26%)
  other arithmetic  0.95 us (1%)
    ppermute x7, waiting for transfers between devices, gather_small(): lax.ppermute(pair, 'range', [(i, i ^ d) for i in range(sections)])  34.4 us
    pallas_call x1, Pallas kernels, march(): return call(received, cells, *launched, *consts, section)  23.6 us
    ppermute x7, starting transfers between devices, gather_small(): lax.ppermute(pair, 'range', [(i, i ^ d) for i in range(sections)])  14 us
    all_to_all x1, waiting for transfers between devices, local(): lax.all_to_all(totals.reshape(owners, TILE_DEV, BINS), ('range', 'radial'...  7.68 us
    all_to_all x1, starting transfers between devices, local(): received = lax.all_to_all(received, 'range', 0, 0, tiled=True)  7.44 us
    all_to_all x1, starting transfers between devices, local(): lax.all_to_all(totals.reshape(owners, TILE_DEV, BINS), ('range', 'radial'...  3.66 us
  transfers between devices with their start and end apart: 10, of which 6 were waited for; matrix products, arithmetic and copies ran while one was open for 0% of the time, Pallas kernels for 1%

profile of v7, /device:TPU:0, one launch (start us, length us, event | category | flops | bytes accessed | tf_op | source)
XLA Modules:
  0.0 93.3 jit_solution(140555564870628003)
XLA Ops:
  0.0 0.0 copy-start.8
  0.0 0.0 copy-start.9
  0.0 0.0 copy-start.7
  0.0 0.0 copy-start
  0.0 0.0 copy-start.1
  0.0 0.0 copy-start.3
  0.0 0.0 copy-start.4
  0.0 7.4 %all-to-all-start = ((bf16[8,16,16,512]{3,2,1,0:T(8,128)(2,1)}), bf16[8,16,16,512]{3,2,1,0:T(8,128)(2,1)S(1)}, u32[]{:S(2)}, u32[]{:S(2)}) async-start(bf16[8,16,16,512]{3,2,1,0:T(8,128)(2,1)} %bitcast.33), calls=%async_computation | async-start | bytes 4194304 | tf_op jit(solution)/shard_map/all_to_all | solution.py:391
  7.5 0.0 copy-start.2
  7.5 0.0 copy-start.5
  7.5 0.0 copy-start.6
  7.5 0.0 copy-done.8
  7.5 0.0 copy-done.9
  7.5 0.1 collective-permute-start
  7.6 0.0 copy-done.7
  7.7 0.0 copy-done
  7.7 0.0 copy-done.1
  7.7 0.0 copy-done.3
  7.7 0.0 copy-done.4
  7.7 0.6 launch.1
  8.4 0.4 collective-permute-done
  8.8 3.9 %collective-permute-start.6 = (s32[2,4,128]{2,1,0:T(4,128)S(1)}, s32[2,4,128]{2,1,0:T(4,128)S(1)}, u32[]{:S(2)}, u32[]{:S(2)}) collective-permute-start(s32[2,4,128]{2,1,0:T(4,128)S(1)} %pad_add_fusion), channel_id=1, source_target_pairs={{0,12},{2,14},{4,8},{6,10},{8,4},{10,6},{12,0},{14,2},{1,13},{3,15... | collective-permute-start | bytes 12296 | tf_op jit(solution)/shard_map/ppermute | solution.py:377
  12.7 0.6 collective-permute-start.5
  13.2 3.3 %collective-permute-start.4 = (s32[2,4,128]{2,1,0:T(4,128)S(1)}, s32[2,4,128]{2,1,0:T(4,128)S(1)}, u32[]{:S(2)}, u32[]{:S(2)}) collective-permute-start(s32[2,4,128]{2,1,0:T(4,128)S(1)} %pad_add_fusion), channel_id=1, source_target_pairs={{0,8},{2,10},{4,12},{6,14},{8,0},{10,2},{12,4},{14,6},{1,9},{3,11}... | collective-permute-start | bytes 12296 | tf_op jit(solution)/shard_map/ppermute | solution.py:377
  16.5 0.0 collective-permute-start.3
  16.5 1.1 %collective-permute-start.1 = (s32[2,4,128]{2,1,0:T(4,128)S(1)}, s32[2,4,128]{2,1,0:T(4,128)S(1)}, u32[]{:S(2)}, u32[]{:S(2)}) collective-permute-start(s32[2,4,128]{2,1,0:T(4,128)S(1)} %pad_add_fusion), channel_id=1, source_target_pairs={{0,2},{2,0},{4,6},{6,4},{8,10},{10,8},{12,14},{14,12},{1,3},{3,1},... | collective-permute-start | bytes 12296 | tf_op jit(solution)/shard_map/ppermute | solution.py:377
  17.6 7.1 %collective-permute-done.1 = s32[2,4,128]{2,1,0:T(4,128)S(1)} collective-permute-done((s32[2,4,128]{2,1,0:T(4,128)S(1)}, s32[2,4,128]{2,1,0:T(4,128)S(1)}, u32[]{:S(2)}, u32[]{:S(2)}) %collective-permute-start.1) | collective-permute-done | bytes 4128 | tf_op jit(solution)/shard_map/ppermute | solution.py:377
  24.7 1.7 %collective-permute-start.2 = (s32[2,4,128]{2,1,0:T(4,128)S(1)}, s32[2,4,128]{2,1,0:T(4,128)S(1)}, u32[]{:S(2)}, u32[]{:S(2)}) collective-permute-start(s32[2,4,128]{2,1,0:T(4,128)S(1)} %pad_add_fusion), channel_id=1, source_target_pairs={{0,4},{2,6},{4,0},{6,2},{8,12},{10,14},{12,8},{14,10},{1,5},{3,7},... | collective-permute-start | bytes 12296 | tf_op jit(solution)/shard_map/ppermute | solution.py:377
  26.4 16.5 %collective-permute-done.2 = s32[2,4,128]{2,1,0:T(4,128)S(1)} collective-permute-done((s32[2,4,128]{2,1,0:T(4,128)S(1)}, s32[2,4,128]{2,1,0:T(4,128)S(1)}, u32[]{:S(2)}, u32[]{:S(2)}) %collective-permute-start.2) | collective-permute-done | bytes 4128 | tf_op jit(solution)/shard_map/ppermute | solution.py:377
  42.9 3.5 %collective-permute-start.7 = (s32[2,4,128]{2,1,0:T(4,128)S(1)}, s32[2,4,128]{2,1,0:T(4,128)S(1)}, u32[]{:S(2)}, u32[]{:S(2)}) collective-permute-start(s32[2,4,128]{2,1,0:T(4,128)S(1)} %pad_add_fusion), channel_id=1, source_target_pairs={{0,14},{2,12},{4,10},{6,8},{8,6},{10,4},{12,2},{14,0},{1,15},{3,13... | collective-permute-start | bytes 12296 | tf_op jit(solution)/shard_map/ppermute | solution.py:377
  46.4 0.0 collective-permute-done.3
  46.4 10.0 %collective-permute-done.4 = s32[2,4,128]{2,1,0:T(4,128)S(1)} collective-permute-done((s32[2,4,128]{2,1,0:T(4,128)S(1)}, s32[2,4,128]{2,1,0:T(4,128)S(1)}, u32[]{:S(2)}, u32[]{:S(2)}) %collective-permute-start.4) | collective-permute-done | bytes 4128 | tf_op jit(solution)/shard_map/ppermute | solution.py:377
  56.4 0.8 collective-permute-done.5
  57.2 0.0 collective-permute-done.6
  57.3 0.0 collective-permute-done.7
  57.3 0.0 all-to-all-done.levels
  57.3 0.0 copy-done.2
  57.3 0.0 copy-done.5
  57.3 0.0 copy-done.6
  57.3 23.6 %march.1 = f32[256,128]{1,0:T(8,128)} custom-call(bf16[8,16,16,512]{3,2,1,0:T(8,128)(2,1)S(1)} %all-to-all-done.levels, s32[8,4,128]{2,1,0:T(4,128)S(1)} %dynamic-slice_bitcast_fusion.cells, f32[2,32,8,128]{3,2,1,0:T(8,128)S(1)} %get-tuple-element.9.launched, f32[2,32,8,128]{3,2,1,0:T(8,128)S(1)} %get-tuple-element.10.entered, ...), custom_call_target="tpu_custom_call" | custom-call | flops 25600000000 | bytes 4194304 | tf_op jit(solution)/shard_map/march/pallas_call | solution.py:367
  81.0 3.7 %all-to-all-start.1 = ((f32[16,16,128]{2,1,0:T(8,128)}), f32[16,16,128]{2,1,0:T(8,128)S(1)}, u32[]{:S(2)}, u32[]{:S(2)}) async-start(f32[16,16,128]{2,1,0:T(8,128)} %bitcast.15), calls=%async_computation.1 | async-start | bytes 262144 | tf_op jit(solution)/shard_map/all_to_all | solution.py:400
  84.7 0.2 convert_reduce_fusion
  84.9 7.7 %all-to-all-done.1 = f32[16,16,128]{2,1,0:T(8,128)S(1)} async-done(((f32[16,16,128]{2,1,0:T(8,128)}), f32[16,16,128]{2,1,0:T(8,128)S(1)}, u32[]{:S(2)}, u32[]{:S(2)}) %all-to-all-start.1) | async-done | bytes 131104 | tf_op jit(solution)/shard_map/all_to_all | solution.py:400
  92.6 0.7 broadcast_divide_fusion
  (17 shorter events, 0.1 us)
Async XLA Ops:
  0.0 7.5 %copy-start.8 = (s32[128,2]{0,1:T(2,128)S(1)}, s32[128,2]{0,1:T(2,128)}, u32[]{:S(2)}) copy-start(s32[128,2]{0,1:T(2,128)} %param.14) | copy-start | bytes 3076
  0.0 7.5 %copy-start.9 = (s32[128,2]{0,1:T(2,128)S(1)}, s32[128,2]{0,1:T(2,128)}, u32[]{:S(2)}) copy-start(s32[128,2]{0,1:T(2,128)} %param.13) | copy-start | bytes 3076
  0.0 7.6 %copy-start.7 = (f32[2,4096]{1,0:T(2,128)S(1)}, f32[2,4096]{1,0:T(2,128)}, u32[]{:S(2)}) copy-start(f32[2,4096]{1,0:T(2,128)} %param.12) | copy-start | bytes 98308
  0.0 7.7 %copy-start = (bf16[2,256,256]{2,1,0:T(8,128)(2,1)S(1)}, bf16[2,256,256]{2,1,0:T(8,128)(2,1)}, u32[]{:S(2)}) copy-start(bf16[2,256,256]{2,1,0:T(8,128)(2,1)} %constant.67.clone.w_inverse) | copy-start | bytes 786436
  0.0 7.7 %copy-start.1 = (bf16[2,256,256]{2,1,0:T(8,128)(2,1)S(1)}, bf16[2,256,256]{2,1,0:T(8,128)(2,1)}, u32[]{:S(2)}) copy-start(bf16[2,256,256]{2,1,0:T(8,128)(2,1)} %constant.66.clone.w_forward) | copy-start | bytes 786436
  0.0 7.7 %copy-start.3 = (f32[2,32,128]{2,1,0:T(8,128)S(1)}, f32[2,32,128]{2,1,0:T(8,128)}, u32[]{:S(2)}) copy-start(f32[2,32,128]{2,1,0:T(8,128)} %constant.69.clone.spread_table.refs_1_) | copy-start | bytes 98308
  0.0 7.7 %copy-start.4 = (f32[2,32,128]{2,1,0:T(8,128)S(1)}, f32[2,32,128]{2,1,0:T(8,128)}, u32[]{:S(2)}) copy-start(f32[2,32,128]{2,1,0:T(8,128)} %constant.68.clone.twiddle_table.refs_0_) | copy-start | bytes 98308
  0.0 57.3 %all-to-all-start = ((bf16[8,16,16,512]{3,2,1,0:T(8,128)(2,1)}), bf16[8,16,16,512]{3,2,1,0:T(8,128)(2,1)S(1)}, u32[]{:S(2)}, u32[]{:S(2)}) async-start(bf16[8,16,16,512]{3,2,1,0:T(8,128)(2,1)} %bitcast.33), calls=%async_computation | async-start | bytes 4194304 | tf_op jit(solution)/shard_map/all_to_all | solution.py:391
  7.5 49.8 %copy-start.2 = (bf16[256,128]{1,0:T(8,128)(2,1)S(1)}, bf16[256,128]{1,0:T(8,128)(2,1)}, u32[]{:S(2)}) copy-start(bf16[256,128]{1,0:T(8,128)(2,1)} %constant.72.clone.refs_4_) | copy-start | bytes 196612
  7.5 49.8 %copy-start.5 = (f32[32,128]{1,0:T(8,128)S(1)}, f32[32,128]{1,0:T(8,128)}, u32[]{:S(2)}) copy-start(f32[32,128]{1,0:T(8,128)} %constant.71.clone.refs_3_) | copy-start | bytes 49156
  7.5 49.8 %copy-start.6 = (f32[32,128]{1,0:T(8,128)S(1)}, f32[32,128]{1,0:T(8,128)}, u32[]{:S(2)}) copy-start(f32[32,128]{1,0:T(8,128)} %constant.70.clone.refs_2_) | copy-start | bytes 49156
  7.5 1.2 %collective-permute-start = (s32[4,128]{1,0:T(4,128)S(1)}, s32[4,128]{1,0:T(4,128)S(1)}, u32[]{:S(2)}, u32[]{:S(2)}) collective-permute-start(s32[4,128]{1,0:T(4,128)S(1)} %pad_add_fusion.1), channel_id=1, source_target_pairs={{0,1},{1,0},{2,3},{3,2},{4,5},{5,4},{6,7},{7,6},{8,9},{9,8},{10,11... | collective-permute-start | bytes 6152 | tf_op jit(solution)/shard_map/ppermute | solution.py:372
  8.8 48.5 %collective-permute-start.6 = (s32[2,4,128]{2,1,0:T(4,128)S(1)}, s32[2,4,128]{2,1,0:T(4,128)S(1)}, u32[]{:S(2)}, u32[]{:S(2)}) collective-permute-start(s32[2,4,128]{2,1,0:T(4,128)S(1)} %pad_add_fusion), channel_id=1, source_target_pairs={{0,12},{2,14},{4,8},{6,10},{8,4},{10,6},{12,0},{14,2},{1,13},{3,15... | collective-permute-start | bytes 12296 | tf_op jit(solution)/shard_map/ppermute | solution.py:377
  12.7 44.6 %collective-permute-start.5 = (s32[2,4,128]{2,1,0:T(4,128)S(1)}, s32[2,4,128]{2,1,0:T(4,128)S(1)}, u32[]{:S(2)}, u32[]{:S(2)}) collective-permute-start(s32[2,4,128]{2,1,0:T(4,128)S(1)} %pad_add_fusion), channel_id=1, source_target_pairs={{0,10},{2,8},{4,14},{6,12},{8,2},{10,0},{12,6},{14,4},{1,11},{3,9}... | collective-permute-start | bytes 12296 | tf_op jit(solution)/shard_map/ppermute | solution.py:377
  13.2 43.2 %collective-permute-start.4 = (s32[2,4,128]{2,1,0:T(4,128)S(1)}, s32[2,4,128]{2,1,0:T(4,128)S(1)}, u32[]{:S(2)}, u32[]{:S(2)}) collective-permute-start(s32[2,4,128]{2,1,0:T(4,128)S(1)} %pad_add_fusion), channel_id=1, source_target_pairs={{0,8},{2,10},{4,12},{6,14},{8,0},{10,2},{12,4},{14,6},{1,9},{3,11}... | collective-permute-start | bytes 12296 | tf_op jit(solution)/shard_map/ppermute | solution.py:377
  16.5 29.9 %collective-permute-start.3 = (s32[2,4,128]{2,1,0:T(4,128)S(1)}, s32[2,4,128]{2,1,0:T(4,128)S(1)}, u32[]{:S(2)}, u32[]{:S(2)}) collective-permute-start(s32[2,4,128]{2,1,0:T(4,128)S(1)} %pad_add_fusion), channel_id=1, source_target_pairs={{0,6},{2,4},{4,2},{6,0},{8,14},{10,12},{12,10},{14,8},{1,7},{3,5},... | collective-permute-start | bytes 12296 | tf_op jit(solution)/shard_map/ppermute | solution.py:377
  16.5 8.2 %collective-permute-start.1 = (s32[2,4,128]{2,1,0:T(4,128)S(1)}, s32[2,4,128]{2,1,0:T(4,128)S(1)}, u32[]{:S(2)}, u32[]{:S(2)}) collective-permute-start(s32[2,4,128]{2,1,0:T(4,128)S(1)} %pad_add_fusion), channel_id=1, source_target_pairs={{0,2},{2,0},{4,6},{6,4},{8,10},{10,8},{12,14},{14,12},{1,3},{3,1},... | collective-permute-start | bytes 12296 | tf_op jit(solution)/shard_map/ppermute | solution.py:377
  24.7 18.2 %collective-permute-start.2 = (s32[2,4,128]{2,1,0:T(4,128)S(1)}, s32[2,4,128]{2,1,0:T(4,128)S(1)}, u32[]{:S(2)}, u32[]{:S(2)}) collective-permute-start(s32[2,4,128]{2,1,0:T(4,128)S(1)} %pad_add_fusion), channel_id=1, source_target_pairs={{0,4},{2,6},{4,0},{6,2},{8,12},{10,14},{12,8},{14,10},{1,5},{3,7},... | collective-permute-start | bytes 12296 | tf_op jit(solution)/shard_map/ppermute | solution.py:377
  42.9 14.4 %collective-permute-start.7 = (s32[2,4,128]{2,1,0:T(4,128)S(1)}, s32[2,4,128]{2,1,0:T(4,128)S(1)}, u32[]{:S(2)}, u32[]{:S(2)}) collective-permute-start(s32[2,4,128]{2,1,0:T(4,128)S(1)} %pad_add_fusion), channel_id=1, source_target_pairs={{0,14},{2,12},{4,10},{6,8},{8,6},{10,4},{12,2},{14,0},{1,15},{3,13... | collective-permute-start | bytes 12296 | tf_op jit(solution)/shard_map/ppermute | solution.py:377
  81.0 11.6 %all-to-all-start.1 = ((f32[16,16,128]{2,1,0:T(8,128)}), f32[16,16,128]{2,1,0:T(8,128)S(1)}, u32[]{:S(2)}, u32[]{:S(2)}) async-start(f32[16,16,128]{2,1,0:T(8,128)} %bitcast.15), calls=%async_computation.1 | async-start | bytes 262144 | tf_op jit(solution)/shard_map/all_to_all | solution.py:400

commit v8 on v7

--- a/solution.py
+++ b/solution.py
@@ -146,11 +146,18 @@
 def joined(pieces):
     re_high, re_low = split(jnp.concatenate([p[0] for p in pieces], axis=0))
     im_high, im_low = split(jnp.concatenate([p[1] for p in pieces], axis=0))
-    return jnp.concatenate([re_high, im_high, re_low, im_low, re_high, im_high], axis=1)
-
-
-def weighted(left, weights):
-    return jnp.dot(left, jnp.concatenate([weights[0], weights[0], weights[1]]), preferred_element_type=F32)
+    return jnp.concatenate([re_high, im_high], axis=1), jnp.concatenate([re_low, im_low], axis=1)
+
+
+def weighted(left, weights, between=()):
+    high, low = left
+    between = list(between) + [lambda: None] * 3
+    total = None
+    for part, weight in ((high, weights[0]), (low, weights[0]), (high, weights[1])):
+        product = jnp.dot(part, weight, preferred_element_type=F32)
+        between.pop(0)()
+        total = product if total is None else total + product
+    return total
 
 
 def spread_rows(table, wide):
@@ -167,7 +174,7 @@
 Q_ROWS = [ql + FOUR * qh for ql in range(FOUR) for qh in range(EIGHT)]
 
 
-def forward(field, w_forward, twiddle):
+def forward(field, w_forward, twiddle, between=()):
     pieces = []
     for ql in range(FOUR):
         column = [(field[0, ql * EIGHT + jl], field[1, ql * EIGHT + jl]) for jl in range(EIGHT)]
@@ -175,15 +182,15 @@
             q = ql + FOUR * qh
             c, s = twiddle[0, q], twiddle[1, q]
             pieces.append((re * c - im * s, re * s + im * c))
-    return weighted(joined(pieces), w_forward)
-
-
-def inverse(product, w_inverse, spread):
+    return weighted(joined(pieces), w_forward, between)
+
+
+def inverse(product, w_inverse, spread, between=()):
     pieces = []
     for q, (re, im) in zip(Q_ROWS, parted(product)):
         c, s = spread[0, q], spread[1, q]
         pieces.append((re * c - im * s, re * s + im * c))
-    return weighted(joined(pieces), w_inverse)
+    return weighted(joined(pieces), w_inverse, between)
 
 
 def leave(back, product, twiddle):
@@ -288,12 +295,13 @@
 
     def turn_of(t, resting, moving):
         ground = ground_of(resting, t)
-        product = forward(field.at[moving], w_forward, twiddle)
-        rotate(resting, t, ground, range(EIGHT // 2))
-        product = inverse(product, w_inverse, spread)
-        rotate(resting, t, ground, range(EIGHT // 2, EIGHT))
+        pieces = [functools.partial(rotate, resting, t, ground, [jl]) for jl in range(EIGHT)]
+        product = forward(field.at[moving], w_forward, twiddle, pieces[:3])
+        binned(moving, jnp.maximum(t - 1, 0) if resting == 0 else t)
+        product = inverse(product, w_inverse, spread, pieces[3:6])
+        for piece in pieces[6:]:
+            piece()
         leave(back.at[moving], product, twiddle)
-        binned(resting, t)
 
     def step(t, carry):
         for half in range(halves):
@@ -314,7 +322,9 @@
         return carry
 
     lax.fori_loop(0, sections, widen, 0)
+    energy[...] = jnp.zeros_like(energy)
     lax.fori_loop(0, steps, step, 0)
+    binned(halves - 1, steps - 1)
 
     lane = lax.broadcasted_iota(jnp.int32, (1, LANES), 1)
     fit = LANES // batch

time: 93.5 us -> 92.4 us (0.988)
  Pallas kernels: 24.3 us -> 23.2 us
    pallas_call x1, Pallas kernels: 23.6 us -> 22.5 us  [march(): return call(received, cells, *launched, *consts, section)]
where the time goes in v8:
time: 92.4 us; the launch traced here: 92.1 us
  waiting for transfers between devices  42.5 us (46%)
  starting transfers between devices  25.1 us (27%)
  Pallas kernels  23.2 us (25%)
  other arithmetic  0.95 us (1%)
    ppermute x7, waiting for transfers between devices, gather_small(): lax.ppermute(pair, 'range', [(i, i ^ d) for i in range(sections)])  34.4 us
    pallas_call x1, Pallas kernels, march(): return call(received, cells, *launched, *consts, section)  22.5 us
    ppermute x7, starting transfers between devices, gather_small(): lax.ppermute(pair, 'range', [(i, i ^ d) for i in range(sections)])  14 us
    all_to_all x1, waiting for transfers between devices, local(): lax.all_to_all(totals.reshape(owners, TILE_DEV, BINS), ('range', 'radial'...  7.68 us
    all_to_all x1, starting transfers between devices, local(): received = lax.all_to_all(received, 'range', 0, 0, tiled=True)  7.44 us
    all_to_all x1, starting transfers between devices, local(): lax.all_to_all(totals.reshape(owners, TILE_DEV, BINS), ('range', 'radial'...  3.66 us
  transfers between devices with their start and end apart: 10, of which 6 were waited for; matrix products, arithmetic and copies ran while one was open for 0% of the time, Pallas kernels for 1%

profile of v8, /device:TPU:0, one launch (start us, length us, event | category | flops | bytes accessed | tf_op | source)
XLA Modules:
  0.0 92.1 jit_solution(14390407177025230496)
XLA Ops:
  0.0 0.0 copy-start.8
  0.0 0.0 copy-start.9
  0.0 0.0 copy-start.7
  0.0 0.0 copy-start
  0.0 0.0 copy-start.1
  0.0 0.0 copy-start.3
  0.0 0.0 copy-start.4
  0.0 7.4 %all-to-all-start = ((bf16[8,16,16,512]{3,2,1,0:T(8,128)(2,1)}), bf16[8,16,16,512]{3,2,1,0:T(8,128)(2,1)S(1)}, u32[]{:S(2)}, u32[]{:S(2)}) async-start(bf16[8,16,16,512]{3,2,1,0:T(8,128)(2,1)} %bitcast.33), calls=%async_computation | async-start | bytes 4194304 | tf_op jit(solution)/shard_map/all_to_all | solution.py:401
  7.5 0.0 copy-start.2
  7.5 0.0 copy-start.5
  7.5 0.0 copy-start.6
  7.5 0.0 copy-done.8
  7.5 0.0 copy-done.9
  7.5 0.1 collective-permute-start
  7.6 0.0 copy-done.7
  7.7 0.0 copy-done
  7.7 0.0 copy-done.1
  7.7 0.0 copy-done.3
  7.7 0.0 copy-done.4
  7.7 0.7 launch.1
  8.4 0.4 collective-permute-done
  8.8 3.9 %collective-permute-start.6 = (s32[2,4,128]{2,1,0:T(4,128)S(1)}, s32[2,4,128]{2,1,0:T(4,128)S(1)}, u32[]{:S(2)}, u32[]{:S(2)}) collective-permute-start(s32[2,4,128]{2,1,0:T(4,128)S(1)} %pad_add_fusion), channel_id=1, source_target_pairs={{0,12},{2,14},{4,8},{6,10},{8,4},{10,6},{12,0},{14,2},{1,13},{3,15... | collective-permute-start | bytes 12296 | tf_op jit(solution)/shard_map/ppermute | solution.py:387
  12.7 0.6 collective-permute-start.5
  13.2 3.3 %collective-permute-start.4 = (s32[2,4,128]{2,1,0:T(4,128)S(1)}, s32[2,4,128]{2,1,0:T(4,128)S(1)}, u32[]{:S(2)}, u32[]{:S(2)}) collective-permute-start(s32[2,4,128]{2,1,0:T(4,128)S(1)} %pad_add_fusion), channel_id=1, source_target_pairs={{0,8},{2,10},{4,12},{6,14},{8,0},{10,2},{12,4},{14,6},{1,9},{3,11}... | collective-permute-start | bytes 12296 | tf_op jit(solution)/shard_map/ppermute | solution.py:387
  16.5 0.0 collective-permute-start.3
  16.5 1.1 %collective-permute-start.1 = (s32[2,4,128]{2,1,0:T(4,128)S(1)}, s32[2,4,128]{2,1,0:T(4,128)S(1)}, u32[]{:S(2)}, u32[]{:S(2)}) collective-permute-start(s32[2,4,128]{2,1,0:T(4,128)S(1)} %pad_add_fusion), channel_id=1, source_target_pairs={{0,2},{2,0},{4,6},{6,4},{8,10},{10,8},{12,14},{14,12},{1,3},{3,1},... | collective-permute-start | bytes 12296 | tf_op jit(solution)/shard_map/ppermute | solution.py:387
  17.6 7.1 %collective-permute-done.1 = s32[2,4,128]{2,1,0:T(4,128)S(1)} collective-permute-done((s32[2,4,128]{2,1,0:T(4,128)S(1)}, s32[2,4,128]{2,1,0:T(4,128)S(1)}, u32[]{:S(2)}, u32[]{:S(2)}) %collective-permute-start.1) | collective-permute-done | bytes 4128 | tf_op jit(solution)/shard_map/ppermute | solution.py:387
  24.7 1.7 %collective-permute-start.2 = (s32[2,4,128]{2,1,0:T(4,128)S(1)}, s32[2,4,128]{2,1,0:T(4,128)S(1)}, u32[]{:S(2)}, u32[]{:S(2)}) collective-permute-start(s32[2,4,128]{2,1,0:T(4,128)S(1)} %pad_add_fusion), channel_id=1, source_target_pairs={{0,4},{2,6},{4,0},{6,2},{8,12},{10,14},{12,8},{14,10},{1,5},{3,7},... | collective-permute-start | bytes 12296 | tf_op jit(solution)/shard_map/ppermute | solution.py:387
  26.4 16.5 %collective-permute-done.2 = s32[2,4,128]{2,1,0:T(4,128)S(1)} collective-permute-done((s32[2,4,128]{2,1,0:T(4,128)S(1)}, s32[2,4,128]{2,1,0:T(4,128)S(1)}, u32[]{:S(2)}, u32[]{:S(2)}) %collective-permute-start.2) | collective-permute-done | bytes 4128 | tf_op jit(solution)/shard_map/ppermute | solution.py:387
  42.9 3.5 %collective-permute-start.7 = (s32[2,4,128]{2,1,0:T(4,128)S(1)}, s32[2,4,128]{2,1,0:T(4,128)S(1)}, u32[]{:S(2)}, u32[]{:S(2)}) collective-permute-start(s32[2,4,128]{2,1,0:T(4,128)S(1)} %pad_add_fusion), channel_id=1, source_target_pairs={{0,14},{2,12},{4,10},{6,8},{8,6},{10,4},{12,2},{14,0},{1,15},{3,13... | collective-permute-start | bytes 12296 | tf_op jit(solution)/shard_map/ppermute | solution.py:387
  46.4 0.0 collective-permute-done.3
  46.4 10.0 %collective-permute-done.4 = s32[2,4,128]{2,1,0:T(4,128)S(1)} collective-permute-done((s32[2,4,128]{2,1,0:T(4,128)S(1)}, s32[2,4,128]{2,1,0:T(4,128)S(1)}, u32[]{:S(2)}, u32[]{:S(2)}) %collective-permute-start.4) | collective-permute-done | bytes 4128 | tf_op jit(solution)/shard_map/ppermute | solution.py:387
  56.4 0.8 collective-permute-done.5
  57.2 0.0 collective-permute-done.6
  57.3 0.0 collective-permute-done.7
  57.3 0.0 all-to-all-done.levels
  57.3 0.0 copy-done.2
  57.3 0.0 copy-done.5
  57.3 0.0 copy-done.6
  57.3 22.5 %march.1 = f32[256,128]{1,0:T(8,128)} custom-call(bf16[8,16,16,512]{3,2,1,0:T(8,128)(2,1)S(1)} %all-to-all-done.levels, s32[8,4,128]{2,1,0:T(4,128)S(1)} %dynamic-slice_bitcast_fusion.cells, f32[2,32,8,128]{3,2,1,0:T(8,128)S(1)} %get-tuple-element.9.launched, f32[2,32,8,128]{3,2,1,0:T(8,128)S(1)} %get-tuple-element.10.entered, ...), custom_call_target="tpu_custom_call" | custom-call | flops 25600000000 | bytes 4194304 | tf_op jit(solution)/shard_map/march/pallas_call | solution.py:377
  79.8 3.7 %all-to-all-start.1 = ((f32[16,16,128]{2,1,0:T(8,128)}), f32[16,16,128]{2,1,0:T(8,128)S(1)}, u32[]{:S(2)}, u32[]{:S(2)}) async-start(f32[16,16,128]{2,1,0:T(8,128)} %bitcast.15), calls=%async_computation.1 | async-start | bytes 262144 | tf_op jit(solution)/shard_map/all_to_all | solution.py:410
  83.5 0.2 convert_reduce_fusion
  83.8 7.7 %all-to-all-done.1 = f32[16,16,128]{2,1,0:T(8,128)S(1)} async-done(((f32[16,16,128]{2,1,0:T(8,128)}), f32[16,16,128]{2,1,0:T(8,128)S(1)}, u32[]{:S(2)}, u32[]{:S(2)}) %all-to-all-start.1) | async-done | bytes 131104 | tf_op jit(solution)/shard_map/all_to_all | solution.py:410
  91.5 0.7 broadcast_divide_fusion
  (17 shorter events, 0.1 us)
Async XLA Ops:
  0.0 7.5 %copy-start.8 = (s32[128,2]{0,1:T(2,128)S(1)}, s32[128,2]{0,1:T(2,128)}, u32[]{:S(2)}) copy-start(s32[128,2]{0,1:T(2,128)} %param.14) | copy-start | bytes 3076
  0.0 7.5 %copy-start.9 = (s32[128,2]{0,1:T(2,128)S(1)}, s32[128,2]{0,1:T(2,128)}, u32[]{:S(2)}) copy-start(s32[128,2]{0,1:T(2,128)} %param.13) | copy-start | bytes 3076
  0.0 7.6 %copy-start.7 = (f32[2,4096]{1,0:T(2,128)S(1)}, f32[2,4096]{1,0:T(2,128)}, u32[]{:S(2)}) copy-start(f32[2,4096]{1,0:T(2,128)} %param.12) | copy-start | bytes 98308
  0.0 7.7 %copy-start = (bf16[2,256,256]{2,1,0:T(8,128)(2,1)S(1)}, bf16[2,256,256]{2,1,0:T(8,128)(2,1)}, u32[]{:S(2)}) copy-start(bf16[2,256,256]{2,1,0:T(8,128)(2,1)} %constant.67.clone.w_inverse) | copy-start | bytes 786436
  0.0 7.7 %copy-start.1 = (bf16[2,256,256]{2,1,0:T(8,128)(2,1)S(1)}, bf16[2,256,256]{2,1,0:T(8,128)(2,1)}, u32[]{:S(2)}) copy-start(bf16[2,256,256]{2,1,0:T(8,128)(2,1)} %constant.66.clone.w_forward) | copy-start | bytes 786436
  0.0 7.7 %copy-start.3 = (f32[2,32,128]{2,1,0:T(8,128)S(1)}, f32[2,32,128]{2,1,0:T(8,128)}, u32[]{:S(2)}) copy-start(f32[2,32,128]{2,1,0:T(8,128)} %constant.69.clone.spread_table.refs_1_) | copy-start | bytes 98308
  0.0 7.7 %copy-start.4 = (f32[2,32,128]{2,1,0:T(8,128)S(1)}, f32[2,32,128]{2,1,0:T(8,128)}, u32[]{:S(2)}) copy-start(f32[2,32,128]{2,1,0:T(8,128)} %constant.68.clone.twiddle_table.refs_0_) | copy-start | bytes 98308
  0.0 57.3 %all-to-all-start = ((bf16[8,16,16,512]{3,2,1,0:T(8,128)(2,1)}), bf16[8,16,16,512]{3,2,1,0:T(8,128)(2,1)S(1)}, u32[]{:S(2)}, u32[]{:S(2)}) async-start(bf16[8,16,16,512]{3,2,1,0:T(8,128)(2,1)} %bitcast.33), calls=%async_computation | async-start | bytes 4194304 | tf_op jit(solution)/shard_map/all_to_all | solution.py:401
  7.5 49.8 %copy-start.2 = (bf16[256,128]{1,0:T(8,128)(2,1)S(1)}, bf16[256,128]{1,0:T(8,128)(2,1)}, u32[]{:S(2)}) copy-start(bf16[256,128]{1,0:T(8,128)(2,1)} %constant.72.clone.refs_4_) | copy-start | bytes 196612
  7.5 49.8 %copy-start.5 = (f32[32,128]{1,0:T(8,128)S(1)}, f32[32,128]{1,0:T(8,128)}, u32[]{:S(2)}) copy-start(f32[32,128]{1,0:T(8,128)} %constant.71.clone.refs_3_) | copy-start | bytes 49156
  7.5 49.8 %copy-start.6 = (f32[32,128]{1,0:T(8,128)S(1)}, f32[32,128]{1,0:T(8,128)}, u32[]{:S(2)}) copy-start(f32[32,128]{1,0:T(8,128)} %constant.70.clone.refs_2_) | copy-start | bytes 49156
  7.5 1.2 %collective-permute-start = (s32[4,128]{1,0:T(4,128)S(1)}, s32[4,128]{1,0:T(4,128)S(1)}, u32[]{:S(2)}, u32[]{:S(2)}) collective-permute-start(s32[4,128]{1,0:T(4,128)S(1)} %pad_add_fusion.1), channel_id=1, source_target_pairs={{0,1},{1,0},{2,3},{3,2},{4,5},{5,4},{6,7},{7,6},{8,9},{9,8},{10,11... | collective-permute-start | bytes 6152 | tf_op jit(solution)/shard_map/ppermute | solution.py:382
  8.8 48.5 %collective-permute-start.6 = (s32[2,4,128]{2,1,0:T(4,128)S(1)}, s32[2,4,128]{2,1,0:T(4,128)S(1)}, u32[]{:S(2)}, u32[]{:S(2)}) collective-permute-start(s32[2,4,128]{2,1,0:T(4,128)S(1)} %pad_add_fusion), channel_id=1, source_target_pairs={{0,12},{2,14},{4,8},{6,10},{8,4},{10,6},{12,0},{14,2},{1,13},{3,15... | collective-permute-start | bytes 12296 | tf_op jit(solution)/shard_map/ppermute | solution.py:387
  12.7 44.6 %collective-permute-start.5 = (s32[2,4,128]{2,1,0:T(4,128)S(1)}, s32[2,4,128]{2,1,0:T(4,128)S(1)}, u32[]{:S(2)}, u32[]{:S(2)}) collective-permute-start(s32[2,4,128]{2,1,0:T(4,128)S(1)} %pad_add_fusion), channel_id=1, source_target_pairs={{0,10},{2,8},{4,14},{6,12},{8,2},{10,0},{12,6},{14,4},{1,11},{3,9}... | collective-permute-start | bytes 12296 | tf_op jit(solution)/shard_map/ppermute | solution.py:387
  13.2 43.2 %collective-permute-start.4 = (s32[2,4,128]{2,1,0:T(4,128)S(1)}, s32[2,4,128]{2,1,0:T(4,128)S(1)}, u32[]{:S(2)}, u32[]{:S(2)}) collective-permute-start(s32[2,4,128]{2,1,0:T(4,128)S(1)} %pad_add_fusion), channel_id=1, source_target_pairs={{0,8},{2,10},{4,12},{6,14},{8,0},{10,2},{12,4},{14,6},{1,9},{3,11}... | collective-permute-start | bytes 12296 | tf_op jit(solution)/shard_map/ppermute | solution.py:387
  16.5 29.9 %collective-permute-start.3 = (s32[2,4,128]{2,1,0:T(4,128)S(1)}, s32[2,4,128]{2,1,0:T(4,128)S(1)}, u32[]{:S(2)}, u32[]{:S(2)}) collective-permute-start(s32[2,4,128]{2,1,0:T(4,128)S(1)} %pad_add_fusion), channel_id=1, source_target_pairs={{0,6},{2,4},{4,2},{6,0},{8,14},{10,12},{12,10},{14,8},{1,7},{3,5},... | collective-permute-start | bytes 12296 | tf_op jit(solution)/shard_map/ppermute | solution.py:387
  16.5 8.2 %collective-permute-start.1 = (s32[2,4,128]{2,1,0:T(4,128)S(1)}, s32[2,4,128]{2,1,0:T(4,128)S(1)}, u32[]{:S(2)}, u32[]{:S(2)}) collective-permute-start(s32[2,4,128]{2,1,0:T(4,128)S(1)} %pad_add_fusion), channel_id=1, source_target_pairs={{0,2},{2,0},{4,6},{6,4},{8,10},{10,8},{12,14},{14,12},{1,3},{3,1},... | collective-permute-start | bytes 12296 | tf_op jit(solution)/shard_map/ppermute | solution.py:387
  24.7 18.2 %collective-permute-start.2 = (s32[2,4,128]{2,1,0:T(4,128)S(1)}, s32[2,4,128]{2,1,0:T(4,128)S(1)}, u32[]{:S(2)}, u32[]{:S(2)}) collective-permute-start(s32[2,4,128]{2,1,0:T(4,128)S(1)} %pad_add_fusion), channel_id=1, source_target_pairs={{0,4},{2,6},{4,0},{6,2},{8,12},{10,14},{12,8},{14,10},{1,5},{3,7},... | collective-permute-start | bytes 12296 | tf_op jit(solution)/shard_map/ppermute | solution.py:387
  42.9 14.4 %collective-permute-start.7 = (s32[2,4,128]{2,1,0:T(4,128)S(1)}, s32[2,4,128]{2,1,0:T(4,128)S(1)}, u32[]{:S(2)}, u32[]{:S(2)}) collective-permute-start(s32[2,4,128]{2,1,0:T(4,128)S(1)} %pad_add_fusion), channel_id=1, source_target_pairs={{0,14},{2,12},{4,10},{6,8},{8,6},{10,4},{12,2},{14,0},{1,15},{3,13... | collective-permute-start | bytes 12296 | tf_op jit(solution)/shard_map/ppermute | solution.py:387
  79.8 11.6 %all-to-all-start.1 = ((f32[16,16,128]{2,1,0:T(8,128)}), f32[16,16,128]{2,1,0:T(8,128)S(1)}, u32[]{:S(2)}, u32[]{:S(2)}) async-start(f32[16,16,128]{2,1,0:T(8,128)} %bitcast.15), calls=%async_computation.1 | async-start | bytes 262144 | tf_op jit(solution)/shard_map/all_to_all | solution.py:410

commit v9 on v7

--- a/solution.py
+++ b/solution.py
@@ -43,7 +43,7 @@
     weights = []
     for matrix in (forward, inverse):
         high, low = split_np(matrix)
-        weights.append(np.stack([high, low]))
+        weights.append(np.concatenate([high, low], axis=1))
     q = np.arange(ROWS)
     angle = -2.0 * np.pi / H * (q[:, None] * n[None, :])
     twiddle = np.stack([np.cos(angle), np.sin(angle)]).astype(np.float32)
@@ -146,11 +146,16 @@
 def joined(pieces):
     re_high, re_low = split(jnp.concatenate([p[0] for p in pieces], axis=0))
     im_high, im_low = split(jnp.concatenate([p[1] for p in pieces], axis=0))
-    return jnp.concatenate([re_high, im_high, re_low, im_low, re_high, im_high], axis=1)
+    return jnp.concatenate(
+        [jnp.concatenate([re_high, im_high], axis=1), jnp.concatenate([re_low, im_low], axis=1)], axis=0
+    )
 
 
 def weighted(left, weights):
-    return jnp.dot(left, jnp.concatenate([weights[0], weights[0], weights[1]]), preferred_element_type=F32)
+    product = jnp.dot(left, weights[...], preferred_element_type=F32)
+    rows, width = left.shape[0] // 2, weights.shape[1] // 2
+    high, low = product[:rows], product[rows:]
+    return high[:, :width] + (high[:, width:] + low[:, :width]) + low[:, width:]
 
 
 def spread_rows(table, wide):
@@ -288,12 +293,15 @@
 
     def turn_of(t, resting, moving):
         ground = ground_of(resting, t)
+        pieces = [functools.partial(rotate, resting, t, ground, [jl]) for jl in range(EIGHT)]
         product = forward(field.at[moving], w_forward, twiddle)
-        rotate(resting, t, ground, range(EIGHT // 2))
+        for piece in pieces[: EIGHT // 2]:
+            piece()
+        binned(moving, jnp.maximum(t - 1, 0) if resting == 0 else t)
         product = inverse(product, w_inverse, spread)
-        rotate(resting, t, ground, range(EIGHT // 2, EIGHT))
+        for piece in pieces[EIGHT // 2 :]:
+            piece()
         leave(back.at[moving], product, twiddle)
-        binned(resting, t)
 
     def step(t, carry):
         for half in range(halves):
@@ -314,7 +322,9 @@
         return carry
 
     lax.fori_loop(0, sections, widen, 0)
+    energy[...] = jnp.zeros_like(energy)
     lax.fori_loop(0, steps, step, 0)
+    binned(halves - 1, steps - 1)
 
     lane = lax.broadcasted_iota(jnp.int32, (1, LANES), 1)
     fit = LANES // batch

time: 93.5 us -> 97.7 us (1.045)
  Pallas kernels: 24.3 us -> 28.6 us
    pallas_call x1, Pallas kernels: 23.6 us -> 27.8 us  [march(): return call(received, cells, *launched, *consts, section)]
where the time goes in v9:
time: 97.7 us; the launch traced here: 97.4 us
  waiting for transfers between devices  42.4 us (43%)
  Pallas kernels  28.6 us (29%)
  starting transfers between devices  25.1 us (26%)
    ppermute x7, waiting for transfers between devices, gather_small(): lax.ppermute(pair, 'range', [(i, i ^ d) for i in range(sections)])  34.4 us
    pallas_call x1, Pallas kernels, march(): return call(received, cells, *launched, *consts, section)  27.8 us
    ppermute x7, starting transfers between devices, gather_small(): lax.ppermute(pair, 'range', [(i, i ^ d) for i in range(sections)])  14 us
    all_to_all x1, waiting for transfers between devices, local(): lax.all_to_all(totals.reshape(owners, TILE_DEV, BINS), ('range', 'radial'...  7.68 us
    all_to_all x1, starting transfers between devices, local(): received = lax.all_to_all(received, 'range', 0, 0, tiled=True)  7.44 us
    all_to_all x1, starting transfers between devices, local(): lax.all_to_all(totals.reshape(owners, TILE_DEV, BINS), ('range', 'radial'...  3.66 us
  transfers between devices with their start and end apart: 10, of which 6 were waited for; matrix products, arithmetic and copies ran while one was open for 0% of the time, Pallas kernels for 1%

profile of v9, /device:TPU:0, one launch (start us, length us, event | category | flops | bytes accessed | tf_op | source)
XLA Modules:
  0.0 97.4 jit_solution(16690556313643237161)
XLA Ops:
  0.0 0.0 copy-start.8
  0.0 0.0 copy-start.9
  0.0 0.0 copy-start.7
  0.0 0.0 copy-start
  0.0 0.0 copy-start.1
  0.0 0.0 copy-start.3
  0.0 0.0 copy-start.4
  0.0 7.4 %all-to-all-start = ((bf16[8,16,16,512]{3,2,1,0:T(8,128)(2,1)}), bf16[8,16,16,512]{3,2,1,0:T(8,128)(2,1)S(1)}, u32[]{:S(2)}, u32[]{:S(2)}) async-start(bf16[8,16,16,512]{3,2,1,0:T(8,128)(2,1)} %bitcast.33), calls=%async_computation | async-start | bytes 4194304 | tf_op jit(solution)/shard_map/all_to_all | solution.py:401
  7.5 0.0 copy-start.2
  7.5 0.0 copy-start.5
  7.5 0.0 copy-start.6
  7.5 0.0 copy-done.8
  7.5 0.0 copy-done.9
  7.5 0.1 collective-permute-start
  7.6 0.0 copy-done.7
  7.7 0.0 copy-done
  7.7 0.0 copy-done.1
  7.7 0.0 copy-done.3
  7.7 0.0 copy-done.4
  7.7 0.8 launch.1
  8.5 0.2 collective-permute-done
  8.8 3.9 %collective-permute-start.6 = (s32[2,4,128]{2,1,0:T(4,128)S(1)}, s32[2,4,128]{2,1,0:T(4,128)S(1)}, u32[]{:S(2)}, u32[]{:S(2)}) collective-permute-start(s32[2,4,128]{2,1,0:T(4,128)S(1)} %pad_add_fusion), channel_id=1, source_target_pairs={{0,12},{2,14},{4,8},{6,10},{8,4},{10,6},{12,0},{14,2},{1,13},{3,15... | collective-permute-start | bytes 12296 | tf_op jit(solution)/shard_map/ppermute | solution.py:387
  12.7 0.6 collective-permute-start.5
  13.2 3.3 %collective-permute-start.4 = (s32[2,4,128]{2,1,0:T(4,128)S(1)}, s32[2,4,128]{2,1,0:T(4,128)S(1)}, u32[]{:S(2)}, u32[]{:S(2)}) collective-permute-start(s32[2,4,128]{2,1,0:T(4,128)S(1)} %pad_add_fusion), channel_id=1, source_target_pairs={{0,8},{2,10},{4,12},{6,14},{8,0},{10,2},{12,4},{14,6},{1,9},{3,11}... | collective-permute-start | bytes 12296 | tf_op jit(solution)/shard_map/ppermute | solution.py:387
  16.5 0.0 collective-permute-start.3
  16.5 1.1 %collective-permute-start.1 = (s32[2,4,128]{2,1,0:T(4,128)S(1)}, s32[2,4,128]{2,1,0:T(4,128)S(1)}, u32[]{:S(2)}, u32[]{:S(2)}) collective-permute-start(s32[2,4,128]{2,1,0:T(4,128)S(1)} %pad_add_fusion), channel_id=1, source_target_pairs={{0,2},{2,0},{4,6},{6,4},{8,10},{10,8},{12,14},{14,12},{1,3},{3,1},... | collective-permute-start | bytes 12296 | tf_op jit(solution)/shard_map/ppermute | solution.py:387
  17.6 7.1 %collective-permute-done.1 = s32[2,4,128]{2,1,0:T(4,128)S(1)} collective-permute-done((s32[2,4,128]{2,1,0:T(4,128)S(1)}, s32[2,4,128]{2,1,0:T(4,128)S(1)}, u32[]{:S(2)}, u32[]{:S(2)}) %collective-permute-start.1) | collective-permute-done | bytes 4128 | tf_op jit(solution)/shard_map/ppermute | solution.py:387
  24.7 1.7 %collective-permute-start.2 = (s32[2,4,128]{2,1,0:T(4,128)S(1)}, s32[2,4,128]{2,1,0:T(4,128)S(1)}, u32[]{:S(2)}, u32[]{:S(2)}) collective-permute-start(s32[2,4,128]{2,1,0:T(4,128)S(1)} %pad_add_fusion), channel_id=1, source_target_pairs={{0,4},{2,6},{4,0},{6,2},{8,12},{10,14},{12,8},{14,10},{1,5},{3,7},... | collective-permute-start | bytes 12296 | tf_op jit(solution)/shard_map/ppermute | solution.py:387
  26.4 16.5 %collective-permute-done.2 = s32[2,4,128]{2,1,0:T(4,128)S(1)} collective-permute-done((s32[2,4,128]{2,1,0:T(4,128)S(1)}, s32[2,4,128]{2,1,0:T(4,128)S(1)}, u32[]{:S(2)}, u32[]{:S(2)}) %collective-permute-start.2) | collective-permute-done | bytes 4128 | tf_op jit(solution)/shard_map/ppermute | solution.py:387
  42.9 3.5 %collective-permute-start.7 = (s32[2,4,128]{2,1,0:T(4,128)S(1)}, s32[2,4,128]{2,1,0:T(4,128)S(1)}, u32[]{:S(2)}, u32[]{:S(2)}) collective-permute-start(s32[2,4,128]{2,1,0:T(4,128)S(1)} %pad_add_fusion), channel_id=1, source_target_pairs={{0,14},{2,12},{4,10},{6,8},{8,6},{10,4},{12,2},{14,0},{1,15},{3,13... | collective-permute-start | bytes 12296 | tf_op jit(solution)/shard_map/ppermute | solution.py:387
  46.4 0.0 collective-permute-done.3
  46.4 10.0 %collective-permute-done.4 = s32[2,4,128]{2,1,0:T(4,128)S(1)} collective-permute-done((s32[2,4,128]{2,1,0:T(4,128)S(1)}, s32[2,4,128]{2,1,0:T(4,128)S(1)}, u32[]{:S(2)}, u32[]{:S(2)}) %collective-permute-start.4) | collective-permute-done | bytes 4128 | tf_op jit(solution)/shard_map/ppermute | solution.py:387
  56.4 0.8 collective-permute-done.5
  57.2 0.0 collective-permute-done.6
  57.3 0.0 collective-permute-done.7
  57.3 0.0 all-to-all-done.levels
  57.3 0.0 copy-done.2
  57.3 0.0 copy-done.5
  57.3 0.0 copy-done.6
  57.3 27.8 %march.1 = f32[256,128]{1,0:T(8,128)} custom-call(bf16[8,16,16,512]{3,2,1,0:T(8,128)(2,1)S(1)} %all-to-all-done.levels, s32[8,4,128]{2,1,0:T(4,128)S(1)} %dynamic-slice_bitcast_fusion.cells, f32[2,32,8,128]{3,2,1,0:T(8,128)S(1)} %get-tuple-element.9.launched, f32[2,32,8,128]{3,2,1,0:T(8,128)S(1)} %get-tuple-element.10.entered, ...), custom_call_target="tpu_custom_call" | custom-call | flops 25600000000 | bytes 4194304 | tf_op jit(solution)/shard_map/march/pallas_call | solution.py:377
  85.1 3.7 %all-to-all-start.1 = ((f32[16,16,128]{2,1,0:T(8,128)}), f32[16,16,128]{2,1,0:T(8,128)S(1)}, u32[]{:S(2)}, u32[]{:S(2)}) async-start(f32[16,16,128]{2,1,0:T(8,128)} %bitcast.15), calls=%async_computation.1 | async-start | bytes 262144 | tf_op jit(solution)/shard_map/all_to_all | solution.py:410
  88.8 0.2 convert_reduce_fusion
  89.1 7.7 %all-to-all-done.1 = f32[16,16,128]{2,1,0:T(8,128)S(1)} async-done(((f32[16,16,128]{2,1,0:T(8,128)}), f32[16,16,128]{2,1,0:T(8,128)S(1)}, u32[]{:S(2)}, u32[]{:S(2)}) %all-to-all-start.1) | async-done | bytes 131104 | tf_op jit(solution)/shard_map/all_to_all | solution.py:410
  96.8 0.7 broadcast_divide_fusion
  (17 shorter events, 0.1 us)
Async XLA Ops:
  0.0 7.5 %copy-start.8 = (s32[128,2]{0,1:T(2,128)S(1)}, s32[128,2]{0,1:T(2,128)}, u32[]{:S(2)}) copy-start(s32[128,2]{0,1:T(2,128)} %param.14) | copy-start | bytes 3076
  0.0 7.5 %copy-start.9 = (s32[128,2]{0,1:T(2,128)S(1)}, s32[128,2]{0,1:T(2,128)}, u32[]{:S(2)}) copy-start(s32[128,2]{0,1:T(2,128)} %param.13) | copy-start | bytes 3076
  0.0 7.6 %copy-start.7 = (f32[2,4096]{1,0:T(2,128)S(1)}, f32[2,4096]{1,0:T(2,128)}, u32[]{:S(2)}) copy-start(f32[2,4096]{1,0:T(2,128)} %param.12) | copy-start | bytes 98308
  0.0 7.7 %copy-start = (bf16[256,512]{1,0:T(8,128)(2,1)S(1)}, bf16[256,512]{1,0:T(8,128)(2,1)}, u32[]{:S(2)}) copy-start(bf16[256,512]{1,0:T(8,128)(2,1)} %constant.67.clone.w_inverse) | copy-start | bytes 786436
  0.0 7.7 %copy-start.1 = (bf16[256,512]{1,0:T(8,128)(2,1)S(1)}, bf16[256,512]{1,0:T(8,128)(2,1)}, u32[]{:S(2)}) copy-start(bf16[256,512]{1,0:T(8,128)(2,1)} %constant.66.clone.w_forward) | copy-start | bytes 786436
  0.0 7.7 %copy-start.3 = (f32[2,32,128]{2,1,0:T(8,128)S(1)}, f32[2,32,128]{2,1,0:T(8,128)}, u32[]{:S(2)}) copy-start(f32[2,32,128]{2,1,0:T(8,128)} %constant.69.clone.spread_table.refs_1_) | copy-start | bytes 98308
  0.0 7.7 %copy-start.4 = (f32[2,32,128]{2,1,0:T(8,128)S(1)}, f32[2,32,128]{2,1,0:T(8,128)}, u32[]{:S(2)}) copy-start(f32[2,32,128]{2,1,0:T(8,128)} %constant.68.clone.twiddle_table.refs_0_) | copy-start | bytes 98308
  0.0 57.3 %all-to-all-start = ((bf16[8,16,16,512]{3,2,1,0:T(8,128)(2,1)}), bf16[8,16,16,512]{3,2,1,0:T(8,128)(2,1)S(1)}, u32[]{:S(2)}, u32[]{:S(2)}) async-start(bf16[8,16,16,512]{3,2,1,0:T(8,128)(2,1)} %bitcast.33), calls=%async_computation | async-start | bytes 4194304 | tf_op jit(solution)/shard_map/all_to_all | solution.py:401
  7.5 49.8 %copy-start.2 = (bf16[256,128]{1,0:T(8,128)(2,1)S(1)}, bf16[256,128]{1,0:T(8,128)(2,1)}, u32[]{:S(2)}) copy-start(bf16[256,128]{1,0:T(8,128)(2,1)} %constant.72.clone.refs_4_) | copy-start | bytes 196612
  7.5 49.8 %copy-start.5 = (f32[32,128]{1,0:T(8,128)S(1)}, f32[32,128]{1,0:T(8,128)}, u32[]{:S(2)}) copy-start(f32[32,128]{1,0:T(8,128)} %constant.71.clone.refs_3_) | copy-start | bytes 49156
  7.5 49.8 %copy-start.6 = (f32[32,128]{1,0:T(8,128)S(1)}, f32[32,128]{1,0:T(8,128)}, u32[]{:S(2)}) copy-start(f32[32,128]{1,0:T(8,128)} %constant.70.clone.refs_2_) | copy-start | bytes 49156
  7.5 1.2 %collective-permute-start = (s32[4,128]{1,0:T(4,128)S(1)}, s32[4,128]{1,0:T(4,128)S(1)}, u32[]{:S(2)}, u32[]{:S(2)}) collective-permute-start(s32[4,128]{1,0:T(4,128)S(1)} %pad_add_fusion.1), channel_id=1, source_target_pairs={{0,1},{1,0},{2,3},{3,2},{4,5},{5,4},{6,7},{7,6},{8,9},{9,8},{10,11... | collective-permute-start | bytes 6152 | tf_op jit(solution)/shard_map/ppermute | solution.py:382
  8.8 48.5 %collective-permute-start.6 = (s32[2,4,128]{2,1,0:T(4,128)S(1)}, s32[2,4,128]{2,1,0:T(4,128)S(1)}, u32[]{:S(2)}, u32[]{:S(2)}) collective-permute-start(s32[2,4,128]{2,1,0:T(4,128)S(1)} %pad_add_fusion), channel_id=1, source_target_pairs={{0,12},{2,14},{4,8},{6,10},{8,4},{10,6},{12,0},{14,2},{1,13},{3,15... | collective-permute-start | bytes 12296 | tf_op jit(solution)/shard_map/ppermute | solution.py:387
  12.7 44.6 %collective-permute-start.5 = (s32[2,4,128]{2,1,0:T(4,128)S(1)}, s32[2,4,128]{2,1,0:T(4,128)S(1)}, u32[]{:S(2)}, u32[]{:S(2)}) collective-permute-start(s32[2,4,128]{2,1,0:T(4,128)S(1)} %pad_add_fusion), channel_id=1, source_target_pairs={{0,10},{2,8},{4,14},{6,12},{8,2},{10,0},{12,6},{14,4},{1,11},{3,9}... | collective-permute-start | bytes 12296 | tf_op jit(solution)/shard_map/ppermute | solution.py:387
  13.2 43.2 %collective-permute-start.4 = (s32[2,4,128]{2,1,0:T(4,128)S(1)}, s32[2,4,128]{2,1,0:T(4,128)S(1)}, u32[]{:S(2)}, u32[]{:S(2)}) collective-permute-start(s32[2,4,128]{2,1,0:T(4,128)S(1)} %pad_add_fusion), channel_id=1, source_target_pairs={{0,8},{2,10},{4,12},{6,14},{8,0},{10,2},{12,4},{14,6},{1,9},{3,11}... | collective-permute-start | bytes 12296 | tf_op jit(solution)/shard_map/ppermute | solution.py:387
  16.5 29.9 %collective-permute-start.3 = (s32[2,4,128]{2,1,0:T(4,128)S(1)}, s32[2,4,128]{2,1,0:T(4,128)S(1)}, u32[]{:S(2)}, u32[]{:S(2)}) collective-permute-start(s32[2,4,128]{2,1,0:T(4,128)S(1)} %pad_add_fusion), channel_id=1, source_target_pairs={{0,6},{2,4},{4,2},{6,0},{8,14},{10,12},{12,10},{14,8},{1,7},{3,5},... | collective-permute-start | bytes 12296 | tf_op jit(solution)/shard_map/ppermute | solution.py:387
  16.5 8.2 %collective-permute-start.1 = (s32[2,4,128]{2,1,0:T(4,128)S(1)}, s32[2,4,128]{2,1,0:T(4,128)S(1)}, u32[]{:S(2)}, u32[]{:S(2)}) collective-permute-start(s32[2,4,128]{2,1,0:T(4,128)S(1)} %pad_add_fusion), channel_id=1, source_target_pairs={{0,2},{2,0},{4,6},{6,4},{8,10},{10,8},{12,14},{14,12},{1,3},{3,1},... | collective-permute-start | bytes 12296 | tf_op jit(solution)/shard_map/ppermute | solution.py:387
  24.7 18.2 %collective-permute-start.2 = (s32[2,4,128]{2,1,0:T(4,128)S(1)}, s32[2,4,128]{2,1,0:T(4,128)S(1)}, u32[]{:S(2)}, u32[]{:S(2)}) collective-permute-start(s32[2,4,128]{2,1,0:T(4,128)S(1)} %pad_add_fusion), channel_id=1, source_target_pairs={{0,4},{2,6},{4,0},{6,2},{8,12},{10,14},{12,8},{14,10},{1,5},{3,7},... | collective-permute-start | bytes 12296 | tf_op jit(solution)/shard_map/ppermute | solution.py:387
  42.9 14.4 %collective-permute-start.7 = (s32[2,4,128]{2,1,0:T(4,128)S(1)}, s32[2,4,128]{2,1,0:T(4,128)S(1)}, u32[]{:S(2)}, u32[]{:S(2)}) collective-permute-start(s32[2,4,128]{2,1,0:T(4,128)S(1)} %pad_add_fusion), channel_id=1, source_target_pairs={{0,14},{2,12},{4,10},{6,8},{8,6},{10,4},{12,2},{14,0},{1,15},{3,13... | collective-permute-start | bytes 12296 | tf_op jit(solution)/shard_map/ppermute | solution.py:387
  85.1 11.6 %all-to-all-start.1 = ((f32[16,16,128]{2,1,0:T(8,128)}), f32[16,16,128]{2,1,0:T(8,128)S(1)}, u32[]{:S(2)}, u32[]{:S(2)}) async-start(f32[16,16,128]{2,1,0:T(8,128)} %bitcast.15), calls=%async_computation.1 | async-start | bytes 262144 | tf_op jit(solution)/shard_map/all_to_all | solution.py:410

commit v10 on v7

--- a/solution.py
+++ b/solution.py
@@ -55,10 +55,10 @@
     tilt = (TILT_SLOPE * rel - 1.0).astype(np.float32)
     depth = np.maximum(rel - 0.75, 0.0) * 4.0
     absorb = np.exp(-ABSORB_RATE * depth * depth).astype(np.float32)
-    bins = np.zeros((2 * LANES, BINS), np.float64)
-    for lane in range(2 * LANES):
-        bins[lane, (lane % LANES) // BIN :: LANES // BIN] = 1.0 / BIN
-    return weights[0], weights[1], twiddle, spread, tilt, absorb, bins.astype(ml_dtypes.bfloat16)
+    bins = np.arange(BINS)
+    order = np.zeros((BINS, BINS))
+    order[bins % (LANES // BIN) * BIN + bins // (LANES // BIN), bins] = 1.0 / BIN
+    return weights[0], weights[1], twiddle, spread, tilt, absorb, order.astype(ml_dtypes.bfloat16)
 
 
 def phase_polynomials():
@@ -157,45 +157,36 @@
     for index in np.ndindex(table.shape[:-2]):
         for row in range(table.shape[-2]):
             place = (*index, row)
-            wide[place] = jnp.broadcast_to(table[(*index, pl.ds(row, 1))], (SUB, LANES))
-
-
-def parted(product):
-    return [(product[i * SUB : (i + 1) * SUB, :LANES], product[i * SUB : (i + 1) * SUB, LANES:]) for i in range(ROWS)]
-
-
-Q_ROWS = [ql + FOUR * qh for ql in range(FOUR) for qh in range(EIGHT)]
-
-
-def forward(field, w_forward, twiddle):
+            wide[place] = jnp.broadcast_to(table[(*index, pl.ds(row, 1))], wide.shape[-2:])
+
+
+def chain(ql, batch, field, back, w_forward, w_inverse, twiddle, spread):
+    column = [(field[0, ql * EIGHT + jl], field[1, ql * EIGHT + jl]) for jl in range(EIGHT)]
     pieces = []
-    for ql in range(FOUR):
-        column = [(field[0, ql * EIGHT + jl], field[1, ql * EIGHT + jl]) for jl in range(EIGHT)]
-        for qh, (re, im) in enumerate(dft8(column, -1)):
-            q = ql + FOUR * qh
-            c, s = twiddle[0, q], twiddle[1, q]
-            pieces.append((re * c - im * s, re * s + im * c))
-    return weighted(joined(pieces), w_forward)
-
-
-def inverse(product, w_inverse, spread):
+    for qh, (re, im) in enumerate(dft8(column, -1)):
+        c, s = twiddle[0, ql + FOUR * qh], twiddle[1, ql + FOUR * qh]
+        pieces.append((re * c - im * s, re * s + im * c))
+    product = weighted(joined(pieces), w_forward)
     pieces = []
-    for q, (re, im) in zip(Q_ROWS, parted(product)):
-        c, s = spread[0, q], spread[1, q]
+    for qh in range(EIGHT):
+        re, im = (product[qh * batch : (qh + 1) * batch, k * LANES : (k + 1) * LANES] for k in range(2))
+        c, s = spread[0, ql + FOUR * qh], spread[1, ql + FOUR * qh]
         pieces.append((re * c - im * s, re * s + im * c))
-    return weighted(joined(pieces), w_inverse)
-
-
-def leave(back, product, twiddle):
+    product = weighted(joined(pieces), w_inverse)
     pieces = []
-    for q, (re, im) in zip(Q_ROWS, parted(product)):
-        c, s = twiddle[0, q], twiddle[1, q]
+    for qh in range(EIGHT):
+        re, im = (product[qh * batch : (qh + 1) * batch, k * LANES : (k + 1) * LANES] for k in range(2))
+        c, s = twiddle[0, ql + FOUR * qh], twiddle[1, ql + FOUR * qh]
         pieces.append((re * c + im * s, im * c - re * s))
-    for ql in range(FOUR):
-        column = dft8(pieces[ql * EIGHT : (ql + 1) * EIGHT], 1)
-        for jl in range(EIGHT):
-            back[0, ql * EIGHT + jl] = column[jl][0]
-            back[1, ql * EIGHT + jl] = column[jl][1]
+    for jl, (re, im) in enumerate(dft8(pieces, 1)):
+        back[0, ql * EIGHT + jl] = re
+        back[1, ql * EIGHT + jl] = im
+
+
+def merged(a, b, distance, lane):
+    a = a + pltpu.roll(a, LANES - distance, 1)
+    b = b + pltpu.roll(b, distance, 1)
+    return jnp.where(lane & distance == 0, a, b)
 
 
 def launch_kernel(start, w_forward, w_inverse, twiddle_table, spread_table, back, field, twiddle, spread):
@@ -207,103 +198,88 @@
             j = EIGHT * jh + jl
             columns.append(tuple(jnp.broadcast_to(start[k, j : j + 1, :], (SUB, LANES)) for k in range(2)))
         enter(field, columns, jl)
-    product = inverse(forward(field, w_forward, twiddle), w_inverse, spread)
-    leave(back, product, twiddle)
+    for ql in range(FOUR):
+        chain(ql, SUB, field, back, w_forward, w_inverse, twiddle, spread)
 
 
 def launch(start, consts):
     vmem = pl.BlockSpec(memory_space=pltpu.VMEM)
     return pl.pallas_call(
         launch_kernel,
-        out_shape=[jax.ShapeDtypeStruct((2, ROWS, SUB, LANES), F32)] * 2,
+        out_shape=jax.ShapeDtypeStruct((2, ROWS, SUB, LANES), F32),
         in_specs=[vmem] * 5,
-        out_specs=[vmem] * 2,
-        scratch_shapes=[pltpu.VMEM((2, ROWS, SUB, LANES), F32)] * 2,
+        out_specs=vmem,
+        scratch_shapes=[pltpu.VMEM((2, ROWS, SUB, LANES), F32)] * 3,
         compiler_params=pltpu.CompilerParams(vmem_limit_bytes=8 * 1024 * 1024),
         cost_estimate=pl.CostEstimate(flops=1_000_000_000, bytes_accessed=1024 * 1024, transcendentals=0),
         name="launch",
     )(start, *consts[:4])
 
 
-def march_kernel(own, levels, cells, launched, entered, w_forward, w_inverse, *refs):
-    tables, (bins, section, totals, wide, field, back, energy, power), wide_tables = refs[:4], refs[4:12], refs[12:]
+def march_kernel(own, levels, cells, launched, w_forward, w_inverse, *refs):
+    tables, (order, section, totals, wide, field, back, power), wide_tables = refs[:4], refs[4:11], refs[11:]
     for table, place in zip(tables, wide_tables):
         spread_rows(table, place)
     twiddle, spread, tilt, absorb = wide_tables
     sine, cosine = phase_polynomials()
     sections, batch, steps, heights = levels.shape
-    halves = batch // SUB
-    lane = lax.broadcasted_iota(jnp.int32, (SUB, LANES), 1)
-    radial = lax.broadcasted_iota(jnp.int32, (SUB, LANES), 0)
+    lane = lax.broadcasted_iota(jnp.int32, (batch, LANES), 1)
+    radial = lax.broadcasted_iota(jnp.int32, (batch, LANES), 0)
+    my_lane = lane == section[0] * own + radial
     at_once = cells.shape[1] // 2
 
-    def rotate(half, t, ground, jls):
-        for jl in jls:
-            column = []
+    def rotate(t, ground, jl):
+        column = []
+        for ql in range(FOUR):
+            c, s = unit(ql * jl, ROWS)
+            column.append(cmul_const((back[0, ql * EIGHT + jl], back[1, ql * EIGHT + jl]), (c, -s)))
+        column = dft4(column, 1)
+        moved, energy = [], []
+        for jh in range(FOUR):
+            j = EIGHT * jh + jl
+            phi = wide[j, pl.ds(t, batch, stride=steps), :] + tilt[j]
+            u = phi * phi
+            sin_poly, cos_poly = sine[-1], cosine[-1]
+            for a, b in zip(sine[-2::-1], cosine[-2::-1]):
+                sin_poly = sin_poly * u + a
+                cos_poly = cos_poly * u + b
+            small = sin_poly * phi
+            double = small * cos_poly
+            turned_c = 1.0 - double * double
+            turned_s = double * (math.sqrt(2.0) - small * small)
+            re, im = column[jh]
+            if (j + 1) * LANES > 3 * H // 4:
+                loss = absorb[j]
+                re, im = re * loss, im * loss
+            re, im = re * turned_c - im * turned_s, re * turned_s + im * turned_c
+            if j < TERRAIN_ROWS:
+                open_air = lane + j * LANES >= ground
+                re, im = jnp.where(open_air, re, 0.0), jnp.where(open_air, im, 0.0)
+            energy.append(re * re + im * im)
+            moved.append((re, im))
+        enter(field, moved, jl)
+        return merged(
+            merged(energy[0], energy[2], 16, lane), merged(energy[1], energy[3], 16, lane), 8, lane
+        )
+
+    def step(t, carry):
+        row = cells[t // at_once, pl.ds(t % at_once, 1), :]
+        ground = jnp.sum(jnp.where(my_lane, row, 0), axis=1, keepdims=True)
+        sums = [rotate(t, ground, jl) for jl in range(EIGHT)]
+        for distance in (4, 2, 1):
+            sums = [merged(a, b, distance, lane) for a, b in zip(sums[: len(sums) // 2], sums[len(sums) // 2 :])]
+        power[pl.ds(pl.multiple_of(t * batch, batch), batch), :] = sums[0]
+
+        @pl.when(t + 1 < steps)
+        def _():
             for ql in range(FOUR):
-                c, s = unit(ql * jl, ROWS)
-                column.append(
-                    cmul_const((back[half, 0, ql * EIGHT + jl], back[half, 1, ql * EIGHT + jl]), (c, -s))
-                )
-            column = dft4(column, 1)
-            moved = []
-            for jh in range(FOUR):
-                j = EIGHT * jh + jl
-                phi = wide[j, pl.ds(half * SUB * steps + t, SUB, stride=steps), :] + tilt[j]
-                u = phi * phi
-                sin_poly, cos_poly = sine[-1], cosine[-1]
-                for a, b in zip(sine[-2::-1], cosine[-2::-1]):
-                    sin_poly = sin_poly * u + a
-                    cos_poly = cos_poly * u + b
-                small = sin_poly * phi
-                double = small * cos_poly
-                turned_c = 1.0 - double * double
-                turned_s = double * (math.sqrt(2.0) - small * small)
-                re, im = column[jh]
-                if (j + 1) * LANES > 3 * H // 4:
-                    loss = absorb[j]
-                    re, im = re * loss, im * loss
-                re, im = re * turned_c - im * turned_s, re * turned_s + im * turned_c
-                if j < TERRAIN_ROWS:
-                    open_air = lane + j * LANES >= ground
-                    re, im = jnp.where(open_air, re, 0.0), jnp.where(open_air, im, 0.0)
-                value = re * re + im * im
-                high = value.astype(BF16).astype(F32)
-                energy[half, j * SUB : (j + 1) * SUB, :LANES] = high
-                energy[half, j * SUB : (j + 1) * SUB, LANES:] = value - high
-                moved.append((re, im))
-            enter(field.at[half], moved, jl)
-
-    def binned(half, t):
-        summed = jnp.dot(energy[half].astype(BF16), bins[...], preferred_element_type=F32)
-        row = summed[:SUB]
-        for j in range(1, ROWS):
-            row = jnp.where(lane // (LANES // BIN) == j, summed[j * SUB : (j + 1) * SUB], row)
-        power[pl.ds(pl.multiple_of(t * batch + half * SUB, SUB), SUB), :] = row
-
-    def ground_of(half, t):
-        row = cells[t // at_once, pl.ds(t % at_once, 1), :]
-        my_lane = lane == section[0] * own + half * SUB + radial
-        return jnp.sum(jnp.where(my_lane, row, 0), axis=1, keepdims=True)
-
-    def turn_of(t, resting, moving):
-        ground = ground_of(resting, t)
-        product = forward(field.at[moving], w_forward, twiddle)
-        rotate(resting, t, ground, range(EIGHT // 2))
-        product = inverse(product, w_inverse, spread)
-        rotate(resting, t, ground, range(EIGHT // 2, EIGHT))
-        leave(back.at[moving], product, twiddle)
-        binned(resting, t)
-
-    def step(t, carry):
-        for half in range(halves):
-            turn_of(t, half, (half + 1) % halves)
+                chain(ql, batch, field, back, w_forward, w_inverse, twiddle, spread)
+
         return carry
 
     power[...] = jnp.zeros_like(power)
-    for half in range(halves):
-        back[half] = launched[...]
-        field[half] = entered[...]
+    for place in np.ndindex(back.shape[:2]):
+        back[place] = jnp.concatenate([launched[place]] * (batch // SUB))
     per_source = heights // LANES
 
     def widen(source, carry):
@@ -331,40 +307,37 @@
     tiles, cell_count = totals.shape[0], tile_row.shape[1]
     hot = (lax.broadcasted_iota(jnp.int32, (tiles, cell_count), 0) == tile_row).astype(F32).astype(BF16)
     value = power[...]
-    high = value.astype(BF16)
-    rest = value - high.astype(F32)
-    middle = rest.astype(BF16)
-    low = (rest - middle.astype(F32)).astype(BF16)
-    gain = jnp.dot(hot, high, preferred_element_type=F32)
-    gain += jnp.dot(hot, middle, preferred_element_type=F32)
-    gain += jnp.dot(hot, low, preferred_element_type=F32)
+    gain = jnp.zeros((tiles, BINS), F32)
+    for _ in range(3):
+        part = value.astype(BF16)
+        value = value - part.astype(F32)
+        part = jnp.dot(part, order[...], preferred_element_type=F32).astype(BF16)
+        gain += jnp.dot(hot, part, preferred_element_type=F32)
     totals[...] = gain
 
 
 def march(section, received, cells, launched, consts, tiles, own):
     sections, batch, steps, heights = received.shape
-    halves = batch // SUB
     vmem = pl.BlockSpec(memory_space=pltpu.VMEM)
     smem = pl.BlockSpec(memory_space=pltpu.SMEM)
     call = pl.pallas_call(
         functools.partial(march_kernel, own),
         out_shape=jax.ShapeDtypeStruct((tiles, BINS), F32),
-        in_specs=[vmem] * 11 + [smem],
+        in_specs=[vmem] * 10 + [smem],
         out_specs=vmem,
         scratch_shapes=[
             pltpu.VMEM((ROWS, batch * steps, LANES), F32),
-            pltpu.VMEM((halves, 2, ROWS, SUB, LANES), F32),
-            pltpu.VMEM((halves, 2, ROWS, SUB, LANES), F32),
-            pltpu.VMEM((halves, ROWS * SUB, 2 * LANES), F32),
+            pltpu.VMEM((2, ROWS, batch, LANES), F32),
+            pltpu.VMEM((2, ROWS, batch, LANES), F32),
             pltpu.VMEM((-(-steps * batch // LANES) * LANES, BINS), F32),
-        ] + [pltpu.VMEM((*table.shape[:-1], SUB, LANES), F32) for table in consts[2:6]],
+        ] + [pltpu.VMEM((*table.shape[:-1], batch, LANES), F32) for table in consts[2:6]],
         compiler_params=pltpu.CompilerParams(vmem_limit_bytes=10 * 1024 * 1024 + 4 * H * batch * steps),
         cost_estimate=pl.CostEstimate(
             flops=steps * 1_600_000_000, bytes_accessed=4 * 1024 * 1024, transcendentals=0
         ),
         name="march",
     )
-    return call(received, cells, *launched, *consts, section)
+    return call(received, cells, launched, *consts, section)
 
 
 def gather_small(value):

time: 93.5 us -> 96.9 us (1.036)
  Pallas kernels: 24.3 us -> 27.7 us
    pallas_call x2, Pallas kernels: 24.3 us -> 27.7 us  [the longest x1 27 us: march(): return call(received, cells, launched, *consts, section)]
where the time goes in v10:
time: 96.9 us; the launch traced here: 96.6 us
  waiting for transfers between devices  42.4 us (44%)
  Pallas kernels  27.7 us (29%)
  starting transfers between devices  25.1 us (26%)
    ppermute x7, waiting for transfers between devices, gather_small(): lax.ppermute(pair, 'range', [(i, i ^ d) for i in range(sections)])  34.4 us
    pallas_call x1, Pallas kernels, march(): return call(received, cells, launched, *consts, section)  27 us
    ppermute x7, starting transfers between devices, gather_small(): lax.ppermute(pair, 'range', [(i, i ^ d) for i in range(sections)])  14 us
    all_to_all x1, waiting for transfers between devices, local(): lax.all_to_all(totals.reshape(owners, TILE_DEV, BINS), ('range', 'radial'...  7.68 us
    all_to_all x1, starting transfers between devices, local(): received = lax.all_to_all(received, 'range', 0, 0, tiled=True)  7.44 us
    all_to_all x1, starting transfers between devices, local(): lax.all_to_all(totals.reshape(owners, TILE_DEV, BINS), ('range', 'radial'...  3.66 us
  transfers between devices with their start and end apart: 10, of which 6 were waited for; matrix products, arithmetic and copies ran while one was open for 0% of the time, Pallas kernels for 1%

profile of v10, /device:TPU:0, one launch (start us, length us, event | category | flops | bytes accessed | tf_op | source)
XLA Modules:
  0.0 96.6 jit_solution(8379859700561011661)
XLA Ops:
  0.0 0.0 copy-start.8
  0.0 0.0 copy-start.9
  0.0 0.0 copy-start.7
  0.0 0.0 copy-start
  0.0 0.0 copy-start.1
  0.0 0.0 copy-start.2
  0.0 0.0 copy-start.3
  0.0 7.4 %all-to-all-start = ((bf16[8,16,16,512]{3,2,1,0:T(8,128)(2,1)}), bf16[8,16,16,512]{3,2,1,0:T(8,128)(2,1)S(1)}, u32[]{:S(2)}, u32[]{:S(2)}) async-start(bf16[8,16,16,512]{3,2,1,0:T(8,128)(2,1)} %bitcast.33), calls=%async_computation | async-start | bytes 4194304 | tf_op jit(solution)/shard_map/all_to_all | solution.py:364
  7.5 0.0 copy-start.4
  7.5 0.0 copy-start.5
  7.5 0.0 copy-start.6
  7.5 0.0 copy-done.8
  7.5 0.0 copy-done.9
  7.5 0.1 collective-permute-start
  7.6 0.0 copy-done.7
  7.7 0.0 copy-done
  7.7 0.0 copy-done.1
  7.7 0.0 copy-done.2
  7.7 0.0 copy-done.3
  7.7 0.8 launch.1.launched
  8.5 0.2 collective-permute-done
  8.8 3.9 %collective-permute-start.6 = (s32[2,4,128]{2,1,0:T(4,128)S(1)}, s32[2,4,128]{2,1,0:T(4,128)S(1)}, u32[]{:S(2)}, u32[]{:S(2)}) collective-permute-start(s32[2,4,128]{2,1,0:T(4,128)S(1)} %pad_add_fusion), channel_id=1, source_target_pairs={{0,12},{2,14},{4,8},{6,10},{8,4},{10,6},{12,0},{14,2},{1,13},{3,15... | collective-permute-start | bytes 12296 | tf_op jit(solution)/shard_map/ppermute | solution.py:350
  12.7 0.6 collective-permute-start.5
  13.2 3.3 %collective-permute-start.4 = (s32[2,4,128]{2,1,0:T(4,128)S(1)}, s32[2,4,128]{2,1,0:T(4,128)S(1)}, u32[]{:S(2)}, u32[]{:S(2)}) collective-permute-start(s32[2,4,128]{2,1,0:T(4,128)S(1)} %pad_add_fusion), channel_id=1, source_target_pairs={{0,8},{2,10},{4,12},{6,14},{8,0},{10,2},{12,4},{14,6},{1,9},{3,11}... | collective-permute-start | bytes 12296 | tf_op jit(solution)/shard_map/ppermute | solution.py:350
  16.5 0.0 collective-permute-start.3
  16.5 1.1 %collective-permute-start.1 = (s32[2,4,128]{2,1,0:T(4,128)S(1)}, s32[2,4,128]{2,1,0:T(4,128)S(1)}, u32[]{:S(2)}, u32[]{:S(2)}) collective-permute-start(s32[2,4,128]{2,1,0:T(4,128)S(1)} %pad_add_fusion), channel_id=1, source_target_pairs={{0,2},{2,0},{4,6},{6,4},{8,10},{10,8},{12,14},{14,12},{1,3},{3,1},... | collective-permute-start | bytes 12296 | tf_op jit(solution)/shard_map/ppermute | solution.py:350
  17.6 7.1 %collective-permute-done.1 = s32[2,4,128]{2,1,0:T(4,128)S(1)} collective-permute-done((s32[2,4,128]{2,1,0:T(4,128)S(1)}, s32[2,4,128]{2,1,0:T(4,128)S(1)}, u32[]{:S(2)}, u32[]{:S(2)}) %collective-permute-start.1) | collective-permute-done | bytes 4128 | tf_op jit(solution)/shard_map/ppermute | solution.py:350
  24.7 1.7 %collective-permute-start.2 = (s32[2,4,128]{2,1,0:T(4,128)S(1)}, s32[2,4,128]{2,1,0:T(4,128)S(1)}, u32[]{:S(2)}, u32[]{:S(2)}) collective-permute-start(s32[2,4,128]{2,1,0:T(4,128)S(1)} %pad_add_fusion), channel_id=1, source_target_pairs={{0,4},{2,6},{4,0},{6,2},{8,12},{10,14},{12,8},{14,10},{1,5},{3,7},... | collective-permute-start | bytes 12296 | tf_op jit(solution)/shard_map/ppermute | solution.py:350
  26.4 16.5 %collective-permute-done.2 = s32[2,4,128]{2,1,0:T(4,128)S(1)} collective-permute-done((s32[2,4,128]{2,1,0:T(4,128)S(1)}, s32[2,4,128]{2,1,0:T(4,128)S(1)}, u32[]{:S(2)}, u32[]{:S(2)}) %collective-permute-start.2) | collective-permute-done | bytes 4128 | tf_op jit(solution)/shard_map/ppermute | solution.py:350
  42.9 3.5 %collective-permute-start.7 = (s32[2,4,128]{2,1,0:T(4,128)S(1)}, s32[2,4,128]{2,1,0:T(4,128)S(1)}, u32[]{:S(2)}, u32[]{:S(2)}) collective-permute-start(s32[2,4,128]{2,1,0:T(4,128)S(1)} %pad_add_fusion), channel_id=1, source_target_pairs={{0,14},{2,12},{4,10},{6,8},{8,6},{10,4},{12,2},{14,0},{1,15},{3,13... | collective-permute-start | bytes 12296 | tf_op jit(solution)/shard_map/ppermute | solution.py:350
  46.4 0.0 collective-permute-done.3
  46.4 10.0 %collective-permute-done.4 = s32[2,4,128]{2,1,0:T(4,128)S(1)} collective-permute-done((s32[2,4,128]{2,1,0:T(4,128)S(1)}, s32[2,4,128]{2,1,0:T(4,128)S(1)}, u32[]{:S(2)}, u32[]{:S(2)}) %collective-permute-start.4) | collective-permute-done | bytes 4128 | tf_op jit(solution)/shard_map/ppermute | solution.py:350
  56.4 0.8 collective-permute-done.5
  57.2 0.0 collective-permute-done.6
  57.3 0.0 collective-permute-done.7
  57.3 0.0 all-to-all-done.levels
  57.3 0.0 copy-done.4
  57.3 0.0 copy-done.5
  57.3 0.0 copy-done.6
  57.3 27.0 %march.1 = f32[256,128]{1,0:T(8,128)} custom-call(bf16[8,16,16,512]{3,2,1,0:T(8,128)(2,1)S(1)} %all-to-all-done.levels, s32[8,4,128]{2,1,0:T(4,128)S(1)} %dynamic-slice_bitcast_fusion.cells, f32[2,32,8,128]{3,2,1,0:T(8,128)S(1)} %launch.1.launched, bf16[2,256,256]{2,1,0:T(8,128)(2,1)S(1)} %copy-done.1, bf16[2,256,256]{2,1,0:T(8,128)(2,1)S(1)} %copy-done, ...), custom_call_target="tpu_custom_call" | custom-call | flops 25600000000 | bytes 4194304 | tf_op jit(solution)/shard_map/march/pallas_call | solution.py:340
  84.3 3.7 %all-to-all-start.1 = ((f32[16,16,128]{2,1,0:T(8,128)}), f32[16,16,128]{2,1,0:T(8,128)S(1)}, u32[]{:S(2)}, u32[]{:S(2)}) async-start(f32[16,16,128]{2,1,0:T(8,128)} %bitcast.15), calls=%async_computation.1 | async-start | bytes 262144 | tf_op jit(solution)/shard_map/all_to_all | solution.py:373
  88.0 0.2 convert_reduce_fusion
  88.2 7.7 %all-to-all-done.1 = f32[16,16,128]{2,1,0:T(8,128)S(1)} async-done(((f32[16,16,128]{2,1,0:T(8,128)}), f32[16,16,128]{2,1,0:T(8,128)S(1)}, u32[]{:S(2)}, u32[]{:S(2)}) %all-to-all-start.1) | async-done | bytes 131104 | tf_op jit(solution)/shard_map/all_to_all | solution.py:373
  95.9 0.7 broadcast_divide_fusion
  (17 shorter events, 0.1 us)
Async XLA Ops:
  0.0 7.5 %copy-start.8 = (s32[128,2]{0,1:T(2,128)S(1)}, s32[128,2]{0,1:T(2,128)}, u32[]{:S(2)}) copy-start(s32[128,2]{0,1:T(2,128)} %param.14) | copy-start | bytes 3076
  0.0 7.5 %copy-start.9 = (s32[128,2]{0,1:T(2,128)S(1)}, s32[128,2]{0,1:T(2,128)}, u32[]{:S(2)}) copy-start(s32[128,2]{0,1:T(2,128)} %param.13) | copy-start | bytes 3076
  0.0 7.6 %copy-start.7 = (f32[2,4096]{1,0:T(2,128)S(1)}, f32[2,4096]{1,0:T(2,128)}, u32[]{:S(2)}) copy-start(f32[2,4096]{1,0:T(2,128)} %param.12) | copy-start | bytes 98308
  0.0 7.7 %copy-start = (bf16[2,256,256]{2,1,0:T(8,128)(2,1)S(1)}, bf16[2,256,256]{2,1,0:T(8,128)(2,1)}, u32[]{:S(2)}) copy-start(bf16[2,256,256]{2,1,0:T(8,128)(2,1)} %constant.67.clone.w_inverse) | copy-start | bytes 786436
  0.0 7.7 %copy-start.1 = (bf16[2,256,256]{2,1,0:T(8,128)(2,1)S(1)}, bf16[2,256,256]{2,1,0:T(8,128)(2,1)}, u32[]{:S(2)}) copy-start(bf16[2,256,256]{2,1,0:T(8,128)(2,1)} %constant.66.clone.w_forward) | copy-start | bytes 786436
  0.0 7.7 %copy-start.2 = (f32[2,32,128]{2,1,0:T(8,128)S(1)}, f32[2,32,128]{2,1,0:T(8,128)}, u32[]{:S(2)}) copy-start(f32[2,32,128]{2,1,0:T(8,128)} %constant.69.clone.spread_table.refs_1_) | copy-start | bytes 98308
  0.0 7.7 %copy-start.3 = (f32[2,32,128]{2,1,0:T(8,128)S(1)}, f32[2,32,128]{2,1,0:T(8,128)}, u32[]{:S(2)}) copy-start(f32[2,32,128]{2,1,0:T(8,128)} %constant.68.clone.twiddle_table.refs_0_) | copy-start | bytes 98308
  0.0 57.3 %all-to-all-start = ((bf16[8,16,16,512]{3,2,1,0:T(8,128)(2,1)}), bf16[8,16,16,512]{3,2,1,0:T(8,128)(2,1)S(1)}, u32[]{:S(2)}, u32[]{:S(2)}) async-start(bf16[8,16,16,512]{3,2,1,0:T(8,128)(2,1)} %bitcast.33), calls=%async_computation | async-start | bytes 4194304 | tf_op jit(solution)/shard_map/all_to_all | solution.py:364
  7.5 49.8 %copy-start.4 = (bf16[128,128]{1,0:T(8,128)(2,1)S(1)}, bf16[128,128]{1,0:T(8,128)(2,1)}, u32[]{:S(2)}) copy-start(bf16[128,128]{1,0:T(8,128)(2,1)} %constant.72.clone.refs_4_) | copy-start | bytes 98308
  7.5 49.8 %copy-start.5 = (f32[32,128]{1,0:T(8,128)S(1)}, f32[32,128]{1,0:T(8,128)}, u32[]{:S(2)}) copy-start(f32[32,128]{1,0:T(8,128)} %constant.71.clone.refs_3_) | copy-start | bytes 49156
  7.5 49.8 %copy-start.6 = (f32[32,128]{1,0:T(8,128)S(1)}, f32[32,128]{1,0:T(8,128)}, u32[]{:S(2)}) copy-start(f32[32,128]{1,0:T(8,128)} %constant.70.clone.refs_2_) | copy-start | bytes 49156
  7.5 1.2 %collective-permute-start = (s32[4,128]{1,0:T(4,128)S(1)}, s32[4,128]{1,0:T(4,128)S(1)}, u32[]{:S(2)}, u32[]{:S(2)}) collective-permute-start(s32[4,128]{1,0:T(4,128)S(1)} %pad_add_fusion.1), channel_id=1, source_target_pairs={{0,1},{1,0},{2,3},{3,2},{4,5},{5,4},{6,7},{7,6},{8,9},{9,8},{10,11... | collective-permute-start | bytes 6152 | tf_op jit(solution)/shard_map/ppermute | solution.py:345
  8.8 48.5 %collective-permute-start.6 = (s32[2,4,128]{2,1,0:T(4,128)S(1)}, s32[2,4,128]{2,1,0:T(4,128)S(1)}, u32[]{:S(2)}, u32[]{:S(2)}) collective-permute-start(s32[2,4,128]{2,1,0:T(4,128)S(1)} %pad_add_fusion), channel_id=1, source_target_pairs={{0,12},{2,14},{4,8},{6,10},{8,4},{10,6},{12,0},{14,2},{1,13},{3,15... | collective-permute-start | bytes 12296 | tf_op jit(solution)/shard_map/ppermute | solution.py:350
  12.7 44.6 %collective-permute-start.5 = (s32[2,4,128]{2,1,0:T(4,128)S(1)}, s32[2,4,128]{2,1,0:T(4,128)S(1)}, u32[]{:S(2)}, u32[]{:S(2)}) collective-permute-start(s32[2,4,128]{2,1,0:T(4,128)S(1)} %pad_add_fusion), channel_id=1, source_target_pairs={{0,10},{2,8},{4,14},{6,12},{8,2},{10,0},{12,6},{14,4},{1,11},{3,9}... | collective-permute-start | bytes 12296 | tf_op jit(solution)/shard_map/ppermute | solution.py:350
  13.2 43.2 %collective-permute-start.4 = (s32[2,4,128]{2,1,0:T(4,128)S(1)}, s32[2,4,128]{2,1,0:T(4,128)S(1)}, u32[]{:S(2)}, u32[]{:S(2)}) collective-permute-start(s32[2,4,128]{2,1,0:T(4,128)S(1)} %pad_add_fusion), channel_id=1, source_target_pairs={{0,8},{2,10},{4,12},{6,14},{8,0},{10,2},{12,4},{14,6},{1,9},{3,11}... | collective-permute-start | bytes 12296 | tf_op jit(solution)/shard_map/ppermute | solution.py:350
  16.5 29.9 %collective-permute-start.3 = (s32[2,4,128]{2,1,0:T(4,128)S(1)}, s32[2,4,128]{2,1,0:T(4,128)S(1)}, u32[]{:S(2)}, u32[]{:S(2)}) collective-permute-start(s32[2,4,128]{2,1,0:T(4,128)S(1)} %pad_add_fusion), channel_id=1, source_target_pairs={{0,6},{2,4},{4,2},{6,0},{8,14},{10,12},{12,10},{14,8},{1,7},{3,5},... | collective-permute-start | bytes 12296 | tf_op jit(solution)/shard_map/ppermute | solution.py:350
  16.5 8.2 %collective-permute-start.1 = (s32[2,4,128]{2,1,0:T(4,128)S(1)}, s32[2,4,128]{2,1,0:T(4,128)S(1)}, u32[]{:S(2)}, u32[]{:S(2)}) collective-permute-start(s32[2,4,128]{2,1,0:T(4,128)S(1)} %pad_add_fusion), channel_id=1, source_target_pairs={{0,2},{2,0},{4,6},{6,4},{8,10},{10,8},{12,14},{14,12},{1,3},{3,1},... | collective-permute-start | bytes 12296 | tf_op jit(solution)/shard_map/ppermute | solution.py:350
  24.7 18.2 %collective-permute-start.2 = (s32[2,4,128]{2,1,0:T(4,128)S(1)}, s32[2,4,128]{2,1,0:T(4,128)S(1)}, u32[]{:S(2)}, u32[]{:S(2)}) collective-permute-start(s32[2,4,128]{2,1,0:T(4,128)S(1)} %pad_add_fusion), channel_id=1, source_target_pairs={{0,4},{2,6},{4,0},{6,2},{8,12},{10,14},{12,8},{14,10},{1,5},{3,7},... | collective-permute-start | bytes 12296 | tf_op jit(solution)/shard_map/ppermute | solution.py:350
  42.9 14.4 %collective-permute-start.7 = (s32[2,4,128]{2,1,0:T(4,128)S(1)}, s32[2,4,128]{2,1,0:T(4,128)S(1)}, u32[]{:S(2)}, u32[]{:S(2)}) collective-permute-start(s32[2,4,128]{2,1,0:T(4,128)S(1)} %pad_add_fusion), channel_id=1, source_target_pairs={{0,14},{2,12},{4,10},{6,8},{8,6},{10,4},{12,2},{14,0},{1,15},{3,13... | collective-permute-start | bytes 12296 | tf_op jit(solution)/shard_map/ppermute | solution.py:350
  84.3 11.6 %all-to-all-start.1 = ((f32[16,16,128]{2,1,0:T(8,128)}), f32[16,16,128]{2,1,0:T(8,128)S(1)}, u32[]{:S(2)}, u32[]{:S(2)}) async-start(f32[16,16,128]{2,1,0:T(8,128)} %bitcast.15), calls=%async_computation.1 | async-start | bytes 262144 | tf_op jit(solution)/shard_map/all_to_all | solution.py:373

commit v11 on v8

--- a/solution.py
+++ b/solution.py
@@ -55,10 +55,10 @@
     tilt = (TILT_SLOPE * rel - 1.0).astype(np.float32)
     depth = np.maximum(rel - 0.75, 0.0) * 4.0
     absorb = np.exp(-ABSORB_RATE * depth * depth).astype(np.float32)
-    bins = np.zeros((2 * LANES, BINS), np.float64)
-    for lane in range(2 * LANES):
-        bins[lane, (lane % LANES) // BIN :: LANES // BIN] = 1.0 / BIN
-    return weights[0], weights[1], twiddle, spread, tilt, absorb, bins.astype(ml_dtypes.bfloat16)
+    bins = np.arange(BINS)
+    order = np.zeros((BINS, BINS))
+    order[bins % (LANES // BIN) * BIN + bins // (LANES // BIN), bins] = 1.0 / BIN
+    return weights[0], weights[1], twiddle, spread, tilt, absorb, order.astype(ml_dtypes.bfloat16)
 
 
 def phase_polynomials():
@@ -205,6 +205,12 @@
             back[1, ql * EIGHT + jl] = column[jl][1]
 
 
+def merged(a, b, distance, lane):
+    a = a + pltpu.roll(a, LANES - distance, 1)
+    b = b + pltpu.roll(b, distance, 1)
+    return jnp.where(lane & distance == 0, a, b)
+
+
 def launch_kernel(start, w_forward, w_inverse, twiddle_table, spread_table, back, field, twiddle, spread):
     spread_rows(twiddle_table, twiddle)
     spread_rows(spread_table, spread)
@@ -233,7 +239,7 @@
 
 
 def march_kernel(own, levels, cells, launched, entered, w_forward, w_inverse, *refs):
-    tables, (bins, section, totals, wide, field, back, energy, power), wide_tables = refs[:4], refs[4:12], refs[12:]
+    tables, (order, section, totals, wide, field, back, power), wide_tables = refs[:4], refs[4:11], refs[11:]
     for table, place in zip(tables, wide_tables):
         spread_rows(table, place)
     twiddle, spread, tilt, absorb = wide_tables
@@ -244,49 +250,41 @@
     radial = lax.broadcasted_iota(jnp.int32, (SUB, LANES), 0)
     at_once = cells.shape[1] // 2
 
-    def rotate(half, t, ground, jls):
-        for jl in jls:
-            column = []
-            for ql in range(FOUR):
-                c, s = unit(ql * jl, ROWS)
-                column.append(
-                    cmul_const((back[half, 0, ql * EIGHT + jl], back[half, 1, ql * EIGHT + jl]), (c, -s))
-                )
-            column = dft4(column, 1)
-            moved = []
-            for jh in range(FOUR):
-                j = EIGHT * jh + jl
-                phi = wide[j, pl.ds(half * SUB * steps + t, SUB, stride=steps), :] + tilt[j]
-                u = phi * phi
-                sin_poly, cos_poly = sine[-1], cosine[-1]
-                for a, b in zip(sine[-2::-1], cosine[-2::-1]):
-                    sin_poly = sin_poly * u + a
-                    cos_poly = cos_poly * u + b
-                small = sin_poly * phi
-                double = small * cos_poly
-                turned_c = 1.0 - double * double
-                turned_s = double * (math.sqrt(2.0) - small * small)
-                re, im = column[jh]
-                if (j + 1) * LANES > 3 * H // 4:
-                    loss = absorb[j]
-                    re, im = re * loss, im * loss
-                re, im = re * turned_c - im * turned_s, re * turned_s + im * turned_c
-                if j < TERRAIN_ROWS:
-                    open_air = lane + j * LANES >= ground
-                    re, im = jnp.where(open_air, re, 0.0), jnp.where(open_air, im, 0.0)
-                value = re * re + im * im
-                high = value.astype(BF16).astype(F32)
-                energy[half, j * SUB : (j + 1) * SUB, :LANES] = high
-                energy[half, j * SUB : (j + 1) * SUB, LANES:] = value - high
-                moved.append((re, im))
-            enter(field.at[half], moved, jl)
-
-    def binned(half, t):
-        summed = jnp.dot(energy[half].astype(BF16), bins[...], preferred_element_type=F32)
-        row = summed[:SUB]
-        for j in range(1, ROWS):
-            row = jnp.where(lane // (LANES // BIN) == j, summed[j * SUB : (j + 1) * SUB], row)
-        power[pl.ds(pl.multiple_of(t * batch + half * SUB, SUB), SUB), :] = row
+    def rotate(half, t, ground, jl, sums):
+        column = []
+        for ql in range(FOUR):
+            c, s = unit(ql * jl, ROWS)
+            column.append(
+                cmul_const((back[half, 0, ql * EIGHT + jl], back[half, 1, ql * EIGHT + jl]), (c, -s))
+            )
+        column = dft4(column, 1)
+        moved, energy = [], []
+        for jh in range(FOUR):
+            j = EIGHT * jh + jl
+            phi = wide[j, pl.ds(half * SUB * steps + t, SUB, stride=steps), :] + tilt[j]
+            u = phi * phi
+            sin_poly, cos_poly = sine[-1], cosine[-1]
+            for a, b in zip(sine[-2::-1], cosine[-2::-1]):
+                sin_poly = sin_poly * u + a
+                cos_poly = cos_poly * u + b
+            small = sin_poly * phi
+            double = small * cos_poly
+            turned_c = 1.0 - double * double
+            turned_s = double * (math.sqrt(2.0) - small * small)
+            re, im = column[jh]
+            if (j + 1) * LANES > 3 * H // 4:
+                loss = absorb[j]
+                re, im = re * loss, im * loss
+            re, im = re * turned_c - im * turned_s, re * turned_s + im * turned_c
+            if j < TERRAIN_ROWS:
+                open_air = lane + j * LANES >= ground
+                re, im = jnp.where(open_air, re, 0.0), jnp.where(open_air, im, 0.0)
+            energy.append(re * re + im * im)
+            moved.append((re, im))
+        enter(field.at[half], moved, jl)
+        sums.append(merged(
+            merged(energy[0], energy[2], 16, lane), merged(energy[1], energy[3], 16, lane), 8, lane
+        ))
 
     def ground_of(half, t):
         row = cells[t // at_once, pl.ds(t % at_once, 1), :]
@@ -295,12 +293,15 @@
 
     def turn_of(t, resting, moving):
         ground = ground_of(resting, t)
-        pieces = [functools.partial(rotate, resting, t, ground, [jl]) for jl in range(EIGHT)]
+        sums = []
+        pieces = [functools.partial(rotate, resting, t, ground, jl, sums) for jl in range(EIGHT)]
         product = forward(field.at[moving], w_forward, twiddle, pieces[:3])
-        binned(moving, jnp.maximum(t - 1, 0) if resting == 0 else t)
         product = inverse(product, w_inverse, spread, pieces[3:6])
         for piece in pieces[6:]:
             piece()
+        for distance in (4, 2, 1):
+            sums = [merged(a, b, distance, lane) for a, b in zip(sums[: len(sums) // 2], sums[len(sums) // 2 :])]
+        power[pl.ds(pl.multiple_of(t * batch + resting * SUB, SUB), SUB), :] = sums[0]
         leave(back.at[moving], product, twiddle)
 
     def step(t, carry):
@@ -322,9 +323,7 @@
         return carry
 
     lax.fori_loop(0, sections, widen, 0)
-    energy[...] = jnp.zeros_like(energy)
     lax.fori_loop(0, steps, step, 0)
-    binned(halves - 1, steps - 1)
 
     lane = lax.broadcasted_iota(jnp.int32, (1, LANES), 1)
     fit = LANES // batch
@@ -341,13 +340,12 @@
     tiles, cell_count = totals.shape[0], tile_row.shape[1]
     hot = (lax.broadcasted_iota(jnp.int32, (tiles, cell_count), 0) == tile_row).astype(F32).astype(BF16)
     value = power[...]
-    high = value.astype(BF16)
-    rest = value - high.astype(F32)
-    middle = rest.astype(BF16)
-    low = (rest - middle.astype(F32)).astype(BF16)
-    gain = jnp.dot(hot, high, preferred_element_type=F32)
-    gain += jnp.dot(hot, middle, preferred_element_type=F32)
-    gain += jnp.dot(hot, low, preferred_element_type=F32)
+    gain = jnp.zeros((tiles, BINS), F32)
+    for _ in range(3):
+        part = value.astype(BF16)
+        value = value - part.astype(F32)
+        part = jnp.dot(part, order[...], preferred_element_type=F32).astype(BF16)
+        gain += jnp.dot(hot, part, preferred_element_type=F32)
     totals[...] = gain
 
 
@@ -365,7 +363,6 @@
             pltpu.VMEM((ROWS, batch * steps, LANES), F32),
             pltpu.VMEM((halves, 2, ROWS, SUB, LANES), F32),
             pltpu.VMEM((halves, 2, ROWS, SUB, LANES), F32),
-            pltpu.VMEM((halves, ROWS * SUB, 2 * LANES), F32),
             pltpu.VMEM((-(-steps * batch // LANES) * LANES, BINS), F32),
         ] + [pltpu.VMEM((*table.shape[:-1], SUB, LANES), F32) for table in consts[2:6]],
         compiler_params=pltpu.CompilerParams(vmem_limit_bytes=10 * 1024 * 1024 + 4 * H * batch * steps),
@@ -382,10 +379,13 @@
     other = lax.ppermute(value, "radial", [(0, 1), (1, 0)])
     pair = jnp.stack([jnp.where(radial == 0, value, other), jnp.where(radial == 0, other, value)])
     section = lax.axis_index("range")
+    next_pair = lax.ppermute(pair, "range", [(i, i ^ 1) for i in range(sections)])
+    even = section % 2 == 0
+    both = jnp.stack([jnp.where(even, pair, next_pair), jnp.where(even, next_pair, pair)])
     held = jnp.zeros((sections, *pair.shape), pair.dtype)
-    for d in range(sections):
-        part = lax.ppermute(pair, "range", [(i, i ^ d) for i in range(sections)]) if d else pair
-        held = lax.dynamic_update_index_in_dim(held, part, section ^ d, 0)
+    for d in range(0, sections, 2):
+        part = lax.ppermute(both, "range", [(i, i ^ d) for i in range(sections)]) if d else both
+        held = lax.dynamic_update_slice_in_dim(held, part, (section ^ d) // 2 * 2, 0)
     return held
 
 

time: 92.4 us -> 92.8 us (level)
  starting transfers between devices: 25.1 us -> 17.8 us
  waiting for transfers between devices: 42.5 us -> 49 us
  Pallas kernels: 23.2 us -> 24.4 us
    ppermute x7 -> x4, starting transfers between devices: 14 us -> 6.59 us  [the longest x3 4.52 us: gather_small(): lax.ppermute(both, 'range', [(i, i ^ d) for i in range(sections)])]
    ppermute x7 -> x4, waiting for transfers between devices: 34.4 us -> 40.2 us  [the longest x3 26.4 us: gather_small(): lax.ppermute(both, 'range', [(i, i ^ d) for i in range(sections)])]
    pallas_call x1, Pallas kernels: 22.5 us -> 23.8 us  [march(): return call(received, cells, *launched, *consts, section)]
  transfers between devices with their start and end apart: 10 -> 7, of which waited for: 6 -> 5; matrix products, arithmetic and copies ran while one was open for 0% -> 0% of each run, Pallas kernels for 1% -> 1%
where the time goes in v11:
time: 92.8 us; the launch traced here: 92.5 us
  waiting for transfers between devices  49 us (53%)
  Pallas kernels  24.4 us (26%)
  starting transfers between devices  17.8 us (19%)
  other arithmetic  0.96 us (1%)
    ppermute x3, waiting for transfers between devices, gather_small(): lax.ppermute(both, 'range', [(i, i ^ d) for i in range(sections)])  26.4 us
    pallas_call x1, Pallas kernels, march(): return call(received, cells, *launched, *consts, section)  23.8 us
    ppermute x1, waiting for transfers between devices, gather_small(): lax.ppermute(pair, 'range', [(i, i ^ 1) for i in range(sections)])  13.8 us
    all_to_all x1, waiting for transfers between devices, local(): lax.all_to_all(totals.reshape(owners, TILE_DEV, BINS), ('range', 'radial'...  7.68 us
    all_to_all x1, starting transfers between devices, local(): received = lax.all_to_all(received, 'range', 0, 0, tiled=True)  7.44 us
    ppermute x3, starting transfers between devices, gather_small(): lax.ppermute(both, 'range', [(i, i ^ d) for i in range(sections)])  4.52 us
    all_to_all x1, starting transfers between devices, local(): lax.all_to_all(totals.reshape(owners, TILE_DEV, BINS), ('range', 'radial'...  3.74 us
    ppermute x1, starting transfers between devices, gather_small(): lax.ppermute(pair, 'range', [(i, i ^ 1) for i in range(sections)])  2.07 us
  transfers between devices with their start and end apart: 7, of which 5 were waited for; matrix products, arithmetic and copies ran while one was open for 0% of the time, Pallas kernels for 1%

profile of v11, /device:TPU:0, one launch (start us, length us, event | category | flops | bytes accessed | tf_op | source)
XLA Modules:
  0.0 92.5 jit_solution(4256794147690744628)
XLA Ops:
  0.0 0.0 copy-start.8
  0.0 0.0 copy-start.9
  0.0 0.0 copy-start.7
  0.0 0.0 copy-start
  0.0 0.0 copy-start.1
  0.0 0.0 copy-start.2
  0.0 0.0 copy-start.3
  0.0 7.4 %all-to-all-start = ((bf16[8,16,16,512]{3,2,1,0:T(8,128)(2,1)}), bf16[8,16,16,512]{3,2,1,0:T(8,128)(2,1)S(1)}, u32[]{:S(2)}, u32[]{:S(2)}) async-start(bf16[8,16,16,512]{3,2,1,0:T(8,128)(2,1)} %bitcast.21), calls=%async_computation | async-start | bytes 4194304 | tf_op jit(solution)/shard_map/all_to_all | solution.py:401
  7.5 0.0 copy-start.4
  7.5 0.0 copy-start.5
  7.5 0.0 copy-start.6
  7.5 0.0 copy-done.8
  7.5 0.0 copy-done.9
  7.5 0.1 collective-permute-start
  7.6 1.1 %collective-permute-done = s32[4,128]{1,0:T(4,128)S(1)} collective-permute-done((s32[4,128]{1,0:T(4,128)S(1)}, s32[4,128]{1,0:T(4,128)S(1)}, u32[]{:S(2)}, u32[]{:S(2)}) %collective-permute-start) | collective-permute-done | bytes 2080 | tf_op jit(solution)/shard_map/ppermute | solution.py:379
  8.8 2.1 %collective-permute-start.1 = (s32[2,4,128]{2,1,0:T(4,128)S(1)}, s32[2,4,128]{2,1,0:T(4,128)S(1)}, u32[]{:S(2)}, u32[]{:S(2)}) collective-permute-start(s32[2,4,128]{2,1,0:T(4,128)S(1)} %pad_add_fusion.1), channel_id=1, source_target_pairs={{0,2},{2,0},{4,6},{6,4},{8,10},{10,8},{12,14},{14,12},{1,3},{3,1},... | collective-permute-start | bytes 12296 | tf_op jit(solution)/shard_map/ppermute | solution.py:382
  10.9 0.0 copy-done.7
  10.9 13.8 %collective-permute-done.1 = s32[2,4,128]{2,1,0:T(4,128)S(1)} collective-permute-done((s32[2,4,128]{2,1,0:T(4,128)S(1)}, s32[2,4,128]{2,1,0:T(4,128)S(1)}, u32[]{:S(2)}, u32[]{:S(2)}) %collective-permute-start.1) | collective-permute-done | bytes 4128 | tf_op jit(solution)/shard_map/ppermute | solution.py:382
  24.7 1.8 %collective-permute-start.2 = (s32[2,2,4,128]{3,2,1,0:T(4,128)S(1)}, s32[2,2,4,128]{3,2,1,0:T(4,128)S(1)}, u32[]{:S(2)}, u32[]{:S(2)}) collective-permute-start(s32[2,2,4,128]{3,2,1,0:T(4,128)S(1)} %get-tuple-element.13), channel_id=1, source_target_pairs={{0,4},{2,6},{4,0},{6,2},{8,12},{10,14},{12,8},{14,10},{1,5},{3,7},... | collective-permute-start | bytes 24584 | tf_op jit(solution)/shard_map/ppermute | solution.py:387
  26.5 0.0 copy-done
  26.5 0.0 copy-done.1
  26.5 0.0 copy-done.2
  26.5 0.0 copy-done.3
  26.5 0.7 launch.1
  27.3 2.1 %collective-permute-start.3 = (s32[2,2,4,128]{3,2,1,0:T(4,128)S(1)}, s32[2,2,4,128]{3,2,1,0:T(4,128)S(1)}, u32[]{:S(2)}, u32[]{:S(2)}) collective-permute-start(s32[2,2,4,128]{3,2,1,0:T(4,128)S(1)} %get-tuple-element.13), channel_id=1, source_target_pairs={{0,8},{2,10},{4,12},{6,14},{8,0},{10,2},{12,4},{14,6},{1,9},{3,11}... | collective-permute-start | bytes 24584 | tf_op jit(solution)/shard_map/ppermute | solution.py:387
  29.4 0.6 collective-permute-start.4
  30.0 12.9 %collective-permute-done.2 = s32[2,2,4,128]{3,2,1,0:T(4,128)S(1)} collective-permute-done((s32[2,2,4,128]{3,2,1,0:T(4,128)S(1)}, s32[2,2,4,128]{3,2,1,0:T(4,128)S(1)}, u32[]{:S(2)}, u32[]{:S(2)}) %collective-permute-start.2) | collective-permute-done | bytes 8224 | tf_op jit(solution)/shard_map/ppermute | solution.py:387
  42.8 13.5 %collective-permute-done.3 = s32[2,2,4,128]{3,2,1,0:T(4,128)S(1)} collective-permute-done((s32[2,2,4,128]{3,2,1,0:T(4,128)S(1)}, s32[2,2,4,128]{3,2,1,0:T(4,128)S(1)}, u32[]{:S(2)}, u32[]{:S(2)}) %collective-permute-start.3) | collective-permute-done | bytes 8224 | tf_op jit(solution)/shard_map/ppermute | solution.py:387
  56.3 0.0 collective-permute-done.4
  56.4 0.0 all-to-all-done.levels
  56.4 0.0 copy-done.4
  56.4 0.0 copy-done.5
  56.4 0.0 copy-done.6
  56.4 23.8 %march.1 = f32[256,128]{1,0:T(8,128)} custom-call(bf16[8,16,16,512]{3,2,1,0:T(8,128)(2,1)S(1)} %all-to-all-done.levels, s32[8,4,128]{2,1,0:T(4,128)S(1)} %dynamic-slice_bitcast_fusion.cells, f32[2,32,8,128]{3,2,1,0:T(8,128)S(1)} %get-tuple-element.9.launched, f32[2,32,8,128]{3,2,1,0:T(8,128)S(1)} %get-tuple-element.10.entered, ...), custom_call_target="tpu_custom_call" | custom-call | flops 25600000000 | bytes 4194304 | tf_op jit(solution)/shard_map/march/pallas_call | solution.py:374
  80.2 3.7 %all-to-all-start.1 = ((f32[16,16,128]{2,1,0:T(8,128)}), f32[16,16,128]{2,1,0:T(8,128)S(1)}, u32[]{:S(2)}, u32[]{:S(2)}) async-start(f32[16,16,128]{2,1,0:T(8,128)} %bitcast.9), calls=%async_computation.1 | async-start | bytes 262144 | tf_op jit(solution)/shard_map/all_to_all | solution.py:410
  84.0 0.2 convert_reduce_fusion
  84.2 7.7 %all-to-all-done.1 = f32[16,16,128]{2,1,0:T(8,128)S(1)} async-done(((f32[16,16,128]{2,1,0:T(8,128)}), f32[16,16,128]{2,1,0:T(8,128)S(1)}, u32[]{:S(2)}, u32[]{:S(2)}) %all-to-all-start.1) | async-done | bytes 131104 | tf_op jit(solution)/shard_map/all_to_all | solution.py:410
  91.9 0.7 broadcast_divide_fusion
  (14 shorter events, 0.1 us)
Async XLA Ops:
  0.0 7.5 %copy-start.8 = (s32[128,2]{0,1:T(2,128)S(1)}, s32[128,2]{0,1:T(2,128)}, u32[]{:S(2)}) copy-start(s32[128,2]{0,1:T(2,128)} %param.14) | copy-start | bytes 3076
  0.0 7.5 %copy-start.9 = (s32[128,2]{0,1:T(2,128)S(1)}, s32[128,2]{0,1:T(2,128)}, u32[]{:S(2)}) copy-start(s32[128,2]{0,1:T(2,128)} %param.13) | copy-start | bytes 3076
  0.0 10.9 %copy-start.7 = (f32[2,4096]{1,0:T(2,128)S(1)}, f32[2,4096]{1,0:T(2,128)}, u32[]{:S(2)}) copy-start(f32[2,4096]{1,0:T(2,128)} %param.12) | copy-start | bytes 98308
  0.0 26.5 %copy-start = (bf16[2,256,256]{2,1,0:T(8,128)(2,1)S(1)}, bf16[2,256,256]{2,1,0:T(8,128)(2,1)}, u32[]{:S(2)}) copy-start(bf16[2,256,256]{2,1,0:T(8,128)(2,1)} %constant.84.clone.w_inverse) | copy-start | bytes 786436
  0.0 26.5 %copy-start.1 = (bf16[2,256,256]{2,1,0:T(8,128)(2,1)S(1)}, bf16[2,256,256]{2,1,0:T(8,128)(2,1)}, u32[]{:S(2)}) copy-start(bf16[2,256,256]{2,1,0:T(8,128)(2,1)} %constant.83.clone.w_forward) | copy-start | bytes 786436
  0.0 26.5 %copy-start.2 = (f32[2,32,128]{2,1,0:T(8,128)S(1)}, f32[2,32,128]{2,1,0:T(8,128)}, u32[]{:S(2)}) copy-start(f32[2,32,128]{2,1,0:T(8,128)} %constant.86.clone.spread_table.refs_1_) | copy-start | bytes 98308
  0.0 26.5 %copy-start.3 = (f32[2,32,128]{2,1,0:T(8,128)S(1)}, f32[2,32,128]{2,1,0:T(8,128)}, u32[]{:S(2)}) copy-start(f32[2,32,128]{2,1,0:T(8,128)} %constant.85.clone.twiddle_table.refs_0_) | copy-start | bytes 98308
  0.0 56.3 %all-to-all-start = ((bf16[8,16,16,512]{3,2,1,0:T(8,128)(2,1)}), bf16[8,16,16,512]{3,2,1,0:T(8,128)(2,1)S(1)}, u32[]{:S(2)}, u32[]{:S(2)}) async-start(bf16[8,16,16,512]{3,2,1,0:T(8,128)(2,1)} %bitcast.21), calls=%async_computation | async-start | bytes 4194304 | tf_op jit(solution)/shard_map/all_to_all | solution.py:401
  7.5 48.9 %copy-start.4 = (bf16[128,128]{1,0:T(8,128)(2,1)S(1)}, bf16[128,128]{1,0:T(8,128)(2,1)}, u32[]{:S(2)}) copy-start(bf16[128,128]{1,0:T(8,128)(2,1)} %constant.89.clone.refs_4_) | copy-start | bytes 98308
  7.5 48.9 %copy-start.5 = (f32[32,128]{1,0:T(8,128)S(1)}, f32[32,128]{1,0:T(8,128)}, u32[]{:S(2)}) copy-start(f32[32,128]{1,0:T(8,128)} %constant.88.clone.refs_3_) | copy-start | bytes 49156
  7.5 48.9 %copy-start.6 = (f32[32,128]{1,0:T(8,128)S(1)}, f32[32,128]{1,0:T(8,128)}, u32[]{:S(2)}) copy-start(f32[32,128]{1,0:T(8,128)} %constant.87.clone.refs_2_) | copy-start | bytes 49156
  7.5 1.2 %collective-permute-start = (s32[4,128]{1,0:T(4,128)S(1)}, s32[4,128]{1,0:T(4,128)S(1)}, u32[]{:S(2)}, u32[]{:S(2)}) collective-permute-start(s32[4,128]{1,0:T(4,128)S(1)} %pad_add_fusion.2), channel_id=1, source_target_pairs={{0,1},{1,0},{2,3},{3,2},{4,5},{5,4},{6,7},{7,6},{8,9},{9,8},{10,11... | collective-permute-start | bytes 6152 | tf_op jit(solution)/shard_map/ppermute | solution.py:379
  8.8 15.9 %collective-permute-start.1 = (s32[2,4,128]{2,1,0:T(4,128)S(1)}, s32[2,4,128]{2,1,0:T(4,128)S(1)}, u32[]{:S(2)}, u32[]{:S(2)}) collective-permute-start(s32[2,4,128]{2,1,0:T(4,128)S(1)} %pad_add_fusion.1), channel_id=1, source_target_pairs={{0,2},{2,0},{4,6},{6,4},{8,10},{10,8},{12,14},{14,12},{1,3},{3,1},... | collective-permute-start | bytes 12296 | tf_op jit(solution)/shard_map/ppermute | solution.py:382
  24.7 18.1 %collective-permute-start.2 = (s32[2,2,4,128]{3,2,1,0:T(4,128)S(1)}, s32[2,2,4,128]{3,2,1,0:T(4,128)S(1)}, u32[]{:S(2)}, u32[]{:S(2)}) collective-permute-start(s32[2,2,4,128]{3,2,1,0:T(4,128)S(1)} %get-tuple-element.13), channel_id=1, source_target_pairs={{0,4},{2,6},{4,0},{6,2},{8,12},{10,14},{12,8},{14,10},{1,5},{3,7},... | collective-permute-start | bytes 24584 | tf_op jit(solution)/shard_map/ppermute | solution.py:387
  27.3 29.1 %collective-permute-start.3 = (s32[2,2,4,128]{3,2,1,0:T(4,128)S(1)}, s32[2,2,4,128]{3,2,1,0:T(4,128)S(1)}, u32[]{:S(2)}, u32[]{:S(2)}) collective-permute-start(s32[2,2,4,128]{3,2,1,0:T(4,128)S(1)} %get-tuple-element.13), channel_id=1, source_target_pairs={{0,8},{2,10},{4,12},{6,14},{8,0},{10,2},{12,4},{14,6},{1,9},{3,11}... | collective-permute-start | bytes 24584 | tf_op jit(solution)/shard_map/ppermute | solution.py:387
  29.4 27.0 %collective-permute-start.4 = (s32[2,2,4,128]{3,2,1,0:T(4,128)S(1)}, s32[2,2,4,128]{3,2,1,0:T(4,128)S(1)}, u32[]{:S(2)}, u32[]{:S(2)}) collective-permute-start(s32[2,2,4,128]{3,2,1,0:T(4,128)S(1)} %get-tuple-element.13), channel_id=1, source_target_pairs={{0,12},{2,14},{4,8},{6,10},{8,4},{10,6},{12,0},{14,2},{1,13},{3,15... | collective-permute-start | bytes 24584 | tf_op jit(solution)/shard_map/ppermute | solution.py:387
  80.2 11.7 %all-to-all-start.1 = ((f32[16,16,128]{2,1,0:T(8,128)}), f32[16,16,128]{2,1,0:T(8,128)S(1)}, u32[]{:S(2)}, u32[]{:S(2)}) async-start(f32[16,16,128]{2,1,0:T(8,128)} %bitcast.9), calls=%async_computation.1 | async-start | bytes 262144 | tf_op jit(solution)/shard_map/all_to_all | solution.py:410

commit v12 on v8

--- a/solution.py
+++ b/solution.py
@@ -23,6 +23,7 @@
 ABSORB_RATE = 0.05
 TERRAIN_ROWS = 4
 SUB = 8
+EARLY_SHARE = 0.6875
 
 F32 = jnp.float32
 BF16 = jnp.bfloat16
@@ -232,13 +233,17 @@
     )(start, *consts[:4])
 
 
-def march_kernel(own, levels, cells, launched, entered, w_forward, w_inverse, *refs):
-    tables, (bins, section, totals, wide, field, back, energy, power), wide_tables = refs[:4], refs[4:12], refs[12:]
+def march_kernel(begin, steps, own, last, levels, cells, launched, entered, totals_in, w_forward, w_inverse, *refs):
+    tables, (bins, section, totals), refs = refs[:4], refs[4:7], refs[7:]
+    if not last:
+        (left_back, left_field), refs = refs[:2], refs[2:]
+    (field, back, energy, power), wide_tables = refs[:4], refs[4:]
     for table, place in zip(tables, wide_tables):
         spread_rows(table, place)
     twiddle, spread, tilt, absorb = wide_tables
     sine, cosine = phase_polynomials()
-    sections, batch, steps, heights = levels.shape
+    heights = levels.shape[2]
+    batch = levels.shape[1] // steps
     halves = batch // SUB
     lane = lax.broadcasted_iota(jnp.int32, (SUB, LANES), 1)
     radial = lax.broadcasted_iota(jnp.int32, (SUB, LANES), 0)
@@ -256,7 +261,12 @@
             moved = []
             for jh in range(FOUR):
                 j = EIGHT * jh + jl
-                phi = wide[j, pl.ds(half * SUB * steps + t, SUB, stride=steps), :] + tilt[j]
+                place = j * LANES
+                raw = levels[
+                    place // heights, pl.ds(pl.multiple_of(t * batch, batch), batch),
+                    place % heights : place % heights + LANES,
+                ]
+                phi = raw.astype(F32)[half * SUB : (half + 1) * SUB] + tilt[j]
                 u = phi * phi
                 sin_poly, cos_poly = sine[-1], cosine[-1]
                 for a, b in zip(sine[-2::-1], cosine[-2::-1]):
@@ -289,7 +299,7 @@
         power[pl.ds(pl.multiple_of(t * batch + half * SUB, SUB), SUB), :] = row
 
     def ground_of(half, t):
-        row = cells[t // at_once, pl.ds(t % at_once, 1), :]
+        row = cells[(begin + t) // at_once, pl.ds((begin + t) % at_once, 1), :]
         my_lane = lane == section[0] * own + half * SUB + radial
         return jnp.sum(jnp.where(my_lane, row, 0), axis=1, keepdims=True)
 
@@ -309,28 +319,22 @@
         return carry
 
     power[...] = jnp.zeros_like(power)
-    for half in range(halves):
-        back[half] = launched[...]
-        field[half] = entered[...]
-    per_source = heights // LANES
-
-    def widen(source, carry):
-        for b in range(batch):
-            for c in range(per_source):
-                raw = levels[source, b, :, c * LANES : (c + 1) * LANES]
-                wide[source * per_source + c, b * steps : (b + 1) * steps, :] = raw.astype(F32)
-        return carry
-
-    lax.fori_loop(0, sections, widen, 0)
+    back[0] = launched[...]
+    for half in range(1, halves):
+        field[half] = entered[half - 1]
     energy[...] = jnp.zeros_like(energy)
     lax.fori_loop(0, steps, step, 0)
     binned(halves - 1, steps - 1)
+    if not last:
+        left_back[...] = back[0]
+        for half in range(1, halves):
+            left_field[half - 1] = field[half]
 
     lane = lax.broadcasted_iota(jnp.int32, (1, LANES), 1)
     fit = LANES // batch
     tile_rows = []
     for t in range(steps):
-        row = cells[t // at_once, at_once + t % at_once, :].reshape(1, LANES)
+        row = cells[(begin + t) // at_once, at_once + (begin + t) % at_once, :].reshape(1, LANES)
         row = pltpu.roll(row, lax.rem(batch * (t % fit) - section[0] * own + LANES, LANES), 1)
         row = jnp.where(lane % batch < own, row, -1)
         if t % fit == 0:
@@ -348,33 +352,96 @@
     gain = jnp.dot(hot, high, preferred_element_type=F32)
     gain += jnp.dot(hot, middle, preferred_element_type=F32)
     gain += jnp.dot(hot, low, preferred_element_type=F32)
-    totals[...] = gain
-
-
-def march(section, received, cells, launched, consts, tiles, own):
-    sections, batch, steps, heights = received.shape
+    totals[...] = totals_in[...] + gain
+
+
+def march(section, begin, steps, received, cells, state, totals, consts, own, last):
+    batch = received.shape[1] // steps
     halves = batch // SUB
     vmem = pl.BlockSpec(memory_space=pltpu.VMEM)
     smem = pl.BlockSpec(memory_space=pltpu.SMEM)
+    outputs = [jax.ShapeDtypeStruct(totals.shape, F32)]
+    if not last:
+        outputs += [jax.ShapeDtypeStruct(part.shape, F32) for part in state]
     call = pl.pallas_call(
-        functools.partial(march_kernel, own),
-        out_shape=jax.ShapeDtypeStruct((tiles, BINS), F32),
-        in_specs=[vmem] * 11 + [smem],
-        out_specs=vmem,
+        functools.partial(march_kernel, begin, steps, own, last),
+        out_shape=outputs,
+        in_specs=[vmem] * 12 + [smem],
+        out_specs=[vmem] * len(outputs),
         scratch_shapes=[
-            pltpu.VMEM((ROWS, batch * steps, LANES), F32),
             pltpu.VMEM((halves, 2, ROWS, SUB, LANES), F32),
             pltpu.VMEM((halves, 2, ROWS, SUB, LANES), F32),
             pltpu.VMEM((halves, ROWS * SUB, 2 * LANES), F32),
             pltpu.VMEM((-(-steps * batch // LANES) * LANES, BINS), F32),
         ] + [pltpu.VMEM((*table.shape[:-1], SUB, LANES), F32) for table in consts[2:6]],
-        compiler_params=pltpu.CompilerParams(vmem_limit_bytes=10 * 1024 * 1024 + 4 * H * batch * steps),
+        compiler_params=pltpu.CompilerParams(vmem_limit_bytes=12 * 1024 * 1024),
         cost_estimate=pl.CostEstimate(
             flops=steps * 1_600_000_000, bytes_accessed=4 * 1024 * 1024, transcendentals=0
         ),
+        input_output_aliases={4: 0} if last else {2: 1, 3: 2, 4: 0},
         name="march",
     )
-    return call(received, cells, *launched, *consts, section)
+    return call(received, cells, *state, totals, *consts, section)
+
+
+def turn_steps(block, rows, begin, end, out):
+    own, steps, heights = block.shape
+    batch = out.shape[0] // (end - begin)
+    for c in range(heights // LANES):
+        column = slice(c * LANES, (c + 1) * LANES)
+        for b in range(own):
+            rows[c, b * steps : (b + 1) * steps, :] = block[b, :, column].astype(F32)
+        for t in range(begin, end):
+            taken = rows[c, pl.ds(t, own, stride=steps), :].astype(BF16)
+            if own < batch:
+                taken = jnp.pad(taken, ((0, batch - own), (0, 0)))
+            out[(t - begin) * batch : (t - begin + 1) * batch, column] = taken
+
+
+def fill_slabs(begin, end, own, batch, owners, levels, slabs, blocks, turned, rows, sems):
+    arrive = [
+        pltpu.make_async_copy(levels.at[pl.ds(owner * own, own)], blocks.at[i], sems.at[0, i])
+        for i, owner in enumerate(owners)
+    ]
+    leave = [pltpu.make_async_copy(turned.at[i], slab, sems.at[1, i]) for i, slab in enumerate(slabs)]
+    for copy in arrive:
+        copy.start()
+    for i in range(len(slabs)):
+        arrive[i].wait()
+        turn_steps(blocks.at[i], rows, begin, end, turned.at[i])
+        leave[i].start()
+    for copy in leave:
+        copy.wait()
+
+
+def slab_scratch(number, own, steps, heights, count):
+    return [
+        pltpu.VMEM((number, own, steps, heights), BF16),
+        pltpu.VMEM((number, count, heights), BF16),
+        pltpu.VMEM((heights // LANES, own * steps, LANES), F32),
+        pltpu.SemaphoreType.DMA((2, number)),
+    ]
+
+
+def deal(levels, begin, end, sections, own, batch):
+    steps, heights = levels.shape[1:]
+    count = (end - begin) * batch
+    anywhere = pl.BlockSpec(memory_space=pl.ANY)
+
+    def kernel(levels, out, *scratch):
+        places = [out.at[i] for i in range(sections)]
+        fill_slabs(begin, end, own, batch, range(sections), levels, places, *scratch)
+
+    return pl.pallas_call(
+        kernel,
+        out_shape=jax.ShapeDtypeStruct((sections, count, heights), BF16),
+        in_specs=[anywhere],
+        out_specs=anywhere,
+        scratch_shapes=slab_scratch(sections, own, steps, heights, count),
+        compiler_params=pltpu.CompilerParams(vmem_limit_bytes=58 * 1024 * 1024),
+        cost_estimate=pl.CostEstimate(flops=1_000_000_000, bytes_accessed=4 * 1024 * 1024, transcendentals=0),
+        name="deal",
+    )(levels)
 
 
 def gather_small(value):
@@ -382,10 +449,13 @@
     other = lax.ppermute(value, "radial", [(0, 1), (1, 0)])
     pair = jnp.stack([jnp.where(radial == 0, value, other), jnp.where(radial == 0, other, value)])
     section = lax.axis_index("range")
+    next_pair = lax.ppermute(pair, "range", [(i, i ^ 1) for i in range(sections)])
+    even = section % 2 == 0
+    both = jnp.stack([jnp.where(even, pair, next_pair), jnp.where(even, next_pair, pair)])
     held = jnp.zeros((sections, *pair.shape), pair.dtype)
-    for d in range(sections):
-        part = lax.ppermute(pair, "range", [(i, i ^ d) for i in range(sections)]) if d else pair
-        held = lax.dynamic_update_index_in_dim(held, part, section ^ d, 0)
+    for d in range(0, sections, 2):
+        part = lax.ppermute(both, "range", [(i, i ^ d) for i in range(sections)]) if d else both
+        held = lax.dynamic_update_slice_in_dim(held, part, (section ^ d) // 2 * 2, 0)
     return held
 
 
@@ -397,14 +467,19 @@
     batch = -(-own // 16) * 16
     section = lax.axis_index("range").astype(jnp.int32).reshape(1)
 
-    received = refractivity.reshape(sections, own, steps, heights)
-    received = lax.all_to_all(received, "range", 0, 0, tiled=True)
-    received = jnp.pad(received, ((0, 0), (0, batch - own), (0, 0), (0, 0)))
+    middle = round(EARLY_SHARE * steps)
+    dealt = deal(refractivity, 0, middle, sections, own, batch)
+    refractivity, dealt = lax.optimization_barrier((refractivity, dealt))
+    early = lax.all_to_all(dealt, "range", 0, 0, tiled=True)
+    late = lax.all_to_all(deal(refractivity, middle, steps, sections, own, batch), "range", 0, 0, tiled=True)
     everyone = gather_small(jnp.concatenate([terrain.T, tile_map.T]))
     cells = lax.dynamic_index_in_dim(everyone, lax.axis_index("radial"), 1, keepdims=False)
     consts = [jnp.asarray(v) for v in tables()]
-    launched = launch(source.reshape(2, ROWS, LANES), consts)
-    totals = march(section, received, cells, launched, consts, TILE_DEV * owners, own)
+    launched, entered = launch(source.reshape(2, ROWS, LANES), consts)
+    state = (launched, jnp.stack([entered] * (batch // SUB - 1)))
+    totals = jnp.zeros((TILE_DEV * owners, BINS), F32)
+    totals, *state = march(section, 0, middle, early, cells, state, totals, consts, own, False)
+    (totals,) = march(section, middle, steps - middle, late, cells, state, totals, consts, own, True)
 
     everyone, totals = lax.optimization_barrier((everyone, totals))
     sent = lax.all_to_all(

time: 92.4 us -> 88.8 us (0.961)
  waiting for transfers between devices: 42.5 us -> 32.7 us
  Pallas kernels: 23.2 us -> 30.2 us
  starting transfers between devices: 25.1 us -> 23.4 us
    ppermute x7 -> x4, waiting for transfers between devices: 34.4 us -> 23 us  [the longest x3 17.7 us: gather_small(): lax.ppermute(both, 'range', [(i, i ^ d) for i in range(sections)])]
    pallas_call x1 -> x4, Pallas kernels: 22.5 us -> 29.5 us  [the longest x2 24.2 us: march(): return call(received, cells, *state, totals, *consts, section)]
    ppermute x7 -> x4, starting transfers between devices: 14 us -> 7.16 us  [the longest x3 5.08 us: gather_small(): lax.ppermute(both, 'range', [(i, i ^ d) for i in range(sections)])]
    all_to_all x1 -> x2, starting transfers between devices: 7.44 us -> 10.9 us  [the longest x1 7.29 us: local(): early = lax.all_to_all(dealt, 'range', 0, 0, tiled=True)]
    all_to_all x1, starting transfers between devices: 3.66 us -> 5.24 us  [local(): lax.all_to_all(totals.reshape(owners, TILE_DEV, BINS), ('range', 'radial'...]
  transfers between devices with their start and end apart: 10 -> 8, of which waited for: 6 -> 6; matrix products, arithmetic and copies ran while one was open for 0% -> 1% of each run, Pallas kernels for 1% -> 21%
where the time goes in v12:
time: 88.8 us; the launch traced here: 88.4 us
  waiting for transfers between devices  32.7 us (37%)
  Pallas kernels  30.2 us (34%)
  starting transfers between devices  23.4 us (26%)
  other arithmetic  0.96 us (1%)
    pallas_call x2, Pallas kernels, march(): return call(received, cells, *state, totals, *consts, section)  24.2 us
    ppermute x3, waiting for transfers between devices, gather_small(): lax.ppermute(both, 'range', [(i, i ^ d) for i in range(sections)])  17.7 us
    all_to_all x1, waiting for transfers between devices, local(): lax.all_to_all(totals.reshape(owners, TILE_DEV, BINS), ('range', 'radial'...  7.68 us
    all_to_all x1, starting transfers between devices, local(): early = lax.all_to_all(dealt, 'range', 0, 0, tiled=True)  7.29 us
    ppermute x1, waiting for transfers between devices, gather_small(): lax.ppermute(pair, 'range', [(i, i ^ 1) for i in range(sections)])  5.32 us
    pallas_call x2, Pallas kernels, deal(): pl.pallas_call(kernel, out_shape=jax.ShapeDtypeStruct((sections, count, h...  5.32 us
    all_to_all x1, starting transfers between devices, local(): lax.all_to_all(totals.reshape(owners, TILE_DEV, BINS), ('range', 'radial'...  5.24 us
    ppermute x3, starting transfers between devices, gather_small(): lax.ppermute(both, 'range', [(i, i ^ d) for i in range(sections)])  5.08 us
  transfers between devices with their start and end apart: 8, of which 6 were waited for; matrix products, arithmetic and copies ran while one was open for 1% of the time, Pallas kernels for 21%

profile of v12, /device:TPU:0, one launch (start us, length us, event | category | flops | bytes accessed | tf_op | source)
XLA Modules:
  0.0 88.4 jit_solution(2260543246770440631)
XLA Ops:
  0.0 3.0 %deal.2 = bf16[8,176,512]{2,1,0:T(8,128)(2,1)} custom-call(bf16[128,16,512]{2,1,0:T(8,128)(2,1)} %levels.2), custom_call_target="tpu_custom_call" | custom-call | flops 1000000000 | bytes 4194304 | tf_op jit(solution)/shard_map/deal/pallas_call | solution.py:435
  3.0 0.0 copy-start.8
  3.0 0.0 copy-start.9
  3.0 7.3 %all-to-all-start.1 = ((bf16[8,176,512]{2,1,0:T(8,128)(2,1)}), bf16[8,176,512]{2,1,0:T(8,128)(2,1)S(1)}, u32[]{:S(2)}, u32[]{:S(2)}) async-start(bf16[8,176,512]{2,1,0:T(8,128)(2,1)} %deal.2), calls=%async_computation.1 | async-start | bytes 2883584 | tf_op jit(solution)/shard_map/all_to_all | solution.py:473
  10.3 0.0 copy-done.8
  10.3 0.0 copy-done.9
  10.3 0.1 collective-permute-start
  10.4 1.1 %collective-permute-done = s32[4,128]{1,0:T(4,128)S(1)} collective-permute-done((s32[4,128]{1,0:T(4,128)S(1)}, s32[4,128]{1,0:T(4,128)S(1)}, u32[]{:S(2)}, u32[]{:S(2)}) %collective-permute-start) | collective-permute-done | bytes 2080 | tf_op jit(solution)/shard_map/ppermute | solution.py:449
  11.5 0.0 copy-start.7
  11.6 0.0 copy-start
  11.6 0.0 copy-start.1
  11.6 0.0 copy-start.3
  11.6 0.0 copy-start.4
  11.6 2.1 %collective-permute-start.1 = (s32[2,4,128]{2,1,0:T(4,128)S(1)}, s32[2,4,128]{2,1,0:T(4,128)S(1)}, u32[]{:S(2)}, u32[]{:S(2)}) collective-permute-start(s32[2,4,128]{2,1,0:T(4,128)S(1)} %pad_add_fusion.1), channel_id=1, source_target_pairs={{0,2},{2,0},{4,6},{6,4},{8,10},{10,8},{12,14},{14,12},{1,3},{3,1},... | collective-permute-start | bytes 12296 | tf_op jit(solution)/shard_map/ppermute | solution.py:452
  13.7 2.4 %deal.3 = bf16[8,80,512]{2,1,0:T(8,128)(2,1)} custom-call(bf16[128,16,512]{2,1,0:T(8,128)(2,1)} %levels.2), custom_call_target="tpu_custom_call" | custom-call | flops 1000000000 | bytes 4194304 | tf_op jit(solution)/shard_map/deal/pallas_call | solution.py:435
  16.1 0.0 copy-done.7
  16.1 5.3 %collective-permute-done.1 = s32[2,4,128]{2,1,0:T(4,128)S(1)} collective-permute-done((s32[2,4,128]{2,1,0:T(4,128)S(1)}, s32[2,4,128]{2,1,0:T(4,128)S(1)}, u32[]{:S(2)}, u32[]{:S(2)}) %collective-permute-start.1) | collective-permute-done | bytes 4128 | tf_op jit(solution)/shard_map/ppermute | solution.py:452
  21.5 2.5 %collective-permute-start.2 = (s32[2,2,4,128]{3,2,1,0:T(4,128)S(1)}, s32[2,2,4,128]{3,2,1,0:T(4,128)S(1)}, u32[]{:S(2)}, u32[]{:S(2)}) collective-permute-start(s32[2,2,4,128]{3,2,1,0:T(4,128)S(1)} %get-tuple-element.23), channel_id=1, source_target_pairs={{0,4},{2,6},{4,0},{6,2},{8,12},{10,14},{12,8},{14,10},{1,5},{3,7},... | collective-permute-start | bytes 24584 | tf_op jit(solution)/shard_map/ppermute | solution.py:457
  24.0 0.0 copy-done
  24.0 0.0 copy-done.1
  24.0 0.0 copy-done.3
  24.0 0.0 copy-done.4
  24.0 0.7 launch.1
  24.7 0.0 copy-start.2
  24.7 0.0 copy-start.5
  24.7 0.0 copy-start.6
  24.8 2.1 %collective-permute-start.3 = (s32[2,2,4,128]{3,2,1,0:T(4,128)S(1)}, s32[2,2,4,128]{3,2,1,0:T(4,128)S(1)}, u32[]{:S(2)}, u32[]{:S(2)}) collective-permute-start(s32[2,2,4,128]{3,2,1,0:T(4,128)S(1)} %get-tuple-element.23), channel_id=1, source_target_pairs={{0,8},{2,10},{4,12},{6,14},{8,0},{10,2},{12,4},{14,6},{1,9},{3,11}... | collective-permute-start | bytes 24584 | tf_op jit(solution)/shard_map/ppermute | solution.py:457
  27.0 0.4 collective-permute-start.4
  27.4 7.3 %collective-permute-done.2 = s32[2,2,4,128]{3,2,1,0:T(4,128)S(1)} collective-permute-done((s32[2,2,4,128]{3,2,1,0:T(4,128)S(1)}, s32[2,2,4,128]{3,2,1,0:T(4,128)S(1)}, u32[]{:S(2)}, u32[]{:S(2)}) %collective-permute-start.2) | collective-permute-done | bytes 8224 | tf_op jit(solution)/shard_map/ppermute | solution.py:457
  34.6 10.5 %collective-permute-done.3 = s32[2,2,4,128]{3,2,1,0:T(4,128)S(1)} collective-permute-done((s32[2,2,4,128]{3,2,1,0:T(4,128)S(1)}, s32[2,2,4,128]{3,2,1,0:T(4,128)S(1)}, u32[]{:S(2)}, u32[]{:S(2)}) %collective-permute-start.3) | collective-permute-done | bytes 8224 | tf_op jit(solution)/shard_map/ppermute | solution.py:457
  45.1 0.0 collective-permute-done.4
  45.1 0.0 all-to-all-done.1.levels
  45.1 3.6 %all-to-all-start = ((bf16[8,80,512]{2,1,0:T(8,128)(2,1)}), bf16[8,80,512]{2,1,0:T(8,128)(2,1)S(1)}, u32[]{:S(2)}, u32[]{:S(2)}) async-start(bf16[8,80,512]{2,1,0:T(8,128)(2,1)} %deal.3), calls=%async_computation | async-start | bytes 1310720 | tf_op jit(solution)/shard_map/all_to_all | solution.py:474
  48.8 0.7 broadcast_in_dim.9.totals_in
  49.4 0.0 copy-done.2
  49.4 0.0 copy-done.5
  49.4 0.0 copy-done.6
  49.4 15.9 %march.2 = (f32[256,128]{1,0:T(8,128)}, f32[2,32,8,128]{3,2,1,0:T(8,128)S(1)}, f32[1,2,32,8,128]{4,3,2,1,0:T(8,128)S(1)}) custom-call(bf16[8,176,512]{2,1,0:T(8,128)(2,1)S(1)} %all-to-all-done.1.levels, s32[8,4,128]{2,1,0:T(4,128)S(1)} %dynamic-slice_bitcast_fusion.cells, ...), custom_call_target="tpu_custom_call", output_to_operand_aliasing={{1}: (2, {}), {2}: (3, {}), {0}: (4, {})} | custom-call | flops 17600000000 | bytes 4194304 | tf_op jit(solution)/shard_map/march/pallas_call | solution.py:384
  65.3 0.9 all-to-all-done.levels
  66.2 8.3 %march.3 = f32[256,128]{1,0:T(8,128)} custom-call(bf16[8,80,512]{2,1,0:T(8,128)(2,1)S(1)} %all-to-all-done.levels, s32[8,4,128]{2,1,0:T(4,128)S(1)} %dynamic-slice_bitcast_fusion.cells, f32[2,32,8,128]{3,2,1,0:T(8,128)S(1)} %get-tuple-element.18.launched, f32[1,2,32,8,128]{4,3,2,1,0:T(8,128)S(1)} %get-tuple-element.19.entered, ...), custom_call_target="tpu_custom_call", output_to_operand_aliasing={{}: (4, {})} | custom-call | flops 8000000000 | bytes 4194304 | tf_op jit(solution)/shard_map/march/pallas_call | solution.py:384
  74.5 5.2 %all-to-all-start.2 = ((f32[16,16,128]{2,1,0:T(8,128)}), f32[16,16,128]{2,1,0:T(8,128)S(1)}, u32[]{:S(2)}, u32[]{:S(2)}) async-start(f32[16,16,128]{2,1,0:T(8,128)} %bitcast.9), calls=%async_computation.2 | async-start | bytes 262144 | tf_op jit(solution)/shard_map/all_to_all | solution.py:485
  79.8 0.2 convert_reduce_fusion
  80.0 7.7 %all-to-all-done.2 = f32[16,16,128]{2,1,0:T(8,128)S(1)} async-done(((f32[16,16,128]{2,1,0:T(8,128)}), f32[16,16,128]{2,1,0:T(8,128)S(1)}, u32[]{:S(2)}, u32[]{:S(2)}) %all-to-all-start.2) | async-done | bytes 131104 | tf_op jit(solution)/shard_map/all_to_all | solution.py:485
  87.7 0.7 broadcast_divide_fusion
  (14 shorter events, 0.1 us)
Async XLA Ops:
  3.0 7.3 %copy-start.8 = (s32[128,2]{0,1:T(2,128)S(1)}, s32[128,2]{0,1:T(2,128)}, u32[]{:S(2)}) copy-start(s32[128,2]{0,1:T(2,128)} %param.14) | copy-start | bytes 3076
  3.0 7.3 %copy-start.9 = (s32[128,2]{0,1:T(2,128)S(1)}, s32[128,2]{0,1:T(2,128)}, u32[]{:S(2)}) copy-start(s32[128,2]{0,1:T(2,128)} %param.13) | copy-start | bytes 3076
  3.0 42.1 %all-to-all-start.1 = ((bf16[8,176,512]{2,1,0:T(8,128)(2,1)}), bf16[8,176,512]{2,1,0:T(8,128)(2,1)S(1)}, u32[]{:S(2)}, u32[]{:S(2)}) async-start(bf16[8,176,512]{2,1,0:T(8,128)(2,1)} %deal.2), calls=%async_computation.1 | async-start | bytes 2883584 | tf_op jit(solution)/shard_map/all_to_all | solution.py:473
  10.3 1.2 %collective-permute-start = (s32[4,128]{1,0:T(4,128)S(1)}, s32[4,128]{1,0:T(4,128)S(1)}, u32[]{:S(2)}, u32[]{:S(2)}) collective-permute-start(s32[4,128]{1,0:T(4,128)S(1)} %pad_add_fusion.2), channel_id=1, source_target_pairs={{0,1},{1,0},{2,3},{3,2},{4,5},{5,4},{6,7},{7,6},{8,9},{9,8},{10,11... | collective-permute-start | bytes 6152 | tf_op jit(solution)/shard_map/ppermute | solution.py:449
  11.5 4.5 %copy-start.7 = (f32[2,4096]{1,0:T(2,128)S(1)}, f32[2,4096]{1,0:T(2,128)}, u32[]{:S(2)}) copy-start(f32[2,4096]{1,0:T(2,128)} %param.12) | copy-start | bytes 98308
  11.6 12.5 %copy-start = (bf16[2,256,256]{2,1,0:T(8,128)(2,1)S(1)}, bf16[2,256,256]{2,1,0:T(8,128)(2,1)}, u32[]{:S(2)}) copy-start(bf16[2,256,256]{2,1,0:T(8,128)(2,1)} %constant.84.clone.w_forward) | copy-start | bytes 786436
  11.6 12.4 %copy-start.1 = (bf16[2,256,256]{2,1,0:T(8,128)(2,1)S(1)}, bf16[2,256,256]{2,1,0:T(8,128)(2,1)}, u32[]{:S(2)}) copy-start(bf16[2,256,256]{2,1,0:T(8,128)(2,1)} %constant.85.clone.w_inverse) | copy-start | bytes 786436
  11.6 12.4 %copy-start.3 = (f32[2,32,128]{2,1,0:T(8,128)S(1)}, f32[2,32,128]{2,1,0:T(8,128)}, u32[]{:S(2)}) copy-start(f32[2,32,128]{2,1,0:T(8,128)} %constant.86.clone.twiddle_table.refs_0_) | copy-start | bytes 98308
  11.6 12.4 %copy-start.4 = (f32[2,32,128]{2,1,0:T(8,128)S(1)}, f32[2,32,128]{2,1,0:T(8,128)}, u32[]{:S(2)}) copy-start(f32[2,32,128]{2,1,0:T(8,128)} %constant.87.clone.spread_table.refs_1_) | copy-start | bytes 98308
  11.6 9.8 %collective-permute-start.1 = (s32[2,4,128]{2,1,0:T(4,128)S(1)}, s32[2,4,128]{2,1,0:T(4,128)S(1)}, u32[]{:S(2)}, u32[]{:S(2)}) collective-permute-start(s32[2,4,128]{2,1,0:T(4,128)S(1)} %pad_add_fusion.1), channel_id=1, source_target_pairs={{0,2},{2,0},{4,6},{6,4},{8,10},{10,8},{12,14},{14,12},{1,3},{3,1},... | collective-permute-start | bytes 12296 | tf_op jit(solution)/shard_map/ppermute | solution.py:452
  21.5 13.2 %collective-permute-start.2 = (s32[2,2,4,128]{3,2,1,0:T(4,128)S(1)}, s32[2,2,4,128]{3,2,1,0:T(4,128)S(1)}, u32[]{:S(2)}, u32[]{:S(2)}) collective-permute-start(s32[2,2,4,128]{3,2,1,0:T(4,128)S(1)} %get-tuple-element.23), channel_id=1, source_target_pairs={{0,4},{2,6},{4,0},{6,2},{8,12},{10,14},{12,8},{14,10},{1,5},{3,7},... | collective-permute-start | bytes 24584 | tf_op jit(solution)/shard_map/ppermute | solution.py:457
  24.7 24.7 %copy-start.2 = (bf16[256,128]{1,0:T(8,128)(2,1)S(1)}, bf16[256,128]{1,0:T(8,128)(2,1)}, u32[]{:S(2)}) copy-start(bf16[256,128]{1,0:T(8,128)(2,1)} %constant.90.clone.refs_4_) | copy-start | bytes 196612
  24.7 24.7 %copy-start.5 = (f32[32,128]{1,0:T(8,128)S(1)}, f32[32,128]{1,0:T(8,128)}, u32[]{:S(2)}) copy-start(f32[32,128]{1,0:T(8,128)} %constant.88.clone.refs_2_) | copy-start | bytes 49156
  24.7 24.7 %copy-start.6 = (f32[32,128]{1,0:T(8,128)S(1)}, f32[32,128]{1,0:T(8,128)}, u32[]{:S(2)}) copy-start(f32[32,128]{1,0:T(8,128)} %constant.89.clone.refs_3_) | copy-start | bytes 49156
  24.8 20.3 %collective-permute-start.3 = (s32[2,2,4,128]{3,2,1,0:T(4,128)S(1)}, s32[2,2,4,128]{3,2,1,0:T(4,128)S(1)}, u32[]{:S(2)}, u32[]{:S(2)}) collective-permute-start(s32[2,2,4,128]{3,2,1,0:T(4,128)S(1)} %get-tuple-element.23), channel_id=1, source_target_pairs={{0,8},{2,10},{4,12},{6,14},{8,0},{10,2},{12,4},{14,6},{1,9},{3,11}... | collective-permute-start | bytes 24584 | tf_op jit(solution)/shard_map/ppermute | solution.py:457
  27.0 18.1 %collective-permute-start.4 = (s32[2,2,4,128]{3,2,1,0:T(4,128)S(1)}, s32[2,2,4,128]{3,2,1,0:T(4,128)S(1)}, u32[]{:S(2)}, u32[]{:S(2)}) collective-permute-start(s32[2,2,4,128]{3,2,1,0:T(4,128)S(1)} %get-tuple-element.23), channel_id=1, source_target_pairs={{0,12},{2,14},{4,8},{6,10},{8,4},{10,6},{12,0},{14,2},{1,13},{3,15... | collective-permute-start | bytes 24584 | tf_op jit(solution)/shard_map/ppermute | solution.py:457
  45.1 21.0 %all-to-all-start = ((bf16[8,80,512]{2,1,0:T(8,128)(2,1)}), bf16[8,80,512]{2,1,0:T(8,128)(2,1)S(1)}, u32[]{:S(2)}, u32[]{:S(2)}) async-start(bf16[8,80,512]{2,1,0:T(8,128)(2,1)} %deal.3), calls=%async_computation | async-start | bytes 1310720 | tf_op jit(solution)/shard_map/all_to_all | solution.py:474
  74.5 13.2 %all-to-all-start.2 = ((f32[16,16,128]{2,1,0:T(8,128)}), f32[16,16,128]{2,1,0:T(8,128)S(1)}, u32[]{:S(2)}, u32[]{:S(2)}) async-start(f32[16,16,128]{2,1,0:T(8,128)} %bitcast.9), calls=%async_computation.2 | async-start | bytes 262144 | tf_op jit(solution)/shard_map/all_to_all | solution.py:485

commit v13 on v12

--- a/solution.py
+++ b/solution.py
@@ -233,7 +233,10 @@
     )(start, *consts[:4])
 
 
-def march_kernel(begin, steps, own, last, levels, cells, launched, entered, totals_in, w_forward, w_inverse, *refs):
+def march_kernel(begin, steps, own, last, levels, cells, launched, entered, *refs):
+    if begin > 0:
+        totals_in, refs = refs[0], refs[1:]
+    (w_forward, w_inverse), refs = refs[:2], refs[2:]
     tables, (bins, section, totals), refs = refs[:4], refs[4:7], refs[7:]
     if not last:
         (left_back, left_field), refs = refs[:2], refs[2:]
@@ -258,7 +261,7 @@
                     cmul_const((back[half, 0, ql * EIGHT + jl], back[half, 1, ql * EIGHT + jl]), (c, -s))
                 )
             column = dft4(column, 1)
-            moved = []
+            moved, value = [], []
             for jh in range(FOUR):
                 j = EIGHT * jh + jl
                 place = j * LANES
@@ -284,18 +287,18 @@
                 if j < TERRAIN_ROWS:
                     open_air = lane + j * LANES >= ground
                     re, im = jnp.where(open_air, re, 0.0), jnp.where(open_air, im, 0.0)
-                value = re * re + im * im
-                high = value.astype(BF16).astype(F32)
-                energy[half, j * SUB : (j + 1) * SUB, :LANES] = high
-                energy[half, j * SUB : (j + 1) * SUB, LANES:] = value - high
+                value.append(re * re + im * im)
                 moved.append((re, im))
             enter(field.at[half], moved, jl)
+            place = FOUR * jl * SUB
+            energy[half, place : place + FOUR * SUB, :] = jnp.concatenate(split(jnp.concatenate(value)), axis=1)
 
     def binned(half, t):
-        summed = jnp.dot(energy[half].astype(BF16), bins[...], preferred_element_type=F32)
+        summed = jnp.dot(energy[half], bins[...], preferred_element_type=F32)
         row = summed[:SUB]
-        for j in range(1, ROWS):
-            row = jnp.where(lane // (LANES // BIN) == j, summed[j * SUB : (j + 1) * SUB], row)
+        for i in range(1, ROWS):
+            j = i // FOUR + EIGHT * (i % FOUR)
+            row = jnp.where(lane // (LANES // BIN) == j, summed[i * SUB : (i + 1) * SUB], row)
         power[pl.ds(pl.multiple_of(t * batch + half * SUB, SUB), SUB), :] = row
 
     def ground_of(half, t):
@@ -313,6 +316,10 @@
             piece()
         leave(back.at[moving], product, twiddle)
 
+    def last_turn(t, resting, before):
+        rotate(resting, t, ground_of(resting, t), range(EIGHT))
+        binned(before, t)
+
     def step(t, carry):
         for half in range(halves):
             turn_of(t, half, (half + 1) % halves)
@@ -323,7 +330,12 @@
     for half in range(1, halves):
         field[half] = entered[half - 1]
     energy[...] = jnp.zeros_like(energy)
-    lax.fori_loop(0, steps, step, 0)
+    whole_steps = steps - 1 if last else steps
+    lax.fori_loop(0, whole_steps, step, 0)
+    if last:
+        for half in range(halves - 1):
+            turn_of(whole_steps, half, half + 1)
+        last_turn(whole_steps, halves - 1, halves - 2)
     binned(halves - 1, steps - 1)
     if not last:
         left_back[...] = back[0]
@@ -352,36 +364,36 @@
     gain = jnp.dot(hot, high, preferred_element_type=F32)
     gain += jnp.dot(hot, middle, preferred_element_type=F32)
     gain += jnp.dot(hot, low, preferred_element_type=F32)
-    totals[...] = totals_in[...] + gain
-
-
-def march(section, begin, steps, received, cells, state, totals, consts, own, last):
+    totals[...] = gain if begin == 0 else totals_in[...] + gain
+
+
+def march(section, begin, steps, received, cells, state, totals, consts, tiles, own, last):
     batch = received.shape[1] // steps
     halves = batch // SUB
     vmem = pl.BlockSpec(memory_space=pltpu.VMEM)
     smem = pl.BlockSpec(memory_space=pltpu.SMEM)
-    outputs = [jax.ShapeDtypeStruct(totals.shape, F32)]
+    outputs = [jax.ShapeDtypeStruct((tiles, BINS), F32)]
     if not last:
         outputs += [jax.ShapeDtypeStruct(part.shape, F32) for part in state]
     call = pl.pallas_call(
         functools.partial(march_kernel, begin, steps, own, last),
         out_shape=outputs,
-        in_specs=[vmem] * 12 + [smem],
+        in_specs=[vmem] * (11 + len(totals)) + [smem],
         out_specs=[vmem] * len(outputs),
         scratch_shapes=[
             pltpu.VMEM((halves, 2, ROWS, SUB, LANES), F32),
             pltpu.VMEM((halves, 2, ROWS, SUB, LANES), F32),
-            pltpu.VMEM((halves, ROWS * SUB, 2 * LANES), F32),
+            pltpu.VMEM((halves, ROWS * SUB, 2 * LANES), BF16),
             pltpu.VMEM((-(-steps * batch // LANES) * LANES, BINS), F32),
         ] + [pltpu.VMEM((*table.shape[:-1], SUB, LANES), F32) for table in consts[2:6]],
         compiler_params=pltpu.CompilerParams(vmem_limit_bytes=12 * 1024 * 1024),
         cost_estimate=pl.CostEstimate(
             flops=steps * 1_600_000_000, bytes_accessed=4 * 1024 * 1024, transcendentals=0
         ),
-        input_output_aliases={4: 0} if last else {2: 1, 3: 2, 4: 0},
+        input_output_aliases={4: 0} if last else {2: 1, 3: 2},
         name="march",
     )
-    return call(received, cells, *state, totals, *consts, section)
+    return call(received, cells, *state, *totals, *consts, section)
 
 
 def turn_steps(block, rows, begin, end, out):
@@ -477,9 +489,9 @@
     consts = [jnp.asarray(v) for v in tables()]
     launched, entered = launch(source.reshape(2, ROWS, LANES), consts)
     state = (launched, jnp.stack([entered] * (batch // SUB - 1)))
-    totals = jnp.zeros((TILE_DEV * owners, BINS), F32)
-    totals, *state = march(section, 0, middle, early, cells, state, totals, consts, own, False)
-    (totals,) = march(section, middle, steps - middle, late, cells, state, totals, consts, own, True)
+    tiles = TILE_DEV * owners
+    totals, *state = march(section, 0, middle, early, cells, state, [], consts, tiles, own, False)
+    (totals,) = march(section, middle, steps - middle, late, cells, state, [totals], consts, tiles, own, True)
 
     everyone, totals = lax.optimization_barrier((everyone, totals))
     sent = lax.all_to_all(

time: 88.8 us -> 87 us (0.980)
  starting transfers between devices: 23.4 us -> 21.9 us
  waiting for transfers between devices: 32.7 us -> 34.2 us
  Pallas kernels: 30.2 us -> 29 us
    all_to_all x1, starting transfers between devices: 5.24 us -> 3.74 us  [local(): lax.all_to_all(totals.reshape(owners, TILE_DEV, BINS), ('range', 'radial'...]
    all_to_all x1, waiting for transfers between devices: 0.87 us -> 2.36 us  [local(): lax.all_to_all(deal(refractivity, middle, steps, sections, own, batch), '...]
    pallas_call x2, Pallas kernels: 24.2 us -> 23 us  [march(): return call(received, cells, *state, *totals, *consts, section)]
  transfers between devices with their start and end apart: 8 -> 8, of which waited for: 6 -> 6; matrix products, arithmetic and copies ran while one was open for 1% -> 0% of each run, Pallas kernels for 21% -> 21%
where the time goes in v13:
time: 87 us; the launch traced here: 86.6 us
  waiting for transfers between devices  34.2 us (39%)
  Pallas kernels  29 us (33%)
  starting transfers between devices  21.9 us (25%)
  other arithmetic  0.96 us (1%)
    pallas_call x2, Pallas kernels, march(): return call(received, cells, *state, *totals, *consts, section)  23 us
    ppermute x3, waiting for transfers between devices, gather_small(): lax.ppermute(both, 'range', [(i, i ^ d) for i in range(sections)])  17.7 us
    all_to_all x1, waiting for transfers between devices, local(): lax.all_to_all(totals.reshape(owners, TILE_DEV, BINS), ('range', 'radial'...  7.68 us
    all_to_all x1, starting transfers between devices, local(): early = lax.all_to_all(dealt, 'range', 0, 0, tiled=True)  7.29 us
    ppermute x1, waiting for transfers between devices, gather_small(): lax.ppermute(pair, 'range', [(i, i ^ 1) for i in range(sections)])  5.32 us
    pallas_call x2, Pallas kernels, deal(): pl.pallas_call(kernel, out_shape=jax.ShapeDtypeStruct((sections, count, h...  5.32 us
    ppermute x3, starting transfers between devices, gather_small(): lax.ppermute(both, 'range', [(i, i ^ d) for i in range(sections)])  5.08 us
    all_to_all x1, starting transfers between devices, local(): lax.all_to_all(totals.reshape(owners, TILE_DEV, BINS), ('range', 'radial'...  3.74 us
  transfers between devices with their start and end apart: 8, of which 6 were waited for; matrix products, arithmetic and copies ran while one was open for 0% of the time, Pallas kernels for 21%

profile of v13, /device:TPU:0, one launch (start us, length us, event | category | flops | bytes accessed | tf_op | source)
XLA Modules:
  0.0 86.6 jit_solution(13462837912688130722)
XLA Ops:
  0.0 3.0 %deal.2 = bf16[8,176,512]{2,1,0:T(8,128)(2,1)} custom-call(bf16[128,16,512]{2,1,0:T(8,128)(2,1)} %levels.2), custom_call_target="tpu_custom_call" | custom-call | flops 1000000000 | bytes 4194304 | tf_op jit(solution)/shard_map/deal/pallas_call | solution.py:447
  3.0 0.0 copy-start.8
  3.0 0.0 copy-start.9
  3.0 7.3 %all-to-all-start.1 = ((bf16[8,176,512]{2,1,0:T(8,128)(2,1)}), bf16[8,176,512]{2,1,0:T(8,128)(2,1)S(1)}, u32[]{:S(2)}, u32[]{:S(2)}) async-start(bf16[8,176,512]{2,1,0:T(8,128)(2,1)} %deal.2), calls=%async_computation.1 | async-start | bytes 2883584 | tf_op jit(solution)/shard_map/all_to_all | solution.py:485
  10.3 0.0 copy-done.8
  10.3 0.0 copy-done.9
  10.3 0.1 collective-permute-start
  10.4 1.1 %collective-permute-done = s32[4,128]{1,0:T(4,128)S(1)} collective-permute-done((s32[4,128]{1,0:T(4,128)S(1)}, s32[4,128]{1,0:T(4,128)S(1)}, u32[]{:S(2)}, u32[]{:S(2)}) %collective-permute-start) | collective-permute-done | bytes 2080 | tf_op jit(solution)/shard_map/ppermute | solution.py:461
  11.5 0.0 copy-start.7
  11.6 0.0 copy-start
  11.6 0.0 copy-start.1
  11.6 0.0 copy-start.3
  11.6 0.0 copy-start.4
  11.6 2.1 %collective-permute-start.1 = (s32[2,4,128]{2,1,0:T(4,128)S(1)}, s32[2,4,128]{2,1,0:T(4,128)S(1)}, u32[]{:S(2)}, u32[]{:S(2)}) collective-permute-start(s32[2,4,128]{2,1,0:T(4,128)S(1)} %pad_add_fusion.1), channel_id=1, source_target_pairs={{0,2},{2,0},{4,6},{6,4},{8,10},{10,8},{12,14},{14,12},{1,3},{3,1},... | collective-permute-start | bytes 12296 | tf_op jit(solution)/shard_map/ppermute | solution.py:464
  13.7 2.4 %deal.3 = bf16[8,80,512]{2,1,0:T(8,128)(2,1)} custom-call(bf16[128,16,512]{2,1,0:T(8,128)(2,1)} %levels.2), custom_call_target="tpu_custom_call" | custom-call | flops 1000000000 | bytes 4194304 | tf_op jit(solution)/shard_map/deal/pallas_call | solution.py:447
  16.1 0.0 copy-done.7
  16.1 5.3 %collective-permute-done.1 = s32[2,4,128]{2,1,0:T(4,128)S(1)} collective-permute-done((s32[2,4,128]{2,1,0:T(4,128)S(1)}, s32[2,4,128]{2,1,0:T(4,128)S(1)}, u32[]{:S(2)}, u32[]{:S(2)}) %collective-permute-start.1) | collective-permute-done | bytes 4128 | tf_op jit(solution)/shard_map/ppermute | solution.py:464
  21.5 2.5 %collective-permute-start.2 = (s32[2,2,4,128]{3,2,1,0:T(4,128)S(1)}, s32[2,2,4,128]{3,2,1,0:T(4,128)S(1)}, u32[]{:S(2)}, u32[]{:S(2)}) collective-permute-start(s32[2,2,4,128]{3,2,1,0:T(4,128)S(1)} %get-tuple-element.23), channel_id=1, source_target_pairs={{0,4},{2,6},{4,0},{6,2},{8,12},{10,14},{12,8},{14,10},{1,5},{3,7},... | collective-permute-start | bytes 24584 | tf_op jit(solution)/shard_map/ppermute | solution.py:469
  24.0 0.0 copy-done
  24.0 0.0 copy-done.1
  24.0 0.0 copy-done.3
  24.0 0.0 copy-done.4
  24.0 0.7 launch.1
  24.7 0.0 copy-start.2
  24.7 0.0 copy-start.5
  24.7 0.0 copy-start.6
  24.8 2.1 %collective-permute-start.3 = (s32[2,2,4,128]{3,2,1,0:T(4,128)S(1)}, s32[2,2,4,128]{3,2,1,0:T(4,128)S(1)}, u32[]{:S(2)}, u32[]{:S(2)}) collective-permute-start(s32[2,2,4,128]{3,2,1,0:T(4,128)S(1)} %get-tuple-element.23), channel_id=1, source_target_pairs={{0,8},{2,10},{4,12},{6,14},{8,0},{10,2},{12,4},{14,6},{1,9},{3,11}... | collective-permute-start | bytes 24584 | tf_op jit(solution)/shard_map/ppermute | solution.py:469
  27.0 0.4 collective-permute-start.4
  27.4 7.3 %collective-permute-done.2 = s32[2,2,4,128]{3,2,1,0:T(4,128)S(1)} collective-permute-done((s32[2,2,4,128]{3,2,1,0:T(4,128)S(1)}, s32[2,2,4,128]{3,2,1,0:T(4,128)S(1)}, u32[]{:S(2)}, u32[]{:S(2)}) %collective-permute-start.2) | collective-permute-done | bytes 8224 | tf_op jit(solution)/shard_map/ppermute | solution.py:469
  34.6 10.5 %collective-permute-done.3 = s32[2,2,4,128]{3,2,1,0:T(4,128)S(1)} collective-permute-done((s32[2,2,4,128]{3,2,1,0:T(4,128)S(1)}, s32[2,2,4,128]{3,2,1,0:T(4,128)S(1)}, u32[]{:S(2)}, u32[]{:S(2)}) %collective-permute-start.3) | collective-permute-done | bytes 8224 | tf_op jit(solution)/shard_map/ppermute | solution.py:469
  45.1 0.0 collective-permute-done.4
  45.1 0.0 all-to-all-done.1.levels
  45.1 3.6 %all-to-all-start = ((bf16[8,80,512]{2,1,0:T(8,128)(2,1)}), bf16[8,80,512]{2,1,0:T(8,128)(2,1)S(1)}, u32[]{:S(2)}, u32[]{:S(2)}) async-start(bf16[8,80,512]{2,1,0:T(8,128)(2,1)} %deal.3), calls=%async_computation | async-start | bytes 1310720 | tf_op jit(solution)/shard_map/all_to_all | solution.py:486
  48.8 0.0 copy-done.2
  48.8 0.0 copy-done.5
  48.8 0.0 copy-done.6
  48.8 15.0 %march.2 = (f32[256,128]{1,0:T(8,128)}, f32[2,32,8,128]{3,2,1,0:T(8,128)S(1)}, f32[1,2,32,8,128]{4,3,2,1,0:T(8,128)S(1)}) custom-call(bf16[8,176,512]{2,1,0:T(8,128)(2,1)S(1)} %all-to-all-done.1.levels, s32[8,4,128]{2,1,0:T(4,128)S(1)} %dynamic-slice_bitcast_fusion.cells, ...), custom_call_target="tpu_custom_call", output_to_operand_aliasing={{1}: (2, {}), {2}: (3, {})} | custom-call | flops 17600000000 | bytes 4194304 | tf_op jit(solution)/shard_map/march/pallas_call | solution.py:396
  63.8 2.4 %all-to-all-done.levels = bf16[8,80,512]{2,1,0:T(8,128)(2,1)S(1)} async-done(((bf16[8,80,512]{2,1,0:T(8,128)(2,1)}), bf16[8,80,512]{2,1,0:T(8,128)(2,1)S(1)}, u32[]{:S(2)}, u32[]{:S(2)}) %all-to-all-start) | async-done | bytes 655392 | tf_op jit(solution)/shard_map/all_to_all | solution.py:486
  66.2 8.0 %march.3 = f32[256,128]{1,0:T(8,128)} custom-call(bf16[8,80,512]{2,1,0:T(8,128)(2,1)S(1)} %all-to-all-done.levels, s32[8,4,128]{2,1,0:T(4,128)S(1)} %dynamic-slice_bitcast_fusion.cells, f32[2,32,8,128]{3,2,1,0:T(8,128)S(1)} %get-tuple-element.18.launched, f32[1,2,32,8,128]{4,3,2,1,0:T(8,128)S(1)} %get-tuple-element.19.entered, ...), custom_call_target="tpu_custom_call", output_to_operand_aliasing={{}: (4, {})} | custom-call | flops 8000000000 | bytes 4194304 | tf_op jit(solution)/shard_map/march/pallas_call | solution.py:396
  74.2 3.7 %all-to-all-start.2 = ((f32[16,16,128]{2,1,0:T(8,128)}), f32[16,16,128]{2,1,0:T(8,128)S(1)}, u32[]{:S(2)}, u32[]{:S(2)}) async-start(f32[16,16,128]{2,1,0:T(8,128)} %bitcast.9), calls=%async_computation.2 | async-start | bytes 262144 | tf_op jit(solution)/shard_map/all_to_all | solution.py:497
  78.0 0.2 convert_reduce_fusion
  78.2 7.7 %all-to-all-done.2 = f32[16,16,128]{2,1,0:T(8,128)S(1)} async-done(((f32[16,16,128]{2,1,0:T(8,128)}), f32[16,16,128]{2,1,0:T(8,128)S(1)}, u32[]{:S(2)}, u32[]{:S(2)}) %all-to-all-start.2) | async-done | bytes 131104 | tf_op jit(solution)/shard_map/all_to_all | solution.py:497
  85.9 0.7 broadcast_divide_fusion
  (14 shorter events, 0.1 us)
Async XLA Ops:
  3.0 7.3 %copy-start.8 = (s32[128,2]{0,1:T(2,128)S(1)}, s32[128,2]{0,1:T(2,128)}, u32[]{:S(2)}) copy-start(s32[128,2]{0,1:T(2,128)} %param.14) | copy-start | bytes 3076
  3.0 7.3 %copy-start.9 = (s32[128,2]{0,1:T(2,128)S(1)}, s32[128,2]{0,1:T(2,128)}, u32[]{:S(2)}) copy-start(s32[128,2]{0,1:T(2,128)} %param.13) | copy-start | bytes 3076
  3.0 42.1 %all-to-all-start.1 = ((bf16[8,176,512]{2,1,0:T(8,128)(2,1)}), bf16[8,176,512]{2,1,0:T(8,128)(2,1)S(1)}, u32[]{:S(2)}, u32[]{:S(2)}) async-start(bf16[8,176,512]{2,1,0:T(8,128)(2,1)} %deal.2), calls=%async_computation.1 | async-start | bytes 2883584 | tf_op jit(solution)/shard_map/all_to_all | solution.py:485
  10.3 1.2 %collective-permute-start = (s32[4,128]{1,0:T(4,128)S(1)}, s32[4,128]{1,0:T(4,128)S(1)}, u32[]{:S(2)}, u32[]{:S(2)}) collective-permute-start(s32[4,128]{1,0:T(4,128)S(1)} %pad_add_fusion.2), channel_id=1, source_target_pairs={{0,1},{1,0},{2,3},{3,2},{4,5},{5,4},{6,7},{7,6},{8,9},{9,8},{10,11... | collective-permute-start | bytes 6152 | tf_op jit(solution)/shard_map/ppermute | solution.py:461
  11.5 4.5 %copy-start.7 = (f32[2,4096]{1,0:T(2,128)S(1)}, f32[2,4096]{1,0:T(2,128)}, u32[]{:S(2)}) copy-start(f32[2,4096]{1,0:T(2,128)} %param.12) | copy-start | bytes 98308
  11.6 12.5 %copy-start = (bf16[2,256,256]{2,1,0:T(8,128)(2,1)S(1)}, bf16[2,256,256]{2,1,0:T(8,128)(2,1)}, u32[]{:S(2)}) copy-start(bf16[2,256,256]{2,1,0:T(8,128)(2,1)} %constant.83.clone.w_forward.refs_0_.refs_1_) | copy-start | bytes 786436
  11.6 12.4 %copy-start.1 = (bf16[2,256,256]{2,1,0:T(8,128)(2,1)S(1)}, bf16[2,256,256]{2,1,0:T(8,128)(2,1)}, u32[]{:S(2)}) copy-start(bf16[2,256,256]{2,1,0:T(8,128)(2,1)} %constant.84.clone.w_inverse.refs_1_.refs_2_) | copy-start | bytes 786436
  11.6 12.4 %copy-start.3 = (f32[2,32,128]{2,1,0:T(8,128)S(1)}, f32[2,32,128]{2,1,0:T(8,128)}, u32[]{:S(2)}) copy-start(f32[2,32,128]{2,1,0:T(8,128)} %constant.85.clone.twiddle_table.refs_2_.refs_3_) | copy-start | bytes 98308
  11.6 12.4 %copy-start.4 = (f32[2,32,128]{2,1,0:T(8,128)S(1)}, f32[2,32,128]{2,1,0:T(8,128)}, u32[]{:S(2)}) copy-start(f32[2,32,128]{2,1,0:T(8,128)} %constant.86.clone.spread_table.refs_3_.refs_4_) | copy-start | bytes 98308
  11.6 9.8 %collective-permute-start.1 = (s32[2,4,128]{2,1,0:T(4,128)S(1)}, s32[2,4,128]{2,1,0:T(4,128)S(1)}, u32[]{:S(2)}, u32[]{:S(2)}) collective-permute-start(s32[2,4,128]{2,1,0:T(4,128)S(1)} %pad_add_fusion.1), channel_id=1, source_target_pairs={{0,2},{2,0},{4,6},{6,4},{8,10},{10,8},{12,14},{14,12},{1,3},{3,1},... | collective-permute-start | bytes 12296 | tf_op jit(solution)/shard_map/ppermute | solution.py:464
  21.5 13.2 %collective-permute-start.2 = (s32[2,2,4,128]{3,2,1,0:T(4,128)S(1)}, s32[2,2,4,128]{3,2,1,0:T(4,128)S(1)}, u32[]{:S(2)}, u32[]{:S(2)}) collective-permute-start(s32[2,2,4,128]{3,2,1,0:T(4,128)S(1)} %get-tuple-element.23), channel_id=1, source_target_pairs={{0,4},{2,6},{4,0},{6,2},{8,12},{10,14},{12,8},{14,10},{1,5},{3,7},... | collective-permute-start | bytes 24584 | tf_op jit(solution)/shard_map/ppermute | solution.py:469
  24.7 24.1 %copy-start.2 = (bf16[256,128]{1,0:T(8,128)(2,1)S(1)}, bf16[256,128]{1,0:T(8,128)(2,1)}, u32[]{:S(2)}) copy-start(bf16[256,128]{1,0:T(8,128)(2,1)} %constant.89.clone.refs_6_.refs_7_) | copy-start | bytes 196612
  24.7 24.1 %copy-start.5 = (f32[32,128]{1,0:T(8,128)S(1)}, f32[32,128]{1,0:T(8,128)}, u32[]{:S(2)}) copy-start(f32[32,128]{1,0:T(8,128)} %constant.87.clone.refs_4_.refs_5_) | copy-start | bytes 49156
  24.7 24.1 %copy-start.6 = (f32[32,128]{1,0:T(8,128)S(1)}, f32[32,128]{1,0:T(8,128)}, u32[]{:S(2)}) copy-start(f32[32,128]{1,0:T(8,128)} %constant.88.clone.refs_5_.refs_6_) | copy-start | bytes 49156
  24.8 20.3 %collective-permute-start.3 = (s32[2,2,4,128]{3,2,1,0:T(4,128)S(1)}, s32[2,2,4,128]{3,2,1,0:T(4,128)S(1)}, u32[]{:S(2)}, u32[]{:S(2)}) collective-permute-start(s32[2,2,4,128]{3,2,1,0:T(4,128)S(1)} %get-tuple-element.23), channel_id=1, source_target_pairs={{0,8},{2,10},{4,12},{6,14},{8,0},{10,2},{12,4},{14,6},{1,9},{3,11}... | collective-permute-start | bytes 24584 | tf_op jit(solution)/shard_map/ppermute | solution.py:469
  27.0 18.1 %collective-permute-start.4 = (s32[2,2,4,128]{3,2,1,0:T(4,128)S(1)}, s32[2,2,4,128]{3,2,1,0:T(4,128)S(1)}, u32[]{:S(2)}, u32[]{:S(2)}) collective-permute-start(s32[2,2,4,128]{3,2,1,0:T(4,128)S(1)} %get-tuple-element.23), channel_id=1, source_target_pairs={{0,12},{2,14},{4,8},{6,10},{8,4},{10,6},{12,0},{14,2},{1,13},{3,15... | collective-permute-start | bytes 24584 | tf_op jit(solution)/shard_map/ppermute | solution.py:469
  45.1 21.0 %all-to-all-start = ((bf16[8,80,512]{2,1,0:T(8,128)(2,1)}), bf16[8,80,512]{2,1,0:T(8,128)(2,1)S(1)}, u32[]{:S(2)}, u32[]{:S(2)}) async-start(bf16[8,80,512]{2,1,0:T(8,128)(2,1)} %deal.3), calls=%async_computation | async-start | bytes 1310720 | tf_op jit(solution)/shard_map/all_to_all | solution.py:486
  74.2 11.7 %all-to-all-start.2 = ((f32[16,16,128]{2,1,0:T(8,128)}), f32[16,16,128]{2,1,0:T(8,128)S(1)}, u32[]{:S(2)}, u32[]{:S(2)}) async-start(f32[16,16,128]{2,1,0:T(8,128)} %bitcast.9), calls=%async_computation.2 | async-start | bytes 262144 | tf_op jit(solution)/shard_map/all_to_all | solution.py:497

commit v14 on v13

--- a/solution.py
+++ b/solution.py
@@ -147,18 +147,16 @@
 def joined(pieces):
     re_high, re_low = split(jnp.concatenate([p[0] for p in pieces], axis=0))
     im_high, im_low = split(jnp.concatenate([p[1] for p in pieces], axis=0))
-    return jnp.concatenate([re_high, im_high], axis=1), jnp.concatenate([re_low, im_low], axis=1)
+    return jnp.concatenate([re_high, im_high, re_low, im_low, re_high, im_high], axis=1)
 
 
 def weighted(left, weights, between=()):
-    high, low = left
-    between = list(between) + [lambda: None] * 3
-    total = None
-    for part, weight in ((high, weights[0]), (low, weights[0]), (high, weights[1])):
-        product = jnp.dot(part, weight, preferred_element_type=F32)
-        between.pop(0)()
-        total = product if total is None else total + product
-    return total
+    product = jnp.dot(
+        left, jnp.concatenate([weights[0], weights[0], weights[1]]), preferred_element_type=F32
+    )
+    for work in between:
+        work()
+    return product
 
 
 def spread_rows(table, wide):

time: 87 us -> 86.9 us (level)
  transfers between devices with their start and end apart: 8 -> 8, of which waited for: 6 -> 6; matrix products, arithmetic and copies ran while one was open for 0% -> 0% of each run, Pallas kernels for 21% -> 20%
where the time goes in v14:
time: 86.9 us; the launch traced here: 86.5 us
  waiting for transfers between devices  34.6 us (40%)
  Pallas kernels  28.5 us (33%)
  starting transfers between devices  21.9 us (25%)
  other arithmetic  0.96 us (1%)
    pallas_call x2, Pallas kernels, march(): return call(received, cells, *state, *totals, *consts, section)  22.6 us
    ppermute x3, waiting for transfers between devices, gather_small(): lax.ppermute(both, 'range', [(i, i ^ d) for i in range(sections)])  17.7 us
    all_to_all x1, waiting for transfers between devices, local(): lax.all_to_all(totals.reshape(owners, TILE_DEV, BINS), ('range', 'radial'...  7.68 us
    all_to_all x1, starting transfers between devices, local(): early = lax.all_to_all(dealt, 'range', 0, 0, tiled=True)  7.29 us
    ppermute x1, waiting for transfers between devices, gather_small(): lax.ppermute(pair, 'range', [(i, i ^ 1) for i in range(sections)])  5.32 us
    pallas_call x2, Pallas kernels, deal(): pl.pallas_call(kernel, out_shape=jax.ShapeDtypeStruct((sections, count, h...  5.32 us
    ppermute x3, starting transfers between devices, gather_small(): lax.ppermute(both, 'range', [(i, i ^ d) for i in range(sections)])  5.08 us
    all_to_all x1, starting transfers between devices, local(): lax.all_to_all(totals.reshape(owners, TILE_DEV, BINS), ('range', 'radial'...  3.74 us
  transfers between devices with their start and end apart: 8, of which 6 were waited for; matrix products, arithmetic and copies ran while one was open for 0% of the time, Pallas kernels for 20%

profile of v14, /device:TPU:0, one launch (start us, length us, event | category | flops | bytes accessed | tf_op | source)
XLA Modules:
  0.0 86.5 jit_solution(12592391868389160600)
XLA Ops:
  0.0 3.0 %deal.2 = bf16[8,176,512]{2,1,0:T(8,128)(2,1)} custom-call(bf16[128,16,512]{2,1,0:T(8,128)(2,1)} %levels.2), custom_call_target="tpu_custom_call" | custom-call | flops 1000000000 | bytes 4194304 | tf_op jit(solution)/shard_map/deal/pallas_call | solution.py:445
  3.0 0.0 copy-start.8
  3.0 0.0 copy-start.9
  3.0 7.3 %all-to-all-start.1 = ((bf16[8,176,512]{2,1,0:T(8,128)(2,1)}), bf16[8,176,512]{2,1,0:T(8,128)(2,1)S(1)}, u32[]{:S(2)}, u32[]{:S(2)}) async-start(bf16[8,176,512]{2,1,0:T(8,128)(2,1)} %deal.2), calls=%async_computation.1 | async-start | bytes 2883584 | tf_op jit(solution)/shard_map/all_to_all | solution.py:483
  10.3 0.0 copy-done.8
  10.3 0.0 copy-done.9
  10.3 0.1 collective-permute-start
  10.4 1.1 %collective-permute-done = s32[4,128]{1,0:T(4,128)S(1)} collective-permute-done((s32[4,128]{1,0:T(4,128)S(1)}, s32[4,128]{1,0:T(4,128)S(1)}, u32[]{:S(2)}, u32[]{:S(2)}) %collective-permute-start) | collective-permute-done | bytes 2080 | tf_op jit(solution)/shard_map/ppermute | solution.py:459
  11.5 0.0 copy-start.7
  11.6 0.0 copy-start
  11.6 0.0 copy-start.1
  11.6 0.0 copy-start.3
  11.6 0.0 copy-start.4
  11.6 2.1 %collective-permute-start.1 = (s32[2,4,128]{2,1,0:T(4,128)S(1)}, s32[2,4,128]{2,1,0:T(4,128)S(1)}, u32[]{:S(2)}, u32[]{:S(2)}) collective-permute-start(s32[2,4,128]{2,1,0:T(4,128)S(1)} %pad_add_fusion.1), channel_id=1, source_target_pairs={{0,2},{2,0},{4,6},{6,4},{8,10},{10,8},{12,14},{14,12},{1,3},{3,1},... | collective-permute-start | bytes 12296 | tf_op jit(solution)/shard_map/ppermute | solution.py:462
  13.7 2.4 %deal.3 = bf16[8,80,512]{2,1,0:T(8,128)(2,1)} custom-call(bf16[128,16,512]{2,1,0:T(8,128)(2,1)} %levels.2), custom_call_target="tpu_custom_call" | custom-call | flops 1000000000 | bytes 4194304 | tf_op jit(solution)/shard_map/deal/pallas_call | solution.py:445
  16.1 0.0 copy-done.7
  16.1 5.3 %collective-permute-done.1 = s32[2,4,128]{2,1,0:T(4,128)S(1)} collective-permute-done((s32[2,4,128]{2,1,0:T(4,128)S(1)}, s32[2,4,128]{2,1,0:T(4,128)S(1)}, u32[]{:S(2)}, u32[]{:S(2)}) %collective-permute-start.1) | collective-permute-done | bytes 4128 | tf_op jit(solution)/shard_map/ppermute | solution.py:462
  21.5 2.5 %collective-permute-start.2 = (s32[2,2,4,128]{3,2,1,0:T(4,128)S(1)}, s32[2,2,4,128]{3,2,1,0:T(4,128)S(1)}, u32[]{:S(2)}, u32[]{:S(2)}) collective-permute-start(s32[2,2,4,128]{3,2,1,0:T(4,128)S(1)} %get-tuple-element.23), channel_id=1, source_target_pairs={{0,4},{2,6},{4,0},{6,2},{8,12},{10,14},{12,8},{14,10},{1,5},{3,7},... | collective-permute-start | bytes 24584 | tf_op jit(solution)/shard_map/ppermute | solution.py:467
  24.0 0.0 copy-done
  24.0 0.0 copy-done.1
  24.0 0.0 copy-done.3
  24.0 0.0 copy-done.4
  24.0 0.6 launch.1
  24.7 0.0 copy-start.2
  24.7 0.0 copy-start.5
  24.7 0.0 copy-start.6
  24.8 2.1 %collective-permute-start.3 = (s32[2,2,4,128]{3,2,1,0:T(4,128)S(1)}, s32[2,2,4,128]{3,2,1,0:T(4,128)S(1)}, u32[]{:S(2)}, u32[]{:S(2)}) collective-permute-start(s32[2,2,4,128]{3,2,1,0:T(4,128)S(1)} %get-tuple-element.23), channel_id=1, source_target_pairs={{0,8},{2,10},{4,12},{6,14},{8,0},{10,2},{12,4},{14,6},{1,9},{3,11}... | collective-permute-start | bytes 24584 | tf_op jit(solution)/shard_map/ppermute | solution.py:467
  26.9 0.4 collective-permute-start.4
  27.3 7.3 %collective-permute-done.2 = s32[2,2,4,128]{3,2,1,0:T(4,128)S(1)} collective-permute-done((s32[2,2,4,128]{3,2,1,0:T(4,128)S(1)}, s32[2,2,4,128]{3,2,1,0:T(4,128)S(1)}, u32[]{:S(2)}, u32[]{:S(2)}) %collective-permute-start.2) | collective-permute-done | bytes 8224 | tf_op jit(solution)/shard_map/ppermute | solution.py:467
  34.6 10.5 %collective-permute-done.3 = s32[2,2,4,128]{3,2,1,0:T(4,128)S(1)} collective-permute-done((s32[2,2,4,128]{3,2,1,0:T(4,128)S(1)}, s32[2,2,4,128]{3,2,1,0:T(4,128)S(1)}, u32[]{:S(2)}, u32[]{:S(2)}) %collective-permute-start.3) | collective-permute-done | bytes 8224 | tf_op jit(solution)/shard_map/ppermute | solution.py:467
  45.1 0.0 collective-permute-done.4
  45.1 0.0 all-to-all-done.1.levels
  45.1 3.6 %all-to-all-start = ((bf16[8,80,512]{2,1,0:T(8,128)(2,1)}), bf16[8,80,512]{2,1,0:T(8,128)(2,1)S(1)}, u32[]{:S(2)}, u32[]{:S(2)}) async-start(bf16[8,80,512]{2,1,0:T(8,128)(2,1)} %deal.3), calls=%async_computation | async-start | bytes 1310720 | tf_op jit(solution)/shard_map/all_to_all | solution.py:484
  48.8 0.0 copy-done.2
  48.8 0.0 copy-done.5
  48.8 0.0 copy-done.6
  48.8 14.7 %march.2 = (f32[256,128]{1,0:T(8,128)}, f32[2,32,8,128]{3,2,1,0:T(8,128)S(1)}, f32[1,2,32,8,128]{4,3,2,1,0:T(8,128)S(1)}) custom-call(bf16[8,176,512]{2,1,0:T(8,128)(2,1)S(1)} %all-to-all-done.1.levels, s32[8,4,128]{2,1,0:T(4,128)S(1)} %dynamic-slice_bitcast_fusion.cells, ...), custom_call_target="tpu_custom_call", output_to_operand_aliasing={{1}: (2, {}), {2}: (3, {})} | custom-call | flops 17600000000 | bytes 4194304 | tf_op jit(solution)/shard_map/march/pallas_call | solution.py:394
  63.5 2.7 %all-to-all-done.levels = bf16[8,80,512]{2,1,0:T(8,128)(2,1)S(1)} async-done(((bf16[8,80,512]{2,1,0:T(8,128)(2,1)}), bf16[8,80,512]{2,1,0:T(8,128)(2,1)S(1)}, u32[]{:S(2)}, u32[]{:S(2)}) %all-to-all-start) | async-done | bytes 655392 | tf_op jit(solution)/shard_map/all_to_all | solution.py:484
  66.2 7.9 %march.3 = f32[256,128]{1,0:T(8,128)} custom-call(bf16[8,80,512]{2,1,0:T(8,128)(2,1)S(1)} %all-to-all-done.levels, s32[8,4,128]{2,1,0:T(4,128)S(1)} %dynamic-slice_bitcast_fusion.cells, f32[2,32,8,128]{3,2,1,0:T(8,128)S(1)} %get-tuple-element.18.launched, f32[1,2,32,8,128]{4,3,2,1,0:T(8,128)S(1)} %get-tuple-element.19.entered, ...), custom_call_target="tpu_custom_call", output_to_operand_aliasing={{}: (4, {})} | custom-call | flops 8000000000 | bytes 4194304 | tf_op jit(solution)/shard_map/march/pallas_call | solution.py:394
  74.1 3.7 %all-to-all-start.2 = ((f32[16,16,128]{2,1,0:T(8,128)}), f32[16,16,128]{2,1,0:T(8,128)S(1)}, u32[]{:S(2)}, u32[]{:S(2)}) async-start(f32[16,16,128]{2,1,0:T(8,128)} %bitcast.9), calls=%async_computation.2 | async-start | bytes 262144 | tf_op jit(solution)/shard_map/all_to_all | solution.py:495
  77.9 0.2 convert_reduce_fusion
  78.1 7.7 %all-to-all-done.2 = f32[16,16,128]{2,1,0:T(8,128)S(1)} async-done(((f32[16,16,128]{2,1,0:T(8,128)}), f32[16,16,128]{2,1,0:T(8,128)S(1)}, u32[]{:S(2)}, u32[]{:S(2)}) %all-to-all-start.2) | async-done | bytes 131104 | tf_op jit(solution)/shard_map/all_to_all | solution.py:495
  85.8 0.7 broadcast_divide_fusion
  (14 shorter events, 0.1 us)
Async XLA Ops:
  3.0 7.3 %copy-start.8 = (s32[128,2]{0,1:T(2,128)S(1)}, s32[128,2]{0,1:T(2,128)}, u32[]{:S(2)}) copy-start(s32[128,2]{0,1:T(2,128)} %param.14) | copy-start | bytes 3076
  3.0 7.3 %copy-start.9 = (s32[128,2]{0,1:T(2,128)S(1)}, s32[128,2]{0,1:T(2,128)}, u32[]{:S(2)}) copy-start(s32[128,2]{0,1:T(2,128)} %param.13) | copy-start | bytes 3076
  3.0 42.1 %all-to-all-start.1 = ((bf16[8,176,512]{2,1,0:T(8,128)(2,1)}), bf16[8,176,512]{2,1,0:T(8,128)(2,1)S(1)}, u32[]{:S(2)}, u32[]{:S(2)}) async-start(bf16[8,176,512]{2,1,0:T(8,128)(2,1)} %deal.2), calls=%async_computation.1 | async-start | bytes 2883584 | tf_op jit(solution)/shard_map/all_to_all | solution.py:483
  10.3 1.2 %collective-permute-start = (s32[4,128]{1,0:T(4,128)S(1)}, s32[4,128]{1,0:T(4,128)S(1)}, u32[]{:S(2)}, u32[]{:S(2)}) collective-permute-start(s32[4,128]{1,0:T(4,128)S(1)} %pad_add_fusion.2), channel_id=1, source_target_pairs={{0,1},{1,0},{2,3},{3,2},{4,5},{5,4},{6,7},{7,6},{8,9},{9,8},{10,11... | collective-permute-start | bytes 6152 | tf_op jit(solution)/shard_map/ppermute | solution.py:459
  11.5 4.5 %copy-start.7 = (f32[2,4096]{1,0:T(2,128)S(1)}, f32[2,4096]{1,0:T(2,128)}, u32[]{:S(2)}) copy-start(f32[2,4096]{1,0:T(2,128)} %param.12) | copy-start | bytes 98308
  11.6 12.5 %copy-start = (bf16[2,256,256]{2,1,0:T(8,128)(2,1)S(1)}, bf16[2,256,256]{2,1,0:T(8,128)(2,1)}, u32[]{:S(2)}) copy-start(bf16[2,256,256]{2,1,0:T(8,128)(2,1)} %constant.83.clone.w_forward.refs_0_.refs_1_) | copy-start | bytes 786436
  11.6 12.4 %copy-start.1 = (bf16[2,256,256]{2,1,0:T(8,128)(2,1)S(1)}, bf16[2,256,256]{2,1,0:T(8,128)(2,1)}, u32[]{:S(2)}) copy-start(bf16[2,256,256]{2,1,0:T(8,128)(2,1)} %constant.84.clone.w_inverse.refs_1_.refs_2_) | copy-start | bytes 786436
  11.6 12.4 %copy-start.3 = (f32[2,32,128]{2,1,0:T(8,128)S(1)}, f32[2,32,128]{2,1,0:T(8,128)}, u32[]{:S(2)}) copy-start(f32[2,32,128]{2,1,0:T(8,128)} %constant.85.clone.twiddle_table.refs_2_.refs_3_) | copy-start | bytes 98308
  11.6 12.4 %copy-start.4 = (f32[2,32,128]{2,1,0:T(8,128)S(1)}, f32[2,32,128]{2,1,0:T(8,128)}, u32[]{:S(2)}) copy-start(f32[2,32,128]{2,1,0:T(8,128)} %constant.86.clone.spread_table.refs_3_.refs_4_) | copy-start | bytes 98308
  11.6 9.8 %collective-permute-start.1 = (s32[2,4,128]{2,1,0:T(4,128)S(1)}, s32[2,4,128]{2,1,0:T(4,128)S(1)}, u32[]{:S(2)}, u32[]{:S(2)}) collective-permute-start(s32[2,4,128]{2,1,0:T(4,128)S(1)} %pad_add_fusion.1), channel_id=1, source_target_pairs={{0,2},{2,0},{4,6},{6,4},{8,10},{10,8},{12,14},{14,12},{1,3},{3,1},... | collective-permute-start | bytes 12296 | tf_op jit(solution)/shard_map/ppermute | solution.py:462
  21.5 13.2 %collective-permute-start.2 = (s32[2,2,4,128]{3,2,1,0:T(4,128)S(1)}, s32[2,2,4,128]{3,2,1,0:T(4,128)S(1)}, u32[]{:S(2)}, u32[]{:S(2)}) collective-permute-start(s32[2,2,4,128]{3,2,1,0:T(4,128)S(1)} %get-tuple-element.23), channel_id=1, source_target_pairs={{0,4},{2,6},{4,0},{6,2},{8,12},{10,14},{12,8},{14,10},{1,5},{3,7},... | collective-permute-start | bytes 24584 | tf_op jit(solution)/shard_map/ppermute | solution.py:467
  24.7 24.1 %copy-start.2 = (bf16[256,128]{1,0:T(8,128)(2,1)S(1)}, bf16[256,128]{1,0:T(8,128)(2,1)}, u32[]{:S(2)}) copy-start(bf16[256,128]{1,0:T(8,128)(2,1)} %constant.89.clone.refs_6_.refs_7_) | copy-start | bytes 196612
  24.7 24.1 %copy-start.5 = (f32[32,128]{1,0:T(8,128)S(1)}, f32[32,128]{1,0:T(8,128)}, u32[]{:S(2)}) copy-start(f32[32,128]{1,0:T(8,128)} %constant.87.clone.refs_4_.refs_5_) | copy-start | bytes 49156
  24.7 24.1 %copy-start.6 = (f32[32,128]{1,0:T(8,128)S(1)}, f32[32,128]{1,0:T(8,128)}, u32[]{:S(2)}) copy-start(f32[32,128]{1,0:T(8,128)} %constant.88.clone.refs_5_.refs_6_) | copy-start | bytes 49156
  24.8 20.3 %collective-permute-start.3 = (s32[2,2,4,128]{3,2,1,0:T(4,128)S(1)}, s32[2,2,4,128]{3,2,1,0:T(4,128)S(1)}, u32[]{:S(2)}, u32[]{:S(2)}) collective-permute-start(s32[2,2,4,128]{3,2,1,0:T(4,128)S(1)} %get-tuple-element.23), channel_id=1, source_target_pairs={{0,8},{2,10},{4,12},{6,14},{8,0},{10,2},{12,4},{14,6},{1,9},{3,11}... | collective-permute-start | bytes 24584 | tf_op jit(solution)/shard_map/ppermute | solution.py:467
  26.9 18.2 %collective-permute-start.4 = (s32[2,2,4,128]{3,2,1,0:T(4,128)S(1)}, s32[2,2,4,128]{3,2,1,0:T(4,128)S(1)}, u32[]{:S(2)}, u32[]{:S(2)}) collective-permute-start(s32[2,2,4,128]{3,2,1,0:T(4,128)S(1)} %get-tuple-element.23), channel_id=1, source_target_pairs={{0,12},{2,14},{4,8},{6,10},{8,4},{10,6},{12,0},{14,2},{1,13},{3,15... | collective-permute-start | bytes 24584 | tf_op jit(solution)/shard_map/ppermute | solution.py:467
  45.1 21.0 %all-to-all-start = ((bf16[8,80,512]{2,1,0:T(8,128)(2,1)}), bf16[8,80,512]{2,1,0:T(8,128)(2,1)S(1)}, u32[]{:S(2)}, u32[]{:S(2)}) async-start(bf16[8,80,512]{2,1,0:T(8,128)(2,1)} %deal.3), calls=%async_computation | async-start | bytes 1310720 | tf_op jit(solution)/shard_map/all_to_all | solution.py:484
  74.1 11.7 %all-to-all-start.2 = ((f32[16,16,128]{2,1,0:T(8,128)}), f32[16,16,128]{2,1,0:T(8,128)S(1)}, u32[]{:S(2)}, u32[]{:S(2)}) async-start(f32[16,16,128]{2,1,0:T(8,128)} %bitcast.9), calls=%async_computation.2 | async-start | bytes 262144 | tf_op jit(solution)/shard_map/all_to_all | solution.py:495

commit v15 on v14

--- a/solution.py
+++ b/solution.py
@@ -329,7 +329,9 @@
         field[half] = entered[half - 1]
     energy[...] = jnp.zeros_like(energy)
     whole_steps = steps - 1 if last else steps
-    lax.fori_loop(0, whole_steps, step, 0)
+    lax.fori_loop(0, whole_steps // 2, lambda i, carry: step(2 * i + 1, step(2 * i, carry)), 0)
+    if whole_steps % 2:
+        step(whole_steps - 1, 0)
     if last:
         for half in range(halves - 1):
             turn_of(whole_steps, half, half + 1)

time: 86.9 us -> 86.8 us (level)
  no operation moved by 1% of the time
where the time goes in v15:
time: 86.8 us; the launch traced here: 86.4 us
  waiting for transfers between devices  34.9 us (40%)
  Pallas kernels  28.1 us (32%)
  starting transfers between devices  21.9 us (25%)
  other arithmetic  0.96 us (1%)
    pallas_call x2, Pallas kernels, march(): return call(received, cells, *state, *totals, *consts, section)  22.2 us
    ppermute x3, waiting for transfers between devices, gather_small(): lax.ppermute(both, 'range', [(i, i ^ d) for i in range(sections)])  17.7 us
    all_to_all x1, waiting for transfers between devices, local(): lax.all_to_all(totals.reshape(owners, TILE_DEV, BINS), ('range', 'radial'...  7.68 us
    all_to_all x1, starting transfers between devices, local(): early = lax.all_to_all(dealt, 'range', 0, 0, tiled=True)  7.29 us
    ppermute x1, waiting for transfers between devices, gather_small(): lax.ppermute(pair, 'range', [(i, i ^ 1) for i in range(sections)])  5.32 us
    pallas_call x2, Pallas kernels, deal(): pl.pallas_call(kernel, out_shape=jax.ShapeDtypeStruct((sections, count, h...  5.32 us
    ppermute x3, starting transfers between devices, gather_small(): lax.ppermute(both, 'range', [(i, i ^ d) for i in range(sections)])  5.08 us
    all_to_all x1, starting transfers between devices, local(): lax.all_to_all(totals.reshape(owners, TILE_DEV, BINS), ('range', 'radial'...  3.74 us
  transfers between devices with their start and end apart: 8, of which 6 were waited for; matrix products, arithmetic and copies ran while one was open for 0% of the time, Pallas kernels for 20%

profile of v15, /device:TPU:0, one launch (start us, length us, event | category | flops | bytes accessed | tf_op | source)
XLA Modules:
  0.0 86.4 jit_solution(8098325887360934747)
XLA Ops:
  0.0 3.0 %deal.2 = bf16[8,176,512]{2,1,0:T(8,128)(2,1)} custom-call(bf16[128,16,512]{2,1,0:T(8,128)(2,1)} %levels.2), custom_call_target="tpu_custom_call" | custom-call | flops 1000000000 | bytes 4194304 | tf_op jit(solution)/shard_map/deal/pallas_call | solution.py:447
  3.0 0.0 copy-start.8
  3.0 0.0 copy-start.9
  3.0 7.3 %all-to-all-start.1 = ((bf16[8,176,512]{2,1,0:T(8,128)(2,1)}), bf16[8,176,512]{2,1,0:T(8,128)(2,1)S(1)}, u32[]{:S(2)}, u32[]{:S(2)}) async-start(bf16[8,176,512]{2,1,0:T(8,128)(2,1)} %deal.2), calls=%async_computation.1 | async-start | bytes 2883584 | tf_op jit(solution)/shard_map/all_to_all | solution.py:485
  10.3 0.0 copy-done.8
  10.3 0.0 copy-done.9
  10.3 0.1 collective-permute-start
  10.4 1.1 %collective-permute-done = s32[4,128]{1,0:T(4,128)S(1)} collective-permute-done((s32[4,128]{1,0:T(4,128)S(1)}, s32[4,128]{1,0:T(4,128)S(1)}, u32[]{:S(2)}, u32[]{:S(2)}) %collective-permute-start) | collective-permute-done | bytes 2080 | tf_op jit(solution)/shard_map/ppermute | solution.py:461
  11.5 0.0 copy-start.7
  11.6 0.0 copy-start
  11.6 0.0 copy-start.1
  11.6 0.0 copy-start.3
  11.6 0.0 copy-start.4
  11.6 2.1 %collective-permute-start.1 = (s32[2,4,128]{2,1,0:T(4,128)S(1)}, s32[2,4,128]{2,1,0:T(4,128)S(1)}, u32[]{:S(2)}, u32[]{:S(2)}) collective-permute-start(s32[2,4,128]{2,1,0:T(4,128)S(1)} %pad_add_fusion.1), channel_id=1, source_target_pairs={{0,2},{2,0},{4,6},{6,4},{8,10},{10,8},{12,14},{14,12},{1,3},{3,1},... | collective-permute-start | bytes 12296 | tf_op jit(solution)/shard_map/ppermute | solution.py:464
  13.7 2.4 %deal.3 = bf16[8,80,512]{2,1,0:T(8,128)(2,1)} custom-call(bf16[128,16,512]{2,1,0:T(8,128)(2,1)} %levels.2), custom_call_target="tpu_custom_call" | custom-call | flops 1000000000 | bytes 4194304 | tf_op jit(solution)/shard_map/deal/pallas_call | solution.py:447
  16.1 0.0 copy-done.7
  16.1 5.3 %collective-permute-done.1 = s32[2,4,128]{2,1,0:T(4,128)S(1)} collective-permute-done((s32[2,4,128]{2,1,0:T(4,128)S(1)}, s32[2,4,128]{2,1,0:T(4,128)S(1)}, u32[]{:S(2)}, u32[]{:S(2)}) %collective-permute-start.1) | collective-permute-done | bytes 4128 | tf_op jit(solution)/shard_map/ppermute | solution.py:464
  21.5 2.5 %collective-permute-start.2 = (s32[2,2,4,128]{3,2,1,0:T(4,128)S(1)}, s32[2,2,4,128]{3,2,1,0:T(4,128)S(1)}, u32[]{:S(2)}, u32[]{:S(2)}) collective-permute-start(s32[2,2,4,128]{3,2,1,0:T(4,128)S(1)} %get-tuple-element.23), channel_id=1, source_target_pairs={{0,4},{2,6},{4,0},{6,2},{8,12},{10,14},{12,8},{14,10},{1,5},{3,7},... | collective-permute-start | bytes 24584 | tf_op jit(solution)/shard_map/ppermute | solution.py:469
  24.0 0.0 copy-done
  24.0 0.0 copy-done.1
  24.0 0.0 copy-done.3
  24.0 0.0 copy-done.4
  24.0 0.6 launch.1
  24.7 0.0 copy-start.2
  24.7 0.0 copy-start.5
  24.7 0.0 copy-start.6
  24.8 2.1 %collective-permute-start.3 = (s32[2,2,4,128]{3,2,1,0:T(4,128)S(1)}, s32[2,2,4,128]{3,2,1,0:T(4,128)S(1)}, u32[]{:S(2)}, u32[]{:S(2)}) collective-permute-start(s32[2,2,4,128]{3,2,1,0:T(4,128)S(1)} %get-tuple-element.23), channel_id=1, source_target_pairs={{0,8},{2,10},{4,12},{6,14},{8,0},{10,2},{12,4},{14,6},{1,9},{3,11}... | collective-permute-start | bytes 24584 | tf_op jit(solution)/shard_map/ppermute | solution.py:469
  26.9 0.4 collective-permute-start.4
  27.3 7.3 %collective-permute-done.2 = s32[2,2,4,128]{3,2,1,0:T(4,128)S(1)} collective-permute-done((s32[2,2,4,128]{3,2,1,0:T(4,128)S(1)}, s32[2,2,4,128]{3,2,1,0:T(4,128)S(1)}, u32[]{:S(2)}, u32[]{:S(2)}) %collective-permute-start.2) | collective-permute-done | bytes 8224 | tf_op jit(solution)/shard_map/ppermute | solution.py:469
  34.6 10.5 %collective-permute-done.3 = s32[2,2,4,128]{3,2,1,0:T(4,128)S(1)} collective-permute-done((s32[2,2,4,128]{3,2,1,0:T(4,128)S(1)}, s32[2,2,4,128]{3,2,1,0:T(4,128)S(1)}, u32[]{:S(2)}, u32[]{:S(2)}) %collective-permute-start.3) | collective-permute-done | bytes 8224 | tf_op jit(solution)/shard_map/ppermute | solution.py:469
  45.1 0.0 collective-permute-done.4
  45.1 0.0 all-to-all-done.1.levels
  45.1 3.6 %all-to-all-start = ((bf16[8,80,512]{2,1,0:T(8,128)(2,1)}), bf16[8,80,512]{2,1,0:T(8,128)(2,1)S(1)}, u32[]{:S(2)}, u32[]{:S(2)}) async-start(bf16[8,80,512]{2,1,0:T(8,128)(2,1)} %deal.3), calls=%async_computation | async-start | bytes 1310720 | tf_op jit(solution)/shard_map/all_to_all | solution.py:486
  48.8 0.0 copy-done.2
  48.8 0.0 copy-done.5
  48.8 0.0 copy-done.6
  48.8 14.3 %march.2 = (f32[256,128]{1,0:T(8,128)}, f32[2,32,8,128]{3,2,1,0:T(8,128)S(1)}, f32[1,2,32,8,128]{4,3,2,1,0:T(8,128)S(1)}) custom-call(bf16[8,176,512]{2,1,0:T(8,128)(2,1)S(1)} %all-to-all-done.1.levels, s32[8,4,128]{2,1,0:T(4,128)S(1)} %dynamic-slice_bitcast_fusion.cells, ...), custom_call_target="tpu_custom_call", output_to_operand_aliasing={{1}: (2, {}), {2}: (3, {})} | custom-call | flops 17600000000 | bytes 4194304 | tf_op jit(solution)/shard_map/march/pallas_call | solution.py:396
  63.1 3.1 %all-to-all-done.levels = bf16[8,80,512]{2,1,0:T(8,128)(2,1)S(1)} async-done(((bf16[8,80,512]{2,1,0:T(8,128)(2,1)}), bf16[8,80,512]{2,1,0:T(8,128)(2,1)S(1)}, u32[]{:S(2)}, u32[]{:S(2)}) %all-to-all-start) | async-done | bytes 655392 | tf_op jit(solution)/shard_map/all_to_all | solution.py:486
  66.2 7.9 %march.3 = f32[256,128]{1,0:T(8,128)} custom-call(bf16[8,80,512]{2,1,0:T(8,128)(2,1)S(1)} %all-to-all-done.levels, s32[8,4,128]{2,1,0:T(4,128)S(1)} %dynamic-slice_bitcast_fusion.cells, f32[2,32,8,128]{3,2,1,0:T(8,128)S(1)} %get-tuple-element.18.launched, f32[1,2,32,8,128]{4,3,2,1,0:T(8,128)S(1)} %get-tuple-element.19.entered, ...), custom_call_target="tpu_custom_call", output_to_operand_aliasing={{}: (4, {})} | custom-call | flops 8000000000 | bytes 4194304 | tf_op jit(solution)/shard_map/march/pallas_call | solution.py:396
  74.0 3.7 %all-to-all-start.2 = ((f32[16,16,128]{2,1,0:T(8,128)}), f32[16,16,128]{2,1,0:T(8,128)S(1)}, u32[]{:S(2)}, u32[]{:S(2)}) async-start(f32[16,16,128]{2,1,0:T(8,128)} %bitcast.9), calls=%async_computation.2 | async-start | bytes 262144 | tf_op jit(solution)/shard_map/all_to_all | solution.py:497
  77.8 0.2 convert_reduce_fusion
  78.0 7.7 %all-to-all-done.2 = f32[16,16,128]{2,1,0:T(8,128)S(1)} async-done(((f32[16,16,128]{2,1,0:T(8,128)}), f32[16,16,128]{2,1,0:T(8,128)S(1)}, u32[]{:S(2)}, u32[]{:S(2)}) %all-to-all-start.2) | async-done | bytes 131104 | tf_op jit(solution)/shard_map/all_to_all | solution.py:497
  85.7 0.7 broadcast_divide_fusion
  (14 shorter events, 0.1 us)
Async XLA Ops:
  3.0 7.3 %copy-start.8 = (s32[128,2]{0,1:T(2,128)S(1)}, s32[128,2]{0,1:T(2,128)}, u32[]{:S(2)}) copy-start(s32[128,2]{0,1:T(2,128)} %param.14) | copy-start | bytes 3076
  3.0 7.3 %copy-start.9 = (s32[128,2]{0,1:T(2,128)S(1)}, s32[128,2]{0,1:T(2,128)}, u32[]{:S(2)}) copy-start(s32[128,2]{0,1:T(2,128)} %param.13) | copy-start | bytes 3076
  3.0 42.1 %all-to-all-start.1 = ((bf16[8,176,512]{2,1,0:T(8,128)(2,1)}), bf16[8,176,512]{2,1,0:T(8,128)(2,1)S(1)}, u32[]{:S(2)}, u32[]{:S(2)}) async-start(bf16[8,176,512]{2,1,0:T(8,128)(2,1)} %deal.2), calls=%async_computation.1 | async-start | bytes 2883584 | tf_op jit(solution)/shard_map/all_to_all | solution.py:485
  10.3 1.2 %collective-permute-start = (s32[4,128]{1,0:T(4,128)S(1)}, s32[4,128]{1,0:T(4,128)S(1)}, u32[]{:S(2)}, u32[]{:S(2)}) collective-permute-start(s32[4,128]{1,0:T(4,128)S(1)} %pad_add_fusion.2), channel_id=1, source_target_pairs={{0,1},{1,0},{2,3},{3,2},{4,5},{5,4},{6,7},{7,6},{8,9},{9,8},{10,11... | collective-permute-start | bytes 6152 | tf_op jit(solution)/shard_map/ppermute | solution.py:461
  11.5 4.5 %copy-start.7 = (f32[2,4096]{1,0:T(2,128)S(1)}, f32[2,4096]{1,0:T(2,128)}, u32[]{:S(2)}) copy-start(f32[2,4096]{1,0:T(2,128)} %param.12) | copy-start | bytes 98308
  11.6 12.5 %copy-start = (bf16[2,256,256]{2,1,0:T(8,128)(2,1)S(1)}, bf16[2,256,256]{2,1,0:T(8,128)(2,1)}, u32[]{:S(2)}) copy-start(bf16[2,256,256]{2,1,0:T(8,128)(2,1)} %constant.83.clone.w_forward.refs_0_.refs_1_) | copy-start | bytes 786436
  11.6 12.4 %copy-start.1 = (bf16[2,256,256]{2,1,0:T(8,128)(2,1)S(1)}, bf16[2,256,256]{2,1,0:T(8,128)(2,1)}, u32[]{:S(2)}) copy-start(bf16[2,256,256]{2,1,0:T(8,128)(2,1)} %constant.84.clone.w_inverse.refs_1_.refs_2_) | copy-start | bytes 786436
  11.6 12.4 %copy-start.3 = (f32[2,32,128]{2,1,0:T(8,128)S(1)}, f32[2,32,128]{2,1,0:T(8,128)}, u32[]{:S(2)}) copy-start(f32[2,32,128]{2,1,0:T(8,128)} %constant.85.clone.twiddle_table.refs_2_.refs_3_) | copy-start | bytes 98308
  11.6 12.4 %copy-start.4 = (f32[2,32,128]{2,1,0:T(8,128)S(1)}, f32[2,32,128]{2,1,0:T(8,128)}, u32[]{:S(2)}) copy-start(f32[2,32,128]{2,1,0:T(8,128)} %constant.86.clone.spread_table.refs_3_.refs_4_) | copy-start | bytes 98308
  11.6 9.8 %collective-permute-start.1 = (s32[2,4,128]{2,1,0:T(4,128)S(1)}, s32[2,4,128]{2,1,0:T(4,128)S(1)}, u32[]{:S(2)}, u32[]{:S(2)}) collective-permute-start(s32[2,4,128]{2,1,0:T(4,128)S(1)} %pad_add_fusion.1), channel_id=1, source_target_pairs={{0,2},{2,0},{4,6},{6,4},{8,10},{10,8},{12,14},{14,12},{1,3},{3,1},... | collective-permute-start | bytes 12296 | tf_op jit(solution)/shard_map/ppermute | solution.py:464
  21.5 13.2 %collective-permute-start.2 = (s32[2,2,4,128]{3,2,1,0:T(4,128)S(1)}, s32[2,2,4,128]{3,2,1,0:T(4,128)S(1)}, u32[]{:S(2)}, u32[]{:S(2)}) collective-permute-start(s32[2,2,4,128]{3,2,1,0:T(4,128)S(1)} %get-tuple-element.23), channel_id=1, source_target_pairs={{0,4},{2,6},{4,0},{6,2},{8,12},{10,14},{12,8},{14,10},{1,5},{3,7},... | collective-permute-start | bytes 24584 | tf_op jit(solution)/shard_map/ppermute | solution.py:469
  24.7 24.1 %copy-start.2 = (bf16[256,128]{1,0:T(8,128)(2,1)S(1)}, bf16[256,128]{1,0:T(8,128)(2,1)}, u32[]{:S(2)}) copy-start(bf16[256,128]{1,0:T(8,128)(2,1)} %constant.89.clone.refs_6_.refs_7_) | copy-start | bytes 196612
  24.7 24.1 %copy-start.5 = (f32[32,128]{1,0:T(8,128)S(1)}, f32[32,128]{1,0:T(8,128)}, u32[]{:S(2)}) copy-start(f32[32,128]{1,0:T(8,128)} %constant.87.clone.refs_4_.refs_5_) | copy-start | bytes 49156
  24.7 24.1 %copy-start.6 = (f32[32,128]{1,0:T(8,128)S(1)}, f32[32,128]{1,0:T(8,128)}, u32[]{:S(2)}) copy-start(f32[32,128]{1,0:T(8,128)} %constant.88.clone.refs_5_.refs_6_) | copy-start | bytes 49156
  24.8 20.3 %collective-permute-start.3 = (s32[2,2,4,128]{3,2,1,0:T(4,128)S(1)}, s32[2,2,4,128]{3,2,1,0:T(4,128)S(1)}, u32[]{:S(2)}, u32[]{:S(2)}) collective-permute-start(s32[2,2,4,128]{3,2,1,0:T(4,128)S(1)} %get-tuple-element.23), channel_id=1, source_target_pairs={{0,8},{2,10},{4,12},{6,14},{8,0},{10,2},{12,4},{14,6},{1,9},{3,11}... | collective-permute-start | bytes 24584 | tf_op jit(solution)/shard_map/ppermute | solution.py:469
  26.9 18.2 %collective-permute-start.4 = (s32[2,2,4,128]{3,2,1,0:T(4,128)S(1)}, s32[2,2,4,128]{3,2,1,0:T(4,128)S(1)}, u32[]{:S(2)}, u32[]{:S(2)}) collective-permute-start(s32[2,2,4,128]{3,2,1,0:T(4,128)S(1)} %get-tuple-element.23), channel_id=1, source_target_pairs={{0,12},{2,14},{4,8},{6,10},{8,4},{10,6},{12,0},{14,2},{1,13},{3,15... | collective-permute-start | bytes 24584 | tf_op jit(solution)/shard_map/ppermute | solution.py:469
  45.1 21.0 %all-to-all-start = ((bf16[8,80,512]{2,1,0:T(8,128)(2,1)}), bf16[8,80,512]{2,1,0:T(8,128)(2,1)S(1)}, u32[]{:S(2)}, u32[]{:S(2)}) async-start(bf16[8,80,512]{2,1,0:T(8,128)(2,1)} %deal.3), calls=%async_computation | async-start | bytes 1310720 | tf_op jit(solution)/shard_map/all_to_all | solution.py:486
  74.0 11.7 %all-to-all-start.2 = ((f32[16,16,128]{2,1,0:T(8,128)}), f32[16,16,128]{2,1,0:T(8,128)S(1)}, u32[]{:S(2)}, u32[]{:S(2)}) async-start(f32[16,16,128]{2,1,0:T(8,128)} %bitcast.9), calls=%async_computation.2 | async-start | bytes 262144 | tf_op jit(solution)/shard_map/all_to_all | solution.py:497

commit v16 on v14

--- a/solution.py
+++ b/solution.py
@@ -39,19 +39,15 @@
     n = np.arange(LANES)
     angle = -2.0 * np.pi / LANES * (n[:, None] * n[None, :] % LANES)
     c, s = np.cos(angle), np.sin(angle)
-    forward = np.block([[c, s], [-s, c]])
-    inverse = np.block([[c, -s], [s, c]])
-    weights = []
-    for matrix in (forward, inverse):
-        high, low = split_np(matrix)
-        weights.append(np.stack([high, low]))
+    high, low = split_np(np.block([[c, s], [-s, c]]))
+    weights = np.stack([high, low])
     q = np.arange(ROWS)
     angle = -2.0 * np.pi / H * (q[:, None] * n[None, :])
-    twiddle = np.stack([np.cos(angle), np.sin(angle)]).astype(np.float32)
+    twiddle = np.stack([np.cos(angle), -np.sin(angle)]).astype(np.float32)
     frequency = q[:, None] + ROWS * n[None, :]
     signed = np.where(frequency >= H // 2, frequency - H, frequency)
     turning = -SPREAD_RATE * (2.0 * np.pi / H * signed) ** 2
-    spread = (np.stack([np.cos(turning), np.sin(turning)]) / H).astype(np.float32)
+    spread = (np.stack([np.cos(turning), -np.sin(turning)]) / H).astype(np.float32)
     rel = np.arange(H).reshape(ROWS, LANES) / H
     tilt = (TILT_SLOPE * rel - 1.0).astype(np.float32)
     depth = np.maximum(rel - 0.75, 0.0) * 4.0
@@ -59,7 +55,7 @@
     bins = np.zeros((2 * LANES, BINS), np.float64)
     for lane in range(2 * LANES):
         bins[lane, (lane % LANES) // BIN :: LANES // BIN] = 1.0 / BIN
-    return weights[0], weights[1], twiddle, spread, tilt, absorb, bins.astype(ml_dtypes.bfloat16)
+    return weights, twiddle, spread, tilt, absorb, bins.astype(ml_dtypes.bfloat16)
 
 
 def phase_polynomials():
@@ -173,30 +169,30 @@
 Q_ROWS = [ql + FOUR * qh for ql in range(FOUR) for qh in range(EIGHT)]
 
 
-def forward(field, w_forward, twiddle, between=()):
+def forward(field, weights, twiddle, between=()):
     pieces = []
     for ql in range(FOUR):
         column = [(field[0, ql * EIGHT + jl], field[1, ql * EIGHT + jl]) for jl in range(EIGHT)]
         for qh, (re, im) in enumerate(dft8(column, -1)):
             q = ql + FOUR * qh
             c, s = twiddle[0, q], twiddle[1, q]
-            pieces.append((re * c - im * s, re * s + im * c))
-    return weighted(joined(pieces), w_forward, between)
-
-
-def inverse(product, w_inverse, spread, between=()):
+            pieces.append((re * c + im * s, im * c - re * s))
+    return weighted(joined(pieces), weights, between)
+
+
+def inverse(product, weights, spread, between=()):
     pieces = []
     for q, (re, im) in zip(Q_ROWS, parted(product)):
         c, s = spread[0, q], spread[1, q]
-        pieces.append((re * c - im * s, re * s + im * c))
-    return weighted(joined(pieces), w_inverse, between)
+        pieces.append((re * c + im * s, re * s - im * c))
+    return weighted(joined(pieces), weights, between)
 
 
 def leave(back, product, twiddle):
     pieces = []
     for q, (re, im) in zip(Q_ROWS, parted(product)):
         c, s = twiddle[0, q], twiddle[1, q]
-        pieces.append((re * c + im * s, im * c - re * s))
+        pieces.append((re * c + im * s, re * s - im * c))
     for ql in range(FOUR):
         column = dft8(pieces[ql * EIGHT : (ql + 1) * EIGHT], 1)
         for jl in range(EIGHT):
@@ -204,16 +200,20 @@
             back[1, ql * EIGHT + jl] = column[jl][1]
 
 
-def launch_kernel(start, w_forward, w_inverse, twiddle_table, spread_table, back, field, twiddle, spread):
-    spread_rows(twiddle_table, twiddle)
-    spread_rows(spread_table, spread)
+def enter_source(field, start):
     for jl in range(EIGHT):
         columns = []
         for jh in range(FOUR):
             j = EIGHT * jh + jl
             columns.append(tuple(jnp.broadcast_to(start[k, j : j + 1, :], (SUB, LANES)) for k in range(2)))
         enter(field, columns, jl)
-    product = inverse(forward(field, w_forward, twiddle), w_inverse, spread)
+
+
+def launch_kernel(start, weights, twiddle_table, spread_table, back, field, twiddle, spread):
+    spread_rows(twiddle_table, twiddle)
+    spread_rows(spread_table, spread)
+    enter_source(field, start)
+    product = inverse(forward(field, weights, twiddle), weights, spread)
     leave(back, product, twiddle)
 
 
@@ -221,20 +221,20 @@
     vmem = pl.BlockSpec(memory_space=pltpu.VMEM)
     return pl.pallas_call(
         launch_kernel,
-        out_shape=[jax.ShapeDtypeStruct((2, ROWS, SUB, LANES), F32)] * 2,
-        in_specs=[vmem] * 5,
-        out_specs=[vmem] * 2,
-        scratch_shapes=[pltpu.VMEM((2, ROWS, SUB, LANES), F32)] * 2,
+        out_shape=jax.ShapeDtypeStruct((2, ROWS, SUB, LANES), F32),
+        in_specs=[vmem] * 4,
+        out_specs=vmem,
+        scratch_shapes=[pltpu.VMEM((2, ROWS, SUB, LANES), F32)] * 3,
         compiler_params=pltpu.CompilerParams(vmem_limit_bytes=8 * 1024 * 1024),
         cost_estimate=pl.CostEstimate(flops=1_000_000_000, bytes_accessed=1024 * 1024, transcendentals=0),
         name="launch",
-    )(start, *consts[:4])
+    )(start, *consts[:3])
 
 
 def march_kernel(begin, steps, own, last, levels, cells, launched, entered, *refs):
     if begin > 0:
         totals_in, refs = refs[0], refs[1:]
-    (w_forward, w_inverse), refs = refs[:2], refs[2:]
+    weights, refs = refs[0], refs[1:]
     tables, (bins, section, totals), refs = refs[:4], refs[4:7], refs[7:]
     if not last:
         (left_back, left_field), refs = refs[:2], refs[2:]
@@ -250,7 +250,7 @@
     radial = lax.broadcasted_iota(jnp.int32, (SUB, LANES), 0)
     at_once = cells.shape[1] // 2
 
-    def rotate(half, t, ground, jls):
+    def rotate(half, t, ground, jls, onward=True):
         for jl in jls:
             column = []
             for ql in range(FOUR):
@@ -287,7 +287,8 @@
                     re, im = jnp.where(open_air, re, 0.0), jnp.where(open_air, im, 0.0)
                 value.append(re * re + im * im)
                 moved.append((re, im))
-            enter(field.at[half], moved, jl)
+            if onward:
+                enter(field.at[half], moved, jl)
             place = FOUR * jl * SUB
             energy[half, place : place + FOUR * SUB, :] = jnp.concatenate(split(jnp.concatenate(value)), axis=1)
 
@@ -307,15 +308,15 @@
     def turn_of(t, resting, moving):
         ground = ground_of(resting, t)
         pieces = [functools.partial(rotate, resting, t, ground, [jl]) for jl in range(EIGHT)]
-        product = forward(field.at[moving], w_forward, twiddle, pieces[:3])
+        product = forward(field.at[moving], weights, twiddle, pieces[:3])
         binned(moving, jnp.maximum(t - 1, 0) if resting == 0 else t)
-        product = inverse(product, w_inverse, spread, pieces[3:6])
+        product = inverse(product, weights, spread, pieces[3:6])
         for piece in pieces[6:]:
             piece()
         leave(back.at[moving], product, twiddle)
 
     def last_turn(t, resting, before):
-        rotate(resting, t, ground_of(resting, t), range(EIGHT))
+        rotate(resting, t, ground_of(resting, t), range(EIGHT), False)
         binned(before, t)
 
     def step(t, carry):
@@ -326,7 +327,10 @@
     power[...] = jnp.zeros_like(power)
     back[0] = launched[...]
     for half in range(1, halves):
-        field[half] = entered[half - 1]
+        if begin == 0:
+            enter_source(field.at[half], entered)
+        else:
+            field[half] = entered[half - 1]
     energy[...] = jnp.zeros_like(energy)
     whole_steps = steps - 1 if last else steps
     lax.fori_loop(0, whole_steps, step, 0)
@@ -372,23 +376,22 @@
     smem = pl.BlockSpec(memory_space=pltpu.SMEM)
     outputs = [jax.ShapeDtypeStruct((tiles, BINS), F32)]
     if not last:
-        outputs += [jax.ShapeDtypeStruct(part.shape, F32) for part in state]
+        outputs += [jax.ShapeDtypeStruct((*lead, 2, ROWS, SUB, LANES), F32) for lead in ((), (halves - 1,))]
     call = pl.pallas_call(
         functools.partial(march_kernel, begin, steps, own, last),
         out_shape=outputs,
-        in_specs=[vmem] * (11 + len(totals)) + [smem],
+        in_specs=[vmem] * (10 + len(totals)) + [smem],
         out_specs=[vmem] * len(outputs),
         scratch_shapes=[
             pltpu.VMEM((halves, 2, ROWS, SUB, LANES), F32),
             pltpu.VMEM((halves, 2, ROWS, SUB, LANES), F32),
             pltpu.VMEM((halves, ROWS * SUB, 2 * LANES), BF16),
             pltpu.VMEM((-(-steps * batch // LANES) * LANES, BINS), F32),
-        ] + [pltpu.VMEM((*table.shape[:-1], SUB, LANES), F32) for table in consts[2:6]],
+        ] + [pltpu.VMEM((*table.shape[:-1], SUB, LANES), F32) for table in consts[1:5]],
         compiler_params=pltpu.CompilerParams(vmem_limit_bytes=12 * 1024 * 1024),
         cost_estimate=pl.CostEstimate(
             flops=steps * 1_600_000_000, bytes_accessed=4 * 1024 * 1024, transcendentals=0
         ),
-        input_output_aliases={4: 0} if last else {2: 1, 3: 2},
         name="march",
     )
     return call(received, cells, *state, *totals, *consts, section)
@@ -485,8 +488,8 @@
     everyone = gather_small(jnp.concatenate([terrain.T, tile_map.T]))
     cells = lax.dynamic_index_in_dim(everyone, lax.axis_index("radial"), 1, keepdims=False)
     consts = [jnp.asarray(v) for v in tables()]
-    launched, entered = launch(source.reshape(2, ROWS, LANES), consts)
-    state = (launched, jnp.stack([entered] * (batch // SUB - 1)))
+    start = source.reshape(2, ROWS, LANES)
+    state = (launch(start, consts), start)
     tiles = TILE_DEV * owners
     totals, *state = march(section, 0, middle, early, cells, state, [], consts, tiles, own, False)
     (totals,) = march(section, middle, steps - middle, late, cells, state, [totals], consts, tiles, own, True)

time: 86.9 us -> 85.9 us (0.988)
  Pallas kernels: 28.5 us -> 27 us
    pallas_call x2, Pallas kernels: 22.6 us -> 21.1 us  [march(): return call(received, cells, *state, *totals, *consts, section)]
where the time goes in v16:
time: 85.9 us; the launch traced here: 85.6 us
  waiting for transfers between devices  35.2 us (41%)
  Pallas kernels  27 us (31%)
  starting transfers between devices  21.9 us (25%)
  other arithmetic  0.96 us (1%)
    pallas_call x2, Pallas kernels, march(): return call(received, cells, *state, *totals, *consts, section)  21.1 us
    ppermute x3, waiting for transfers between devices, gather_small(): lax.ppermute(both, 'range', [(i, i ^ d) for i in range(sections)])  17.8 us
    all_to_all x1, waiting for transfers between devices, local(): lax.all_to_all(totals.reshape(owners, TILE_DEV, BINS), ('range', 'radial'...  7.68 us
    all_to_all x1, starting transfers between devices, local(): early = lax.all_to_all(dealt, 'range', 0, 0, tiled=True)  7.29 us
    ppermute x1, waiting for transfers between devices, gather_small(): lax.ppermute(pair, 'range', [(i, i ^ 1) for i in range(sections)])  5.34 us
    pallas_call x2, Pallas kernels, deal(): pl.pallas_call(kernel, out_shape=jax.ShapeDtypeStruct((sections, count, h...  5.3 us
    ppermute x3, starting transfers between devices, gather_small(): lax.ppermute(both, 'range', [(i, i ^ d) for i in range(sections)])  5.08 us
    all_to_all x1, starting transfers between devices, local(): lax.all_to_all(totals.reshape(owners, TILE_DEV, BINS), ('range', 'radial'...  3.74 us
  transfers between devices with their start and end apart: 8, of which 6 were waited for; matrix products, arithmetic and copies ran while one was open for 0% of the time, Pallas kernels for 20%

profile of v16, /device:TPU:0, one launch (start us, length us, event | category | flops | bytes accessed | tf_op | source)
XLA Modules:
  0.0 85.6 jit_solution(11093909724004671742)
XLA Ops:
  0.0 2.9 %deal.2 = bf16[8,176,512]{2,1,0:T(8,128)(2,1)} custom-call(bf16[128,16,512]{2,1,0:T(8,128)(2,1)} %levels.2), custom_call_target="tpu_custom_call" | custom-call | flops 1000000000 | bytes 4194304 | tf_op jit(solution)/shard_map/deal/pallas_call | solution.py:448
  2.9 0.0 copy-start.7
  3.0 0.0 copy-start.8
  3.0 7.3 %all-to-all-start.1 = ((bf16[8,176,512]{2,1,0:T(8,128)(2,1)}), bf16[8,176,512]{2,1,0:T(8,128)(2,1)S(1)}, u32[]{:S(2)}, u32[]{:S(2)}) async-start(bf16[8,176,512]{2,1,0:T(8,128)(2,1)} %deal.2), calls=%async_computation.1 | async-start | bytes 2883584 | tf_op jit(solution)/shard_map/all_to_all | solution.py:486
  10.3 0.0 copy-done.7
  10.3 0.0 copy-done.8
  10.3 0.1 collective-permute-start
  10.4 1.1 %collective-permute-done = s32[4,128]{1,0:T(4,128)S(1)} collective-permute-done((s32[4,128]{1,0:T(4,128)S(1)}, s32[4,128]{1,0:T(4,128)S(1)}, u32[]{:S(2)}, u32[]{:S(2)}) %collective-permute-start) | collective-permute-done | bytes 2080 | tf_op jit(solution)/shard_map/ppermute | solution.py:462
  11.5 0.0 copy-start.6
  11.5 0.0 copy-start
  11.6 0.0 copy-start.2
  11.6 0.0 copy-start.3
  11.6 2.1 %collective-permute-start.1 = (s32[2,4,128]{2,1,0:T(4,128)S(1)}, s32[2,4,128]{2,1,0:T(4,128)S(1)}, u32[]{:S(2)}, u32[]{:S(2)}) collective-permute-start(s32[2,4,128]{2,1,0:T(4,128)S(1)} %pad_add_fusion.1), channel_id=1, source_target_pairs={{0,2},{2,0},{4,6},{6,4},{8,10},{10,8},{12,14},{14,12},{1,3},{3,1},... | collective-permute-start | bytes 12296 | tf_op jit(solution)/shard_map/ppermute | solution.py:465
  13.7 2.4 %deal.3 = bf16[8,80,512]{2,1,0:T(8,128)(2,1)} custom-call(bf16[128,16,512]{2,1,0:T(8,128)(2,1)} %levels.2), custom_call_target="tpu_custom_call" | custom-call | flops 1000000000 | bytes 4194304 | tf_op jit(solution)/shard_map/deal/pallas_call | solution.py:448
  16.1 0.0 copy-done.6
  16.1 5.3 %collective-permute-done.1 = s32[2,4,128]{2,1,0:T(4,128)S(1)} collective-permute-done((s32[2,4,128]{2,1,0:T(4,128)S(1)}, s32[2,4,128]{2,1,0:T(4,128)S(1)}, u32[]{:S(2)}, u32[]{:S(2)}) %collective-permute-start.1) | collective-permute-done | bytes 4128 | tf_op jit(solution)/shard_map/ppermute | solution.py:465
  21.5 2.5 %collective-permute-start.2 = (s32[2,2,4,128]{3,2,1,0:T(4,128)S(1)}, s32[2,2,4,128]{3,2,1,0:T(4,128)S(1)}, u32[]{:S(2)}, u32[]{:S(2)}) collective-permute-start(s32[2,2,4,128]{3,2,1,0:T(4,128)S(1)} %get-tuple-element.19), channel_id=1, source_target_pairs={{0,4},{2,6},{4,0},{6,2},{8,12},{10,14},{12,8},{14,10},{1,5},{3,7},... | collective-permute-start | bytes 24584 | tf_op jit(solution)/shard_map/ppermute | solution.py:470
  24.0 0.0 copy-done
  24.0 0.0 copy-done.2
  24.0 0.0 copy-done.3
  24.0 0.6 launch.1.launched
  24.7 0.0 copy-start.1
  24.7 0.0 copy-start.4
  24.7 0.0 copy-start.5
  24.8 2.1 %collective-permute-start.3 = (s32[2,2,4,128]{3,2,1,0:T(4,128)S(1)}, s32[2,2,4,128]{3,2,1,0:T(4,128)S(1)}, u32[]{:S(2)}, u32[]{:S(2)}) collective-permute-start(s32[2,2,4,128]{3,2,1,0:T(4,128)S(1)} %get-tuple-element.19), channel_id=1, source_target_pairs={{0,8},{2,10},{4,12},{6,14},{8,0},{10,2},{12,4},{14,6},{1,9},{3,11}... | collective-permute-start | bytes 24584 | tf_op jit(solution)/shard_map/ppermute | solution.py:470
  26.9 0.4 collective-permute-start.4
  27.3 7.3 %collective-permute-done.2 = s32[2,2,4,128]{3,2,1,0:T(4,128)S(1)} collective-permute-done((s32[2,2,4,128]{3,2,1,0:T(4,128)S(1)}, s32[2,2,4,128]{3,2,1,0:T(4,128)S(1)}, u32[]{:S(2)}, u32[]{:S(2)}) %collective-permute-start.2) | collective-permute-done | bytes 8224 | tf_op jit(solution)/shard_map/ppermute | solution.py:470
  34.6 10.5 %collective-permute-done.3 = s32[2,2,4,128]{3,2,1,0:T(4,128)S(1)} collective-permute-done((s32[2,2,4,128]{3,2,1,0:T(4,128)S(1)}, s32[2,2,4,128]{3,2,1,0:T(4,128)S(1)}, u32[]{:S(2)}, u32[]{:S(2)}) %collective-permute-start.3) | collective-permute-done | bytes 8224 | tf_op jit(solution)/shard_map/ppermute | solution.py:470
  45.1 0.0 collective-permute-done.4
  45.1 0.0 all-to-all-done.1.levels
  45.1 3.6 %all-to-all-start = ((bf16[8,80,512]{2,1,0:T(8,128)(2,1)}), bf16[8,80,512]{2,1,0:T(8,128)(2,1)S(1)}, u32[]{:S(2)}, u32[]{:S(2)}) async-start(bf16[8,80,512]{2,1,0:T(8,128)(2,1)} %deal.3), calls=%async_computation | async-start | bytes 1310720 | tf_op jit(solution)/shard_map/all_to_all | solution.py:487
  48.8 0.0 copy-done.1
  48.8 0.0 copy-done.4
  48.8 0.0 copy-done.5
  48.8 14.0 %march.2 = (f32[256,128]{1,0:T(8,128)S(1)}, f32[2,32,8,128]{3,2,1,0:T(8,128)S(1)}, f32[1,2,32,8,128]{4,3,2,1,0:T(8,128)S(1)}) custom-call(bf16[8,176,512]{2,1,0:T(8,128)(2,1)S(1)} %all-to-all-done.1.levels, s32[8,4,128]{2,1,0:T(4,128)S(1)} %dynamic-slice_bitcast_fusion.cells, f32[2,32,8,128]{3,2,1,0:T(8,128)S(1)} %launch.1.launched, ...), custom_call_target="tpu_custom_call" | custom-call | flops 17600000000 | bytes 4194304 | tf_op jit(solution)/shard_map/march/pallas_call | solution.py:397
  62.8 3.3 %all-to-all-done.levels = bf16[8,80,512]{2,1,0:T(8,128)(2,1)S(1)} async-done(((bf16[8,80,512]{2,1,0:T(8,128)(2,1)}), bf16[8,80,512]{2,1,0:T(8,128)(2,1)S(1)}, u32[]{:S(2)}, u32[]{:S(2)}) %all-to-all-start) | async-done | bytes 655392 | tf_op jit(solution)/shard_map/all_to_all | solution.py:487
  66.2 7.0 %march.3 = f32[256,128]{1,0:T(8,128)} custom-call(bf16[8,80,512]{2,1,0:T(8,128)(2,1)S(1)} %all-to-all-done.levels, s32[8,4,128]{2,1,0:T(4,128)S(1)} %dynamic-slice_bitcast_fusion.cells, f32[2,32,8,128]{3,2,1,0:T(8,128)S(1)} %get-tuple-element.14.launched, f32[1,2,32,8,128]{4,3,2,1,0:T(8,128)S(1)} %get-tuple-element.15.entered, ...), custom_call_target="tpu_custom_call" | custom-call | flops 8000000000 | bytes 4194304 | tf_op jit(solution)/shard_map/march/pallas_call | solution.py:397
  73.2 3.7 %all-to-all-start.2 = ((f32[16,16,128]{2,1,0:T(8,128)}), f32[16,16,128]{2,1,0:T(8,128)S(1)}, u32[]{:S(2)}, u32[]{:S(2)}) async-start(f32[16,16,128]{2,1,0:T(8,128)} %bitcast.8), calls=%async_computation.2 | async-start | bytes 262144 | tf_op jit(solution)/shard_map/all_to_all | solution.py:498
  77.0 0.2 convert_reduce_fusion
  77.2 7.7 %all-to-all-done.2 = f32[16,16,128]{2,1,0:T(8,128)S(1)} async-done(((f32[16,16,128]{2,1,0:T(8,128)}), f32[16,16,128]{2,1,0:T(8,128)S(1)}, u32[]{:S(2)}, u32[]{:S(2)}) %all-to-all-start.2) | async-done | bytes 131104 | tf_op jit(solution)/shard_map/all_to_all | solution.py:498
  84.9 0.7 broadcast_divide_fusion
  (14 shorter events, 0.1 us)
Async XLA Ops:
  2.9 7.3 %copy-start.7 = (s32[128,2]{0,1:T(2,128)S(1)}, s32[128,2]{0,1:T(2,128)}, u32[]{:S(2)}) copy-start(s32[128,2]{0,1:T(2,128)} %param.13) | copy-start | bytes 3076
  3.0 7.3 %copy-start.8 = (s32[128,2]{0,1:T(2,128)S(1)}, s32[128,2]{0,1:T(2,128)}, u32[]{:S(2)}) copy-start(s32[128,2]{0,1:T(2,128)} %param.12) | copy-start | bytes 3076
  3.0 42.1 %all-to-all-start.1 = ((bf16[8,176,512]{2,1,0:T(8,128)(2,1)}), bf16[8,176,512]{2,1,0:T(8,128)(2,1)S(1)}, u32[]{:S(2)}, u32[]{:S(2)}) async-start(bf16[8,176,512]{2,1,0:T(8,128)(2,1)} %deal.2), calls=%async_computation.1 | async-start | bytes 2883584 | tf_op jit(solution)/shard_map/all_to_all | solution.py:486
  10.3 1.2 %collective-permute-start = (s32[4,128]{1,0:T(4,128)S(1)}, s32[4,128]{1,0:T(4,128)S(1)}, u32[]{:S(2)}, u32[]{:S(2)}) collective-permute-start(s32[4,128]{1,0:T(4,128)S(1)} %pad_add_fusion.2), channel_id=1, source_target_pairs={{0,1},{1,0},{2,3},{3,2},{4,5},{5,4},{6,7},{7,6},{8,9},{9,8},{10,11... | collective-permute-start | bytes 6152 | tf_op jit(solution)/shard_map/ppermute | solution.py:462
  11.5 4.5 %copy-start.6 = (f32[2,4096]{1,0:T(2,128)S(1)}, f32[2,4096]{1,0:T(2,128)}, u32[]{:S(2)}) copy-start(f32[2,4096]{1,0:T(2,128)} %param.11) | copy-start | bytes 98308
  11.5 12.5 %copy-start = (bf16[2,256,256]{2,1,0:T(8,128)(2,1)S(1)}, bf16[2,256,256]{2,1,0:T(8,128)(2,1)}, u32[]{:S(2)}) copy-start(bf16[2,256,256]{2,1,0:T(8,128)(2,1)} %constant.81.clone.weights.refs_0_.refs_1_) | copy-start | bytes 786436
  11.6 12.4 %copy-start.2 = (f32[2,32,128]{2,1,0:T(8,128)S(1)}, f32[2,32,128]{2,1,0:T(8,128)}, u32[]{:S(2)}) copy-start(f32[2,32,128]{2,1,0:T(8,128)} %constant.82.clone.twiddle_table.refs_1_.refs_2_) | copy-start | bytes 98308
  11.6 12.4 %copy-start.3 = (f32[2,32,128]{2,1,0:T(8,128)S(1)}, f32[2,32,128]{2,1,0:T(8,128)}, u32[]{:S(2)}) copy-start(f32[2,32,128]{2,1,0:T(8,128)} %constant.83.clone.spread_table.refs_2_.refs_3_) | copy-start | bytes 98308
  11.6 9.8 %collective-permute-start.1 = (s32[2,4,128]{2,1,0:T(4,128)S(1)}, s32[2,4,128]{2,1,0:T(4,128)S(1)}, u32[]{:S(2)}, u32[]{:S(2)}) collective-permute-start(s32[2,4,128]{2,1,0:T(4,128)S(1)} %pad_add_fusion.1), channel_id=1, source_target_pairs={{0,2},{2,0},{4,6},{6,4},{8,10},{10,8},{12,14},{14,12},{1,3},{3,1},... | collective-permute-start | bytes 12296 | tf_op jit(solution)/shard_map/ppermute | solution.py:465
  21.5 13.2 %collective-permute-start.2 = (s32[2,2,4,128]{3,2,1,0:T(4,128)S(1)}, s32[2,2,4,128]{3,2,1,0:T(4,128)S(1)}, u32[]{:S(2)}, u32[]{:S(2)}) collective-permute-start(s32[2,2,4,128]{3,2,1,0:T(4,128)S(1)} %get-tuple-element.19), channel_id=1, source_target_pairs={{0,4},{2,6},{4,0},{6,2},{8,12},{10,14},{12,8},{14,10},{1,5},{3,7},... | collective-permute-start | bytes 24584 | tf_op jit(solution)/shard_map/ppermute | solution.py:470
  24.7 24.1 %copy-start.1 = (bf16[256,128]{1,0:T(8,128)(2,1)S(1)}, bf16[256,128]{1,0:T(8,128)(2,1)}, u32[]{:S(2)}) copy-start(bf16[256,128]{1,0:T(8,128)(2,1)} %constant.86.clone.refs_5_.refs_6_) | copy-start | bytes 196612
  24.7 24.1 %copy-start.4 = (f32[32,128]{1,0:T(8,128)S(1)}, f32[32,128]{1,0:T(8,128)}, u32[]{:S(2)}) copy-start(f32[32,128]{1,0:T(8,128)} %constant.84.clone.refs_3_.refs_4_) | copy-start | bytes 49156
  24.7 24.1 %copy-start.5 = (f32[32,128]{1,0:T(8,128)S(1)}, f32[32,128]{1,0:T(8,128)}, u32[]{:S(2)}) copy-start(f32[32,128]{1,0:T(8,128)} %constant.85.clone.refs_4_.refs_5_) | copy-start | bytes 49156
  24.8 20.3 %collective-permute-start.3 = (s32[2,2,4,128]{3,2,1,0:T(4,128)S(1)}, s32[2,2,4,128]{3,2,1,0:T(4,128)S(1)}, u32[]{:S(2)}, u32[]{:S(2)}) collective-permute-start(s32[2,2,4,128]{3,2,1,0:T(4,128)S(1)} %get-tuple-element.19), channel_id=1, source_target_pairs={{0,8},{2,10},{4,12},{6,14},{8,0},{10,2},{12,4},{14,6},{1,9},{3,11}... | collective-permute-start | bytes 24584 | tf_op jit(solution)/shard_map/ppermute | solution.py:470
  26.9 18.2 %collective-permute-start.4 = (s32[2,2,4,128]{3,2,1,0:T(4,128)S(1)}, s32[2,2,4,128]{3,2,1,0:T(4,128)S(1)}, u32[]{:S(2)}, u32[]{:S(2)}) collective-permute-start(s32[2,2,4,128]{3,2,1,0:T(4,128)S(1)} %get-tuple-element.19), channel_id=1, source_target_pairs={{0,12},{2,14},{4,8},{6,10},{8,4},{10,6},{12,0},{14,2},{1,13},{3,15... | collective-permute-start | bytes 24584 | tf_op jit(solution)/shard_map/ppermute | solution.py:470
  45.1 21.0 %all-to-all-start = ((bf16[8,80,512]{2,1,0:T(8,128)(2,1)}), bf16[8,80,512]{2,1,0:T(8,128)(2,1)S(1)}, u32[]{:S(2)}, u32[]{:S(2)}) async-start(bf16[8,80,512]{2,1,0:T(8,128)(2,1)} %deal.3), calls=%async_computation | async-start | bytes 1310720 | tf_op jit(solution)/shard_map/all_to_all | solution.py:487
  73.2 11.7 %all-to-all-start.2 = ((f32[16,16,128]{2,1,0:T(8,128)}), f32[16,16,128]{2,1,0:T(8,128)S(1)}, u32[]{:S(2)}, u32[]{:S(2)}) async-start(f32[16,16,128]{2,1,0:T(8,128)} %bitcast.8), calls=%async_computation.2 | async-start | bytes 262144 | tf_op jit(solution)/shard_map/all_to_all | solution.py:498

commit v17 on v16

--- a/solution.py
+++ b/solution.py
@@ -23,7 +23,7 @@
 ABSORB_RATE = 0.05
 TERRAIN_ROWS = 4
 SUB = 8
-EARLY_SHARE = 0.6875
+EARLY_SHARE = 0.75
 
 F32 = jnp.float32
 BF16 = jnp.bfloat16

time: 85.9 us -> 87.9 us (1.023)
  starting transfers between devices: 21.9 us -> 23.9 us
    all_to_all x1, waiting for transfers between devices: 3.32 us -> 0.01 us  [local(): lax.all_to_all(deal(refractivity, middle, steps, sections, own, batch), '...]
    all_to_all x1, starting transfers between devices: 3.74 us -> 6.1 us  [local(): lax.all_to_all(totals.reshape(owners, TILE_DEV, BINS), ('range', 'radial'...]
    ppermute x3, waiting for transfers between devices: 17.8 us -> 19.5 us  [gather_small(): lax.ppermute(both, 'range', [(i, i ^ d) for i in range(sections)])]
    ppermute x1, waiting for transfers between devices: 5.34 us -> 6.77 us  [gather_small(): lax.ppermute(pair, 'range', [(i, i ^ 1) for i in range(sections)])]
  transfers between devices with their start and end apart: 8 -> 8, of which waited for: 6 -> 5; matrix products, arithmetic and copies ran while one was open for 0% -> 0% of each run, Pallas kernels for 20% -> 21%
where the time goes in v17:
time: 87.9 us; the launch traced here: 87.5 us
  waiting for transfers between devices  35.1 us (40%)
  Pallas kernels  27.1 us (31%)
  starting transfers between devices  23.9 us (27%)
  other arithmetic  0.96 us (1%)
    pallas_call x2, Pallas kernels, march(): return call(received, cells, *state, *totals, *consts, section)  21 us
    ppermute x3, waiting for transfers between devices, gather_small(): lax.ppermute(both, 'range', [(i, i ^ d) for i in range(sections)])  19.5 us
    all_to_all x1, waiting for transfers between devices, local(): lax.all_to_all(totals.reshape(owners, TILE_DEV, BINS), ('range', 'radial'...  7.68 us
    all_to_all x1, starting transfers between devices, local(): early = lax.all_to_all(dealt, 'range', 0, 0, tiled=True)  7.29 us
    ppermute x1, waiting for transfers between devices, gather_small(): lax.ppermute(pair, 'range', [(i, i ^ 1) for i in range(sections)])  6.77 us
    all_to_all x1, starting transfers between devices, local(): lax.all_to_all(totals.reshape(owners, TILE_DEV, BINS), ('range', 'radial'...  6.1 us
    pallas_call x2, Pallas kernels, deal(): pl.pallas_call(kernel, out_shape=jax.ShapeDtypeStruct((sections, count, h...  5.37 us
    ppermute x3, starting transfers between devices, gather_small(): lax.ppermute(both, 'range', [(i, i ^ d) for i in range(sections)])  4.73 us
  transfers between devices with their start and end apart: 8, of which 5 were waited for; matrix products, arithmetic and copies ran while one was open for 0% of the time, Pallas kernels for 21%

profile of v17, /device:TPU:0, one launch (start us, length us, event | category | flops | bytes accessed | tf_op | source)
XLA Modules:
  0.0 87.5 jit_solution(7334168478773246239)
XLA Ops:
  0.0 3.0 %deal.2 = bf16[8,192,512]{2,1,0:T(8,128)(2,1)} custom-call(bf16[128,16,512]{2,1,0:T(8,128)(2,1)} %levels.2), custom_call_target="tpu_custom_call" | custom-call | flops 1000000000 | bytes 4194304 | tf_op jit(solution)/shard_map/deal/pallas_call | solution.py:448
  3.0 0.0 copy-start.7
  3.1 0.0 copy-start.8
  3.1 7.3 %all-to-all-start.1 = ((bf16[8,192,512]{2,1,0:T(8,128)(2,1)}), bf16[8,192,512]{2,1,0:T(8,128)(2,1)S(1)}, u32[]{:S(2)}, u32[]{:S(2)}) async-start(bf16[8,192,512]{2,1,0:T(8,128)(2,1)} %deal.2), calls=%async_computation.1 | async-start | bytes 3145728 | tf_op jit(solution)/shard_map/all_to_all | solution.py:486
  10.4 0.0 copy-done.7
  10.4 0.0 copy-done.8
  10.4 0.1 collective-permute-start
  10.5 1.1 %collective-permute-done = s32[4,128]{1,0:T(4,128)S(1)} collective-permute-done((s32[4,128]{1,0:T(4,128)S(1)}, s32[4,128]{1,0:T(4,128)S(1)}, u32[]{:S(2)}, u32[]{:S(2)}) %collective-permute-start) | collective-permute-done | bytes 2080 | tf_op jit(solution)/shard_map/ppermute | solution.py:462
  11.6 0.0 copy-start.6
  11.6 0.0 copy-start
  11.6 0.0 copy-start.2
  11.7 0.0 copy-start.3
  11.7 2.1 %collective-permute-start.1 = (s32[2,4,128]{2,1,0:T(4,128)S(1)}, s32[2,4,128]{2,1,0:T(4,128)S(1)}, u32[]{:S(2)}, u32[]{:S(2)}) collective-permute-start(s32[2,4,128]{2,1,0:T(4,128)S(1)} %pad_add_fusion.1), channel_id=1, source_target_pairs={{0,2},{2,0},{4,6},{6,4},{8,10},{10,8},{12,14},{14,12},{1,3},{3,1},... | collective-permute-start | bytes 12296 | tf_op jit(solution)/shard_map/ppermute | solution.py:465
  13.8 2.3 %deal.3 = bf16[8,64,512]{2,1,0:T(8,128)(2,1)} custom-call(bf16[128,16,512]{2,1,0:T(8,128)(2,1)} %levels.2), custom_call_target="tpu_custom_call" | custom-call | flops 1000000000 | bytes 4194304 | tf_op jit(solution)/shard_map/deal/pallas_call | solution.py:448
  16.1 0.0 copy-done.6
  16.2 6.8 %collective-permute-done.1 = s32[2,4,128]{2,1,0:T(4,128)S(1)} collective-permute-done((s32[2,4,128]{2,1,0:T(4,128)S(1)}, s32[2,4,128]{2,1,0:T(4,128)S(1)}, u32[]{:S(2)}, u32[]{:S(2)}) %collective-permute-start.1) | collective-permute-done | bytes 4128 | tf_op jit(solution)/shard_map/ppermute | solution.py:465
  23.0 2.2 %collective-permute-start.2 = (s32[2,2,4,128]{3,2,1,0:T(4,128)S(1)}, s32[2,2,4,128]{3,2,1,0:T(4,128)S(1)}, u32[]{:S(2)}, u32[]{:S(2)}) collective-permute-start(s32[2,2,4,128]{3,2,1,0:T(4,128)S(1)} %get-tuple-element.19), channel_id=1, source_target_pairs={{0,4},{2,6},{4,0},{6,2},{8,12},{10,14},{12,8},{14,10},{1,5},{3,7},... | collective-permute-start | bytes 24584 | tf_op jit(solution)/shard_map/ppermute | solution.py:470
  25.1 0.0 copy-done
  25.1 0.0 copy-done.2
  25.1 0.0 copy-done.3
  25.2 0.0 copy-start.1
  25.2 0.0 copy-start.4
  25.2 0.0 copy-start.5
  25.2 0.6 launch.1.launched
  25.9 2.1 %collective-permute-start.3 = (s32[2,2,4,128]{3,2,1,0:T(4,128)S(1)}, s32[2,2,4,128]{3,2,1,0:T(4,128)S(1)}, u32[]{:S(2)}, u32[]{:S(2)}) collective-permute-start(s32[2,2,4,128]{3,2,1,0:T(4,128)S(1)} %get-tuple-element.19), channel_id=1, source_target_pairs={{0,8},{2,10},{4,12},{6,14},{8,0},{10,2},{12,4},{14,6},{1,9},{3,11}... | collective-permute-start | bytes 24584 | tf_op jit(solution)/shard_map/ppermute | solution.py:470
  28.1 0.4 collective-permute-start.4
  28.5 8.5 %collective-permute-done.2 = s32[2,2,4,128]{3,2,1,0:T(4,128)S(1)} collective-permute-done((s32[2,2,4,128]{3,2,1,0:T(4,128)S(1)}, s32[2,2,4,128]{3,2,1,0:T(4,128)S(1)}, u32[]{:S(2)}, u32[]{:S(2)}) %collective-permute-start.2) | collective-permute-done | bytes 8224 | tf_op jit(solution)/shard_map/ppermute | solution.py:470
  37.0 11.0 %collective-permute-done.3 = s32[2,2,4,128]{3,2,1,0:T(4,128)S(1)} collective-permute-done((s32[2,2,4,128]{3,2,1,0:T(4,128)S(1)}, s32[2,2,4,128]{3,2,1,0:T(4,128)S(1)}, u32[]{:S(2)}, u32[]{:S(2)}) %collective-permute-start.3) | collective-permute-done | bytes 8224 | tf_op jit(solution)/shard_map/ppermute | solution.py:470
  48.0 0.0 collective-permute-done.4
  48.0 0.0 all-to-all-done.1.levels
  48.0 3.6 %all-to-all-start = ((bf16[8,64,512]{2,1,0:T(8,128)(2,1)}), bf16[8,64,512]{2,1,0:T(8,128)(2,1)S(1)}, u32[]{:S(2)}, u32[]{:S(2)}) async-start(bf16[8,64,512]{2,1,0:T(8,128)(2,1)} %deal.3), calls=%async_computation | async-start | bytes 1048576 | tf_op jit(solution)/shard_map/all_to_all | solution.py:487
  51.7 0.0 copy-done.1
  51.7 0.0 copy-done.4
  51.7 0.0 copy-done.5
  51.7 15.3 %march.2 = (f32[256,128]{1,0:T(8,128)S(1)}, f32[2,32,8,128]{3,2,1,0:T(8,128)S(1)}, f32[1,2,32,8,128]{4,3,2,1,0:T(8,128)S(1)}) custom-call(bf16[8,192,512]{2,1,0:T(8,128)(2,1)S(1)} %all-to-all-done.1.levels, s32[8,4,128]{2,1,0:T(4,128)S(1)} %dynamic-slice_bitcast_fusion.cells, f32[2,32,8,128]{3,2,1,0:T(8,128)S(1)} %launch.1.launched, ...), custom_call_target="tpu_custom_call" | custom-call | flops 19200000000 | bytes 4194304 | tf_op jit(solution)/shard_map/march/pallas_call | solution.py:397
  67.0 0.0 all-to-all-done.levels
  67.0 5.8 %march.3 = f32[256,128]{1,0:T(8,128)} custom-call(bf16[8,64,512]{2,1,0:T(8,128)(2,1)S(1)} %all-to-all-done.levels, s32[8,4,128]{2,1,0:T(4,128)S(1)} %dynamic-slice_bitcast_fusion.cells, f32[2,32,8,128]{3,2,1,0:T(8,128)S(1)} %get-tuple-element.14.launched, f32[1,2,32,8,128]{4,3,2,1,0:T(8,128)S(1)} %get-tuple-element.15.entered, ...), custom_call_target="tpu_custom_call" | custom-call | flops 6400000000 | bytes 4194304 | tf_op jit(solution)/shard_map/march/pallas_call | solution.py:397
  72.8 6.1 %all-to-all-start.2 = ((f32[16,16,128]{2,1,0:T(8,128)}), f32[16,16,128]{2,1,0:T(8,128)S(1)}, u32[]{:S(2)}, u32[]{:S(2)}) async-start(f32[16,16,128]{2,1,0:T(8,128)} %bitcast.8), calls=%async_computation.2 | async-start | bytes 262144 | tf_op jit(solution)/shard_map/all_to_all | solution.py:498
  78.9 0.2 convert_reduce_fusion
  79.1 7.7 %all-to-all-done.2 = f32[16,16,128]{2,1,0:T(8,128)S(1)} async-done(((f32[16,16,128]{2,1,0:T(8,128)}), f32[16,16,128]{2,1,0:T(8,128)S(1)}, u32[]{:S(2)}, u32[]{:S(2)}) %all-to-all-start.2) | async-done | bytes 131104 | tf_op jit(solution)/shard_map/all_to_all | solution.py:498
  86.8 0.7 broadcast_divide_fusion
  (14 shorter events, 0.1 us)
Async XLA Ops:
  3.0 7.3 %copy-start.7 = (s32[128,2]{0,1:T(2,128)S(1)}, s32[128,2]{0,1:T(2,128)}, u32[]{:S(2)}) copy-start(s32[128,2]{0,1:T(2,128)} %param.13) | copy-start | bytes 3076
  3.1 7.3 %copy-start.8 = (s32[128,2]{0,1:T(2,128)S(1)}, s32[128,2]{0,1:T(2,128)}, u32[]{:S(2)}) copy-start(s32[128,2]{0,1:T(2,128)} %param.12) | copy-start | bytes 3076
  3.1 44.9 %all-to-all-start.1 = ((bf16[8,192,512]{2,1,0:T(8,128)(2,1)}), bf16[8,192,512]{2,1,0:T(8,128)(2,1)S(1)}, u32[]{:S(2)}, u32[]{:S(2)}) async-start(bf16[8,192,512]{2,1,0:T(8,128)(2,1)} %deal.2), calls=%async_computation.1 | async-start | bytes 3145728 | tf_op jit(solution)/shard_map/all_to_all | solution.py:486
  10.4 1.2 %collective-permute-start = (s32[4,128]{1,0:T(4,128)S(1)}, s32[4,128]{1,0:T(4,128)S(1)}, u32[]{:S(2)}, u32[]{:S(2)}) collective-permute-start(s32[4,128]{1,0:T(4,128)S(1)} %pad_add_fusion.2), channel_id=1, source_target_pairs={{0,1},{1,0},{2,3},{3,2},{4,5},{5,4},{6,7},{7,6},{8,9},{9,8},{10,11... | collective-permute-start | bytes 6152 | tf_op jit(solution)/shard_map/ppermute | solution.py:462
  11.6 4.5 %copy-start.6 = (f32[2,4096]{1,0:T(2,128)S(1)}, f32[2,4096]{1,0:T(2,128)}, u32[]{:S(2)}) copy-start(f32[2,4096]{1,0:T(2,128)} %param.11) | copy-start | bytes 98308
  11.6 13.5 %copy-start = (bf16[2,256,256]{2,1,0:T(8,128)(2,1)S(1)}, bf16[2,256,256]{2,1,0:T(8,128)(2,1)}, u32[]{:S(2)}) copy-start(bf16[2,256,256]{2,1,0:T(8,128)(2,1)} %constant.81.clone.weights.refs_0_.refs_1_) | copy-start | bytes 786436
  11.6 13.5 %copy-start.2 = (f32[2,32,128]{2,1,0:T(8,128)S(1)}, f32[2,32,128]{2,1,0:T(8,128)}, u32[]{:S(2)}) copy-start(f32[2,32,128]{2,1,0:T(8,128)} %constant.82.clone.twiddle_table.refs_1_.refs_2_) | copy-start | bytes 98308
  11.7 13.5 %copy-start.3 = (f32[2,32,128]{2,1,0:T(8,128)S(1)}, f32[2,32,128]{2,1,0:T(8,128)}, u32[]{:S(2)}) copy-start(f32[2,32,128]{2,1,0:T(8,128)} %constant.83.clone.spread_table.refs_2_.refs_3_) | copy-start | bytes 98308
  11.7 11.2 %collective-permute-start.1 = (s32[2,4,128]{2,1,0:T(4,128)S(1)}, s32[2,4,128]{2,1,0:T(4,128)S(1)}, u32[]{:S(2)}, u32[]{:S(2)}) collective-permute-start(s32[2,4,128]{2,1,0:T(4,128)S(1)} %pad_add_fusion.1), channel_id=1, source_target_pairs={{0,2},{2,0},{4,6},{6,4},{8,10},{10,8},{12,14},{14,12},{1,3},{3,1},... | collective-permute-start | bytes 12296 | tf_op jit(solution)/shard_map/ppermute | solution.py:465
  23.0 14.0 %collective-permute-start.2 = (s32[2,2,4,128]{3,2,1,0:T(4,128)S(1)}, s32[2,2,4,128]{3,2,1,0:T(4,128)S(1)}, u32[]{:S(2)}, u32[]{:S(2)}) collective-permute-start(s32[2,2,4,128]{3,2,1,0:T(4,128)S(1)} %get-tuple-element.19), channel_id=1, source_target_pairs={{0,4},{2,6},{4,0},{6,2},{8,12},{10,14},{12,8},{14,10},{1,5},{3,7},... | collective-permute-start | bytes 24584 | tf_op jit(solution)/shard_map/ppermute | solution.py:470
  25.2 26.5 %copy-start.1 = (bf16[256,128]{1,0:T(8,128)(2,1)S(1)}, bf16[256,128]{1,0:T(8,128)(2,1)}, u32[]{:S(2)}) copy-start(bf16[256,128]{1,0:T(8,128)(2,1)} %constant.86.clone.refs_5_.refs_6_) | copy-start | bytes 196612
  25.2 26.5 %copy-start.4 = (f32[32,128]{1,0:T(8,128)S(1)}, f32[32,128]{1,0:T(8,128)}, u32[]{:S(2)}) copy-start(f32[32,128]{1,0:T(8,128)} %constant.84.clone.refs_3_.refs_4_) | copy-start | bytes 49156
  25.2 26.5 %copy-start.5 = (f32[32,128]{1,0:T(8,128)S(1)}, f32[32,128]{1,0:T(8,128)}, u32[]{:S(2)}) copy-start(f32[32,128]{1,0:T(8,128)} %constant.85.clone.refs_4_.refs_5_) | copy-start | bytes 49156
  25.9 22.1 %collective-permute-start.3 = (s32[2,2,4,128]{3,2,1,0:T(4,128)S(1)}, s32[2,2,4,128]{3,2,1,0:T(4,128)S(1)}, u32[]{:S(2)}, u32[]{:S(2)}) collective-permute-start(s32[2,2,4,128]{3,2,1,0:T(4,128)S(1)} %get-tuple-element.19), channel_id=1, source_target_pairs={{0,8},{2,10},{4,12},{6,14},{8,0},{10,2},{12,4},{14,6},{1,9},{3,11}... | collective-permute-start | bytes 24584 | tf_op jit(solution)/shard_map/ppermute | solution.py:470
  28.1 19.9 %collective-permute-start.4 = (s32[2,2,4,128]{3,2,1,0:T(4,128)S(1)}, s32[2,2,4,128]{3,2,1,0:T(4,128)S(1)}, u32[]{:S(2)}, u32[]{:S(2)}) collective-permute-start(s32[2,2,4,128]{3,2,1,0:T(4,128)S(1)} %get-tuple-element.19), channel_id=1, source_target_pairs={{0,12},{2,14},{4,8},{6,10},{8,4},{10,6},{12,0},{14,2},{1,13},{3,15... | collective-permute-start | bytes 24584 | tf_op jit(solution)/shard_map/ppermute | solution.py:470
  48.0 18.9 %all-to-all-start = ((bf16[8,64,512]{2,1,0:T(8,128)(2,1)}), bf16[8,64,512]{2,1,0:T(8,128)(2,1)S(1)}, u32[]{:S(2)}, u32[]{:S(2)}) async-start(bf16[8,64,512]{2,1,0:T(8,128)(2,1)} %deal.3), calls=%async_computation | async-start | bytes 1048576 | tf_op jit(solution)/shard_map/all_to_all | solution.py:487
  72.8 14.0 %all-to-all-start.2 = ((f32[16,16,128]{2,1,0:T(8,128)}), f32[16,16,128]{2,1,0:T(8,128)S(1)}, u32[]{:S(2)}, u32[]{:S(2)}) async-start(f32[16,16,128]{2,1,0:T(8,128)} %bitcast.8), calls=%async_computation.2 | async-start | bytes 262144 | tf_op jit(solution)/shard_map/all_to_all | solution.py:498

commit v18 on v16

--- a/solution.py
+++ b/solution.py
@@ -308,11 +308,9 @@
     def turn_of(t, resting, moving):
         ground = ground_of(resting, t)
         pieces = [functools.partial(rotate, resting, t, ground, [jl]) for jl in range(EIGHT)]
-        product = forward(field.at[moving], weights, twiddle, pieces[:3])
+        product = forward(field.at[moving], weights, twiddle, pieces[:4])
         binned(moving, jnp.maximum(t - 1, 0) if resting == 0 else t)
-        product = inverse(product, weights, spread, pieces[3:6])
-        for piece in pieces[6:]:
-            piece()
+        product = inverse(product, weights, spread, pieces[4:])
         leave(back.at[moving], product, twiddle)
 
     def last_turn(t, resting, before):
@@ -421,7 +419,7 @@
         copy.start()
     for i in range(len(slabs)):
         arrive[i].wait()
-        turn_steps(blocks.at[i], rows, begin, end, turned.at[i])
+        turn_steps(blocks.at[i], rows.at[i % 2], begin, end, turned.at[i])
         leave[i].start()
     for copy in leave:
         copy.wait()
@@ -431,7 +429,7 @@
     return [
         pltpu.VMEM((number, own, steps, heights), BF16),
         pltpu.VMEM((number, count, heights), BF16),
-        pltpu.VMEM((heights // LANES, own * steps, LANES), F32),
+        pltpu.VMEM((2, heights // LANES, own * steps, LANES), F32),
         pltpu.SemaphoreType.DMA((2, number)),
     ]
 

time: 85.9 us -> 85.9 us (level)
  no operation moved by 1% of the time
where the time goes in v18:
time: 85.9 us; the launch traced here: 85.6 us
  waiting for transfers between devices  35.2 us (41%)
  Pallas kernels  27 us (31%)
  starting transfers between devices  21.9 us (25%)
  other arithmetic  0.96 us (1%)
    pallas_call x2, Pallas kernels, march(): return call(received, cells, *state, *totals, *consts, section)  21.1 us
    ppermute x3, waiting for transfers between devices, gather_small(): lax.ppermute(both, 'range', [(i, i ^ d) for i in range(sections)])  17.8 us
    all_to_all x1, waiting for transfers between devices, local(): lax.all_to_all(totals.reshape(owners, TILE_DEV, BINS), ('range', 'radial'...  7.68 us
    all_to_all x1, starting transfers between devices, local(): early = lax.all_to_all(dealt, 'range', 0, 0, tiled=True)  7.29 us
    ppermute x1, waiting for transfers between devices, gather_small(): lax.ppermute(pair, 'range', [(i, i ^ 1) for i in range(sections)])  5.34 us
    pallas_call x2, Pallas kernels, deal(): pl.pallas_call(kernel, out_shape=jax.ShapeDtypeStruct((sections, count, h...  5.3 us
    ppermute x3, starting transfers between devices, gather_small(): lax.ppermute(both, 'range', [(i, i ^ d) for i in range(sections)])  5.08 us
    all_to_all x1, starting transfers between devices, local(): lax.all_to_all(totals.reshape(owners, TILE_DEV, BINS), ('range', 'radial'...  3.74 us
  transfers between devices with their start and end apart: 8, of which 6 were waited for; matrix products, arithmetic and copies ran while one was open for 0% of the time, Pallas kernels for 20%

profile of v18, /device:TPU:0, one launch (start us, length us, event | category | flops | bytes accessed | tf_op | source)
XLA Modules:
  0.0 85.6 jit_solution(18360464813382462066)
XLA Ops:
  0.0 2.9 %deal.2 = bf16[8,176,512]{2,1,0:T(8,128)(2,1)} custom-call(bf16[128,16,512]{2,1,0:T(8,128)(2,1)} %levels.2), custom_call_target="tpu_custom_call" | custom-call | flops 1000000000 | bytes 4194304 | tf_op jit(solution)/shard_map/deal/pallas_call | solution.py:446
  2.9 0.0 copy-start.7
  3.0 0.0 copy-start.8
  3.0 7.3 %all-to-all-start.1 = ((bf16[8,176,512]{2,1,0:T(8,128)(2,1)}), bf16[8,176,512]{2,1,0:T(8,128)(2,1)S(1)}, u32[]{:S(2)}, u32[]{:S(2)}) async-start(bf16[8,176,512]{2,1,0:T(8,128)(2,1)} %deal.2), calls=%async_computation.1 | async-start | bytes 2883584 | tf_op jit(solution)/shard_map/all_to_all | solution.py:484
  10.3 0.0 copy-done.7
  10.3 0.0 copy-done.8
  10.3 0.1 collective-permute-start
  10.4 1.1 %collective-permute-done = s32[4,128]{1,0:T(4,128)S(1)} collective-permute-done((s32[4,128]{1,0:T(4,128)S(1)}, s32[4,128]{1,0:T(4,128)S(1)}, u32[]{:S(2)}, u32[]{:S(2)}) %collective-permute-start) | collective-permute-done | bytes 2080 | tf_op jit(solution)/shard_map/ppermute | solution.py:460
  11.5 0.0 copy-start.6
  11.5 0.0 copy-start
  11.6 0.0 copy-start.2
  11.6 0.0 copy-start.3
  11.6 2.1 %collective-permute-start.1 = (s32[2,4,128]{2,1,0:T(4,128)S(1)}, s32[2,4,128]{2,1,0:T(4,128)S(1)}, u32[]{:S(2)}, u32[]{:S(2)}) collective-permute-start(s32[2,4,128]{2,1,0:T(4,128)S(1)} %pad_add_fusion.1), channel_id=1, source_target_pairs={{0,2},{2,0},{4,6},{6,4},{8,10},{10,8},{12,14},{14,12},{1,3},{3,1},... | collective-permute-start | bytes 12296 | tf_op jit(solution)/shard_map/ppermute | solution.py:463
  13.7 2.4 %deal.3 = bf16[8,80,512]{2,1,0:T(8,128)(2,1)} custom-call(bf16[128,16,512]{2,1,0:T(8,128)(2,1)} %levels.2), custom_call_target="tpu_custom_call" | custom-call | flops 1000000000 | bytes 4194304 | tf_op jit(solution)/shard_map/deal/pallas_call | solution.py:446
  16.1 0.0 copy-done.6
  16.1 5.3 %collective-permute-done.1 = s32[2,4,128]{2,1,0:T(4,128)S(1)} collective-permute-done((s32[2,4,128]{2,1,0:T(4,128)S(1)}, s32[2,4,128]{2,1,0:T(4,128)S(1)}, u32[]{:S(2)}, u32[]{:S(2)}) %collective-permute-start.1) | collective-permute-done | bytes 4128 | tf_op jit(solution)/shard_map/ppermute | solution.py:463
  21.5 2.5 %collective-permute-start.2 = (s32[2,2,4,128]{3,2,1,0:T(4,128)S(1)}, s32[2,2,4,128]{3,2,1,0:T(4,128)S(1)}, u32[]{:S(2)}, u32[]{:S(2)}) collective-permute-start(s32[2,2,4,128]{3,2,1,0:T(4,128)S(1)} %get-tuple-element.19), channel_id=1, source_target_pairs={{0,4},{2,6},{4,0},{6,2},{8,12},{10,14},{12,8},{14,10},{1,5},{3,7},... | collective-permute-start | bytes 24584 | tf_op jit(solution)/shard_map/ppermute | solution.py:468
  24.0 0.0 copy-done
  24.0 0.0 copy-done.2
  24.0 0.0 copy-done.3
  24.0 0.6 launch.1.launched
  24.7 0.0 copy-start.1
  24.7 0.0 copy-start.4
  24.7 0.0 copy-start.5
  24.8 2.1 %collective-permute-start.3 = (s32[2,2,4,128]{3,2,1,0:T(4,128)S(1)}, s32[2,2,4,128]{3,2,1,0:T(4,128)S(1)}, u32[]{:S(2)}, u32[]{:S(2)}) collective-permute-start(s32[2,2,4,128]{3,2,1,0:T(4,128)S(1)} %get-tuple-element.19), channel_id=1, source_target_pairs={{0,8},{2,10},{4,12},{6,14},{8,0},{10,2},{12,4},{14,6},{1,9},{3,11}... | collective-permute-start | bytes 24584 | tf_op jit(solution)/shard_map/ppermute | solution.py:468
  26.9 0.4 collective-permute-start.4
  27.3 7.3 %collective-permute-done.2 = s32[2,2,4,128]{3,2,1,0:T(4,128)S(1)} collective-permute-done((s32[2,2,4,128]{3,2,1,0:T(4,128)S(1)}, s32[2,2,4,128]{3,2,1,0:T(4,128)S(1)}, u32[]{:S(2)}, u32[]{:S(2)}) %collective-permute-start.2) | collective-permute-done | bytes 8224 | tf_op jit(solution)/shard_map/ppermute | solution.py:468
  34.6 10.5 %collective-permute-done.3 = s32[2,2,4,128]{3,2,1,0:T(4,128)S(1)} collective-permute-done((s32[2,2,4,128]{3,2,1,0:T(4,128)S(1)}, s32[2,2,4,128]{3,2,1,0:T(4,128)S(1)}, u32[]{:S(2)}, u32[]{:S(2)}) %collective-permute-start.3) | collective-permute-done | bytes 8224 | tf_op jit(solution)/shard_map/ppermute | solution.py:468
  45.1 0.0 collective-permute-done.4
  45.1 0.0 all-to-all-done.1.levels
  45.1 3.6 %all-to-all-start = ((bf16[8,80,512]{2,1,0:T(8,128)(2,1)}), bf16[8,80,512]{2,1,0:T(8,128)(2,1)S(1)}, u32[]{:S(2)}, u32[]{:S(2)}) async-start(bf16[8,80,512]{2,1,0:T(8,128)(2,1)} %deal.3), calls=%async_computation | async-start | bytes 1310720 | tf_op jit(solution)/shard_map/all_to_all | solution.py:485
  48.8 0.0 copy-done.1
  48.8 0.0 copy-done.4
  48.8 0.0 copy-done.5
  48.8 14.0 %march.2 = (f32[256,128]{1,0:T(8,128)S(1)}, f32[2,32,8,128]{3,2,1,0:T(8,128)S(1)}, f32[1,2,32,8,128]{4,3,2,1,0:T(8,128)S(1)}) custom-call(bf16[8,176,512]{2,1,0:T(8,128)(2,1)S(1)} %all-to-all-done.1.levels, s32[8,4,128]{2,1,0:T(4,128)S(1)} %dynamic-slice_bitcast_fusion.cells, f32[2,32,8,128]{3,2,1,0:T(8,128)S(1)} %launch.1.launched, ...), custom_call_target="tpu_custom_call" | custom-call | flops 17600000000 | bytes 4194304 | tf_op jit(solution)/shard_map/march/pallas_call | solution.py:395
  62.8 3.3 %all-to-all-done.levels = bf16[8,80,512]{2,1,0:T(8,128)(2,1)S(1)} async-done(((bf16[8,80,512]{2,1,0:T(8,128)(2,1)}), bf16[8,80,512]{2,1,0:T(8,128)(2,1)S(1)}, u32[]{:S(2)}, u32[]{:S(2)}) %all-to-all-start) | async-done | bytes 655392 | tf_op jit(solution)/shard_map/all_to_all | solution.py:485
  66.2 7.0 %march.3 = f32[256,128]{1,0:T(8,128)} custom-call(bf16[8,80,512]{2,1,0:T(8,128)(2,1)S(1)} %all-to-all-done.levels, s32[8,4,128]{2,1,0:T(4,128)S(1)} %dynamic-slice_bitcast_fusion.cells, f32[2,32,8,128]{3,2,1,0:T(8,128)S(1)} %get-tuple-element.14.launched, f32[1,2,32,8,128]{4,3,2,1,0:T(8,128)S(1)} %get-tuple-element.15.entered, ...), custom_call_target="tpu_custom_call" | custom-call | flops 8000000000 | bytes 4194304 | tf_op jit(solution)/shard_map/march/pallas_call | solution.py:395
  73.2 3.7 %all-to-all-start.2 = ((f32[16,16,128]{2,1,0:T(8,128)}), f32[16,16,128]{2,1,0:T(8,128)S(1)}, u32[]{:S(2)}, u32[]{:S(2)}) async-start(f32[16,16,128]{2,1,0:T(8,128)} %bitcast.8), calls=%async_computation.2 | async-start | bytes 262144 | tf_op jit(solution)/shard_map/all_to_all | solution.py:496
  77.0 0.2 convert_reduce_fusion
  77.2 7.7 %all-to-all-done.2 = f32[16,16,128]{2,1,0:T(8,128)S(1)} async-done(((f32[16,16,128]{2,1,0:T(8,128)}), f32[16,16,128]{2,1,0:T(8,128)S(1)}, u32[]{:S(2)}, u32[]{:S(2)}) %all-to-all-start.2) | async-done | bytes 131104 | tf_op jit(solution)/shard_map/all_to_all | solution.py:496
  84.9 0.7 broadcast_divide_fusion
  (14 shorter events, 0.1 us)
Async XLA Ops:
  2.9 7.3 %copy-start.7 = (s32[128,2]{0,1:T(2,128)S(1)}, s32[128,2]{0,1:T(2,128)}, u32[]{:S(2)}) copy-start(s32[128,2]{0,1:T(2,128)} %param.13) | copy-start | bytes 3076
  3.0 7.3 %copy-start.8 = (s32[128,2]{0,1:T(2,128)S(1)}, s32[128,2]{0,1:T(2,128)}, u32[]{:S(2)}) copy-start(s32[128,2]{0,1:T(2,128)} %param.12) | copy-start | bytes 3076
  3.0 42.1 %all-to-all-start.1 = ((bf16[8,176,512]{2,1,0:T(8,128)(2,1)}), bf16[8,176,512]{2,1,0:T(8,128)(2,1)S(1)}, u32[]{:S(2)}, u32[]{:S(2)}) async-start(bf16[8,176,512]{2,1,0:T(8,128)(2,1)} %deal.2), calls=%async_computation.1 | async-start | bytes 2883584 | tf_op jit(solution)/shard_map/all_to_all | solution.py:484
  10.3 1.2 %collective-permute-start = (s32[4,128]{1,0:T(4,128)S(1)}, s32[4,128]{1,0:T(4,128)S(1)}, u32[]{:S(2)}, u32[]{:S(2)}) collective-permute-start(s32[4,128]{1,0:T(4,128)S(1)} %pad_add_fusion.2), channel_id=1, source_target_pairs={{0,1},{1,0},{2,3},{3,2},{4,5},{5,4},{6,7},{7,6},{8,9},{9,8},{10,11... | collective-permute-start | bytes 6152 | tf_op jit(solution)/shard_map/ppermute | solution.py:460
  11.5 4.5 %copy-start.6 = (f32[2,4096]{1,0:T(2,128)S(1)}, f32[2,4096]{1,0:T(2,128)}, u32[]{:S(2)}) copy-start(f32[2,4096]{1,0:T(2,128)} %param.11) | copy-start | bytes 98308
  11.5 12.5 %copy-start = (bf16[2,256,256]{2,1,0:T(8,128)(2,1)S(1)}, bf16[2,256,256]{2,1,0:T(8,128)(2,1)}, u32[]{:S(2)}) copy-start(bf16[2,256,256]{2,1,0:T(8,128)(2,1)} %constant.81.clone.weights.refs_0_.refs_1_) | copy-start | bytes 786436
  11.6 12.4 %copy-start.2 = (f32[2,32,128]{2,1,0:T(8,128)S(1)}, f32[2,32,128]{2,1,0:T(8,128)}, u32[]{:S(2)}) copy-start(f32[2,32,128]{2,1,0:T(8,128)} %constant.82.clone.twiddle_table.refs_1_.refs_2_) | copy-start | bytes 98308
  11.6 12.4 %copy-start.3 = (f32[2,32,128]{2,1,0:T(8,128)S(1)}, f32[2,32,128]{2,1,0:T(8,128)}, u32[]{:S(2)}) copy-start(f32[2,32,128]{2,1,0:T(8,128)} %constant.83.clone.spread_table.refs_2_.refs_3_) | copy-start | bytes 98308
  11.6 9.8 %collective-permute-start.1 = (s32[2,4,128]{2,1,0:T(4,128)S(1)}, s32[2,4,128]{2,1,0:T(4,128)S(1)}, u32[]{:S(2)}, u32[]{:S(2)}) collective-permute-start(s32[2,4,128]{2,1,0:T(4,128)S(1)} %pad_add_fusion.1), channel_id=1, source_target_pairs={{0,2},{2,0},{4,6},{6,4},{8,10},{10,8},{12,14},{14,12},{1,3},{3,1},... | collective-permute-start | bytes 12296 | tf_op jit(solution)/shard_map/ppermute | solution.py:463
  21.5 13.2 %collective-permute-start.2 = (s32[2,2,4,128]{3,2,1,0:T(4,128)S(1)}, s32[2,2,4,128]{3,2,1,0:T(4,128)S(1)}, u32[]{:S(2)}, u32[]{:S(2)}) collective-permute-start(s32[2,2,4,128]{3,2,1,0:T(4,128)S(1)} %get-tuple-element.19), channel_id=1, source_target_pairs={{0,4},{2,6},{4,0},{6,2},{8,12},{10,14},{12,8},{14,10},{1,5},{3,7},... | collective-permute-start | bytes 24584 | tf_op jit(solution)/shard_map/ppermute | solution.py:468
  24.7 24.1 %copy-start.1 = (bf16[256,128]{1,0:T(8,128)(2,1)S(1)}, bf16[256,128]{1,0:T(8,128)(2,1)}, u32[]{:S(2)}) copy-start(bf16[256,128]{1,0:T(8,128)(2,1)} %constant.86.clone.refs_5_.refs_6_) | copy-start | bytes 196612
  24.7 24.1 %copy-start.4 = (f32[32,128]{1,0:T(8,128)S(1)}, f32[32,128]{1,0:T(8,128)}, u32[]{:S(2)}) copy-start(f32[32,128]{1,0:T(8,128)} %constant.84.clone.refs_3_.refs_4_) | copy-start | bytes 49156
  24.7 24.1 %copy-start.5 = (f32[32,128]{1,0:T(8,128)S(1)}, f32[32,128]{1,0:T(8,128)}, u32[]{:S(2)}) copy-start(f32[32,128]{1,0:T(8,128)} %constant.85.clone.refs_4_.refs_5_) | copy-start | bytes 49156
  24.8 20.3 %collective-permute-start.3 = (s32[2,2,4,128]{3,2,1,0:T(4,128)S(1)}, s32[2,2,4,128]{3,2,1,0:T(4,128)S(1)}, u32[]{:S(2)}, u32[]{:S(2)}) collective-permute-start(s32[2,2,4,128]{3,2,1,0:T(4,128)S(1)} %get-tuple-element.19), channel_id=1, source_target_pairs={{0,8},{2,10},{4,12},{6,14},{8,0},{10,2},{12,4},{14,6},{1,9},{3,11}... | collective-permute-start | bytes 24584 | tf_op jit(solution)/shard_map/ppermute | solution.py:468
  26.9 18.2 %collective-permute-start.4 = (s32[2,2,4,128]{3,2,1,0:T(4,128)S(1)}, s32[2,2,4,128]{3,2,1,0:T(4,128)S(1)}, u32[]{:S(2)}, u32[]{:S(2)}) collective-permute-start(s32[2,2,4,128]{3,2,1,0:T(4,128)S(1)} %get-tuple-element.19), channel_id=1, source_target_pairs={{0,12},{2,14},{4,8},{6,10},{8,4},{10,6},{12,0},{14,2},{1,13},{3,15... | collective-permute-start | bytes 24584 | tf_op jit(solution)/shard_map/ppermute | solution.py:468
  45.1 21.0 %all-to-all-start = ((bf16[8,80,512]{2,1,0:T(8,128)(2,1)}), bf16[8,80,512]{2,1,0:T(8,128)(2,1)S(1)}, u32[]{:S(2)}, u32[]{:S(2)}) async-start(bf16[8,80,512]{2,1,0:T(8,128)(2,1)} %deal.3), calls=%async_computation | async-start | bytes 1310720 | tf_op jit(solution)/shard_map/all_to_all | solution.py:485
  73.2 11.7 %all-to-all-start.2 = ((f32[16,16,128]{2,1,0:T(8,128)}), f32[16,16,128]{2,1,0:T(8,128)S(1)}, u32[]{:S(2)}, u32[]{:S(2)}) async-start(f32[16,16,128]{2,1,0:T(8,128)} %bitcast.8), calls=%async_computation.2 | async-start | bytes 262144 | tf_op jit(solution)/shard_map/all_to_all | solution.py:496

commit v19 on v16

--- a/solution.py
+++ b/solution.py
@@ -421,7 +421,7 @@
         copy.start()
     for i in range(len(slabs)):
         arrive[i].wait()
-        turn_steps(blocks.at[i], rows, begin, end, turned.at[i])
+        turn_steps(blocks.at[i], rows.at[i % 2], begin, end, turned.at[i])
         leave[i].start()
     for copy in leave:
         copy.wait()
@@ -431,7 +431,7 @@
     return [
         pltpu.VMEM((number, own, steps, heights), BF16),
         pltpu.VMEM((number, count, heights), BF16),
-        pltpu.VMEM((heights // LANES, own * steps, LANES), F32),
+        pltpu.VMEM((2, heights // LANES, own * steps, LANES), F32),
         pltpu.SemaphoreType.DMA((2, number)),
     ]
 

time: 85.9 us -> 85.9 us (level)
  no operation moved by 1% of the time
where the time goes in v19:
time: 85.9 us; the launch traced here: 85.6 us
  waiting for transfers between devices  35.2 us (41%)
  Pallas kernels  27 us (31%)
  starting transfers between devices  21.9 us (25%)
  other arithmetic  0.96 us (1%)
    pallas_call x2, Pallas kernels, march(): return call(received, cells, *state, *totals, *consts, section)  21.1 us
    ppermute x3, waiting for transfers between devices, gather_small(): lax.ppermute(both, 'range', [(i, i ^ d) for i in range(sections)])  17.8 us
    all_to_all x1, waiting for transfers between devices, local(): lax.all_to_all(totals.reshape(owners, TILE_DEV, BINS), ('range', 'radial'...  7.68 us
    all_to_all x1, starting transfers between devices, local(): early = lax.all_to_all(dealt, 'range', 0, 0, tiled=True)  7.29 us
    ppermute x1, waiting for transfers between devices, gather_small(): lax.ppermute(pair, 'range', [(i, i ^ 1) for i in range(sections)])  5.34 us
    pallas_call x2, Pallas kernels, deal(): pl.pallas_call(kernel, out_shape=jax.ShapeDtypeStruct((sections, count, h...  5.3 us
    ppermute x3, starting transfers between devices, gather_small(): lax.ppermute(both, 'range', [(i, i ^ d) for i in range(sections)])  5.08 us
    all_to_all x1, starting transfers between devices, local(): lax.all_to_all(totals.reshape(owners, TILE_DEV, BINS), ('range', 'radial'...  3.74 us
  transfers between devices with their start and end apart: 8, of which 6 were waited for; matrix products, arithmetic and copies ran while one was open for 0% of the time, Pallas kernels for 20%

profile of v19, /device:TPU:0, one launch (start us, length us, event | category | flops | bytes accessed | tf_op | source)
XLA Modules:
  0.0 85.6 jit_solution(18360464813382462066)
XLA Ops:
  0.0 2.9 %deal.2 = bf16[8,176,512]{2,1,0:T(8,128)(2,1)} custom-call(bf16[128,16,512]{2,1,0:T(8,128)(2,1)} %levels.2), custom_call_target="tpu_custom_call" | custom-call | flops 1000000000 | bytes 4194304 | tf_op jit(solution)/shard_map/deal/pallas_call | solution.py:448
  2.9 0.0 copy-start.7
  3.0 0.0 copy-start.8
  3.0 7.3 %all-to-all-start.1 = ((bf16[8,176,512]{2,1,0:T(8,128)(2,1)}), bf16[8,176,512]{2,1,0:T(8,128)(2,1)S(1)}, u32[]{:S(2)}, u32[]{:S(2)}) async-start(bf16[8,176,512]{2,1,0:T(8,128)(2,1)} %deal.2), calls=%async_computation.1 | async-start | bytes 2883584 | tf_op jit(solution)/shard_map/all_to_all | solution.py:486
  10.3 0.0 copy-done.7
  10.3 0.0 copy-done.8
  10.3 0.1 collective-permute-start
  10.4 1.1 %collective-permute-done = s32[4,128]{1,0:T(4,128)S(1)} collective-permute-done((s32[4,128]{1,0:T(4,128)S(1)}, s32[4,128]{1,0:T(4,128)S(1)}, u32[]{:S(2)}, u32[]{:S(2)}) %collective-permute-start) | collective-permute-done | bytes 2080 | tf_op jit(solution)/shard_map/ppermute | solution.py:462
  11.5 0.0 copy-start.6
  11.5 0.0 copy-start
  11.6 0.0 copy-start.2
  11.6 0.0 copy-start.3
  11.6 2.1 %collective-permute-start.1 = (s32[2,4,128]{2,1,0:T(4,128)S(1)}, s32[2,4,128]{2,1,0:T(4,128)S(1)}, u32[]{:S(2)}, u32[]{:S(2)}) collective-permute-start(s32[2,4,128]{2,1,0:T(4,128)S(1)} %pad_add_fusion.1), channel_id=1, source_target_pairs={{0,2},{2,0},{4,6},{6,4},{8,10},{10,8},{12,14},{14,12},{1,3},{3,1},... | collective-permute-start | bytes 12296 | tf_op jit(solution)/shard_map/ppermute | solution.py:465
  13.7 2.4 %deal.3 = bf16[8,80,512]{2,1,0:T(8,128)(2,1)} custom-call(bf16[128,16,512]{2,1,0:T(8,128)(2,1)} %levels.2), custom_call_target="tpu_custom_call" | custom-call | flops 1000000000 | bytes 4194304 | tf_op jit(solution)/shard_map/deal/pallas_call | solution.py:448
  16.1 0.0 copy-done.6
  16.1 5.3 %collective-permute-done.1 = s32[2,4,128]{2,1,0:T(4,128)S(1)} collective-permute-done((s32[2,4,128]{2,1,0:T(4,128)S(1)}, s32[2,4,128]{2,1,0:T(4,128)S(1)}, u32[]{:S(2)}, u32[]{:S(2)}) %collective-permute-start.1) | collective-permute-done | bytes 4128 | tf_op jit(solution)/shard_map/ppermute | solution.py:465
  21.5 2.5 %collective-permute-start.2 = (s32[2,2,4,128]{3,2,1,0:T(4,128)S(1)}, s32[2,2,4,128]{3,2,1,0:T(4,128)S(1)}, u32[]{:S(2)}, u32[]{:S(2)}) collective-permute-start(s32[2,2,4,128]{3,2,1,0:T(4,128)S(1)} %get-tuple-element.19), channel_id=1, source_target_pairs={{0,4},{2,6},{4,0},{6,2},{8,12},{10,14},{12,8},{14,10},{1,5},{3,7},... | collective-permute-start | bytes 24584 | tf_op jit(solution)/shard_map/ppermute | solution.py:470
  24.0 0.0 copy-done
  24.0 0.0 copy-done.2
  24.0 0.0 copy-done.3
  24.0 0.6 launch.1.launched
  24.7 0.0 copy-start.1
  24.7 0.0 copy-start.4
  24.7 0.0 copy-start.5
  24.8 2.1 %collective-permute-start.3 = (s32[2,2,4,128]{3,2,1,0:T(4,128)S(1)}, s32[2,2,4,128]{3,2,1,0:T(4,128)S(1)}, u32[]{:S(2)}, u32[]{:S(2)}) collective-permute-start(s32[2,2,4,128]{3,2,1,0:T(4,128)S(1)} %get-tuple-element.19), channel_id=1, source_target_pairs={{0,8},{2,10},{4,12},{6,14},{8,0},{10,2},{12,4},{14,6},{1,9},{3,11}... | collective-permute-start | bytes 24584 | tf_op jit(solution)/shard_map/ppermute | solution.py:470
  26.9 0.4 collective-permute-start.4
  27.3 7.3 %collective-permute-done.2 = s32[2,2,4,128]{3,2,1,0:T(4,128)S(1)} collective-permute-done((s32[2,2,4,128]{3,2,1,0:T(4,128)S(1)}, s32[2,2,4,128]{3,2,1,0:T(4,128)S(1)}, u32[]{:S(2)}, u32[]{:S(2)}) %collective-permute-start.2) | collective-permute-done | bytes 8224 | tf_op jit(solution)/shard_map/ppermute | solution.py:470
  34.6 10.5 %collective-permute-done.3 = s32[2,2,4,128]{3,2,1,0:T(4,128)S(1)} collective-permute-done((s32[2,2,4,128]{3,2,1,0:T(4,128)S(1)}, s32[2,2,4,128]{3,2,1,0:T(4,128)S(1)}, u32[]{:S(2)}, u32[]{:S(2)}) %collective-permute-start.3) | collective-permute-done | bytes 8224 | tf_op jit(solution)/shard_map/ppermute | solution.py:470
  45.1 0.0 collective-permute-done.4
  45.1 0.0 all-to-all-done.1.levels
  45.1 3.6 %all-to-all-start = ((bf16[8,80,512]{2,1,0:T(8,128)(2,1)}), bf16[8,80,512]{2,1,0:T(8,128)(2,1)S(1)}, u32[]{:S(2)}, u32[]{:S(2)}) async-start(bf16[8,80,512]{2,1,0:T(8,128)(2,1)} %deal.3), calls=%async_computation | async-start | bytes 1310720 | tf_op jit(solution)/shard_map/all_to_all | solution.py:487
  48.8 0.0 copy-done.1
  48.8 0.0 copy-done.4
  48.8 0.0 copy-done.5
  48.8 14.0 %march.2 = (f32[256,128]{1,0:T(8,128)S(1)}, f32[2,32,8,128]{3,2,1,0:T(8,128)S(1)}, f32[1,2,32,8,128]{4,3,2,1,0:T(8,128)S(1)}) custom-call(bf16[8,176,512]{2,1,0:T(8,128)(2,1)S(1)} %all-to-all-done.1.levels, s32[8,4,128]{2,1,0:T(4,128)S(1)} %dynamic-slice_bitcast_fusion.cells, f32[2,32,8,128]{3,2,1,0:T(8,128)S(1)} %launch.1.launched, ...), custom_call_target="tpu_custom_call" | custom-call | flops 17600000000 | bytes 4194304 | tf_op jit(solution)/shard_map/march/pallas_call | solution.py:397
  62.8 3.3 %all-to-all-done.levels = bf16[8,80,512]{2,1,0:T(8,128)(2,1)S(1)} async-done(((bf16[8,80,512]{2,1,0:T(8,128)(2,1)}), bf16[8,80,512]{2,1,0:T(8,128)(2,1)S(1)}, u32[]{:S(2)}, u32[]{:S(2)}) %all-to-all-start) | async-done | bytes 655392 | tf_op jit(solution)/shard_map/all_to_all | solution.py:487
  66.2 7.0 %march.3 = f32[256,128]{1,0:T(8,128)} custom-call(bf16[8,80,512]{2,1,0:T(8,128)(2,1)S(1)} %all-to-all-done.levels, s32[8,4,128]{2,1,0:T(4,128)S(1)} %dynamic-slice_bitcast_fusion.cells, f32[2,32,8,128]{3,2,1,0:T(8,128)S(1)} %get-tuple-element.14.launched, f32[1,2,32,8,128]{4,3,2,1,0:T(8,128)S(1)} %get-tuple-element.15.entered, ...), custom_call_target="tpu_custom_call" | custom-call | flops 8000000000 | bytes 4194304 | tf_op jit(solution)/shard_map/march/pallas_call | solution.py:397
  73.2 3.7 %all-to-all-start.2 = ((f32[16,16,128]{2,1,0:T(8,128)}), f32[16,16,128]{2,1,0:T(8,128)S(1)}, u32[]{:S(2)}, u32[]{:S(2)}) async-start(f32[16,16,128]{2,1,0:T(8,128)} %bitcast.8), calls=%async_computation.2 | async-start | bytes 262144 | tf_op jit(solution)/shard_map/all_to_all | solution.py:498
  77.0 0.2 convert_reduce_fusion
  77.2 7.7 %all-to-all-done.2 = f32[16,16,128]{2,1,0:T(8,128)S(1)} async-done(((f32[16,16,128]{2,1,0:T(8,128)}), f32[16,16,128]{2,1,0:T(8,128)S(1)}, u32[]{:S(2)}, u32[]{:S(2)}) %all-to-all-start.2) | async-done | bytes 131104 | tf_op jit(solution)/shard_map/all_to_all | solution.py:498
  84.9 0.7 broadcast_divide_fusion
  (14 shorter events, 0.1 us)
Async XLA Ops:
  2.9 7.3 %copy-start.7 = (s32[128,2]{0,1:T(2,128)S(1)}, s32[128,2]{0,1:T(2,128)}, u32[]{:S(2)}) copy-start(s32[128,2]{0,1:T(2,128)} %param.13) | copy-start | bytes 3076
  3.0 7.3 %copy-start.8 = (s32[128,2]{0,1:T(2,128)S(1)}, s32[128,2]{0,1:T(2,128)}, u32[]{:S(2)}) copy-start(s32[128,2]{0,1:T(2,128)} %param.12) | copy-start | bytes 3076
  3.0 42.1 %all-to-all-start.1 = ((bf16[8,176,512]{2,1,0:T(8,128)(2,1)}), bf16[8,176,512]{2,1,0:T(8,128)(2,1)S(1)}, u32[]{:S(2)}, u32[]{:S(2)}) async-start(bf16[8,176,512]{2,1,0:T(8,128)(2,1)} %deal.2), calls=%async_computation.1 | async-start | bytes 2883584 | tf_op jit(solution)/shard_map/all_to_all | solution.py:486
  10.3 1.2 %collective-permute-start = (s32[4,128]{1,0:T(4,128)S(1)}, s32[4,128]{1,0:T(4,128)S(1)}, u32[]{:S(2)}, u32[]{:S(2)}) collective-permute-start(s32[4,128]{1,0:T(4,128)S(1)} %pad_add_fusion.2), channel_id=1, source_target_pairs={{0,1},{1,0},{2,3},{3,2},{4,5},{5,4},{6,7},{7,6},{8,9},{9,8},{10,11... | collective-permute-start | bytes 6152 | tf_op jit(solution)/shard_map/ppermute | solution.py:462
  11.5 4.5 %copy-start.6 = (f32[2,4096]{1,0:T(2,128)S(1)}, f32[2,4096]{1,0:T(2,128)}, u32[]{:S(2)}) copy-start(f32[2,4096]{1,0:T(2,128)} %param.11) | copy-start | bytes 98308
  11.5 12.5 %copy-start = (bf16[2,256,256]{2,1,0:T(8,128)(2,1)S(1)}, bf16[2,256,256]{2,1,0:T(8,128)(2,1)}, u32[]{:S(2)}) copy-start(bf16[2,256,256]{2,1,0:T(8,128)(2,1)} %constant.81.clone.weights.refs_0_.refs_1_) | copy-start | bytes 786436
  11.6 12.4 %copy-start.2 = (f32[2,32,128]{2,1,0:T(8,128)S(1)}, f32[2,32,128]{2,1,0:T(8,128)}, u32[]{:S(2)}) copy-start(f32[2,32,128]{2,1,0:T(8,128)} %constant.82.clone.twiddle_table.refs_1_.refs_2_) | copy-start | bytes 98308
  11.6 12.4 %copy-start.3 = (f32[2,32,128]{2,1,0:T(8,128)S(1)}, f32[2,32,128]{2,1,0:T(8,128)}, u32[]{:S(2)}) copy-start(f32[2,32,128]{2,1,0:T(8,128)} %constant.83.clone.spread_table.refs_2_.refs_3_) | copy-start | bytes 98308
  11.6 9.8 %collective-permute-start.1 = (s32[2,4,128]{2,1,0:T(4,128)S(1)}, s32[2,4,128]{2,1,0:T(4,128)S(1)}, u32[]{:S(2)}, u32[]{:S(2)}) collective-permute-start(s32[2,4,128]{2,1,0:T(4,128)S(1)} %pad_add_fusion.1), channel_id=1, source_target_pairs={{0,2},{2,0},{4,6},{6,4},{8,10},{10,8},{12,14},{14,12},{1,3},{3,1},... | collective-permute-start | bytes 12296 | tf_op jit(solution)/shard_map/ppermute | solution.py:465
  21.5 13.2 %collective-permute-start.2 = (s32[2,2,4,128]{3,2,1,0:T(4,128)S(1)}, s32[2,2,4,128]{3,2,1,0:T(4,128)S(1)}, u32[]{:S(2)}, u32[]{:S(2)}) collective-permute-start(s32[2,2,4,128]{3,2,1,0:T(4,128)S(1)} %get-tuple-element.19), channel_id=1, source_target_pairs={{0,4},{2,6},{4,0},{6,2},{8,12},{10,14},{12,8},{14,10},{1,5},{3,7},... | collective-permute-start | bytes 24584 | tf_op jit(solution)/shard_map/ppermute | solution.py:470
  24.7 24.1 %copy-start.1 = (bf16[256,128]{1,0:T(8,128)(2,1)S(1)}, bf16[256,128]{1,0:T(8,128)(2,1)}, u32[]{:S(2)}) copy-start(bf16[256,128]{1,0:T(8,128)(2,1)} %constant.86.clone.refs_5_.refs_6_) | copy-start | bytes 196612
  24.7 24.1 %copy-start.4 = (f32[32,128]{1,0:T(8,128)S(1)}, f32[32,128]{1,0:T(8,128)}, u32[]{:S(2)}) copy-start(f32[32,128]{1,0:T(8,128)} %constant.84.clone.refs_3_.refs_4_) | copy-start | bytes 49156
  24.7 24.1 %copy-start.5 = (f32[32,128]{1,0:T(8,128)S(1)}, f32[32,128]{1,0:T(8,128)}, u32[]{:S(2)}) copy-start(f32[32,128]{1,0:T(8,128)} %constant.85.clone.refs_4_.refs_5_) | copy-start | bytes 49156
  24.8 20.3 %collective-permute-start.3 = (s32[2,2,4,128]{3,2,1,0:T(4,128)S(1)}, s32[2,2,4,128]{3,2,1,0:T(4,128)S(1)}, u32[]{:S(2)}, u32[]{:S(2)}) collective-permute-start(s32[2,2,4,128]{3,2,1,0:T(4,128)S(1)} %get-tuple-element.19), channel_id=1, source_target_pairs={{0,8},{2,10},{4,12},{6,14},{8,0},{10,2},{12,4},{14,6},{1,9},{3,11}... | collective-permute-start | bytes 24584 | tf_op jit(solution)/shard_map/ppermute | solution.py:470
  26.9 18.2 %collective-permute-start.4 = (s32[2,2,4,128]{3,2,1,0:T(4,128)S(1)}, s32[2,2,4,128]{3,2,1,0:T(4,128)S(1)}, u32[]{:S(2)}, u32[]{:S(2)}) collective-permute-start(s32[2,2,4,128]{3,2,1,0:T(4,128)S(1)} %get-tuple-element.19), channel_id=1, source_target_pairs={{0,12},{2,14},{4,8},{6,10},{8,4},{10,6},{12,0},{14,2},{1,13},{3,15... | collective-permute-start | bytes 24584 | tf_op jit(solution)/shard_map/ppermute | solution.py:470
  45.1 21.0 %all-to-all-start = ((bf16[8,80,512]{2,1,0:T(8,128)(2,1)}), bf16[8,80,512]{2,1,0:T(8,128)(2,1)S(1)}, u32[]{:S(2)}, u32[]{:S(2)}) async-start(bf16[8,80,512]{2,1,0:T(8,128)(2,1)} %deal.3), calls=%async_computation | async-start | bytes 1310720 | tf_op jit(solution)/shard_map/all_to_all | solution.py:487
  73.2 11.7 %all-to-all-start.2 = ((f32[16,16,128]{2,1,0:T(8,128)}), f32[16,16,128]{2,1,0:T(8,128)S(1)}, u32[]{:S(2)}, u32[]{:S(2)}) async-start(f32[16,16,128]{2,1,0:T(8,128)} %bitcast.8), calls=%async_computation.2 | async-start | bytes 262144 | tf_op jit(solution)/shard_map/all_to_all | solution.py:498
